TPU v7x, 32 devices: a whole 2x2x4 slice. The times are simulated.
32 devices in a mesh: dom: 8 (over z, x), sub: 4 (over y, core).
Axes of the slice: x: 2, y: 2, z: 4, core: 2. Of those that a mesh axis runs over, the one named last changes fastest.
Arguments:
- solution: float32 [56, 9, 512], P(None, None, ('dom', 'sub')), may hold values from -1.5 to 1.5
- stiffness: float32 [3, 56, 56], replicated, may hold values from -0.75 to 0.75
- star_matrices: float32 [3, 9, 9, 512], P(None, None, None, ('dom', 'sub')), may hold values from -4.3 to 4.3
- face_restrict: float32 [4, 21, 56], replicated, may hold values from -0.75 to 0.75
- face_lift: float32 [4, 56, 21], replicated, may hold values from -1.25 to 1.25
- orient_maps: float32 [3, 21, 21], replicated, may hold values from -1.25 to 1.25
- flux_local: float32 [4, 9, 9, 512], P(None, None, None, ('dom', 'sub')), may hold values from -1 to 1
- flux_remote: float32 [4, 9, 9, 512], P(None, None, None, ('dom', 'sub')), may hold values from -1 to 1
- cluster_rate: int32 [512], P(('dom', 'sub')), may hold values from 1 to 2, as said below
- send_list: int32 [32, 4, 4], P(('dom', 'sub')), may hold values from 0 to 15, as said below
- neighbour_slot: int32 [4, 512], P(None, ('dom', 'sub')), may hold values from 0 to 31, as said below
- neighbour_face: int32 [4, 512], P(None, ('dom', 'sub')), may hold values from 0 to 3
- neighbour_turn: int32 [4, 512], P(None, ('dom', 'sub')), may hold values from 0 to 2
Outputs:
- new_solution: float32 [56, 9, 512], P(None, None, ('dom', 'sub'))
Inputs may be any that keep to these rules, and one draw needn't show every extreme that they name: `cluster_rate`: 1 is the slow cluster, 2 the fast one. Among the 16 elements of one device at most 8 are fast, and some device has exactly 8. `send_list`: row p of a device's lists names elements of that device sent toward neighbour p (0: previous along dom, 1: next along dom, 2: previous along sub, 3: next along sub, cyclically); the four rows of a device hold each of its 16 elements exactly once. In every row the fast elements stand before the slow ones, at most 2 of them, and some row has exactly 2. `neighbour_slot`: A value below 16 names an element of the same device; the value 16 + p * 4 + k names the k-th element received from neighbour p, and each of these 16 values appears exactly once among one device's faces.
All inputs are finite; a program needn't handle non-finite values.
Results may differ from a plain program's by a relative error of at most 0.0001.
Values sent between devices are 32-bit elements; how exact they have to be, the bound alone decides.
No kernel may reach another device: no remote copies, remote signals or barrier semaphores. Data moves between devices by JAX's collectives and lax.ppermute only.
A program may use at most 64 MiB of HBM per device.

v0:
```python
import math

import jax
import jax.numpy as jnp
from jax import lax
from jax.experimental import pallas as pl
from jax.experimental.pallas import tpu as pltpu
from jax.sharding import PartitionSpec as P

DERIVS = 6
LANES = 128
HALF = 64
ROWS = 8
F32 = jnp.float32
BF16 = jnp.bfloat16


def taylor_weight(lower, upper, degree):
    return (upper ** (degree + 1) - lower ** (degree + 1)) / math.factorial(degree + 1)


def weight_at(lower, upper, degree):
    result = jnp.float32(taylor_weight(lower, upper, 1))
    for option in range(2, DERIVS):
        result = jnp.where(degree == option, jnp.float32(taylor_weight(lower, upper, option)), result)
    return result


def split(values):
    high = values.astype(BF16)
    low = (values - high.astype(F32)).astype(BF16)
    return high, low


def stack_left(values):
    high, low = split(values)
    return jnp.concatenate([high, low, high], axis=1)


def stack_right(values):
    high, low = split(values)
    return jnp.concatenate([high, high, low], axis=0)


def product(left, right):
    return jnp.dot(left, right, preferred_element_type=F32)


def lane_index(shape):
    return lax.broadcasted_iota(jnp.int32, shape, len(shape) - 1)


def lower_half(shape):
    return lane_index(shape) < HALF


def swap_halves(values):
    return pltpu.roll(values, HALF, values.ndim - 1)


def pack(values_ref, packed_ref):
    modes = values_ref.shape[2]
    packed_ref[...] = jnp.zeros(packed_ref.shape, F32)
    packed_ref[:, :, 0:modes] = values_ref[:, 0:ROWS, :]
    packed_ref[:, :, HALF : HALF + modes] = values_ref[:, ROWS : 2 * ROWS, :]


def turn_matrices(source_ref, work_ref):
    fields, kinds, elements = source_ref.shape[0], source_ref.shape[2], source_ref.shape[3]
    tiles = []
    for pair in range((fields + 1) // 2):
        for row in range(2 * pair, min(2 * pair + 2, fields)):
            for col in range(fields):
                at = (row % 2) * HALF + col * 4
                work_ref[pair, at : at + kinds, 0:elements] = source_ref[row, col]
        tiles.append(work_ref[pair].T[0:elements, :])
    return tiles


def spread(tile, index):
    return jnp.take_along_axis(tile, index, axis=1, mode="promise_in_bounds")


def star_coefficients(star_ref, work_ref, star_out):
    fields, kinds = star_ref.shape[0], star_ref.shape[2]
    tiles = turn_matrices(star_ref, work_ref)
    lanes = lane_index((ROWS, LANES))
    base = (lanes // HALF) * HALF
    lower = lanes < HALF
    for row in range(fields):
        first, second = tiles[row // 2][0:ROWS], tiles[row // 2][ROWS : 2 * ROWS]
        if row % 2 == 0:
            both = jnp.where(lower, first, swap_halves(second))
        else:
            both = jnp.where(lower, swap_halves(first), second)
        for kind in range(kinds):
            for col in range(fields):
                star_out[(row * kinds + kind) * fields + col] = spread(both, base + (col * 4 + kind))


def star_mix(columns, star_ref, fields, kinds):
    sums = [None] * fields
    for row in range(fields):
        for kind in range(kinds):
            part = columns[row * ROWS : (row + 1) * ROWS, kind * LANES : (kind + 1) * LANES]
            for col in range(fields):
                term = star_ref[(row * kinds + kind) * fields + col] * part
                sums[col] = term if sums[col] is None else sums[col] + term
    return jnp.concatenate(sums, axis=0)


def stiffness_blocks(stiffness_ref, block_ref):
    kinds, modes = stiffness_ref.shape[0], stiffness_ref.shape[1]
    block_ref[...] = jnp.zeros(block_ref.shape, F32)
    for kind in range(kinds):
        block_ref[kind, 0:modes, 0:modes] = stiffness_ref[kind]
        block_ref[kind, HALF : HALF + modes, HALF : HALF + modes] = stiffness_ref[kind]


def derive_operator(block_ref):
    return jnp.concatenate([-block_ref[kind].T for kind in range(block_ref.shape[0])], axis=1)


def predict_kernel(
    solution_ref, stiffness_ref, star_ref, send_ref,
    early_out, late_out, to_before_dom, to_after_dom, to_before_sub, to_after_sub,
    packed_ref, work_ref, coef_ref, block_ref, derive_ref, early_rows, late_rows,
):
    fields, kinds = star_ref.shape[0], star_ref.shape[2]
    pairs = (fields + 1) // 2
    pack(solution_ref, packed_ref)
    stiffness_blocks(stiffness_ref, block_ref)
    derive_ref[...] = stack_right(derive_operator(block_ref))
    star_coefficients(star_ref, work_ref, coef_ref)
    start = packed_ref[...].reshape(fields * ROWS, LANES)

    def step(degree, carry):
        current, early, late = carry
        current = star_mix(product(stack_left(current), derive_ref[...]), coef_ref, fields, kinds)
        early = early + weight_at(0.0, 0.5, degree) * current
        late = late + weight_at(0.5, 1.0, degree) * current
        return current, early, late

    _, early, late = lax.fori_loop(
        1, DERIVS, step, (start, taylor_weight(0.0, 0.5, 0) * start, taylor_weight(0.5, 1.0, 0) * start)
    )
    early_out[...] = early.reshape(fields, ROWS, LANES)
    late_out[...] = late.reshape(fields, ROWS, LANES)
    rows_by_pair(early, early_rows, fields)
    rows_by_pair(late, late_rows, fields)
    sends = send_ref.shape[2]
    fast = sends // 2
    for side, out in enumerate((to_before_dom, to_after_dom, to_before_sub, to_after_sub)):
        out[...] = jnp.zeros(out.shape, F32)
        for place in range(sends):
            element = send_ref[0, side, place]
            for pair in range(pairs):
                row = pair * sends + place
                out[row : row + 1, :] = early_rows[pair, pl.ds(element, 1), :]
            if place >= fast:
                for pair in range(pairs):
                    row = pairs * sends + pair * fast + place - fast
                    out[row : row + 1, :] = late_rows[pair, pl.ds(element, 1), :]


def rows_by_pair(packed, out_ref, fields):
    lower = lower_half((ROWS, LANES))
    for pair in range((fields + 1) // 2):
        even = packed[2 * pair * ROWS : (2 * pair + 1) * ROWS]
        odd = jnp.zeros_like(even)
        if 2 * pair + 1 < fields:
            odd = packed[(2 * pair + 1) * ROWS : (2 * pair + 2) * ROWS]
        out_ref[pair, 0:ROWS, :] = jnp.where(lower, even, swap_halves(odd))
        out_ref[pair, ROWS : 2 * ROWS, :] = jnp.where(lower, swap_halves(even), odd)


def flux_local_coefficients(flux_ref, work_ref, out_ref):
    fields = flux_ref.shape[0]
    tiles = turn_matrices(flux_ref, work_ref)
    lanes = lane_index((ROWS, LANES))
    for row in range(fields):
        for col in range(fields):
            index = (row % 2) * HALF + col * 4 + lanes % 4
            for half in range(2):
                tile = tiles[row // 2][half * ROWS : (half + 1) * ROWS]
                out_ref[row * fields + col, half] = spread(tile, index)


def flux_remote_coefficients(flux_ref, work_ref, out_ref):
    fields, faces = flux_ref.shape[0], flux_ref.shape[2]
    pairs = (fields + 1) // 2
    tiles = turn_matrices(flux_ref, work_ref)
    lanes = lane_index((ROWS, LANES))
    base = (lanes // HALF) * HALF
    for pair in range(pairs):
        for face in range(faces):
            for col in range(fields):
                at = (face * pairs + pair) * fields + col
                for half in range(2):
                    tile = tiles[pair][half * ROWS : (half + 1) * ROWS]
                    out_ref[at, half * ROWS : (half + 1) * ROWS, :] = spread(tile, base + (col * 4 + face))


def local_terms(packed, star_ref, flux_ref, volume_ref, trace_ref, lift_ref, fields, kinds):
    left = stack_left(packed)
    volume = star_mix(product(left, volume_ref[...]), star_ref, fields, kinds)
    traces = product(left, trace_ref[...])
    sums = []
    for col in range(fields):
        halves = []
        for half in range(2):
            total = None
            for row in range(fields):
                part = traces[row * ROWS : (row + 1) * ROWS, half * LANES : (half + 1) * LANES]
                term = flux_ref[row * fields + col, half] * part
                total = term if total is None else total + term
            halves.append(total)
        sums.append(jnp.concatenate(halves, axis=1))
    return volume + product(stack_left(jnp.concatenate(sums, axis=0)), lift_ref[...])


def prepare_kernel(
    solution_ref, early_ref, stiffness_ref, star_ref, restrict_ref, lift_ref, orient_ref, flux_local_ref,
    flux_remote_ref, slot_ref, face_ref, turn_ref,
    base_out, star_out, local_out, remote_out, derive_out, volume_out, trace_out, local_lift_out, compose_out,
    remote_lift_out, choose_out, mask_out,
    packed_ref, work_ref, block_ref, wide_ref, face_work_ref, orient_work_ref, code_ref,
):
    fields, kinds = star_ref.shape[0], star_ref.shape[2]
    face_modes, faces, modes = restrict_ref.shape
    turns = orient_ref.shape[0]
    work_ref[...] = jnp.zeros(work_ref.shape, F32)
    star_coefficients(star_ref, work_ref, star_out)
    flux_local_coefficients(flux_local_ref, work_ref, local_out)
    flux_remote_coefficients(flux_remote_ref, work_ref, remote_out)

    stiffness_blocks(stiffness_ref, block_ref)
    derive_out[...] = stack_right(derive_operator(block_ref))
    volume_out[...] = stack_right(jnp.concatenate([block_ref[kind] for kind in range(kinds)], axis=1))

    wide_ref[...] = jnp.zeros(wide_ref.shape, F32)
    for mode in range(face_modes):
        at = mode * faces
        wide_ref[at : at + faces, 0:modes] = restrict_ref[mode]
        wide_ref[LANES + at : LANES + at + faces, HALF : HALF + modes] = restrict_ref[mode]
    trace_out[...] = stack_right(wide_ref[...].T)
    for mode in range(face_modes):
        at = mode * faces
        wide_ref[at : at + faces, 0:modes] = -lift_ref[mode]
        wide_ref[LANES + at : LANES + at + faces, HALF : HALF + modes] = -lift_ref[mode]
    local_lift_out[...] = stack_right(wide_ref[...])

    face_work_ref[...] = jnp.zeros(face_work_ref.shape, F32)
    orient_work_ref[...] = jnp.zeros(orient_work_ref.shape, F32)
    for turn in range(turns):
        orient_work_ref[turn * face_modes : (turn + 1) * face_modes, 0:face_modes] = orient_ref[turn]
    for face in range(faces):
        face_work_ref[0:face_modes, face * LANES : face * LANES + modes] = restrict_ref[:, face, :]
        face_work_ref[0:face_modes, face * LANES + HALF : face * LANES + HALF + modes] = restrict_ref[:, face, :]
    composed = jnp.dot(
        orient_work_ref[...], face_work_ref[...], precision=lax.Precision.HIGHEST, preferred_element_type=F32
    )
    stacked = jnp.concatenate([composed[:, face * LANES : (face + 1) * LANES] for face in range(faces)], axis=0)
    compose_out[...] = stack_right(stacked.T)
    for face in range(faces):
        orient_work_ref[...] = jnp.zeros(orient_work_ref.shape, F32)
        for turn in range(turns):
            rows = slice(turn * face_modes, (turn + 1) * face_modes)
            orient_work_ref[rows, 0:modes] = -lift_ref[:, face, :]
            orient_work_ref[rows, HALF : HALF + modes] = -lift_ref[:, face, :]
        high, low = split(orient_work_ref[...])
        remote_lift_out[face, 0] = high
        remote_lift_out[face, 1] = low

    elements = slot_ref.shape[1]
    code_ref[...] = jnp.zeros(code_ref.shape, F32)
    code_ref[0:faces, 0:elements] = slot_ref[...].astype(F32)
    code_ref[faces : 2 * faces, 0:elements] = (face_ref[...] * turns + turn_ref[...]).astype(F32)
    codes = code_ref[...].T[0:elements, :]
    sources = choose_out.shape[1] // 2
    source_lane = (lane_index((elements, 2 * sources)) % sources).astype(F32)
    lanes = lane_index((elements, mask_out.shape[1]))
    in_face = lanes % HALF
    lane_code = jnp.where(in_face < turns * face_modes, (lanes // HALF) * turns + in_face // face_modes, -1)
    lane_code = lane_code.astype(F32)
    picks, masks = [], []
    for face in range(faces):
        picks.append(jnp.where(codes[:, face : face + 1] == source_lane, 1.0, 0.0))
        masks.append(jnp.where(codes[:, faces + face : faces + face + 1] == lane_code, 1.0, 0.0))
    choose_out[...] = jnp.concatenate(picks, axis=0).astype(BF16)
    mask_out[...] = jnp.concatenate(masks, axis=0)

    pack(solution_ref, packed_ref)
    early = early_ref[...].reshape(fields * ROWS, LANES)
    terms = local_terms(early, star_out, local_out, volume_out, trace_out, local_lift_out, fields, kinds)
    base_out[...] = packed_ref[...] + terms.reshape(fields, ROWS, LANES)


def remote_terms(rows_ref, remote_ref, compose_ref, lift_ref, choose_ref, mask_ref, fields):
    pairs = rows_ref.shape[0]
    faces = lift_ref.shape[0]
    elements = choose_ref.shape[0] // faces
    sources = jnp.concatenate([rows_ref[pair] for pair in range(pairs)], axis=1)
    gathered = product(choose_ref[...], jnp.concatenate(split(sources), axis=0))
    result = None
    for face in range(faces):
        sums = []
        for col in range(fields):
            total = None
            for pair in range(pairs):
                part = gathered[face * elements : (face + 1) * elements, pair * LANES : (pair + 1) * LANES]
                term = remote_ref[(face * pairs + pair) * fields + col] * part
                total = term if total is None else total + term
            sums.append(total)
        turned = product(stack_left(jnp.concatenate(sums, axis=0)), compose_ref[...])
        mask = mask_ref[face * elements : (face + 1) * elements, :]
        chosen = turned.reshape(fields, elements, turned.shape[1]) * mask[None]
        left = stack_left(chosen.reshape(turned.shape))
        copies = turned.shape[1] // lift_ref.shape[2]
        high, low = lift_ref[face, 0], lift_ref[face, 1]
        right = jnp.concatenate([high] * (2 * copies) + [low] * copies, axis=0)
        lifted = product(left, right)
        result = lifted if result is None else result + lifted
    result = result.reshape(fields, 2, ROWS, LANES)
    return jnp.where(lower_half((ROWS, LANES))[None], result[:, 0], result[:, 1])


def middle_kernel(
    base_ref, early_ref, late_ref, star_ref, remote_ref, derive_ref, compose_ref, lift_ref, choose_ref, mask_ref,
    rate_ref, send_ref, from_before_dom, from_after_dom, from_before_sub, from_after_sub,
    middle_out, late_out, to_before_dom, to_after_dom, to_before_sub, to_after_sub,
    rows_ref, late_rows,
):
    fields = base_ref.shape[0]
    kinds = star_ref.shape[0] // (fields * fields)
    pairs = rows_ref.shape[0]
    sends = send_ref.shape[2]
    fast = sends // 2
    elements = 2 * ROWS
    rows_by_pair(early_ref[...].reshape(fields * ROWS, LANES), rows_ref, fields)
    for side, arrived in enumerate((from_before_dom, from_after_dom, from_before_sub, from_after_sub)):
        at = elements + side * sends
        for pair in range(pairs):
            rows_ref[pair, at : at + sends, :] = arrived[pair * sends : (pair + 1) * sends, :]
    middle = base_ref[...] + remote_terms(
        rows_ref, remote_ref, compose_ref, lift_ref, choose_ref, mask_ref, fields
    )
    middle_out[...] = middle
    start = middle.reshape(fields * ROWS, LANES)

    def step(degree, carry):
        current, early = carry
        current = star_mix(product(stack_left(current), derive_ref[...]), star_ref, fields, kinds)
        return current, early + weight_at(0.0, 0.5, degree) * current

    _, restart = lax.fori_loop(1, DERIVS, step, (start, taylor_weight(0.0, 0.5, 0) * start))
    sublane = lax.broadcasted_iota(jnp.int32, (ROWS, LANES), 0)
    lower = lower_half((ROWS, LANES))
    is_fast = jnp.zeros((ROWS, LANES), jnp.int32)
    for element in range(elements):
        here = (sublane == element % ROWS) & (lower if element < ROWS else jnp.logical_not(lower))
        is_fast = jnp.where(here, rate_ref[element], is_fast)
    late = jnp.where((is_fast == 2)[None], restart.reshape(fields, ROWS, LANES), late_ref[...])
    late_out[...] = late
    rows_by_pair(late.reshape(fields * ROWS, LANES), late_rows, fields)
    for side, out in enumerate((to_before_dom, to_after_dom, to_before_sub, to_after_sub)):
        out[...] = jnp.zeros(out.shape, F32)
        for place in range(fast):
            element = send_ref[0, side, place]
            for pair in range(pairs):
                row = pair * fast + place
                out[row : row + 1, :] = late_rows[pair, pl.ds(element, 1), :]


def local_kernel(middle_ref, late_ref, star_ref, flux_ref, volume_ref, trace_ref, lift_ref, base_out):
    fields = middle_ref.shape[0]
    kinds = star_ref.shape[0] // (fields * fields)
    late = late_ref[...].reshape(fields * ROWS, LANES)
    terms = local_terms(late, star_ref, flux_ref, volume_ref, trace_ref, lift_ref, fields, kinds)
    base_out[...] = middle_ref[...] + terms.reshape(fields, ROWS, LANES)


def final_kernel(
    base_ref, late_ref, remote_ref, compose_ref, lift_ref, choose_ref, mask_ref,
    first_before_dom, first_after_dom, first_before_sub, first_after_sub,
    second_before_dom, second_after_dom, second_before_sub, second_after_sub,
    result_out, rows_ref,
):
    fields = base_ref.shape[0]
    modes = result_out.shape[2]
    pairs = rows_ref.shape[0]
    elements = 2 * ROWS
    sends = (rows_ref.shape[1] - elements) // 4
    fast = sends // 2
    rows_by_pair(late_ref[...].reshape(fields * ROWS, LANES), rows_ref, fields)
    firsts = (first_before_dom, first_after_dom, first_before_sub, first_after_sub)
    seconds = (second_before_dom, second_after_dom, second_before_sub, second_after_sub)
    for side, (first, second) in enumerate(zip(firsts, seconds)):
        at = elements + side * sends
        for pair in range(pairs):
            rows_ref[pair, at : at + fast, :] = second[pair * fast : (pair + 1) * fast, :]
            row = pairs * sends + pair * fast
            rows_ref[pair, at + fast : at + sends, :] = first[row : row + fast, :]
    result = base_ref[...] + remote_terms(
        rows_ref, remote_ref, compose_ref, lift_ref, choose_ref, mask_ref, fields
    )
    result_out[:, 0:ROWS, :] = result[:, :, 0:modes]
    result_out[:, ROWS : 2 * ROWS, :] = result[:, :, HALF : HALF + modes]


VMEM = pl.BlockSpec(memory_space=pltpu.VMEM)
SMEM = pl.BlockSpec(memory_space=pltpu.SMEM)


def call(kernel, ins, outs, scratch, args, name, flops):
    shapes = [jax.ShapeDtypeStruct(shape, dtype) for shape, dtype in outs]
    return pl.pallas_call(
        kernel,
        out_shape=shapes,
        in_specs=ins,
        out_specs=[VMEM] * len(outs),
        scratch_shapes=[pltpu.VMEM(shape, dtype) for shape, dtype in scratch],
        compiler_params=pltpu.CompilerParams(vmem_limit_bytes=16 * 1024 * 1024),
        cost_estimate=pl.CostEstimate(flops=flops, bytes_accessed=4_000_000, transcendentals=0),
        name=name,
    )(*args)


def exchange(to_before_dom, to_after_dom, to_before_sub, to_after_sub):
    arrived = []
    for axis, to_before, to_after in (("dom", to_before_dom, to_after_dom), ("sub", to_before_sub, to_after_sub)):
        size = lax.axis_size(axis)
        up = [(i, (i + 1) % size) for i in range(size)]
        down = [(j, i) for i, j in up]
        arrived.append(lax.ppermute(to_after, axis, up))
        arrived.append(lax.ppermute(to_before, axis, down))
    return arrived


def up_to(count, multiple):
    return -(-count // multiple) * multiple


def local(
    solution, stiffness, star_matrices, face_restrict, face_lift, orient_maps, flux_local, flux_remote,
    cluster_rate, send_list, neighbour_slot, neighbour_face, neighbour_turn,
):
    fields, elements = solution.shape[1], solution.shape[2]
    kinds = stiffness.shape[0]
    faces = face_restrict.shape[0]
    sides, sends = send_list.shape[1], send_list.shape[2]
    fast = sends // 2
    pairs = (fields + 1) // 2
    assert elements == 2 * ROWS and solution.shape[0] <= HALF
    values = jnp.transpose(solution, (1, 2, 0))
    star = jnp.transpose(star_matrices, (1, 2, 0, 3))
    local_part = jnp.transpose(flux_local, (1, 2, 0, 3))
    remote_part = jnp.transpose(flux_remote, (1, 2, 0, 3))
    restrict = jnp.transpose(face_restrict, (1, 0, 2))
    lift = jnp.transpose(face_lift, (2, 0, 1))

    packed = (fields, ROWS, LANES)
    first_shape = (up_to(pairs * (sends + fast), ROWS), LANES)
    second_shape = (up_to(pairs * fast, ROWS), LANES)
    work = (pairs, LANES, LANES)
    star_shape = (fields * fields * kinds, ROWS, LANES)
    combos = faces * HALF
    sources = elements + sides * sends

    early, late, *outgoing = call(
        predict_kernel,
        [VMEM, VMEM, VMEM, SMEM],
        [(packed, F32)] * 2 + [(first_shape, F32)] * sides,
        [
            (packed, F32), (work, F32), (star_shape, F32), ((kinds, LANES, LANES), F32),
            ((3 * LANES, kinds * LANES), BF16), ((pairs, elements, LANES), F32), ((pairs, elements, LANES), F32),
        ],
        (values, stiffness, star, send_list),
        "predict", 100_000_000,
    )
    first = exchange(*outgoing)
    (
        base, star_coef, local_coef, remote_coef, derive_op, volume_op, trace_op, local_lift, compose_op, remote_lift,
        choose, mask,
    ) = call(
        prepare_kernel,
        [VMEM] * 12,
        [
            (packed, F32), (star_shape, F32), ((fields * fields, 2, ROWS, LANES), F32),
            ((faces * pairs * fields, elements, LANES), F32),
            ((3 * LANES, kinds * LANES), BF16), ((3 * LANES, kinds * LANES), BF16), ((3 * LANES, 2 * LANES), BF16),
            ((6 * LANES, LANES), BF16), ((3 * LANES, combos), BF16), ((faces, 2, HALF, LANES), BF16),
            ((faces * elements, 2 * sources), BF16), ((faces * elements, combos), F32),
        ],
        [
            (packed, F32), (work, F32), ((kinds, LANES, LANES), F32), ((2 * LANES, LANES), F32),
            ((LANES, faces * LANES), F32), ((HALF, LANES), F32), ((LANES, LANES), F32),
        ],
        (
            values, early, stiffness, star, restrict, lift, orient_maps, local_part, remote_part,
            neighbour_slot, neighbour_face, neighbour_turn,
        ),
        "prepare", 200_000_000,
    )
    middle, late_value, *outgoing = call(
        middle_kernel,
        [VMEM] * 10 + [SMEM] * 2 + [VMEM] * 4,
        [(packed, F32)] * 2 + [(second_shape, F32)] * sides,
        [((pairs, sources, LANES), F32), ((pairs, elements, LANES), F32)],
        (
            base, early, late, star_coef, remote_coef, derive_op, compose_op, remote_lift, choose, mask,
            cluster_rate, send_list, *first,
        ),
        "middle", 200_000_000,
    )
    second = exchange(*outgoing)
    (base,) = call(
        local_kernel,
        [VMEM] * 7,
        [(packed, F32)],
        [],
        (middle, late_value, star_coef, local_coef, volume_op, trace_op, local_lift),
        "local_late", 200_000_000,
    )
    (result,) = call(
        final_kernel,
        [VMEM] * 15,
        [(values.shape, F32)],
        [((pairs, sources, LANES), F32)],
        (base, late_value, remote_coef, compose_op, remote_lift, choose, mask, *first, *second),
        "final", 200_000_000,
    )
    return jnp.transpose(result, (2, 0, 1))


def solution(mesh):
    placed = (
        P(None, None, ("dom", "sub")),
        P(),
        P(None, None, None, ("dom", "sub")),
        P(),
        P(),
        P(),
        P(None, None, None, ("dom", "sub")),
        P(None, None, None, ("dom", "sub")),
        P(("dom", "sub")),
        P(("dom", "sub"), None, None),
        P(None, ("dom", "sub")),
        P(None, ("dom", "sub")),
        P(None, ("dom", "sub")),
    )
    return jax.shard_map(
        local, mesh=mesh, in_specs=placed, out_specs=P(None, None, ("dom", "sub")), check_vma=False
    )
```

profile of v0, /device:TPU:1, one launch (start us, length us, event | category | flops | bytes accessed | tf_op | source)
XLA Modules:
  0.0 39.6 jit_solution(7793290996228462839)
XLA Ops:
  0.0 0.0 copy-start
  0.0 0.9 %copy-done = f32[3,9,9,16]{3,0,2,1:T(4,128)S(1)} copy-done((f32[3,9,9,16]{3,0,2,1:T(4,128)S(1)}, f32[3,9,9,16]{3,0,2,1:T(4,128)}, u32[]{:S(2)}) %copy-start) | copy-done | bytes 15576
  0.9 0.0 copy-start.3
  0.9 0.9 %copy-done.3 = f32[3,56,56]{2,1,0:T(8,128)S(1)} copy-done((f32[3,56,56]{2,1,0:T(8,128)S(1)}, f32[3,56,56]{2,1,0:T(8,128)}, u32[]{:S(2)}) %copy-start.3) | copy-done | bytes 37656
  1.8 0.0 copy-start.4
  1.8 0.9 %copy-done.4 = f32[56,9,16]{0,2,1:T(8,128)S(1)} copy-done((f32[56,9,16]{0,2,1:T(8,128)S(1)}, f32[56,9,16]{0,2,1:T(8,128)}, u32[]{:S(2)}) %copy-start.4) | copy-done | bytes 32280
  2.7 0.0 copy-start.11
  2.7 0.7 %copy-done.11 = s32[1,4,4]{2,1,0:T(4,128)S(1)} copy-done((s32[1,4,4]{2,1,0:T(4,128)S(1)}, s32[1,4,4]{2,1,0:T(4,128)}, u32[]{:S(2)}) %copy-start.11) | copy-done | bytes 88
  3.4 3.3 %predict.1 = (f32[9,8,128]{2,1,0:T(8,128)S(1)}, f32[9,8,128]{2,1,0:T(8,128)S(1)}, f32[32,128]{1,0:T(8,128)S(1)}, f32[32,128]{1,0:T(8,128)S(1)}, f32[32,128]{1,0:T(8,128)S(1)}, /*index=5*/f32[32,128]{1,0:T(8,128)S(1)}) custom-call(f32[9,16,56]{2,1,0:T(8,128)S(1)} %bitcast.11, f32[3,56,56]{2,1,0:T(8,128)S(1)} %copy-done.3, f32[9,9,3,16]{3,2,1,0:T(4,128)S(1)} %bitcast.7, ...), custom_call_target="tpu_custom_call" | custom-call | flops 100000000 | bytes 4000000 | tf_op jit(solution)/shard_map/predict/pallas_call | solution.py:417
  6.7 2.1 %collective-permute-start = (f32[32,128]{1,0:T(8,128)S(1)}, f32[32,128]{1,0:T(8,128)S(1)}, u32[]{:S(2)}, u32[]{:S(2)}) collective-permute-start(f32[32,128]{1,0:T(8,128)S(1)} %get-tuple-element.39), channel_id=1, source_target_pairs={{0,4},{4,8},{8,12},{12,16},{16,20},{20,24},{24,28},{28,0},{1,5},{5... | collective-permute-start | bytes 49160 | tf_op jit(solution)/shard_map/ppermute | solution.py:435
  8.7 3.1 %collective-permute-start.1 = (f32[32,128]{1,0:T(8,128)S(1)}, f32[32,128]{1,0:T(8,128)S(1)}, u32[]{:S(2)}, u32[]{:S(2)}) collective-permute-start(f32[32,128]{1,0:T(8,128)S(1)} %get-tuple-element.40), channel_id=1, source_target_pairs={{4,0},{8,4},{12,8},{16,12},{20,16},{24,20},{28,24},{0,28},{5,1},{9... | collective-permute-start | bytes 49160 | tf_op jit(solution)/shard_map/ppermute | solution.py:436
  11.9 2.2 %collective-permute-start.2 = (f32[32,128]{1,0:T(8,128)S(1)}, f32[32,128]{1,0:T(8,128)S(1)}, u32[]{:S(2)}, u32[]{:S(2)}) collective-permute-start(f32[32,128]{1,0:T(8,128)S(1)} %get-tuple-element.41), channel_id=1, source_target_pairs={{0,1},{1,2},{2,3},{3,0},{4,5},{5,6},{6,7},{7,4},{8,9},{9,10},{10,1... | collective-permute-start | bytes 49160 | tf_op jit(solution)/shard_map/ppermute | solution.py:435
  14.1 0.0 collective-permute-start.3
  14.1 0.0 copy-start.1
  14.1 0.9 %copy-done.1 = f32[4,9,9,16]{3,0,2,1:T(4,128)S(1)} copy-done((f32[4,9,9,16]{3,0,2,1:T(4,128)S(1)}, f32[4,9,9,16]{3,0,2,1:T(4,128)}, u32[]{:S(2)}) %copy-start.1) | copy-done | bytes 20760
  15.0 0.0 copy-start.2
  15.0 0.9 %copy-done.2 = f32[4,9,9,16]{3,0,2,1:T(4,128)S(1)} copy-done((f32[4,9,9,16]{3,0,2,1:T(4,128)S(1)}, f32[4,9,9,16]{3,0,2,1:T(4,128)}, u32[]{:S(2)}) %copy-start.2) | copy-done | bytes 20760
  15.9 0.0 copy-start.5
  15.9 0.8 %copy-done.5 = f32[4,21,56]{2,0,1:T(4,128)S(1)} copy-done((f32[4,21,56]{2,0,1:T(4,128)S(1)}, f32[4,21,56]{2,0,1:T(4,128)}, u32[]{:S(2)}) %copy-start.5) | copy-done | bytes 18840
  16.7 0.0 copy-start.6
  16.7 0.8 %copy-done.6 = f32[4,56,21]{1,0,2:T(4,128)S(1)} copy-done((f32[4,56,21]{1,0,2:T(4,128)S(1)}, f32[4,56,21]{1,0,2:T(4,128)}, u32[]{:S(2)}) %copy-start.6) | copy-done | bytes 18840
  17.5 0.0 copy-start.7
  17.5 0.8 %copy-done.7 = f32[3,21,21]{2,1,0:T(8,128)S(1)} copy-done((f32[3,21,21]{2,1,0:T(8,128)S(1)}, f32[3,21,21]{2,1,0:T(8,128)}, u32[]{:S(2)}) %copy-start.7) | copy-done | bytes 5316
  18.2 0.0 copy-start.8
  18.2 0.7 %copy-done.8 = s32[4,16]{1,0:T(4,128)S(1)} copy-done((s32[4,16]{1,0:T(4,128)S(1)}, s32[4,16]{1,0:T(4,128)}, u32[]{:S(2)}) %copy-start.8) | copy-done | bytes 280
  18.9 0.0 copy-start.9
  18.9 0.7 %copy-done.9 = s32[4,16]{1,0:T(4,128)S(1)} copy-done((s32[4,16]{1,0:T(4,128)S(1)}, s32[4,16]{1,0:T(4,128)}, u32[]{:S(2)}) %copy-start.9) | copy-done | bytes 280
  19.6 0.0 copy-start.10
  19.6 0.7 %copy-done.10 = s32[4,16]{1,0:T(4,128)S(1)} copy-done((s32[4,16]{1,0:T(4,128)S(1)}, s32[4,16]{1,0:T(4,128)}, u32[]{:S(2)}) %copy-start.10) | copy-done | bytes 280
  20.3 3.3 %prepare.1 = (f32[9,8,128]{2,1,0:T(8,128)S(1)}, f32[243,8,128]{2,1,0:T(8,128)S(1)}, f32[81,2,8,128]{3,2,1,0:T(8,128)S(1)}, f32[180,16,128]{2,1,0:T(8,128)S(1)}, ...) custom-call(f32[9,16,56]{2,1,0:T(8,128)S(1)} %bitcast.12, ...), custom_call_target="tpu_custom_call" | custom-call | flops 200000000 | bytes 4000000 | tf_op jit(solution)/shard_map/prepare/pallas_call | solution.py:417
  23.6 0.0 collective-permute-done.from_before_dom.first_before_dom
  23.6 0.0 collective-permute-done.1.from_after_dom.first_after_dom
  23.6 0.0 collective-permute-done.2.from_before_sub.first_before_sub
  23.6 0.0 collective-permute-done.3.from_after_sub.first_after_sub
  23.6 0.0 copy-start.12
  23.6 0.7 %copy-done.12 = s32[1,4,4]{2,1,0:T(4,128)S(1)} copy-done((s32[1,4,4]{2,1,0:T(4,128)S(1)}, s32[1,4,4]{2,1,0:T(4,128)}, u32[]{:S(2)}) %copy-start.12) | copy-done | bytes 88
  24.3 0.0 copy-start.13
  24.3 0.7 %copy-done.13 = s32[16]{0:T(128)S(1)} copy-done((s32[16]{0:T(128)S(1)}, s32[16]{0:T(128)}, u32[]{:S(2)}) %copy-start.13) | copy-done | bytes 88
  25.0 3.1 %middle.1 = (f32[9,8,128]{2,1,0:T(8,128)S(1)}, f32[9,8,128]{2,1,0:T(8,128)S(1)}, f32[16,128]{1,0:T(8,128)S(1)}, f32[16,128]{1,0:T(8,128)S(1)}, f32[16,128]{1,0:T(8,128)S(1)}, /*index=5*/f32[16,128]{1,0:T(8,128)S(1)}) custom-call(f32[9,8,128]{2,1,0:T(8,128)S(1)} %get-tuple-element.30.base_ref, f32[9,8,128]{2,1,0:T(8,128)S(1)} %get-tuple-element.29.early_ref, ...), custom_call_target="tpu_custom_call" | custom-call | flops 200000000 | bytes 4000000 | tf_op jit(solution)/shard_map/middle/pallas_call | solution.py:417
  28.1 0.1 collective-permute-start.4
  28.2 4.1 %collective-permute-start.5 = (f32[16,128]{1,0:T(8,128)S(1)}, f32[16,128]{1,0:T(8,128)S(1)}, u32[]{:S(2)}, u32[]{:S(2)}) collective-permute-start(f32[16,128]{1,0:T(8,128)S(1)} %get-tuple-element.50), channel_id=1, source_target_pairs={{4,0},{8,4},{12,8},{16,12},{20,16},{24,20},{28,24},{0,28},{5,1},{9... | collective-permute-start | bytes 24584 | tf_op jit(solution)/shard_map/ppermute | solution.py:436
  32.3 2.3 %collective-permute-start.6 = (f32[16,128]{1,0:T(8,128)S(1)}, f32[16,128]{1,0:T(8,128)S(1)}, u32[]{:S(2)}, u32[]{:S(2)}) collective-permute-start(f32[16,128]{1,0:T(8,128)S(1)} %get-tuple-element.51), channel_id=1, source_target_pairs={{0,1},{1,2},{2,3},{3,0},{4,5},{5,6},{6,7},{7,4},{8,9},{9,10},{10,1... | collective-permute-start | bytes 24584 | tf_op jit(solution)/shard_map/ppermute | solution.py:435
  34.6 0.0 collective-permute-start.7
  34.6 0.4 %local_late.1.base_ref = f32[9,8,128]{2,1,0:T(8,128)S(1)} custom-call(f32[9,8,128]{2,1,0:T(8,128)S(1)} %get-tuple-element.43.middle_ref, f32[9,8,128]{2,1,0:T(8,128)S(1)} %get-tuple-element.44.late_ref, f32[243,8,128]{2,1,0:T(8,128)S(1)} %get-tuple-element.32.star_ref, f32[81,2,8,128]{3,2,1,0:T(8,128)S(1)} %get-tuple-element.45.flux_ref, ...), custom_call_target="tpu_custom_call" | custom-call | flops 200000000 | bytes 4000000 | tf_op jit(solution)/shard_map/local_late/pallas_call | solution.py:417
  35.1 0.0 collective-permute-done.4.second_before_dom
  35.1 0.0 collective-permute-done.5.second_after_dom
  35.1 0.3 collective-permute-done.6.second_before_sub
  35.4 2.3 %collective-permute-done.7.second_after_sub = f32[16,128]{1,0:T(8,128)S(1)} collective-permute-done((f32[16,128]{1,0:T(8,128)S(1)}, f32[16,128]{1,0:T(8,128)S(1)}, u32[]{:S(2)}, u32[]{:S(2)}) %collective-permute-start.7) | collective-permute-done | bytes 8224 | tf_op jit(solution)/shard_map/ppermute | solution.py:436
  37.7 1.9 %final.1 = f32[9,16,56]{2,1,0:T(8,128)} custom-call(f32[9,8,128]{2,1,0:T(8,128)S(1)} %local_late.1.base_ref, f32[9,8,128]{2,1,0:T(8,128)S(1)} %get-tuple-element.44.late_ref, f32[180,16,128]{2,1,0:T(8,128)S(1)} %get-tuple-element.33.remote_ref, bf16[384,256]{1,0:T(8,128)(2,1)S(1)} %get-tuple-element.35.compose_ref, ...), custom_call_target="tpu_custom_call" | custom-call | flops 200000000 | bytes 4000000 | tf_op jit(solution)/shard_map/final/pallas_call | solution.py:417
Async XLA Ops:
  0.0 0.9 %copy-start = (f32[3,9,9,16]{3,0,2,1:T(4,128)S(1)}, f32[3,9,9,16]{3,0,2,1:T(4,128)}, u32[]{:S(2)}) copy-start(f32[3,9,9,16]{3,0,2,1:T(4,128)} %param.15) | copy-start | bytes 46660
  0.9 0.9 %copy-start.3 = (f32[3,56,56]{2,1,0:T(8,128)S(1)}, f32[3,56,56]{2,1,0:T(8,128)}, u32[]{:S(2)}) copy-start(f32[3,56,56]{2,1,0:T(8,128)} %stiffness_ref.3) | copy-start | bytes 112900
  1.8 0.9 %copy-start.4 = (f32[56,9,16]{0,2,1:T(8,128)S(1)}, f32[56,9,16]{0,2,1:T(8,128)}, u32[]{:S(2)}) copy-start(f32[56,9,16]{0,2,1:T(8,128)} %param.13) | copy-start | bytes 96772
  2.7 0.7 %copy-start.11 = (s32[1,4,4]{2,1,0:T(4,128)S(1)}, s32[1,4,4]{2,1,0:T(4,128)}, u32[]{:S(2)}) copy-start(s32[1,4,4]{2,1,0:T(4,128)} %send_ref.3) | copy-start | bytes 196
  6.7 16.9 %collective-permute-start = (f32[32,128]{1,0:T(8,128)S(1)}, f32[32,128]{1,0:T(8,128)S(1)}, u32[]{:S(2)}, u32[]{:S(2)}) collective-permute-start(f32[32,128]{1,0:T(8,128)S(1)} %get-tuple-element.39), channel_id=1, source_target_pairs={{0,4},{4,8},{8,12},{12,16},{16,20},{20,24},{24,28},{28,0},{1,5},{5... | collective-permute-start | bytes 49160 | tf_op jit(solution)/shard_map/ppermute | solution.py:435
  8.7 14.9 %collective-permute-start.1 = (f32[32,128]{1,0:T(8,128)S(1)}, f32[32,128]{1,0:T(8,128)S(1)}, u32[]{:S(2)}, u32[]{:S(2)}) collective-permute-start(f32[32,128]{1,0:T(8,128)S(1)} %get-tuple-element.40), channel_id=1, source_target_pairs={{4,0},{8,4},{12,8},{16,12},{20,16},{24,20},{28,24},{0,28},{5,1},{9... | collective-permute-start | bytes 49160 | tf_op jit(solution)/shard_map/ppermute | solution.py:436
  11.9 11.8 %collective-permute-start.2 = (f32[32,128]{1,0:T(8,128)S(1)}, f32[32,128]{1,0:T(8,128)S(1)}, u32[]{:S(2)}, u32[]{:S(2)}) collective-permute-start(f32[32,128]{1,0:T(8,128)S(1)} %get-tuple-element.41), channel_id=1, source_target_pairs={{0,1},{1,2},{2,3},{3,0},{4,5},{5,6},{6,7},{7,4},{8,9},{9,10},{10,1... | collective-permute-start | bytes 49160 | tf_op jit(solution)/shard_map/ppermute | solution.py:435
  14.1 9.6 %collective-permute-start.3 = (f32[32,128]{1,0:T(8,128)S(1)}, f32[32,128]{1,0:T(8,128)S(1)}, u32[]{:S(2)}, u32[]{:S(2)}) collective-permute-start(f32[32,128]{1,0:T(8,128)S(1)} %get-tuple-element.42), channel_id=1, source_target_pairs={{1,0},{2,1},{3,2},{0,3},{5,4},{6,5},{7,6},{4,7},{9,8},{10,9},{11,1... | collective-permute-start | bytes 49160 | tf_op jit(solution)/shard_map/ppermute | solution.py:436
  14.1 0.9 %copy-start.1 = (f32[4,9,9,16]{3,0,2,1:T(4,128)S(1)}, f32[4,9,9,16]{3,0,2,1:T(4,128)}, u32[]{:S(2)}) copy-start(f32[4,9,9,16]{3,0,2,1:T(4,128)} %param.19) | copy-start | bytes 62212
  15.0 0.9 %copy-start.2 = (f32[4,9,9,16]{3,0,2,1:T(4,128)S(1)}, f32[4,9,9,16]{3,0,2,1:T(4,128)}, u32[]{:S(2)}) copy-start(f32[4,9,9,16]{3,0,2,1:T(4,128)} %param.20) | copy-start | bytes 62212
  15.9 0.8 %copy-start.5 = (f32[4,21,56]{2,0,1:T(4,128)S(1)}, f32[4,21,56]{2,0,1:T(4,128)}, u32[]{:S(2)}) copy-start(f32[4,21,56]{2,0,1:T(4,128)} %param.16) | copy-start | bytes 56452
  16.7 0.8 %copy-start.6 = (f32[4,56,21]{1,0,2:T(4,128)S(1)}, f32[4,56,21]{1,0,2:T(4,128)}, u32[]{:S(2)}) copy-start(f32[4,56,21]{1,0,2:T(4,128)} %param.17) | copy-start | bytes 56452
  17.5 0.8 %copy-start.7 = (f32[3,21,21]{2,1,0:T(8,128)S(1)}, f32[3,21,21]{2,1,0:T(8,128)}, u32[]{:S(2)}) copy-start(f32[3,21,21]{2,1,0:T(8,128)} %orient_ref.1) | copy-start | bytes 15880
  18.2 0.7 %copy-start.8 = (s32[4,16]{1,0:T(4,128)S(1)}, s32[4,16]{1,0:T(4,128)}, u32[]{:S(2)}) copy-start(s32[4,16]{1,0:T(4,128)} %slot_ref.1) | copy-start | bytes 772
  18.9 0.7 %copy-start.9 = (s32[4,16]{1,0:T(4,128)S(1)}, s32[4,16]{1,0:T(4,128)}, u32[]{:S(2)}) copy-start(s32[4,16]{1,0:T(4,128)} %face_ref.1) | copy-start | bytes 772
  19.6 0.7 %copy-start.10 = (s32[4,16]{1,0:T(4,128)S(1)}, s32[4,16]{1,0:T(4,128)}, u32[]{:S(2)}) copy-start(s32[4,16]{1,0:T(4,128)} %turn_ref.1) | copy-start | bytes 772
  23.6 0.7 %copy-start.12 = (s32[1,4,4]{2,1,0:T(4,128)S(1)}, s32[1,4,4]{2,1,0:T(4,128)}, u32[]{:S(2)}) copy-start(s32[1,4,4]{2,1,0:T(4,128)} %send_ref.3) | copy-start | bytes 196
  24.3 0.7 %copy-start.13 = (s32[16]{0:T(128)S(1)}, s32[16]{0:T(128)}, u32[]{:S(2)}) copy-start(s32[16]{0:T(128)} %rate_ref.1) | copy-start | bytes 196
  28.1 7.0 %collective-permute-start.4 = (f32[16,128]{1,0:T(8,128)S(1)}, f32[16,128]{1,0:T(8,128)S(1)}, u32[]{:S(2)}, u32[]{:S(2)}) collective-permute-start(f32[16,128]{1,0:T(8,128)S(1)} %get-tuple-element.49), channel_id=1, source_target_pairs={{0,4},{4,8},{8,12},{12,16},{16,20},{20,24},{24,28},{28,0},{1,5},{5... | collective-permute-start | bytes 24584 | tf_op jit(solution)/shard_map/ppermute | solution.py:435
  28.2 6.9 %collective-permute-start.5 = (f32[16,128]{1,0:T(8,128)S(1)}, f32[16,128]{1,0:T(8,128)S(1)}, u32[]{:S(2)}, u32[]{:S(2)}) collective-permute-start(f32[16,128]{1,0:T(8,128)S(1)} %get-tuple-element.50), channel_id=1, source_target_pairs={{4,0},{8,4},{12,8},{16,12},{20,16},{24,20},{28,24},{0,28},{5,1},{9... | collective-permute-start | bytes 24584 | tf_op jit(solution)/shard_map/ppermute | solution.py:436
  32.3 3.1 %collective-permute-start.6 = (f32[16,128]{1,0:T(8,128)S(1)}, f32[16,128]{1,0:T(8,128)S(1)}, u32[]{:S(2)}, u32[]{:S(2)}) collective-permute-start(f32[16,128]{1,0:T(8,128)S(1)} %get-tuple-element.51), channel_id=1, source_target_pairs={{0,1},{1,2},{2,3},{3,0},{4,5},{5,6},{6,7},{7,4},{8,9},{9,10},{10,1... | collective-permute-start | bytes 24584 | tf_op jit(solution)/shard_map/ppermute | solution.py:435
  34.6 3.1 %collective-permute-start.7 = (f32[16,128]{1,0:T(8,128)S(1)}, f32[16,128]{1,0:T(8,128)S(1)}, u32[]{:S(2)}, u32[]{:S(2)}) collective-permute-start(f32[16,128]{1,0:T(8,128)S(1)} %get-tuple-element.52), channel_id=1, source_target_pairs={{1,0},{2,1},{3,2},{0,3},{5,4},{6,5},{7,6},{4,7},{9,8},{10,9},{11,1... | collective-permute-start | bytes 24584 | tf_op jit(solution)/shard_map/ppermute | solution.py:436
where the time goes:
time: 40.1 us; the launch traced here: 39.6 us
  starting transfers between devices  13.9 us (35%)
  Pallas kernels  12 us (30%)
  local copies, waits for them, and re-layouts  10.9 us (27%)
  waiting for transfers between devices  2.62 us (7%)
    pallas_call x5, Pallas kernels, call(): pl.pallas_call(kernel, out_shape=shapes, in_specs=ins, out_specs=[VMEM] *...  12 us
    unnamed x28, local copies, waits for them, and re-layouts  10.9 us
    ppermute x4, starting transfers between devices, exchange(): arrived.append(lax.ppermute(to_before, axis, down))  7.26 us
    ppermute x4, starting transfers between devices, exchange(): arrived.append(lax.ppermute(to_after, axis, up))  6.66 us
    ppermute x4, waiting for transfers between devices, exchange(): arrived.append(lax.ppermute(to_before, axis, down))  2.29 us
  transfers between devices with their start and end apart: 8, of which 2 were waited for; matrix products, arithmetic and copies ran while one was open for 0% of the time, Pallas kernels for 9%

commit v1 on v0

--- a/solution.py
+++ b/solution.py
@@ -13,6 +13,7 @@
 ROWS = 8
 F32 = jnp.float32
 BF16 = jnp.bfloat16
+LATER = ("flux_local", "flux_remote", "face_restrict", "face_lift", "orient_maps", "slot", "face", "turn")
 
 
 def taylor_weight(lower, upper, degree):
@@ -121,17 +122,32 @@
     return jnp.concatenate([-block_ref[kind].T for kind in range(block_ref.shape[0])], axis=1)
 
 
-def predict_kernel(
-    solution_ref, stiffness_ref, star_ref, send_ref,
-    early_out, late_out, to_before_dom, to_after_dom, to_before_sub, to_after_sub,
-    packed_ref, work_ref, coef_ref, block_ref, derive_ref, early_rows, late_rows,
-):
+def predict_kernel(*refs):
+    later = len(LATER)
+    solution_hbm, stiffness_hbm, star_hbm, send_hbm = refs[0:4]
+    later_hbm, refs = refs[4 : 4 + later], refs[4 + later :]
+    early_out, late_out, to_before_dom, to_after_dom, to_before_sub, to_after_sub = refs[0:6]
+    packed_ref, coef_ref, derive_ref, block_ref = refs[6:10]
+    later_out, refs = refs[10 : 10 + later], refs[10 + later :]
+    work_ref, early_rows, late_rows, solution_ref, stiffness_ref, star_ref, send_ref, sems = refs
+
+    sources = (stiffness_hbm, star_hbm, solution_hbm, send_hbm, *later_hbm)
+    targets = (stiffness_ref, star_ref, solution_ref, send_ref, *later_out)
+    copies = [
+        pltpu.make_async_copy(source, target, sems.at[number])
+        for number, (source, target) in enumerate(zip(sources, targets))
+    ]
+    for copy in copies:
+        copy.start()
     fields, kinds = star_ref.shape[0], star_ref.shape[2]
     pairs = (fields + 1) // 2
-    pack(solution_ref, packed_ref)
+    copies[0].wait()
     stiffness_blocks(stiffness_ref, block_ref)
     derive_ref[...] = stack_right(derive_operator(block_ref))
+    copies[1].wait()
     star_coefficients(star_ref, work_ref, coef_ref)
+    copies[2].wait()
+    pack(solution_ref, packed_ref)
     start = packed_ref[...].reshape(fields * ROWS, LANES)
 
     def step(degree, carry):
@@ -148,6 +164,7 @@
     late_out[...] = late.reshape(fields, ROWS, LANES)
     rows_by_pair(early, early_rows, fields)
     rows_by_pair(late, late_rows, fields)
+    copies[3].wait()
     sends = send_ref.shape[2]
     fast = sends // 2
     for side, out in enumerate((to_before_dom, to_after_dom, to_before_sub, to_after_sub)):
@@ -161,6 +178,8 @@
                 for pair in range(pairs):
                     row = pairs * sends + pair * fast + place - fast
                     out[row : row + 1, :] = late_rows[pair, pl.ds(element, 1), :]
+    for copy in copies[4:]:
+        copy.wait()
 
 
 def rows_by_pair(packed, out_ref, fields):
@@ -220,22 +239,19 @@
 
 
 def prepare_kernel(
-    solution_ref, early_ref, stiffness_ref, star_ref, restrict_ref, lift_ref, orient_ref, flux_local_ref,
-    flux_remote_ref, slot_ref, face_ref, turn_ref,
-    base_out, star_out, local_out, remote_out, derive_out, volume_out, trace_out, local_lift_out, compose_out,
+    packed_ref, early_ref, block_ref, star_ref, flux_local_ref, flux_remote_ref, restrict_ref, lift_ref, orient_ref,
+    slot_ref, face_ref, turn_ref,
+    base_out, local_out, remote_out, volume_out, trace_out, local_lift_out, compose_out,
     remote_lift_out, choose_out, mask_out,
-    packed_ref, work_ref, block_ref, wide_ref, face_work_ref, orient_work_ref, code_ref,
+    work_ref, wide_ref, face_work_ref, orient_work_ref, code_ref,
 ):
-    fields, kinds = star_ref.shape[0], star_ref.shape[2]
+    fields, kinds = packed_ref.shape[0], block_ref.shape[0]
     face_modes, faces, modes = restrict_ref.shape
     turns = orient_ref.shape[0]
     work_ref[...] = jnp.zeros(work_ref.shape, F32)
-    star_coefficients(star_ref, work_ref, star_out)
     flux_local_coefficients(flux_local_ref, work_ref, local_out)
     flux_remote_coefficients(flux_remote_ref, work_ref, remote_out)
 
-    stiffness_blocks(stiffness_ref, block_ref)
-    derive_out[...] = stack_right(derive_operator(block_ref))
     volume_out[...] = stack_right(jnp.concatenate([block_ref[kind] for kind in range(kinds)], axis=1))
 
     wide_ref[...] = jnp.zeros(wide_ref.shape, F32)
@@ -290,9 +306,8 @@
     choose_out[...] = jnp.concatenate(picks, axis=0).astype(BF16)
     mask_out[...] = jnp.concatenate(masks, axis=0)
 
-    pack(solution_ref, packed_ref)
     early = early_ref[...].reshape(fields * ROWS, LANES)
-    terms = local_terms(early, star_out, local_out, volume_out, trace_out, local_lift_out, fields, kinds)
+    terms = local_terms(early, star_ref, local_out, volume_out, trace_out, local_lift_out, fields, kinds)
     base_out[...] = packed_ref[...] + terms.reshape(fields, ROWS, LANES)
 
 
@@ -327,10 +342,16 @@
 
 def middle_kernel(
     base_ref, early_ref, late_ref, star_ref, remote_ref, derive_ref, compose_ref, lift_ref, choose_ref, mask_ref,
-    rate_ref, send_ref, from_before_dom, from_after_dom, from_before_sub, from_after_sub,
+    rate_hbm, send_hbm, from_before_dom, from_after_dom, from_before_sub, from_after_sub,
     middle_out, late_out, to_before_dom, to_after_dom, to_before_sub, to_after_sub,
-    rows_ref, late_rows,
+    rows_ref, late_rows, rate_ref, send_ref, sems,
 ):
+    copies = [
+        pltpu.make_async_copy(rate_hbm, rate_ref, sems.at[0]),
+        pltpu.make_async_copy(send_hbm, send_ref, sems.at[1]),
+    ]
+    for copy in copies:
+        copy.start()
     fields = base_ref.shape[0]
     kinds = star_ref.shape[0] // (fields * fields)
     pairs = rows_ref.shape[0]
@@ -354,6 +375,8 @@
         return current, early + weight_at(0.0, 0.5, degree) * current
 
     _, restart = lax.fori_loop(1, DERIVS, step, (start, taylor_weight(0.0, 0.5, 0) * start))
+    for copy in copies:
+        copy.wait()
     sublane = lax.broadcasted_iota(jnp.int32, (ROWS, LANES), 0)
     lower = lower_half((ROWS, LANES))
     is_fast = jnp.zeros((ROWS, LANES), jnp.int32)
@@ -409,17 +432,20 @@
 
 
 VMEM = pl.BlockSpec(memory_space=pltpu.VMEM)
-SMEM = pl.BlockSpec(memory_space=pltpu.SMEM)
+HBM = pl.BlockSpec(memory_space=pltpu.HBM)
 
 
 def call(kernel, ins, outs, scratch, args, name, flops):
     shapes = [jax.ShapeDtypeStruct(shape, dtype) for shape, dtype in outs]
+    args = [
+        pltpu.with_memory_space_constraint(arg, pltpu.HBM) if spec is HBM else arg for spec, arg in zip(ins, args)
+    ]
     return pl.pallas_call(
         kernel,
         out_shape=shapes,
         in_specs=ins,
         out_specs=[VMEM] * len(outs),
-        scratch_shapes=[pltpu.VMEM(shape, dtype) for shape, dtype in scratch],
+        scratch_shapes=[pltpu.VMEM(*one) if isinstance(one, tuple) else one for one in scratch],
         compiler_params=pltpu.CompilerParams(vmem_limit_bytes=16 * 1024 * 1024),
         cost_estimate=pl.CostEstimate(flops=flops, bytes_accessed=4_000_000, transcendentals=0),
         name=name,
@@ -467,46 +493,53 @@
     combos = faces * HALF
     sources = elements + sides * sends
 
-    early, late, *outgoing = call(
+    waiting = (local_part, remote_part, restrict, lift, orient_maps, neighbour_slot, neighbour_face, neighbour_turn)
+    made = call(
         predict_kernel,
-        [VMEM, VMEM, VMEM, SMEM],
-        [(packed, F32)] * 2 + [(first_shape, F32)] * sides,
+        [HBM] * (4 + len(LATER)),
+        [(packed, F32)] * 2 + [(first_shape, F32)] * sides + [
+            (packed, F32), (star_shape, F32), ((3 * LANES, kinds * LANES), BF16), ((kinds, LANES, LANES), F32),
+        ] + [(array.shape, array.dtype) for array in waiting],
         [
-            (packed, F32), (work, F32), (star_shape, F32), ((kinds, LANES, LANES), F32),
-            ((3 * LANES, kinds * LANES), BF16), ((pairs, elements, LANES), F32), ((pairs, elements, LANES), F32),
+            (work, F32), ((pairs, elements, LANES), F32), ((pairs, elements, LANES), F32),
+            (values.shape, F32), (stiffness.shape, F32), (star.shape, F32),
+            pltpu.SMEM(send_list.shape, jnp.int32), pltpu.SemaphoreType.DMA((4 + len(LATER),)),
         ],
-        (values, stiffness, star, send_list),
+        (values, stiffness, star, send_list, *waiting),
         "predict", 100_000_000,
     )
+    early, late, outgoing = made[0], made[1], made[2 : 2 + sides]
+    start, star_coef, derive_op, blocks = made[2 + sides : 6 + sides]
+    waiting = made[6 + sides :]
     first = exchange(*outgoing)
     (
-        base, star_coef, local_coef, remote_coef, derive_op, volume_op, trace_op, local_lift, compose_op, remote_lift,
-        choose, mask,
+        base, local_coef, remote_coef, volume_op, trace_op, local_lift, compose_op, remote_lift, choose, mask,
     ) = call(
         prepare_kernel,
         [VMEM] * 12,
         [
-            (packed, F32), (star_shape, F32), ((fields * fields, 2, ROWS, LANES), F32),
+            (packed, F32), ((fields * fields, 2, ROWS, LANES), F32),
             ((faces * pairs * fields, elements, LANES), F32),
-            ((3 * LANES, kinds * LANES), BF16), ((3 * LANES, kinds * LANES), BF16), ((3 * LANES, 2 * LANES), BF16),
+            ((3 * LANES, kinds * LANES), BF16), ((3 * LANES, 2 * LANES), BF16),
             ((6 * LANES, LANES), BF16), ((3 * LANES, combos), BF16), ((faces, 2, HALF, LANES), BF16),
             ((faces * elements, 2 * sources), BF16), ((faces * elements, combos), F32),
         ],
         [
-            (packed, F32), (work, F32), ((kinds, LANES, LANES), F32), ((2 * LANES, LANES), F32),
+            (work, F32), ((2 * LANES, LANES), F32),
             ((LANES, faces * LANES), F32), ((HALF, LANES), F32), ((LANES, LANES), F32),
         ],
-        (
-            values, early, stiffness, star, restrict, lift, orient_maps, local_part, remote_part,
-            neighbour_slot, neighbour_face, neighbour_turn,
-        ),
+        (start, early, blocks, star_coef, *waiting),
         "prepare", 200_000_000,
     )
     middle, late_value, *outgoing = call(
         middle_kernel,
-        [VMEM] * 10 + [SMEM] * 2 + [VMEM] * 4,
+        [VMEM] * 10 + [HBM] * 2 + [VMEM] * 4,
         [(packed, F32)] * 2 + [(second_shape, F32)] * sides,
-        [((pairs, sources, LANES), F32), ((pairs, elements, LANES), F32)],
+        [
+            ((pairs, sources, LANES), F32), ((pairs, elements, LANES), F32),
+            pltpu.SMEM(cluster_rate.shape, jnp.int32), pltpu.SMEM(send_list.shape, jnp.int32),
+            pltpu.SemaphoreType.DMA((2,)),
+        ],
         (
             base, early, late, star_coef, remote_coef, derive_op, compose_op, remote_lift, choose, mask,
             cluster_rate, send_list, *first,

time: 40.1 us -> 27.5 us (0.69); the launches traced: 39.6 us -> 27.4 us
  local copies, waits for them, and re-layouts: 10.9 us -> 0 us
  Pallas kernels: 12 us -> 10.7 us
  waiting for transfers between devices: 2.62 us -> 3.79 us
  starting transfers between devices: 13.9 us -> 12.8 us
    unnamed x28 -> x0, local copies, waits for them, and re-layouts: 10.9 us -> none
    pallas_call x5, Pallas kernels: 12 us -> 10.7 us  [call(): pl.pallas_call(kernel, out_shape=shapes, in_specs=ins, out_specs=[VMEM] *...]
    ppermute x4, waiting for transfers between devices: 2.29 us -> 3.46 us  [exchange(): arrived.append(lax.ppermute(to_before, axis, down))]
    ppermute x4, starting transfers between devices: 6.66 us -> 5.51 us  [exchange(): arrived.append(lax.ppermute(to_after, axis, up))]
  transfers between devices with their start and end apart: 8 -> 8, of which waited for: 2 -> 3; matrix products, arithmetic and copies ran while one was open for 0% -> 0% of each run, Pallas kernels for 9% -> 9%
where the time goes in v1:
time: 27.5 us; the launch traced here: 27.4 us
  starting transfers between devices  12.8 us (47%)
  Pallas kernels  10.7 us (39%)
  waiting for transfers between devices  3.79 us (14%)
    pallas_call x5, Pallas kernels, call(): pl.pallas_call(kernel, out_shape=shapes, in_specs=ins, out_specs=[VMEM] *...  10.7 us
    ppermute x4, starting transfers between devices, exchange(): arrived.append(lax.ppermute(to_before, axis, down))  7.26 us
    ppermute x4, starting transfers between devices, exchange(): arrived.append(lax.ppermute(to_after, axis, up))  5.51 us
    ppermute x4, waiting for transfers between devices, exchange(): arrived.append(lax.ppermute(to_before, axis, down))  3.46 us
  transfers between devices with their start and end apart: 8, of which 3 were waited for; matrix products, arithmetic and copies ran while one was open for 0% of the time, Pallas kernels for 9%

profile of v1, /device:TPU:1, one launch (start us, length us, event | category | flops | bytes accessed | tf_op | source)
XLA Modules:
  0.0 27.4 jit_solution(15145995493181252456)
XLA Ops:
  0.0 3.9 %predict.1 = (f32[9,8,128]{2,1,0:T(8,128)S(1)}, f32[9,8,128]{2,1,0:T(8,128)S(1)}, f32[32,128]{1,0:T(8,128)S(1)}, f32[32,128]{1,0:T(8,128)S(1)}, f32[32,128]{1,0:...) custom-call(f32[9,16,56]{2,1,0:T(8,128)} %bitcast.10, ...), custom_call_target="tpu_custom_call" | custom-call | flops 100000000 | bytes 4000000 | tf_op jit(solution)/shard_map/predict/pallas_call | solution.py:443
  3.9 2.1 %collective-permute-start = (f32[32,128]{1,0:T(8,128)S(1)}, f32[32,128]{1,0:T(8,128)S(1)}, u32[]{:S(2)}, u32[]{:S(2)}) collective-permute-start(f32[32,128]{1,0:T(8,128)S(1)} %get-tuple-element.59), channel_id=1, source_target_pairs={{0,4},{4,8},{8,12},{12,16},{16,20},{20,24},{24,28},{28,0},{1,5},{5... | collective-permute-start | bytes 49160 | tf_op jit(solution)/shard_map/ppermute | solution.py:461
  6.0 3.1 %collective-permute-start.1 = (f32[32,128]{1,0:T(8,128)S(1)}, f32[32,128]{1,0:T(8,128)S(1)}, u32[]{:S(2)}, u32[]{:S(2)}) collective-permute-start(f32[32,128]{1,0:T(8,128)S(1)} %get-tuple-element.60), channel_id=1, source_target_pairs={{4,0},{8,4},{12,8},{16,12},{20,16},{24,20},{28,24},{0,28},{5,1},{9... | collective-permute-start | bytes 49160 | tf_op jit(solution)/shard_map/ppermute | solution.py:462
  9.1 2.2 %collective-permute-start.2 = (f32[32,128]{1,0:T(8,128)S(1)}, f32[32,128]{1,0:T(8,128)S(1)}, u32[]{:S(2)}, u32[]{:S(2)}) collective-permute-start(f32[32,128]{1,0:T(8,128)S(1)} %get-tuple-element.61), channel_id=1, source_target_pairs={{0,1},{1,2},{2,3},{3,0},{4,5},{5,6},{6,7},{7,4},{8,9},{9,10},{10,1... | collective-permute-start | bytes 49160 | tf_op jit(solution)/shard_map/ppermute | solution.py:461
  11.3 0.0 collective-permute-start.3
  11.3 2.0 %prepare.1 = (f32[9,8,128]{2,1,0:T(8,128)S(1)}, f32[81,2,8,128]{3,2,1,0:T(8,128)S(1)}, f32[180,16,128]{2,1,0:T(8,128)S(1)}, bf16[384,384]{1,0:T(8,128)(2,1)S(1)}...) custom-call(f32[9,8,128]{2,1,0:T(8,128)S(1)} %get-tuple-element.39.p, ...), custom_call_target="tpu_custom_call" | custom-call | flops 200000000 | bytes 4000000 | tf_op jit(solution)/shard_map/prepare/pallas_call | solution.py:443
  13.3 0.0 collective-permute-done.from_before_dom.first_before_dom
  13.3 0.0 collective-permute-done.1.from_after_dom.first_after_dom
  13.3 0.0 collective-permute-done.2.from_before_sub.first_before_sub
  13.3 1.2 %collective-permute-done.3.from_after_sub.first_after_sub = f32[32,128]{1,0:T(8,128)S(1)} collective-permute-done((f32[32,128]{1,0:T(8,128)S(1)}, f32[32,128]{1,0:T(8,128)S(1)}, u32[]{:S(2)}, u32[]{:S(2)}) %collective-permute-start.3) | collective-permute-done | bytes 16416 | tf_op jit(solution)/shard_map/ppermute | solution.py:462
  14.5 2.5 %middle.1 = (f32[9,8,128]{2,1,0:T(8,128)S(1)}, f32[9,8,128]{2,1,0:T(8,128)S(1)}, f32[16,128]{1,0:T(8,128)S(1)}, f32[16,128]{1,0:T(8,128)S(1)}, f32[16,128]{1,0:T(8,128)S(1)}, /*index=5*/f32[16,128]{1,0:T(8,128)S(1)}) custom-call(f32[9,8,128]{2,1,0:T(8,128)S(1)} %get-tuple-element.51.base_ref, f32[9,8,128]{2,1,0:T(8,128)S(1)} %get-tuple-element.40.early_ref, ...), custom_call_target="tpu_custom_call" | custom-call | flops 200000000 | bytes 4000000 | tf_op jit(solution)/shard_map/middle/pallas_call | solution.py:443
  17.0 0.1 collective-permute-start.4
  17.1 4.1 %collective-permute-start.5 = (f32[16,128]{1,0:T(8,128)S(1)}, f32[16,128]{1,0:T(8,128)S(1)}, u32[]{:S(2)}, u32[]{:S(2)}) collective-permute-start(f32[16,128]{1,0:T(8,128)S(1)} %get-tuple-element.70), channel_id=1, source_target_pairs={{4,0},{8,4},{12,8},{16,12},{20,16},{24,20},{28,24},{0,28},{5,1},{9... | collective-permute-start | bytes 24584 | tf_op jit(solution)/shard_map/ppermute | solution.py:462
  21.3 1.2 %collective-permute-start.6 = (f32[16,128]{1,0:T(8,128)S(1)}, f32[16,128]{1,0:T(8,128)S(1)}, u32[]{:S(2)}, u32[]{:S(2)}) collective-permute-start(f32[16,128]{1,0:T(8,128)S(1)} %get-tuple-element.71), channel_id=1, source_target_pairs={{0,1},{1,2},{2,3},{3,0},{4,5},{5,6},{6,7},{7,4},{8,9},{9,10},{10,1... | collective-permute-start | bytes 24584 | tf_op jit(solution)/shard_map/ppermute | solution.py:461
  22.4 0.0 collective-permute-start.7
  22.4 0.4 %local_late.1.base_ref = f32[9,8,128]{2,1,0:T(8,128)S(1)} custom-call(f32[9,8,128]{2,1,0:T(8,128)S(1)} %get-tuple-element.63.middle_ref, f32[9,8,128]{2,1,0:T(8,128)S(1)} %get-tuple-element.64.late_ref, f32[243,8,128]{2,1,0:T(8,128)S(1)} %get-tuple-element.42.star_ref, f32[81,2,8,128]{3,2,1,0:T(8,128)S(1)} %get-tuple-element.65.flux_ref, ...), custom_call_target="tpu_custom_call" | custom-call | flops 200000000 | bytes 4000000 | tf_op jit(solution)/shard_map/local_late/pallas_call | solution.py:443
  22.9 0.0 collective-permute-done.4.second_before_dom
  22.9 0.0 collective-permute-done.5.second_after_dom
  22.9 0.3 %collective-permute-done.6.second_before_sub = f32[16,128]{1,0:T(8,128)S(1)} collective-permute-done((f32[16,128]{1,0:T(8,128)S(1)}, f32[16,128]{1,0:T(8,128)S(1)}, u32[]{:S(2)}, u32[]{:S(2)}) %collective-permute-start.6) | collective-permute-done | bytes 8224 | tf_op jit(solution)/shard_map/ppermute | solution.py:461
  23.2 2.3 %collective-permute-done.7.second_after_sub = f32[16,128]{1,0:T(8,128)S(1)} collective-permute-done((f32[16,128]{1,0:T(8,128)S(1)}, f32[16,128]{1,0:T(8,128)S(1)}, u32[]{:S(2)}, u32[]{:S(2)}) %collective-permute-start.7) | collective-permute-done | bytes 8224 | tf_op jit(solution)/shard_map/ppermute | solution.py:462
  25.5 1.9 %final.1 = f32[9,16,56]{2,1,0:T(8,128)} custom-call(f32[9,8,128]{2,1,0:T(8,128)S(1)} %local_late.1.base_ref, f32[9,8,128]{2,1,0:T(8,128)S(1)} %get-tuple-element.64.late_ref, f32[180,16,128]{2,1,0:T(8,128)S(1)} %get-tuple-element.53.remote_ref, bf16[384,256]{1,0:T(8,128)(2,1)S(1)} %get-tuple-element.55.compose_ref, ...), custom_call_target="tpu_custom_call" | custom-call | flops 200000000 | bytes 4000000 | tf_op jit(solution)/shard_map/final/pallas_call | solution.py:443
Async XLA Ops:
  3.9 9.4 %collective-permute-start = (f32[32,128]{1,0:T(8,128)S(1)}, f32[32,128]{1,0:T(8,128)S(1)}, u32[]{:S(2)}, u32[]{:S(2)}) collective-permute-start(f32[32,128]{1,0:T(8,128)S(1)} %get-tuple-element.59), channel_id=1, source_target_pairs={{0,4},{4,8},{8,12},{12,16},{16,20},{20,24},{24,28},{28,0},{1,5},{5... | collective-permute-start | bytes 49160 | tf_op jit(solution)/shard_map/ppermute | solution.py:461
  6.0 7.3 %collective-permute-start.1 = (f32[32,128]{1,0:T(8,128)S(1)}, f32[32,128]{1,0:T(8,128)S(1)}, u32[]{:S(2)}, u32[]{:S(2)}) collective-permute-start(f32[32,128]{1,0:T(8,128)S(1)} %get-tuple-element.60), channel_id=1, source_target_pairs={{4,0},{8,4},{12,8},{16,12},{20,16},{24,20},{28,24},{0,28},{5,1},{9... | collective-permute-start | bytes 49160 | tf_op jit(solution)/shard_map/ppermute | solution.py:462
  9.1 4.2 %collective-permute-start.2 = (f32[32,128]{1,0:T(8,128)S(1)}, f32[32,128]{1,0:T(8,128)S(1)}, u32[]{:S(2)}, u32[]{:S(2)}) collective-permute-start(f32[32,128]{1,0:T(8,128)S(1)} %get-tuple-element.61), channel_id=1, source_target_pairs={{0,1},{1,2},{2,3},{3,0},{4,5},{5,6},{6,7},{7,4},{8,9},{9,10},{10,1... | collective-permute-start | bytes 49160 | tf_op jit(solution)/shard_map/ppermute | solution.py:461
  11.3 3.2 %collective-permute-start.3 = (f32[32,128]{1,0:T(8,128)S(1)}, f32[32,128]{1,0:T(8,128)S(1)}, u32[]{:S(2)}, u32[]{:S(2)}) collective-permute-start(f32[32,128]{1,0:T(8,128)S(1)} %get-tuple-element.62), channel_id=1, source_target_pairs={{1,0},{2,1},{3,2},{0,3},{5,4},{6,5},{7,6},{4,7},{9,8},{10,9},{11,1... | collective-permute-start | bytes 49160 | tf_op jit(solution)/shard_map/ppermute | solution.py:462
  17.0 5.8 %collective-permute-start.4 = (f32[16,128]{1,0:T(8,128)S(1)}, f32[16,128]{1,0:T(8,128)S(1)}, u32[]{:S(2)}, u32[]{:S(2)}) collective-permute-start(f32[16,128]{1,0:T(8,128)S(1)} %get-tuple-element.69), channel_id=1, source_target_pairs={{0,4},{4,8},{8,12},{12,16},{16,20},{20,24},{24,28},{28,0},{1,5},{5... | collective-permute-start | bytes 24584 | tf_op jit(solution)/shard_map/ppermute | solution.py:461
  17.1 5.8 %collective-permute-start.5 = (f32[16,128]{1,0:T(8,128)S(1)}, f32[16,128]{1,0:T(8,128)S(1)}, u32[]{:S(2)}, u32[]{:S(2)}) collective-permute-start(f32[16,128]{1,0:T(8,128)S(1)} %get-tuple-element.70), channel_id=1, source_target_pairs={{4,0},{8,4},{12,8},{16,12},{20,16},{24,20},{28,24},{0,28},{5,1},{9... | collective-permute-start | bytes 24584 | tf_op jit(solution)/shard_map/ppermute | solution.py:462
  21.3 1.9 %collective-permute-start.6 = (f32[16,128]{1,0:T(8,128)S(1)}, f32[16,128]{1,0:T(8,128)S(1)}, u32[]{:S(2)}, u32[]{:S(2)}) collective-permute-start(f32[16,128]{1,0:T(8,128)S(1)} %get-tuple-element.71), channel_id=1, source_target_pairs={{0,1},{1,2},{2,3},{3,0},{4,5},{5,6},{6,7},{7,4},{8,9},{9,10},{10,1... | collective-permute-start | bytes 24584 | tf_op jit(solution)/shard_map/ppermute | solution.py:461
  22.4 3.1 %collective-permute-start.7 = (f32[16,128]{1,0:T(8,128)S(1)}, f32[16,128]{1,0:T(8,128)S(1)}, u32[]{:S(2)}, u32[]{:S(2)}) collective-permute-start(f32[16,128]{1,0:T(8,128)S(1)} %get-tuple-element.72), channel_id=1, source_target_pairs={{1,0},{2,1},{3,2},{0,3},{5,4},{6,5},{7,6},{4,7},{9,8},{10,9},{11,1... | collective-permute-start | bytes 24584 | tf_op jit(solution)/shard_map/ppermute | solution.py:462

commit v2 on v1

--- a/solution.py
+++ b/solution.py
@@ -45,6 +45,15 @@
 
 def product(left, right):
     return jnp.dot(left, right, preferred_element_type=F32)
+
+
+def odd_place(axis):
+    return lax.rem(lax.axis_index(axis), 2)
+
+
+def message_side(slot):
+    odd = odd_place("dom" if slot < 2 else "sub")
+    return slot + odd if slot % 2 == 0 else slot - odd
 
 
 def lane_index(shape):
@@ -126,7 +135,7 @@
     later = len(LATER)
     solution_hbm, stiffness_hbm, star_hbm, send_hbm = refs[0:4]
     later_hbm, refs = refs[4 : 4 + later], refs[4 + later :]
-    early_out, late_out, to_before_dom, to_after_dom, to_before_sub, to_after_sub = refs[0:6]
+    early_out, late_out, far_dom_out, near_dom_out, far_sub_out, near_sub_out = refs[0:6]
     packed_ref, coef_ref, derive_ref, block_ref = refs[6:10]
     later_out, refs = refs[10 : 10 + later], refs[10 + later :]
     work_ref, early_rows, late_rows, solution_ref, stiffness_ref, star_ref, send_ref, sems = refs
@@ -167,10 +176,10 @@
     copies[3].wait()
     sends = send_ref.shape[2]
     fast = sends // 2
-    for side, out in enumerate((to_before_dom, to_after_dom, to_before_sub, to_after_sub)):
+    for side, out in enumerate((far_dom_out, near_dom_out, far_sub_out, near_sub_out)):
         out[...] = jnp.zeros(out.shape, F32)
         for place in range(sends):
-            element = send_ref[0, side, place]
+            element = send_ref[0, message_side(side), place]
             for pair in range(pairs):
                 row = pair * sends + place
                 out[row : row + 1, :] = early_rows[pair, pl.ds(element, 1), :]
@@ -290,7 +299,12 @@
 
     elements = slot_ref.shape[1]
     code_ref[...] = jnp.zeros(code_ref.shape, F32)
-    code_ref[0:faces, 0:elements] = slot_ref[...].astype(F32)
+    slots = slot_ref[...]
+    sends = (choose_out.shape[1] // 2 - elements) // 4
+    group = (slots - elements) // sends
+    odd = jnp.where(group < 2, odd_place("dom"), odd_place("sub"))
+    moved = slots + jnp.where(group % 2 == 0, sends, -sends) * odd
+    code_ref[0:faces, 0:elements] = jnp.where(slots < elements, slots, moved).astype(F32)
     code_ref[faces : 2 * faces, 0:elements] = (face_ref[...] * turns + turn_ref[...]).astype(F32)
     codes = code_ref[...].T[0:elements, :]
     sources = choose_out.shape[1] // 2
@@ -342,8 +356,8 @@
 
 def middle_kernel(
     base_ref, early_ref, late_ref, star_ref, remote_ref, derive_ref, compose_ref, lift_ref, choose_ref, mask_ref,
-    rate_hbm, send_hbm, from_before_dom, from_after_dom, from_before_sub, from_after_sub,
-    middle_out, late_out, to_before_dom, to_after_dom, to_before_sub, to_after_sub,
+    rate_hbm, send_hbm, far_dom, near_dom, far_sub, near_sub,
+    middle_out, late_out, far_dom_out, near_dom_out, far_sub_out, near_sub_out,
     rows_ref, late_rows, rate_ref, send_ref, sems,
 ):
     copies = [
@@ -359,7 +373,7 @@
     fast = sends // 2
     elements = 2 * ROWS
     rows_by_pair(early_ref[...].reshape(fields * ROWS, LANES), rows_ref, fields)
-    for side, arrived in enumerate((from_before_dom, from_after_dom, from_before_sub, from_after_sub)):
+    for side, arrived in enumerate((far_dom, near_dom, far_sub, near_sub)):
         at = elements + side * sends
         for pair in range(pairs):
             rows_ref[pair, at : at + sends, :] = arrived[pair * sends : (pair + 1) * sends, :]
@@ -386,10 +400,10 @@
     late = jnp.where((is_fast == 2)[None], restart.reshape(fields, ROWS, LANES), late_ref[...])
     late_out[...] = late
     rows_by_pair(late.reshape(fields * ROWS, LANES), late_rows, fields)
-    for side, out in enumerate((to_before_dom, to_after_dom, to_before_sub, to_after_sub)):
+    for side, out in enumerate((far_dom_out, near_dom_out, far_sub_out, near_sub_out)):
         out[...] = jnp.zeros(out.shape, F32)
         for place in range(fast):
-            element = send_ref[0, side, place]
+            element = send_ref[0, message_side(side), place]
             for pair in range(pairs):
                 row = pair * fast + place
                 out[row : row + 1, :] = late_rows[pair, pl.ds(element, 1), :]
@@ -405,8 +419,8 @@
 
 def final_kernel(
     base_ref, late_ref, remote_ref, compose_ref, lift_ref, choose_ref, mask_ref,
-    first_before_dom, first_after_dom, first_before_sub, first_after_sub,
-    second_before_dom, second_after_dom, second_before_sub, second_after_sub,
+    first_far_dom, first_near_dom, first_far_sub, first_near_sub,
+    second_far_dom, second_near_dom, second_far_sub, second_near_sub,
     result_out, rows_ref,
 ):
     fields = base_ref.shape[0]
@@ -416,8 +430,8 @@
     sends = (rows_ref.shape[1] - elements) // 4
     fast = sends // 2
     rows_by_pair(late_ref[...].reshape(fields * ROWS, LANES), rows_ref, fields)
-    firsts = (first_before_dom, first_after_dom, first_before_sub, first_after_sub)
-    seconds = (second_before_dom, second_after_dom, second_before_sub, second_after_sub)
+    firsts = (first_far_dom, first_near_dom, first_far_sub, first_near_sub)
+    seconds = (second_far_dom, second_near_dom, second_far_sub, second_near_sub)
     for side, (first, second) in enumerate(zip(firsts, seconds)):
         at = elements + side * sends
         for pair in range(pairs):
@@ -452,14 +466,16 @@
     )(*args)
 
 
-def exchange(to_before_dom, to_after_dom, to_before_sub, to_after_sub):
-    arrived = []
-    for axis, to_before, to_after in (("dom", to_before_dom, to_after_dom), ("sub", to_before_sub, to_after_sub)):
+def exchange(outgoing):
+    arrived = [None] * 4
+    for slot, axis, first in ((0, "dom", 1), (2, "sub", 1), (1, "dom", 0), (3, "sub", 0)):
         size = lax.axis_size(axis)
-        up = [(i, (i + 1) % size) for i in range(size)]
-        down = [(j, i) for i, j in up]
-        arrived.append(lax.ppermute(to_after, axis, up))
-        arrived.append(lax.ppermute(to_before, axis, down))
+        assert size % 2 == 0
+        pairs = []
+        for even in range(first, size, 2):
+            odd = (even + 1) % size
+            pairs += [(even, odd), (odd, even)]
+        arrived[slot] = lax.ppermute(outgoing[slot], axis, pairs)
     return arrived
 
 
@@ -511,7 +527,7 @@
     early, late, outgoing = made[0], made[1], made[2 : 2 + sides]
     start, star_coef, derive_op, blocks = made[2 + sides : 6 + sides]
     waiting = made[6 + sides :]
-    first = exchange(*outgoing)
+    first = exchange(outgoing)
     (
         base, local_coef, remote_coef, volume_op, trace_op, local_lift, compose_op, remote_lift, choose, mask,
     ) = call(
@@ -546,7 +562,7 @@
         ),
         "middle", 200_000_000,
     )
-    second = exchange(*outgoing)
+    second = exchange(outgoing)
     (base,) = call(
         local_kernel,
         [VMEM] * 7,

time: 27.5 us -> 24.8 us (0.902)
  the two profiles are of different devices: /device:TPU:1 before, /device:TPU:0 now
where the time goes in v2:
time: 24.8 us; the launch traced here: 24.7 us
  starting transfers between devices  12.1 us (49%)
  Pallas kernels  10.7 us (43%)
  waiting for transfers between devices  1.78 us (7%)
    ppermute x8, starting transfers between devices, exchange(): arrived[slot] = lax.ppermute(outgoing[slot], axis, pairs)  12.1 us
    pallas_call x5, Pallas kernels, call(): pl.pallas_call(kernel, out_shape=shapes, in_specs=ins, out_specs=[VMEM] *...  10.7 us
    ppermute x8, waiting for transfers between devices, exchange(): arrived[slot] = lax.ppermute(outgoing[slot], axis, pairs)  1.78 us
  transfers between devices with their start and end apart: 8, of which 3 were waited for; matrix products, arithmetic and copies ran while one was open for 0% of the time, Pallas kernels for 10%

profile of v2, /device:TPU:0, one launch (start us, length us, event | category | flops | bytes accessed | tf_op | source)
XLA Modules:
  0.0 24.7 jit_solution(3419990844769217094)
XLA Ops:
  0.0 3.9 %predict.1 = (f32[9,8,128]{2,1,0:T(8,128)S(1)}, f32[9,8,128]{2,1,0:T(8,128)S(1)}, f32[32,128]{1,0:T(8,128)S(1)}, f32[32,128]{1,0:T(8,128)S(1)}, f32[32,128]{1,0:...) custom-call(f32[9,16,56]{2,1,0:T(8,128)} %bitcast.10, ...), custom_call_target="tpu_custom_call" | custom-call | flops 100000000 | bytes 4000000 | tf_op jit(solution)/shard_map/predict/pallas_call | solution.py:457
  4.0 6.0 %collective-permute-start = (f32[32,128]{1,0:T(8,128)S(1)}, f32[32,128]{1,0:T(8,128)S(1)}, u32[]{:S(2)}, u32[]{:S(2)}) collective-permute-start(f32[32,128]{1,0:T(8,128)S(1)} %get-tuple-element.59), channel_id=1, source_target_pairs={{4,8},{8,4},{12,16},{16,12},{20,24},{24,20},{28,0},{0,28},{5,9},{9... | collective-permute-start | bytes 49160 | tf_op jit(solution)/shard_map/ppermute | solution.py:478
  10.0 0.0 collective-permute-start.1
  10.0 0.7 %collective-permute-start.2 = (f32[32,128]{1,0:T(8,128)S(1)}, f32[32,128]{1,0:T(8,128)S(1)}, u32[]{:S(2)}, u32[]{:S(2)}) collective-permute-start(f32[32,128]{1,0:T(8,128)S(1)} %get-tuple-element.61), channel_id=1, source_target_pairs={{1,2},{2,1},{3,0},{0,3},{5,6},{6,5},{7,4},{4,7},{9,10},{10,9},{11,... | collective-permute-start | bytes 49160 | tf_op jit(solution)/shard_map/ppermute | solution.py:478
  10.7 1.0 %collective-permute-start.3 = (f32[32,128]{1,0:T(8,128)S(1)}, f32[32,128]{1,0:T(8,128)S(1)}, u32[]{:S(2)}, u32[]{:S(2)}) collective-permute-start(f32[32,128]{1,0:T(8,128)S(1)} %get-tuple-element.62), channel_id=1, source_target_pairs={{0,1},{1,0},{2,3},{3,2},{4,5},{5,4},{6,7},{7,6},{8,9},{9,8},{10,11... | collective-permute-start | bytes 49160 | tf_op jit(solution)/shard_map/ppermute | solution.py:478
  11.6 2.0 %prepare.1 = (f32[9,8,128]{2,1,0:T(8,128)S(1)}, f32[81,2,8,128]{3,2,1,0:T(8,128)S(1)}, f32[180,16,128]{2,1,0:T(8,128)S(1)}, bf16[384,384]{1,0:T(8,128)(2,1)S(1)}...) custom-call(f32[9,8,128]{2,1,0:T(8,128)S(1)} %get-tuple-element.39.p, ...), custom_call_target="tpu_custom_call" | custom-call | flops 200000000 | bytes 4000000 | tf_op jit(solution)/shard_map/prepare/pallas_call | solution.py:457
  13.6 0.0 collective-permute-done.far_dom.first_far_dom
  13.6 0.1 collective-permute-done.1.near_dom.first_near_dom
  13.7 0.0 collective-permute-done.2.far_sub.first_far_sub
  13.7 0.0 collective-permute-done.3.near_sub.first_near_sub
  13.7 2.5 %middle.1 = (f32[9,8,128]{2,1,0:T(8,128)S(1)}, f32[9,8,128]{2,1,0:T(8,128)S(1)}, f32[16,128]{1,0:T(8,128)S(1)}, f32[16,128]{1,0:T(8,128)S(1)}, f32[16,128]{1,0:T(8,128)S(1)}, /*index=5*/f32[16,128]{1,0:T(8,128)S(1)}) custom-call(f32[9,8,128]{2,1,0:T(8,128)S(1)} %get-tuple-element.51.base_ref, f32[9,8,128]{2,1,0:T(8,128)S(1)} %get-tuple-element.40.early_ref, ...), custom_call_target="tpu_custom_call" | custom-call | flops 200000000 | bytes 4000000 | tf_op jit(solution)/shard_map/middle/pallas_call | solution.py:457
  16.3 2.8 %collective-permute-start.4 = (f32[16,128]{1,0:T(8,128)S(1)}, f32[16,128]{1,0:T(8,128)S(1)}, u32[]{:S(2)}, u32[]{:S(2)}) collective-permute-start(f32[16,128]{1,0:T(8,128)S(1)} %get-tuple-element.69), channel_id=1, source_target_pairs={{4,8},{8,4},{12,16},{16,12},{20,24},{24,20},{28,0},{0,28},{5,9},{9... | collective-permute-start | bytes 24584 | tf_op jit(solution)/shard_map/ppermute | solution.py:478
  19.1 0.0 collective-permute-start.5
  19.1 0.0 collective-permute-start.6
  19.1 1.6 %collective-permute-start.7 = (f32[16,128]{1,0:T(8,128)S(1)}, f32[16,128]{1,0:T(8,128)S(1)}, u32[]{:S(2)}, u32[]{:S(2)}) collective-permute-start(f32[16,128]{1,0:T(8,128)S(1)} %get-tuple-element.72), channel_id=1, source_target_pairs={{0,1},{1,0},{2,3},{3,2},{4,5},{5,4},{6,7},{7,6},{8,9},{9,8},{10,11... | collective-permute-start | bytes 24584 | tf_op jit(solution)/shard_map/ppermute | solution.py:478
  20.7 0.4 %local_late.1.base_ref = f32[9,8,128]{2,1,0:T(8,128)S(1)} custom-call(f32[9,8,128]{2,1,0:T(8,128)S(1)} %get-tuple-element.63.middle_ref, f32[9,8,128]{2,1,0:T(8,128)S(1)} %get-tuple-element.64.late_ref, f32[243,8,128]{2,1,0:T(8,128)S(1)} %get-tuple-element.42.star_ref, f32[81,2,8,128]{3,2,1,0:T(8,128)S(1)} %get-tuple-element.65.flux_ref, ...), custom_call_target="tpu_custom_call" | custom-call | flops 200000000 | bytes 4000000 | tf_op jit(solution)/shard_map/local_late/pallas_call | solution.py:457
  21.1 1.6 %collective-permute-done.4.second_far_dom = f32[16,128]{1,0:T(8,128)S(1)} collective-permute-done((f32[16,128]{1,0:T(8,128)S(1)}, f32[16,128]{1,0:T(8,128)S(1)}, u32[]{:S(2)}, u32[]{:S(2)}) %collective-permute-start.4) | collective-permute-done | bytes 8224 | tf_op jit(solution)/shard_map/ppermute | solution.py:478
  22.7 0.1 collective-permute-done.5.second_near_dom
  22.8 0.0 collective-permute-done.6.second_far_sub
  22.8 0.0 collective-permute-done.7.second_near_sub
  22.8 1.9 %final.1 = f32[9,16,56]{2,1,0:T(8,128)} custom-call(f32[9,8,128]{2,1,0:T(8,128)S(1)} %local_late.1.base_ref, f32[9,8,128]{2,1,0:T(8,128)S(1)} %get-tuple-element.64.late_ref, f32[180,16,128]{2,1,0:T(8,128)S(1)} %get-tuple-element.53.remote_ref, bf16[384,256]{1,0:T(8,128)(2,1)S(1)} %get-tuple-element.55.compose_ref, ...), custom_call_target="tpu_custom_call" | custom-call | flops 200000000 | bytes 4000000 | tf_op jit(solution)/shard_map/final/pallas_call | solution.py:457
Async XLA Ops:
  4.0 9.7 %collective-permute-start = (f32[32,128]{1,0:T(8,128)S(1)}, f32[32,128]{1,0:T(8,128)S(1)}, u32[]{:S(2)}, u32[]{:S(2)}) collective-permute-start(f32[32,128]{1,0:T(8,128)S(1)} %get-tuple-element.59), channel_id=1, source_target_pairs={{4,8},{8,4},{12,16},{16,12},{20,24},{24,20},{28,0},{0,28},{5,9},{9... | collective-permute-start | bytes 49160 | tf_op jit(solution)/shard_map/ppermute | solution.py:478
  10.0 3.7 %collective-permute-start.1 = (f32[32,128]{1,0:T(8,128)S(1)}, f32[32,128]{1,0:T(8,128)S(1)}, u32[]{:S(2)}, u32[]{:S(2)}) collective-permute-start(f32[32,128]{1,0:T(8,128)S(1)} %get-tuple-element.60), channel_id=1, source_target_pairs={{0,4},{4,0},{8,12},{12,8},{16,20},{20,16},{24,28},{28,24},{1,5},{5... | collective-permute-start | bytes 49160 | tf_op jit(solution)/shard_map/ppermute | solution.py:478
  10.0 3.7 %collective-permute-start.2 = (f32[32,128]{1,0:T(8,128)S(1)}, f32[32,128]{1,0:T(8,128)S(1)}, u32[]{:S(2)}, u32[]{:S(2)}) collective-permute-start(f32[32,128]{1,0:T(8,128)S(1)} %get-tuple-element.61), channel_id=1, source_target_pairs={{1,2},{2,1},{3,0},{0,3},{5,6},{6,5},{7,4},{4,7},{9,10},{10,9},{11,... | collective-permute-start | bytes 49160 | tf_op jit(solution)/shard_map/ppermute | solution.py:478
  10.7 3.1 %collective-permute-start.3 = (f32[32,128]{1,0:T(8,128)S(1)}, f32[32,128]{1,0:T(8,128)S(1)}, u32[]{:S(2)}, u32[]{:S(2)}) collective-permute-start(f32[32,128]{1,0:T(8,128)S(1)} %get-tuple-element.62), channel_id=1, source_target_pairs={{0,1},{1,0},{2,3},{3,2},{4,5},{5,4},{6,7},{7,6},{8,9},{9,8},{10,11... | collective-permute-start | bytes 49160 | tf_op jit(solution)/shard_map/ppermute | solution.py:478
  16.3 6.4 %collective-permute-start.4 = (f32[16,128]{1,0:T(8,128)S(1)}, f32[16,128]{1,0:T(8,128)S(1)}, u32[]{:S(2)}, u32[]{:S(2)}) collective-permute-start(f32[16,128]{1,0:T(8,128)S(1)} %get-tuple-element.69), channel_id=1, source_target_pairs={{4,8},{8,4},{12,16},{16,12},{20,24},{24,20},{28,0},{0,28},{5,9},{9... | collective-permute-start | bytes 24584 | tf_op jit(solution)/shard_map/ppermute | solution.py:478
  19.1 3.7 %collective-permute-start.5 = (f32[16,128]{1,0:T(8,128)S(1)}, f32[16,128]{1,0:T(8,128)S(1)}, u32[]{:S(2)}, u32[]{:S(2)}) collective-permute-start(f32[16,128]{1,0:T(8,128)S(1)} %get-tuple-element.70), channel_id=1, source_target_pairs={{0,4},{4,0},{8,12},{12,8},{16,20},{20,16},{24,28},{28,24},{1,5},{5... | collective-permute-start | bytes 24584 | tf_op jit(solution)/shard_map/ppermute | solution.py:478
  19.1 3.7 %collective-permute-start.6 = (f32[16,128]{1,0:T(8,128)S(1)}, f32[16,128]{1,0:T(8,128)S(1)}, u32[]{:S(2)}, u32[]{:S(2)}) collective-permute-start(f32[16,128]{1,0:T(8,128)S(1)} %get-tuple-element.71), channel_id=1, source_target_pairs={{1,2},{2,1},{3,0},{0,3},{5,6},{6,5},{7,4},{4,7},{9,10},{10,9},{11,... | collective-permute-start | bytes 24584 | tf_op jit(solution)/shard_map/ppermute | solution.py:478
  19.1 3.7 %collective-permute-start.7 = (f32[16,128]{1,0:T(8,128)S(1)}, f32[16,128]{1,0:T(8,128)S(1)}, u32[]{:S(2)}, u32[]{:S(2)}) collective-permute-start(f32[16,128]{1,0:T(8,128)S(1)} %get-tuple-element.72), channel_id=1, source_target_pairs={{0,1},{1,0},{2,3},{3,2},{4,5},{5,4},{6,7},{7,6},{8,9},{9,8},{10,11... | collective-permute-start | bytes 24584 | tf_op jit(solution)/shard_map/ppermute | solution.py:478

commit v3 on v2

--- a/solution.py
+++ b/solution.py
@@ -91,21 +91,30 @@
     return jnp.take_along_axis(tile, index, axis=1, mode="promise_in_bounds")
 
 
-def star_coefficients(star_ref, work_ref, star_out):
-    fields, kinds = star_ref.shape[0], star_ref.shape[2]
-    tiles = turn_matrices(star_ref, work_ref)
+def star_coefficients(star_ref, stage_ref, star_out):
+    fields, kinds, elements = star_ref.shape[0], star_ref.shape[2], star_ref.shape[3]
     lanes = lane_index((ROWS, LANES))
-    base = (lanes // HALF) * HALF
-    lower = lanes < HALF
+    sublanes = lax.broadcasted_iota(jnp.int32, (ROWS, LANES), 0)
+    pick = jnp.where((lanes % ROWS == sublanes) & (lanes < 2 * elements), 1.0, 0.0)
+    to_lane = lane_index((LANES, LANES))
+    from_lane = lax.broadcasted_iota(jnp.int32, (LANES, LANES), 0)
+    same_half = (from_lane % elements) // ROWS == to_lane // HALF
+    right = jnp.where(same_half & (from_lane < 2 * elements), 1.0, 0.0).astype(BF16)
+    filled = lane_index(stage_ref.shape[1:]) < elements
     for row in range(fields):
-        first, second = tiles[row // 2][0:ROWS], tiles[row // 2][ROWS : 2 * ROWS]
-        if row % 2 == 0:
-            both = jnp.where(lower, first, swap_halves(second))
-        else:
-            both = jnp.where(lower, swap_halves(first), second)
+        for col in range(fields):
+            stage_ref[row, col * 4 : col * 4 + kinds, 0:elements] = star_ref[row, col]
+        values = jnp.where(filled, stage_ref[row], 0.0)
+        high = values.astype(BF16).astype(F32)
+        stage_ref[row] = high + pltpu.roll(values - high, elements, 1)
+        spreads = []
         for kind in range(kinds):
             for col in range(fields):
-                star_out[(row * kinds + kind) * fields + col] = spread(both, base + (col * 4 + kind))
+                at = col * 4 + kind
+                spreads.append(stage_ref[row, at : at + 1, :] * pick)
+        spread_out = product(jnp.concatenate(spreads, axis=0).astype(BF16), right)
+        count = kinds * fields
+        star_out[row * count : (row + 1) * count] = spread_out.reshape(count, ROWS, LANES)
 
 
 def star_mix(columns, star_ref, fields, kinds):
@@ -287,15 +296,13 @@
     )
     stacked = jnp.concatenate([composed[:, face * LANES : (face + 1) * LANES] for face in range(faces)], axis=0)
     compose_out[...] = stack_right(stacked.T)
+    wide_ref[...] = jnp.zeros(wide_ref.shape, F32)
     for face in range(faces):
-        orient_work_ref[...] = jnp.zeros(orient_work_ref.shape, F32)
         for turn in range(turns):
-            rows = slice(turn * face_modes, (turn + 1) * face_modes)
-            orient_work_ref[rows, 0:modes] = -lift_ref[:, face, :]
-            orient_work_ref[rows, HALF : HALF + modes] = -lift_ref[:, face, :]
-        high, low = split(orient_work_ref[...])
-        remote_lift_out[face, 0] = high
-        remote_lift_out[face, 1] = low
+            rows = slice(face * HALF + turn * face_modes, face * HALF + (turn + 1) * face_modes)
+            wide_ref[rows, 0:modes] = -lift_ref[:, face, :]
+            wide_ref[rows, HALF : HALF + modes] = -lift_ref[:, face, :]
+    remote_lift_out[...] = stack_right(wide_ref[...])
 
     elements = slot_ref.shape[1]
     code_ref[...] = jnp.zeros(code_ref.shape, F32)
@@ -327,11 +334,11 @@
 
 def remote_terms(rows_ref, remote_ref, compose_ref, lift_ref, choose_ref, mask_ref, fields):
     pairs = rows_ref.shape[0]
-    faces = lift_ref.shape[0]
+    faces = lift_ref.shape[0] // (3 * HALF)
     elements = choose_ref.shape[0] // faces
     sources = jnp.concatenate([rows_ref[pair] for pair in range(pairs)], axis=1)
     gathered = product(choose_ref[...], jnp.concatenate(split(sources), axis=0))
-    result = None
+    folded = []
     for face in range(faces):
         sums = []
         for col in range(fields):
@@ -343,13 +350,12 @@
             sums.append(total)
         turned = product(stack_left(jnp.concatenate(sums, axis=0)), compose_ref[...])
         mask = mask_ref[face * elements : (face + 1) * elements, :]
-        chosen = turned.reshape(fields, elements, turned.shape[1]) * mask[None]
-        left = stack_left(chosen.reshape(turned.shape))
-        copies = turned.shape[1] // lift_ref.shape[2]
-        high, low = lift_ref[face, 0], lift_ref[face, 1]
-        right = jnp.concatenate([high] * (2 * copies) + [low] * copies, axis=0)
-        lifted = product(left, right)
-        result = lifted if result is None else result + lifted
+        chosen = (turned.reshape(fields, elements, turned.shape[1]) * mask[None]).reshape(turned.shape)
+        both = chosen[:, 0:LANES] + chosen[:, LANES : 2 * LANES]
+        folded.append(both + swap_halves(both))
+    lower = lower_half(folded[0].shape)
+    left = [jnp.where(lower, folded[face], folded[face + 1]) for face in range(0, faces, 2)]
+    result = product(stack_left(jnp.concatenate(left, axis=1)), lift_ref[...])
     result = result.reshape(fields, 2, ROWS, LANES)
     return jnp.where(lower_half((ROWS, LANES))[None], result[:, 0], result[:, 1])
 
@@ -517,7 +523,8 @@
             (packed, F32), (star_shape, F32), ((3 * LANES, kinds * LANES), BF16), ((kinds, LANES, LANES), F32),
         ] + [(array.shape, array.dtype) for array in waiting],
         [
-            (work, F32), ((pairs, elements, LANES), F32), ((pairs, elements, LANES), F32),
+            ((fields, up_to(4 * fields, ROWS), LANES), F32),
+            ((pairs, elements, LANES), F32), ((pairs, elements, LANES), F32),
             (values.shape, F32), (stiffness.shape, F32), (star.shape, F32),
             pltpu.SMEM(send_list.shape, jnp.int32), pltpu.SemaphoreType.DMA((4 + len(LATER),)),
         ],
@@ -537,7 +544,7 @@
             (packed, F32), ((fields * fields, 2, ROWS, LANES), F32),
             ((faces * pairs * fields, elements, LANES), F32),
             ((3 * LANES, kinds * LANES), BF16), ((3 * LANES, 2 * LANES), BF16),
-            ((6 * LANES, LANES), BF16), ((3 * LANES, combos), BF16), ((faces, 2, HALF, LANES), BF16),
+            ((6 * LANES, LANES), BF16), ((3 * LANES, combos), BF16), ((3 * faces * HALF, LANES), BF16),
             ((faces * elements, 2 * sources), BF16), ((faces * elements, combos), F32),
         ],
         [

time: 24.8 us -> 23.1 us (0.931)
  Pallas kernels: 10.7 us -> 9.09 us
    pallas_call x5, Pallas kernels: 10.7 us -> 9.09 us  [call(): pl.pallas_call(kernel, out_shape=shapes, in_specs=ins, out_specs=[VMEM] *...]
where the time goes in v3:
time: 23.1 us; the launch traced here: 23 us
  starting transfers between devices  12.1 us (52%)
  Pallas kernels  9.09 us (39%)
  waiting for transfers between devices  1.79 us (8%)
    ppermute x8, starting transfers between devices, exchange(): arrived[slot] = lax.ppermute(outgoing[slot], axis, pairs)  12.1 us
    pallas_call x5, Pallas kernels, call(): pl.pallas_call(kernel, out_shape=shapes, in_specs=ins, out_specs=[VMEM] *...  9.09 us
    ppermute x8, waiting for transfers between devices, exchange(): arrived[slot] = lax.ppermute(outgoing[slot], axis, pairs)  1.79 us
  transfers between devices with their start and end apart: 8, of which 3 were waited for; matrix products, arithmetic and copies ran while one was open for 0% of the time, Pallas kernels for 10%

profile of v3, /device:TPU:0, one launch (start us, length us, event | category | flops | bytes accessed | tf_op | source)
XLA Modules:
  0.0 23.0 jit_solution(17716019029377475051)
XLA Ops:
  0.0 3.1 %predict.1 = (f32[9,8,128]{2,1,0:T(8,128)S(1)}, f32[9,8,128]{2,1,0:T(8,128)S(1)}, f32[32,128]{1,0:T(8,128)S(1)}, f32[32,128]{1,0:T(8,128)S(1)}, f32[32,128]{1,0:...) custom-call(f32[9,16,56]{2,1,0:T(8,128)} %bitcast.10, ...), custom_call_target="tpu_custom_call" | custom-call | flops 100000000 | bytes 4000000 | tf_op jit(solution)/shard_map/predict/pallas_call | solution.py:463
  3.1 6.0 %collective-permute-start = (f32[32,128]{1,0:T(8,128)S(1)}, f32[32,128]{1,0:T(8,128)S(1)}, u32[]{:S(2)}, u32[]{:S(2)}) collective-permute-start(f32[32,128]{1,0:T(8,128)S(1)} %get-tuple-element.59), channel_id=1, source_target_pairs={{4,8},{8,4},{12,16},{16,12},{20,24},{24,20},{28,0},{0,28},{5,9},{9... | collective-permute-start | bytes 49160 | tf_op jit(solution)/shard_map/ppermute | solution.py:484
  9.1 0.0 collective-permute-start.1
  9.1 0.7 %collective-permute-start.2 = (f32[32,128]{1,0:T(8,128)S(1)}, f32[32,128]{1,0:T(8,128)S(1)}, u32[]{:S(2)}, u32[]{:S(2)}) collective-permute-start(f32[32,128]{1,0:T(8,128)S(1)} %get-tuple-element.61), channel_id=1, source_target_pairs={{1,2},{2,1},{3,0},{0,3},{5,6},{6,5},{7,4},{4,7},{9,10},{10,9},{11,... | collective-permute-start | bytes 49160 | tf_op jit(solution)/shard_map/ppermute | solution.py:484
  9.8 1.0 %collective-permute-start.3 = (f32[32,128]{1,0:T(8,128)S(1)}, f32[32,128]{1,0:T(8,128)S(1)}, u32[]{:S(2)}, u32[]{:S(2)}) collective-permute-start(f32[32,128]{1,0:T(8,128)S(1)} %get-tuple-element.62), channel_id=1, source_target_pairs={{0,1},{1,0},{2,3},{3,2},{4,5},{5,4},{6,7},{7,6},{8,9},{9,8},{10,11... | collective-permute-start | bytes 49160 | tf_op jit(solution)/shard_map/ppermute | solution.py:484
  10.7 2.0 %prepare.1 = (f32[9,8,128]{2,1,0:T(8,128)S(1)}, f32[81,2,8,128]{3,2,1,0:T(8,128)S(1)}, f32[180,16,128]{2,1,0:T(8,128)S(1)}, bf16[384,384]{1,0:T(8,128)(2,1)S(1)}...) custom-call(f32[9,8,128]{2,1,0:T(8,128)S(1)} %get-tuple-element.39.p, ...), custom_call_target="tpu_custom_call" | custom-call | flops 200000000 | bytes 4000000 | tf_op jit(solution)/shard_map/prepare/pallas_call | solution.py:463
  12.7 0.0 collective-permute-done.far_dom.first_far_dom
  12.7 0.1 collective-permute-done.1.near_dom.first_near_dom
  12.9 0.0 collective-permute-done.2.far_sub.first_far_sub
  12.9 0.0 collective-permute-done.3.near_sub.first_near_sub
  12.9 2.1 %middle.1 = (f32[9,8,128]{2,1,0:T(8,128)S(1)}, f32[9,8,128]{2,1,0:T(8,128)S(1)}, f32[16,128]{1,0:T(8,128)S(1)}, f32[16,128]{1,0:T(8,128)S(1)}, f32[16,128]{1,0:T(8,128)S(1)}, /*index=5*/f32[16,128]{1,0:T(8,128)S(1)}) custom-call(f32[9,8,128]{2,1,0:T(8,128)S(1)} %get-tuple-element.51.base_ref, f32[9,8,128]{2,1,0:T(8,128)S(1)} %get-tuple-element.40.early_ref, ...), custom_call_target="tpu_custom_call" | custom-call | flops 200000000 | bytes 4000000 | tf_op jit(solution)/shard_map/middle/pallas_call | solution.py:463
  15.0 2.8 %collective-permute-start.4 = (f32[16,128]{1,0:T(8,128)S(1)}, f32[16,128]{1,0:T(8,128)S(1)}, u32[]{:S(2)}, u32[]{:S(2)}) collective-permute-start(f32[16,128]{1,0:T(8,128)S(1)} %get-tuple-element.69), channel_id=1, source_target_pairs={{4,8},{8,4},{12,16},{16,12},{20,24},{24,20},{28,0},{0,28},{5,9},{9... | collective-permute-start | bytes 24584 | tf_op jit(solution)/shard_map/ppermute | solution.py:484
  17.8 0.0 collective-permute-start.5
  17.8 0.0 collective-permute-start.6
  17.8 1.6 %collective-permute-start.7 = (f32[16,128]{1,0:T(8,128)S(1)}, f32[16,128]{1,0:T(8,128)S(1)}, u32[]{:S(2)}, u32[]{:S(2)}) collective-permute-start(f32[16,128]{1,0:T(8,128)S(1)} %get-tuple-element.72), channel_id=1, source_target_pairs={{0,1},{1,0},{2,3},{3,2},{4,5},{5,4},{6,7},{7,6},{8,9},{9,8},{10,11... | collective-permute-start | bytes 24584 | tf_op jit(solution)/shard_map/ppermute | solution.py:484
  19.4 0.4 %local_late.1.base_ref = f32[9,8,128]{2,1,0:T(8,128)S(1)} custom-call(f32[9,8,128]{2,1,0:T(8,128)S(1)} %get-tuple-element.63.middle_ref, f32[9,8,128]{2,1,0:T(8,128)S(1)} %get-tuple-element.64.late_ref, f32[243,8,128]{2,1,0:T(8,128)S(1)} %get-tuple-element.42.star_ref, f32[81,2,8,128]{3,2,1,0:T(8,128)S(1)} %get-tuple-element.65.flux_ref, ...), custom_call_target="tpu_custom_call" | custom-call | flops 200000000 | bytes 4000000 | tf_op jit(solution)/shard_map/local_late/pallas_call | solution.py:463
  19.8 1.6 %collective-permute-done.4.second_far_dom = f32[16,128]{1,0:T(8,128)S(1)} collective-permute-done((f32[16,128]{1,0:T(8,128)S(1)}, f32[16,128]{1,0:T(8,128)S(1)}, u32[]{:S(2)}, u32[]{:S(2)}) %collective-permute-start.4) | collective-permute-done | bytes 8224 | tf_op jit(solution)/shard_map/ppermute | solution.py:484
  21.4 0.1 collective-permute-done.5.second_near_dom
  21.5 0.0 collective-permute-done.6.second_far_sub
  21.5 0.0 collective-permute-done.7.second_near_sub
  21.5 1.5 %final.1 = f32[9,16,56]{2,1,0:T(8,128)} custom-call(f32[9,8,128]{2,1,0:T(8,128)S(1)} %local_late.1.base_ref, f32[9,8,128]{2,1,0:T(8,128)S(1)} %get-tuple-element.64.late_ref, f32[180,16,128]{2,1,0:T(8,128)S(1)} %get-tuple-element.53.remote_ref, bf16[384,256]{1,0:T(8,128)(2,1)S(1)} %get-tuple-element.55.compose_ref, ...), custom_call_target="tpu_custom_call" | custom-call | flops 200000000 | bytes 4000000 | tf_op jit(solution)/shard_map/final/pallas_call | solution.py:463
Async XLA Ops:
  3.1 9.7 %collective-permute-start = (f32[32,128]{1,0:T(8,128)S(1)}, f32[32,128]{1,0:T(8,128)S(1)}, u32[]{:S(2)}, u32[]{:S(2)}) collective-permute-start(f32[32,128]{1,0:T(8,128)S(1)} %get-tuple-element.59), channel_id=1, source_target_pairs={{4,8},{8,4},{12,16},{16,12},{20,24},{24,20},{28,0},{0,28},{5,9},{9... | collective-permute-start | bytes 49160 | tf_op jit(solution)/shard_map/ppermute | solution.py:484
  9.1 3.7 %collective-permute-start.1 = (f32[32,128]{1,0:T(8,128)S(1)}, f32[32,128]{1,0:T(8,128)S(1)}, u32[]{:S(2)}, u32[]{:S(2)}) collective-permute-start(f32[32,128]{1,0:T(8,128)S(1)} %get-tuple-element.60), channel_id=1, source_target_pairs={{0,4},{4,0},{8,12},{12,8},{16,20},{20,16},{24,28},{28,24},{1,5},{5... | collective-permute-start | bytes 49160 | tf_op jit(solution)/shard_map/ppermute | solution.py:484
  9.1 3.7 %collective-permute-start.2 = (f32[32,128]{1,0:T(8,128)S(1)}, f32[32,128]{1,0:T(8,128)S(1)}, u32[]{:S(2)}, u32[]{:S(2)}) collective-permute-start(f32[32,128]{1,0:T(8,128)S(1)} %get-tuple-element.61), channel_id=1, source_target_pairs={{1,2},{2,1},{3,0},{0,3},{5,6},{6,5},{7,4},{4,7},{9,10},{10,9},{11,... | collective-permute-start | bytes 49160 | tf_op jit(solution)/shard_map/ppermute | solution.py:484
  9.8 3.1 %collective-permute-start.3 = (f32[32,128]{1,0:T(8,128)S(1)}, f32[32,128]{1,0:T(8,128)S(1)}, u32[]{:S(2)}, u32[]{:S(2)}) collective-permute-start(f32[32,128]{1,0:T(8,128)S(1)} %get-tuple-element.62), channel_id=1, source_target_pairs={{0,1},{1,0},{2,3},{3,2},{4,5},{5,4},{6,7},{7,6},{8,9},{9,8},{10,11... | collective-permute-start | bytes 49160 | tf_op jit(solution)/shard_map/ppermute | solution.py:484
  15.0 6.4 %collective-permute-start.4 = (f32[16,128]{1,0:T(8,128)S(1)}, f32[16,128]{1,0:T(8,128)S(1)}, u32[]{:S(2)}, u32[]{:S(2)}) collective-permute-start(f32[16,128]{1,0:T(8,128)S(1)} %get-tuple-element.69), channel_id=1, source_target_pairs={{4,8},{8,4},{12,16},{16,12},{20,24},{24,20},{28,0},{0,28},{5,9},{9... | collective-permute-start | bytes 24584 | tf_op jit(solution)/shard_map/ppermute | solution.py:484
  17.8 3.7 %collective-permute-start.5 = (f32[16,128]{1,0:T(8,128)S(1)}, f32[16,128]{1,0:T(8,128)S(1)}, u32[]{:S(2)}, u32[]{:S(2)}) collective-permute-start(f32[16,128]{1,0:T(8,128)S(1)} %get-tuple-element.70), channel_id=1, source_target_pairs={{0,4},{4,0},{8,12},{12,8},{16,20},{20,16},{24,28},{28,24},{1,5},{5... | collective-permute-start | bytes 24584 | tf_op jit(solution)/shard_map/ppermute | solution.py:484
  17.8 3.7 %collective-permute-start.6 = (f32[16,128]{1,0:T(8,128)S(1)}, f32[16,128]{1,0:T(8,128)S(1)}, u32[]{:S(2)}, u32[]{:S(2)}) collective-permute-start(f32[16,128]{1,0:T(8,128)S(1)} %get-tuple-element.71), channel_id=1, source_target_pairs={{1,2},{2,1},{3,0},{0,3},{5,6},{6,5},{7,4},{4,7},{9,10},{10,9},{11,... | collective-permute-start | bytes 24584 | tf_op jit(solution)/shard_map/ppermute | solution.py:484
  17.8 3.7 %collective-permute-start.7 = (f32[16,128]{1,0:T(8,128)S(1)}, f32[16,128]{1,0:T(8,128)S(1)}, u32[]{:S(2)}, u32[]{:S(2)}) collective-permute-start(f32[16,128]{1,0:T(8,128)S(1)} %get-tuple-element.72), channel_id=1, source_target_pairs={{0,1},{1,0},{2,3},{3,2},{4,5},{5,4},{6,7},{7,6},{8,9},{9,8},{10,11... | collective-permute-start | bytes 24584 | tf_op jit(solution)/shard_map/ppermute | solution.py:484

commit v4 on v3

--- a/solution.py
+++ b/solution.py
@@ -54,6 +54,11 @@
 def message_side(slot):
     odd = odd_place("dom" if slot < 2 else "sub")
     return slot + odd if slot % 2 == 0 else slot - odd
+
+
+def partner_place(slot):
+    odd = odd_place("dom" if slot < 2 else "sub")
+    return odd if slot % 2 == 0 else 1 - odd
 
 
 def lane_index(shape):
@@ -364,9 +369,13 @@
     base_ref, early_ref, late_ref, star_ref, remote_ref, derive_ref, compose_ref, lift_ref, choose_ref, mask_ref,
     rate_hbm, send_hbm, far_dom, near_dom, far_sub, near_sub,
     middle_out, late_out, far_dom_out, near_dom_out, far_sub_out, near_sub_out,
-    rows_ref, late_rows, rate_ref, send_ref, sems,
+    rows_ref, late_rows, rate_ref, send_ref, arrived_ref, sems,
 ):
     copies = [
+        pltpu.make_async_copy(gathered.at[partner_place(side)], arrived_ref.at[side], sems.at[2 + side])
+        for side, gathered in enumerate((far_dom, near_dom, far_sub, near_sub))
+    ]
+    copies += [
         pltpu.make_async_copy(rate_hbm, rate_ref, sems.at[0]),
         pltpu.make_async_copy(send_hbm, send_ref, sems.at[1]),
     ]
@@ -379,10 +388,11 @@
     fast = sends // 2
     elements = 2 * ROWS
     rows_by_pair(early_ref[...].reshape(fields * ROWS, LANES), rows_ref, fields)
-    for side, arrived in enumerate((far_dom, near_dom, far_sub, near_sub)):
+    for side in range(4):
         at = elements + side * sends
+        copies[side].wait()
         for pair in range(pairs):
-            rows_ref[pair, at : at + sends, :] = arrived[pair * sends : (pair + 1) * sends, :]
+            rows_ref[pair, at : at + sends, :] = arrived_ref[side, pair * sends : (pair + 1) * sends, :]
     middle = base_ref[...] + remote_terms(
         rows_ref, remote_ref, compose_ref, lift_ref, choose_ref, mask_ref, fields
     )
@@ -395,7 +405,7 @@
         return current, early + weight_at(0.0, 0.5, degree) * current
 
     _, restart = lax.fori_loop(1, DERIVS, step, (start, taylor_weight(0.0, 0.5, 0) * start))
-    for copy in copies:
+    for copy in copies[4:]:
         copy.wait()
     sublane = lax.broadcasted_iota(jnp.int32, (ROWS, LANES), 0)
     lower = lower_half((ROWS, LANES))
@@ -427,7 +437,7 @@
     base_ref, late_ref, remote_ref, compose_ref, lift_ref, choose_ref, mask_ref,
     first_far_dom, first_near_dom, first_far_sub, first_near_sub,
     second_far_dom, second_near_dom, second_far_sub, second_near_sub,
-    result_out, rows_ref,
+    result_out, rows_ref, first_ref, second_ref, sems,
 ):
     fields = base_ref.shape[0]
     modes = result_out.shape[2]
@@ -435,15 +445,24 @@
     elements = 2 * ROWS
     sends = (rows_ref.shape[1] - elements) // 4
     fast = sends // 2
-    rows_by_pair(late_ref[...].reshape(fields * ROWS, LANES), rows_ref, fields)
     firsts = (first_far_dom, first_near_dom, first_far_sub, first_near_sub)
     seconds = (second_far_dom, second_near_dom, second_far_sub, second_near_sub)
+    copies = []
     for side, (first, second) in enumerate(zip(firsts, seconds)):
+        place = partner_place(side)
+        copies.append(pltpu.make_async_copy(first.at[place], first_ref.at[side], sems.at[2 * side]))
+        copies.append(pltpu.make_async_copy(second.at[place], second_ref.at[side], sems.at[2 * side + 1]))
+    for copy in copies:
+        copy.start()
+    rows_by_pair(late_ref[...].reshape(fields * ROWS, LANES), rows_ref, fields)
+    for copy in copies:
+        copy.wait()
+    for side in range(4):
         at = elements + side * sends
         for pair in range(pairs):
-            rows_ref[pair, at : at + fast, :] = second[pair * fast : (pair + 1) * fast, :]
+            rows_ref[pair, at : at + fast, :] = second_ref[side, pair * fast : (pair + 1) * fast, :]
             row = pairs * sends + pair * fast
-            rows_ref[pair, at + fast : at + sends, :] = first[row : row + fast, :]
+            rows_ref[pair, at + fast : at + sends, :] = first_ref[side, row : row + fast, :]
     result = base_ref[...] + remote_terms(
         rows_ref, remote_ref, compose_ref, lift_ref, choose_ref, mask_ref, fields
     )
@@ -480,8 +499,8 @@
         pairs = []
         for even in range(first, size, 2):
             odd = (even + 1) % size
-            pairs += [(even, odd), (odd, even)]
-        arrived[slot] = lax.ppermute(outgoing[slot], axis, pairs)
+            pairs += [[even, odd]]
+        arrived[slot] = lax.all_gather(outgoing[slot], axis, axis_index_groups=pairs)
     return arrived
 
 
@@ -556,12 +575,12 @@
     )
     middle, late_value, *outgoing = call(
         middle_kernel,
-        [VMEM] * 10 + [HBM] * 2 + [VMEM] * 4,
+        [VMEM] * 10 + [HBM] * 6,
         [(packed, F32)] * 2 + [(second_shape, F32)] * sides,
         [
             ((pairs, sources, LANES), F32), ((pairs, elements, LANES), F32),
             pltpu.SMEM(cluster_rate.shape, jnp.int32), pltpu.SMEM(send_list.shape, jnp.int32),
-            pltpu.SemaphoreType.DMA((2,)),
+            ((sides, *first_shape), F32), pltpu.SemaphoreType.DMA((2 + sides,)),
         ],
         (
             base, early, late, star_coef, remote_coef, derive_op, compose_op, remote_lift, choose, mask,
@@ -580,9 +599,12 @@
     )
     (result,) = call(
         final_kernel,
-        [VMEM] * 15,
+        [VMEM] * 7 + [HBM] * 8,
         [(values.shape, F32)],
-        [((pairs, sources, LANES), F32)],
+        [
+            ((pairs, sources, LANES), F32), ((sides, *first_shape), F32), ((sides, *second_shape), F32),
+            pltpu.SemaphoreType.DMA((2 * sides,)),
+        ],
         (base, late_value, remote_coef, compose_op, remote_lift, choose, mask, *first, *second),
         "final", 200_000_000,
     )

time: 23.1 us -> 47.5 us (2.06)
  blocking collectives: 0 us -> 36.4 us
  starting transfers between devices: 12.1 us -> 0 us
  waiting for transfers between devices: 1.79 us -> 0 us
  Pallas kernels: 9.09 us -> 10.7 us
    all_gather x0 -> x8, blocking collectives: none -> 36.4 us  [exchange(): lax.all_gather(outgoing[slot], axis, axis_index_groups=pairs)]
    ppermute x8 -> x0, starting transfers between devices: 12.1 us -> none  [exchange(): arrived[slot] = lax.ppermute(outgoing[slot], axis, pairs)]
    ppermute x8 -> x0, waiting for transfers between devices: 1.79 us -> none  [exchange(): arrived[slot] = lax.ppermute(outgoing[slot], axis, pairs)]
    pallas_call x5, Pallas kernels: 9.09 us -> 10.7 us  [call(): pl.pallas_call(kernel, out_shape=shapes, in_specs=ins, out_specs=[VMEM] *...]
  transfers between devices with their start and end apart: 8 -> 0, of which waited for: 3 -> 0; matrix products, arithmetic and copies ran while one was open for 0% -> 0% of each run, Pallas kernels for 10% -> 0%
where the time goes in v4:
time: 47.5 us; the launch traced here: 47.2 us
  blocking collectives  36.4 us (77%)
  Pallas kernels  10.7 us (23%)
    all_gather x8, blocking collectives, exchange(): lax.all_gather(outgoing[slot], axis, axis_index_groups=pairs)  36.4 us
    pallas_call x5, Pallas kernels, call(): pl.pallas_call(kernel, out_shape=shapes, in_specs=ins, out_specs=[VMEM] *...  10.7 us

profile of v4, /device:TPU:0, one launch (start us, length us, event | category | flops | bytes accessed | tf_op | source)
XLA Modules:
  0.0 47.2 jit_solution(7422951097887067590)
XLA Ops:
  0.0 3.1 %predict.1 = (f32[9,8,128]{2,1,0:T(8,128)S(1)}, f32[9,8,128]{2,1,0:T(8,128)S(1)}, f32[32,128]{1,0:T(8,128)S(1)}, f32[32,128]{1,0:T(8,128)S(1)}, f32[32,128]{1,0:...) custom-call(f32[9,16,56]{2,1,0:T(8,128)} %bitcast.26, ...), custom_call_target="tpu_custom_call" | custom-call | flops 100000000 | bytes 4000000 | tf_op jit(solution)/shard_map/predict/pallas_call | solution.py:482
  3.1 2.0 %prepare.1 = (f32[9,8,128]{2,1,0:T(8,128)S(1)}, f32[81,2,8,128]{3,2,1,0:T(8,128)S(1)}, f32[180,16,128]{2,1,0:T(8,128)S(1)}, bf16[384,384]{1,0:T(8,128)(2,1)S(1)}...) custom-call(f32[9,8,128]{2,1,0:T(8,128)S(1)} %get-tuple-element.39.p, ...), custom_call_target="tpu_custom_call" | custom-call | flops 200000000 | bytes 4000000 | tf_op jit(solution)/shard_map/prepare/pallas_call | solution.py:482
  5.1 8.5 %all-gather = f32[64,128]{1,0:T(8,128)} all-gather(f32[32,128]{1,0:T(8,128)S(1)} %get-tuple-element.59), channel_id=2, replica_groups={{4,8},{12,16},{20,24},{28,0},{5,9},{13,17},{21,25},{29,1},{6,10},{14,18..., dimensions={0}, use_global_device_ids=true | all-gather | bytes 49152 | tf_op jit(solution)/shard_map/all_gather | solution.py:503
  13.5 4.5 %all-gather.1 = f32[64,128]{1,0:T(8,128)} all-gather(f32[32,128]{1,0:T(8,128)S(1)} %get-tuple-element.60), channel_id=3, replica_groups={{0,4},{8,12},{16,20},{24,28},{1,5},{9,13},{17,21},{25,29},{2,6},{10,14}..., dimensions={0}, use_global_device_ids=true | all-gather | bytes 49152 | tf_op jit(solution)/shard_map/all_gather | solution.py:503
  18.0 3.9 %all-gather.2 = f32[64,128]{1,0:T(8,128)} all-gather(f32[32,128]{1,0:T(8,128)S(1)} %get-tuple-element.61), channel_id=4, replica_groups={{1,2},{3,0},{5,6},{7,4},{9,10},{11,8},{13,14},{15,12},{17,18},{19,16},{..., dimensions={0}, use_global_device_ids=true | all-gather | bytes 49152 | tf_op jit(solution)/shard_map/all_gather | solution.py:503
  22.0 2.0 %all-gather.3 = f32[64,128]{1,0:T(8,128)} all-gather(f32[32,128]{1,0:T(8,128)S(1)} %get-tuple-element.62), channel_id=5, replica_groups={{0,1},{2,3},{4,5},{6,7},{8,9},{10,11},{12,13},{14,15},{16,17},{18,19},{..., dimensions={0}, use_global_device_ids=true | all-gather | bytes 49152 | tf_op jit(solution)/shard_map/all_gather | solution.py:503
  23.9 2.9 %middle.1 = (f32[9,8,128]{2,1,0:T(8,128)S(1)}, f32[9,8,128]{2,1,0:T(8,128)S(1)}, f32[16,128]{1,0:T(8,128)S(1)}, f32[16,128]{1,0:T(8,128)S(1)}, f32[16,128]{1,0:T(8,128)S(1)}, /*index=5*/f32[16,128]{1,0:T(8,128)S(1)}) custom-call(f32[9,8,128]{2,1,0:T(8,128)S(1)} %get-tuple-element.51.base_ref, f32[9,8,128]{2,1,0:T(8,128)S(1)} %get-tuple-element.40.early_ref, ...), custom_call_target="tpu_custom_call" | custom-call | flops 200000000 | bytes 4000000 | tf_op jit(solution)/shard_map/middle/pallas_call | solution.py:482
  26.8 0.4 local_late.1.base_ref
  27.3 7.3 %all-gather.4 = f32[32,128]{1,0:T(8,128)} all-gather(f32[16,128]{1,0:T(8,128)S(1)} %get-tuple-element.69), channel_id=6, replica_groups={{4,8},{12,16},{20,24},{28,0},{5,9},{13,17},{21,25},{29,1},{6,10},{14,18..., dimensions={0}, use_global_device_ids=true | all-gather | bytes 24576 | tf_op jit(solution)/shard_map/all_gather | solution.py:503
  34.6 4.5 %all-gather.5 = f32[32,128]{1,0:T(8,128)} all-gather(f32[16,128]{1,0:T(8,128)S(1)} %get-tuple-element.70), channel_id=7, replica_groups={{0,4},{8,12},{16,20},{24,28},{1,5},{9,13},{17,21},{25,29},{2,6},{10,14}..., dimensions={0}, use_global_device_ids=true | all-gather | bytes 24576 | tf_op jit(solution)/shard_map/all_gather | solution.py:503
  39.0 3.9 %all-gather.6 = f32[32,128]{1,0:T(8,128)} all-gather(f32[16,128]{1,0:T(8,128)S(1)} %get-tuple-element.71), channel_id=8, replica_groups={{1,2},{3,0},{5,6},{7,4},{9,10},{11,8},{13,14},{15,12},{17,18},{19,16},{..., dimensions={0}, use_global_device_ids=true | all-gather | bytes 24576 | tf_op jit(solution)/shard_map/all_gather | solution.py:503
  42.9 1.9 %all-gather.7 = f32[32,128]{1,0:T(8,128)} all-gather(f32[16,128]{1,0:T(8,128)S(1)} %get-tuple-element.72), channel_id=9, replica_groups={{0,1},{2,3},{4,5},{6,7},{8,9},{10,11},{12,13},{14,15},{16,17},{18,19},{..., dimensions={0}, use_global_device_ids=true | all-gather | bytes 24576 | tf_op jit(solution)/shard_map/all_gather | solution.py:503
  44.8 2.3 %final.1 = f32[9,16,56]{2,1,0:T(8,128)} custom-call(f32[9,8,128]{2,1,0:T(8,128)S(1)} %local_late.1.base_ref, f32[9,8,128]{2,1,0:T(8,128)S(1)} %get-tuple-element.64.late_ref, f32[180,16,128]{2,1,0:T(8,128)S(1)} %get-tuple-element.53.remote_ref, bf16[384,256]{1,0:T(8,128)(2,1)S(1)} %get-tuple-element.55.compose_ref, ...), custom_call_target="tpu_custom_call" | custom-call | flops 200000000 | bytes 4000000 | tf_op jit(solution)/shard_map/final/pallas_call | solution.py:482

commit v5 on v3

--- a/solution.py
+++ b/solution.py
@@ -14,6 +14,8 @@
 F32 = jnp.float32
 BF16 = jnp.bfloat16
 LATER = ("flux_local", "flux_remote", "face_restrict", "face_lift", "orient_maps", "slot", "face", "turn")
+AXES = ("dom", "sub")
+SWAPS = (("dom", False), ("sub", False), ("sub", True), ("dom", True))
 
 
 def taylor_weight(lower, upper, degree):
@@ -52,8 +54,15 @@
 
 
 def message_side(slot):
-    odd = odd_place("dom" if slot < 2 else "sub")
-    return slot + odd if slot % 2 == 0 else slot - odd
+    axis, far = SWAPS[slot]
+    odd = odd_place(axis)
+    return 2 * AXES.index(axis) + (odd if far else 1 - odd)
+
+
+def ghost_slot(side):
+    axis = AXES[side // 2]
+    even_far = side % 2 == 0
+    return jnp.where(odd_place(axis) == 0, SWAPS.index((axis, even_far)), SWAPS.index((axis, not even_far)))
 
 
 def lane_index(shape):
@@ -128,29 +137,27 @@
     return jnp.concatenate(sums, axis=0)
 
 
-def stiffness_blocks(stiffness_ref, block_ref):
+def stiffness_blocks(stiffness_ref, block_ref, turned):
     kinds, modes = stiffness_ref.shape[0], stiffness_ref.shape[1]
     block_ref[...] = jnp.zeros(block_ref.shape, F32)
     for kind in range(kinds):
-        block_ref[kind, 0:modes, 0:modes] = stiffness_ref[kind]
-        block_ref[kind, HALF : HALF + modes, HALF : HALF + modes] = stiffness_ref[kind]
-
-
-def derive_operator(block_ref):
-    return jnp.concatenate([-block_ref[kind].T for kind in range(block_ref.shape[0])], axis=1)
+        matrix = -stiffness_ref[kind].T if turned else stiffness_ref[kind]
+        block_ref[kind, 0:modes, 0:modes] = matrix
+        block_ref[kind, HALF : HALF + modes, HALF : HALF + modes] = matrix
+    return jnp.concatenate([block_ref[kind] for kind in range(kinds)], axis=1)
 
 
 def predict_kernel(*refs):
     later = len(LATER)
     solution_hbm, stiffness_hbm, star_hbm, send_hbm = refs[0:4]
     later_hbm, refs = refs[4 : 4 + later], refs[4 + later :]
-    early_out, late_out, far_dom_out, near_dom_out, far_sub_out, near_sub_out = refs[0:6]
-    packed_ref, coef_ref, derive_ref, block_ref = refs[6:10]
+    early_out, late_out, near_dom_out, near_sub_out, far_sub_out, far_dom_out = refs[0:6]
+    packed_ref, coef_ref, derive_ref, stiffness_ref = refs[6:10]
     later_out, refs = refs[10 : 10 + later], refs[10 + later :]
-    work_ref, early_rows, late_rows, solution_ref, stiffness_ref, star_ref, send_ref, sems = refs
-
-    sources = (stiffness_hbm, star_hbm, solution_hbm, send_hbm, *later_hbm)
-    targets = (stiffness_ref, star_ref, solution_ref, send_ref, *later_out)
+    work_ref, early_rows, late_rows, solution_ref, block_ref, star_ref, send_ref, sems = refs
+
+    sources = (star_hbm, stiffness_hbm, solution_hbm, send_hbm, *later_hbm)
+    targets = (star_ref, stiffness_ref, solution_ref, send_ref, *later_out)
     copies = [
         pltpu.make_async_copy(source, target, sems.at[number])
         for number, (source, target) in enumerate(zip(sources, targets))
@@ -159,12 +166,10 @@
         copy.start()
     fields, kinds = star_ref.shape[0], star_ref.shape[2]
     pairs = (fields + 1) // 2
-    copies[0].wait()
-    stiffness_blocks(stiffness_ref, block_ref)
-    derive_ref[...] = stack_right(derive_operator(block_ref))
-    copies[1].wait()
+    for copy in copies[0:3]:
+        copy.wait()
+    derive_ref[...] = stack_right(stiffness_blocks(stiffness_ref, block_ref, True))
     star_coefficients(star_ref, work_ref, coef_ref)
-    copies[2].wait()
     pack(solution_ref, packed_ref)
     start = packed_ref[...].reshape(fields * ROWS, LANES)
 
@@ -185,7 +190,7 @@
     copies[3].wait()
     sends = send_ref.shape[2]
     fast = sends // 2
-    for side, out in enumerate((far_dom_out, near_dom_out, far_sub_out, near_sub_out)):
+    for side, out in enumerate((near_dom_out, near_sub_out, far_sub_out, far_dom_out)):
         out[...] = jnp.zeros(out.shape, F32)
         for place in range(sends):
             element = send_ref[0, message_side(side), place]
@@ -257,20 +262,20 @@
 
 
 def prepare_kernel(
-    packed_ref, early_ref, block_ref, star_ref, flux_local_ref, flux_remote_ref, restrict_ref, lift_ref, orient_ref,
+    packed_ref, early_ref, stiffness_ref, star_ref, flux_local_ref, flux_remote_ref, restrict_ref, lift_ref, orient_ref,
     slot_ref, face_ref, turn_ref,
     base_out, local_out, remote_out, volume_out, trace_out, local_lift_out, compose_out,
     remote_lift_out, choose_out, mask_out,
-    work_ref, wide_ref, face_work_ref, orient_work_ref, code_ref,
+    work_ref, block_ref, wide_ref, face_work_ref, orient_work_ref, code_ref,
 ):
-    fields, kinds = packed_ref.shape[0], block_ref.shape[0]
+    fields, kinds = packed_ref.shape[0], stiffness_ref.shape[0]
     face_modes, faces, modes = restrict_ref.shape
     turns = orient_ref.shape[0]
     work_ref[...] = jnp.zeros(work_ref.shape, F32)
     flux_local_coefficients(flux_local_ref, work_ref, local_out)
     flux_remote_coefficients(flux_remote_ref, work_ref, remote_out)
 
-    volume_out[...] = stack_right(jnp.concatenate([block_ref[kind] for kind in range(kinds)], axis=1))
+    volume_out[...] = stack_right(stiffness_blocks(stiffness_ref, block_ref, False))
 
     wide_ref[...] = jnp.zeros(wide_ref.shape, F32)
     for mode in range(face_modes):
@@ -295,7 +300,8 @@
         orient_work_ref[...], face_work_ref[...], precision=lax.Precision.HIGHEST, preferred_element_type=F32
     )
     stacked = jnp.concatenate([composed[:, face * LANES : (face + 1) * LANES] for face in range(faces)], axis=0)
-    compose_out[...] = stack_right(stacked.T)
+    high, low = split(stacked.T[0:HALF])
+    compose_out[...] = jnp.concatenate([high, high, low, jnp.zeros_like(low)], axis=0)
     wide_ref[...] = jnp.zeros(wide_ref.shape, F32)
     for face in range(faces):
         for turn in range(turns):
@@ -309,8 +315,9 @@
     slots = slot_ref[...]
     sends = (choose_out.shape[1] // 2 - elements) // 4
     group = (slots - elements) // sends
-    odd = jnp.where(group < 2, odd_place("dom"), odd_place("sub"))
-    moved = slots + jnp.where(group % 2 == 0, sends, -sends) * odd
+    moved = slots
+    for side in range(4):
+        moved = jnp.where(group == side, slots + (ghost_slot(side) - side) * sends, moved)
     code_ref[0:faces, 0:elements] = jnp.where(slots < elements, slots, moved).astype(F32)
     code_ref[faces : 2 * faces, 0:elements] = (face_ref[...] * turns + turn_ref[...]).astype(F32)
     codes = code_ref[...].T[0:elements, :]
@@ -348,7 +355,10 @@
                 term = remote_ref[(face * pairs + pair) * fields + col] * part
                 total = term if total is None else total + term
             sums.append(total)
-        turned = product(stack_left(jnp.concatenate(sums, axis=0)), compose_ref[...])
+        mixed = jnp.concatenate(sums, axis=0)
+        high, low = split(mixed + swap_halves(mixed))
+        first = jnp.where(lower_half(high.shape), high, low)
+        turned = product(jnp.concatenate([first, high], axis=1), compose_ref[...])
         mask = mask_ref[face * elements : (face + 1) * elements, :]
         chosen = (turned.reshape(fields, elements, turned.shape[1]) * mask[None]).reshape(turned.shape)
         both = chosen[:, 0:LANES] + chosen[:, LANES : 2 * LANES]
@@ -362,8 +372,8 @@
 
 def middle_kernel(
     base_ref, early_ref, late_ref, star_ref, remote_ref, derive_ref, compose_ref, lift_ref, choose_ref, mask_ref,
-    rate_hbm, send_hbm, far_dom, near_dom, far_sub, near_sub,
-    middle_out, late_out, far_dom_out, near_dom_out, far_sub_out, near_sub_out,
+    rate_hbm, send_hbm, near_dom, near_sub, far_sub, far_dom,
+    middle_out, late_out, near_dom_out, near_sub_out, far_sub_out, far_dom_out,
     rows_ref, late_rows, rate_ref, send_ref, sems,
 ):
     copies = [
@@ -379,7 +389,7 @@
     fast = sends // 2
     elements = 2 * ROWS
     rows_by_pair(early_ref[...].reshape(fields * ROWS, LANES), rows_ref, fields)
-    for side, arrived in enumerate((far_dom, near_dom, far_sub, near_sub)):
+    for side, arrived in enumerate((near_dom, near_sub, far_sub, far_dom)):
         at = elements + side * sends
         for pair in range(pairs):
             rows_ref[pair, at : at + sends, :] = arrived[pair * sends : (pair + 1) * sends, :]
@@ -406,7 +416,7 @@
     late = jnp.where((is_fast == 2)[None], restart.reshape(fields, ROWS, LANES), late_ref[...])
     late_out[...] = late
     rows_by_pair(late.reshape(fields * ROWS, LANES), late_rows, fields)
-    for side, out in enumerate((far_dom_out, near_dom_out, far_sub_out, near_sub_out)):
+    for side, out in enumerate((near_dom_out, near_sub_out, far_sub_out, far_dom_out)):
         out[...] = jnp.zeros(out.shape, F32)
         for place in range(fast):
             element = send_ref[0, message_side(side), place]
@@ -425,8 +435,8 @@
 
 def final_kernel(
     base_ref, late_ref, remote_ref, compose_ref, lift_ref, choose_ref, mask_ref,
-    first_far_dom, first_near_dom, first_far_sub, first_near_sub,
-    second_far_dom, second_near_dom, second_far_sub, second_near_sub,
+    first_near_dom, first_near_sub, first_far_sub, first_far_dom,
+    second_near_dom, second_near_sub, second_far_sub, second_far_dom,
     result_out, rows_ref,
 ):
     fields = base_ref.shape[0]
@@ -436,8 +446,8 @@
     sends = (rows_ref.shape[1] - elements) // 4
     fast = sends // 2
     rows_by_pair(late_ref[...].reshape(fields * ROWS, LANES), rows_ref, fields)
-    firsts = (first_far_dom, first_near_dom, first_far_sub, first_near_sub)
-    seconds = (second_far_dom, second_near_dom, second_far_sub, second_near_sub)
+    firsts = (first_near_dom, first_near_sub, first_far_sub, first_far_dom)
+    seconds = (second_near_dom, second_near_sub, second_far_sub, second_far_dom)
     for side, (first, second) in enumerate(zip(firsts, seconds)):
         at = elements + side * sends
         for pair in range(pairs):
@@ -473,15 +483,15 @@
 
 
 def exchange(outgoing):
-    arrived = [None] * 4
-    for slot, axis, first in ((0, "dom", 1), (2, "sub", 1), (1, "dom", 0), (3, "sub", 0)):
+    arrived = []
+    for (axis, far), message in zip(SWAPS, outgoing):
         size = lax.axis_size(axis)
         assert size % 2 == 0
         pairs = []
-        for even in range(first, size, 2):
-            odd = (even + 1) % size
-            pairs += [(even, odd), (odd, even)]
-        arrived[slot] = lax.ppermute(outgoing[slot], axis, pairs)
+        for first in range(1 if far else 0, size, 2):
+            second = (first + 1) % size
+            pairs += [(first, second), (second, first)]
+        arrived.append(lax.ppermute(message, axis, pairs))
     return arrived
 
 
@@ -520,19 +530,19 @@
         predict_kernel,
         [HBM] * (4 + len(LATER)),
         [(packed, F32)] * 2 + [(first_shape, F32)] * sides + [
-            (packed, F32), (star_shape, F32), ((3 * LANES, kinds * LANES), BF16), ((kinds, LANES, LANES), F32),
+            (packed, F32), (star_shape, F32), ((3 * LANES, kinds * LANES), BF16), (stiffness.shape, F32),
         ] + [(array.shape, array.dtype) for array in waiting],
         [
             ((fields, up_to(4 * fields, ROWS), LANES), F32),
             ((pairs, elements, LANES), F32), ((pairs, elements, LANES), F32),
-            (values.shape, F32), (stiffness.shape, F32), (star.shape, F32),
+            (values.shape, F32), ((kinds, LANES, LANES), F32), (star.shape, F32),
             pltpu.SMEM(send_list.shape, jnp.int32), pltpu.SemaphoreType.DMA((4 + len(LATER),)),
         ],
         (values, stiffness, star, send_list, *waiting),
         "predict", 100_000_000,
     )
     early, late, outgoing = made[0], made[1], made[2 : 2 + sides]
-    start, star_coef, derive_op, blocks = made[2 + sides : 6 + sides]
+    start, star_coef, derive_op, stiffness_kept = made[2 + sides : 6 + sides]
     waiting = made[6 + sides :]
     first = exchange(outgoing)
     (
@@ -544,14 +554,14 @@
             (packed, F32), ((fields * fields, 2, ROWS, LANES), F32),
             ((faces * pairs * fields, elements, LANES), F32),
             ((3 * LANES, kinds * LANES), BF16), ((3 * LANES, 2 * LANES), BF16),
-            ((6 * LANES, LANES), BF16), ((3 * LANES, combos), BF16), ((3 * faces * HALF, LANES), BF16),
+            ((6 * LANES, LANES), BF16), ((2 * LANES, combos), BF16), ((3 * faces * HALF, LANES), BF16),
             ((faces * elements, 2 * sources), BF16), ((faces * elements, combos), F32),
         ],
         [
-            (work, F32), ((2 * LANES, LANES), F32),
+            (work, F32), ((kinds, LANES, LANES), F32), ((2 * LANES, LANES), F32),
             ((LANES, faces * LANES), F32), ((HALF, LANES), F32), ((LANES, LANES), F32),
         ],
-        (start, early, blocks, star_coef, *waiting),
+        (start, early, stiffness_kept, star_coef, *waiting),
         "prepare", 200_000_000,
     )
     middle, late_value, *outgoing = call(

time: 23.1 us -> 24.9 us (1.078)
  waiting for transfers between devices: 1.79 us -> 2.94 us
  starting transfers between devices: 12.1 us -> 12.6 us
    ppermute x8, waiting for transfers between devices: 1.79 us -> 2.94 us  [exchange(): arrived.append(lax.ppermute(message, axis, pairs))]
    ppermute x8, starting transfers between devices: 12.1 us -> 12.6 us  [exchange(): arrived.append(lax.ppermute(message, axis, pairs))]
  transfers between devices with their start and end apart: 8 -> 8, of which waited for: 3 -> 2; matrix products, arithmetic and copies ran while one was open for 0% -> 0% of each run, Pallas kernels for 10% -> 11%
where the time goes in v5:
time: 24.9 us; the launch traced here: 24.8 us
  starting transfers between devices  12.6 us (51%)
  Pallas kernels  9.16 us (37%)
  waiting for transfers between devices  2.94 us (12%)
    ppermute x8, starting transfers between devices, exchange(): arrived.append(lax.ppermute(message, axis, pairs))  12.6 us
    pallas_call x5, Pallas kernels, call(): pl.pallas_call(kernel, out_shape=shapes, in_specs=ins, out_specs=[VMEM] *...  9.16 us
    ppermute x8, waiting for transfers between devices, exchange(): arrived.append(lax.ppermute(message, axis, pairs))  2.94 us
  transfers between devices with their start and end apart: 8, of which 2 were waited for; matrix products, arithmetic and copies ran while one was open for 0% of the time, Pallas kernels for 11%

profile of v5, /device:TPU:0, one launch (start us, length us, event | category | flops | bytes accessed | tf_op | source)
XLA Modules:
  0.0 24.8 jit_solution(16418312955175073164)
XLA Ops:
  0.0 2.9 %predict.1 = (f32[9,8,128]{2,1,0:T(8,128)S(1)}, f32[9,8,128]{2,1,0:T(8,128)S(1)}, f32[32,128]{1,0:T(8,128)S(1)}, f32[32,128]{1,0:T(8,128)S(1)}, f32[32,128]{1,0:...) custom-call(f32[9,16,56]{2,1,0:T(8,128)} %bitcast.10, ...), custom_call_target="tpu_custom_call" | custom-call | flops 100000000 | bytes 4000000 | tf_op jit(solution)/shard_map/predict/pallas_call | solution.py:473
  2.9 3.0 %collective-permute-start = (f32[32,128]{1,0:T(8,128)S(1)}, f32[32,128]{1,0:T(8,128)S(1)}, u32[]{:S(2)}, u32[]{:S(2)}) collective-permute-start(f32[32,128]{1,0:T(8,128)S(1)} %get-tuple-element.59), channel_id=1, source_target_pairs={{0,4},{4,0},{8,12},{12,8},{16,20},{20,16},{24,28},{28,24},{1,5},{5... | collective-permute-start | bytes 49160 | tf_op jit(solution)/shard_map/ppermute | solution.py:494
  5.9 0.0 collective-permute-start.1
  5.9 1.6 %collective-permute-start.2 = (f32[32,128]{1,0:T(8,128)S(1)}, f32[32,128]{1,0:T(8,128)S(1)}, u32[]{:S(2)}, u32[]{:S(2)}) collective-permute-start(f32[32,128]{1,0:T(8,128)S(1)} %get-tuple-element.61), channel_id=1, source_target_pairs={{1,2},{2,1},{3,0},{0,3},{5,6},{6,5},{7,4},{4,7},{9,10},{10,9},{11,... | collective-permute-start | bytes 49160 | tf_op jit(solution)/shard_map/ppermute | solution.py:494
  7.6 3.6 %collective-permute-start.3 = (f32[32,128]{1,0:T(8,128)S(1)}, f32[32,128]{1,0:T(8,128)S(1)}, u32[]{:S(2)}, u32[]{:S(2)}) collective-permute-start(f32[32,128]{1,0:T(8,128)S(1)} %get-tuple-element.62), channel_id=1, source_target_pairs={{4,8},{8,4},{12,16},{16,12},{20,24},{24,20},{28,0},{0,28},{5,9},{9... | collective-permute-start | bytes 49160 | tf_op jit(solution)/shard_map/ppermute | solution.py:494
  11.2 2.2 %prepare.1 = (f32[9,8,128]{2,1,0:T(8,128)S(1)}, f32[81,2,8,128]{3,2,1,0:T(8,128)S(1)}, f32[180,16,128]{2,1,0:T(8,128)S(1)}, bf16[384,384]{1,0:T(8,128)(2,1)S(1)}...) custom-call(f32[9,8,128]{2,1,0:T(8,128)S(1)} %get-tuple-element.39.p, ...), custom_call_target="tpu_custom_call" | custom-call | flops 200000000 | bytes 4000000 | tf_op jit(solution)/shard_map/prepare/pallas_call | solution.py:473
  13.3 0.0 collective-permute-done.near_dom.first_near_dom
  13.4 0.0 collective-permute-done.1.near_sub.first_near_sub
  13.4 0.0 collective-permute-done.2.far_sub.first_far_sub
  13.4 0.6 %collective-permute-done.3.far_dom.first_far_dom = f32[32,128]{1,0:T(8,128)S(1)} collective-permute-done((f32[32,128]{1,0:T(8,128)S(1)}, f32[32,128]{1,0:T(8,128)S(1)}, u32[]{:S(2)}, u32[]{:S(2)}) %collective-permute-start.3) | collective-permute-done | bytes 16416 | tf_op jit(solution)/shard_map/ppermute | solution.py:494
  14.0 2.1 %middle.1 = (f32[9,8,128]{2,1,0:T(8,128)S(1)}, f32[9,8,128]{2,1,0:T(8,128)S(1)}, f32[16,128]{1,0:T(8,128)S(1)}, f32[16,128]{1,0:T(8,128)S(1)}, f32[16,128]{1,0:T(8,128)S(1)}, /*index=5*/f32[16,128]{1,0:T(8,128)S(1)}) custom-call(f32[9,8,128]{2,1,0:T(8,128)S(1)} %get-tuple-element.51.base_ref, f32[9,8,128]{2,1,0:T(8,128)S(1)} %get-tuple-element.40.early_ref, ...), custom_call_target="tpu_custom_call" | custom-call | flops 200000000 | bytes 4000000 | tf_op jit(solution)/shard_map/middle/pallas_call | solution.py:473
  16.2 0.1 collective-permute-start.4
  16.2 0.1 collective-permute-start.5
  16.3 0.6 %collective-permute-start.6 = (f32[16,128]{1,0:T(8,128)S(1)}, f32[16,128]{1,0:T(8,128)S(1)}, u32[]{:S(2)}, u32[]{:S(2)}) collective-permute-start(f32[16,128]{1,0:T(8,128)S(1)} %get-tuple-element.71), channel_id=1, source_target_pairs={{1,2},{2,1},{3,0},{0,3},{5,6},{6,5},{7,4},{4,7},{9,10},{10,9},{11,... | collective-permute-start | bytes 24584 | tf_op jit(solution)/shard_map/ppermute | solution.py:494
  16.9 3.6 %collective-permute-start.7 = (f32[16,128]{1,0:T(8,128)S(1)}, f32[16,128]{1,0:T(8,128)S(1)}, u32[]{:S(2)}, u32[]{:S(2)}) collective-permute-start(f32[16,128]{1,0:T(8,128)S(1)} %get-tuple-element.72), channel_id=1, source_target_pairs={{4,8},{8,4},{12,16},{16,12},{20,24},{24,20},{28,0},{0,28},{5,9},{9... | collective-permute-start | bytes 24584 | tf_op jit(solution)/shard_map/ppermute | solution.py:494
  20.5 0.4 %local_late.1.base_ref = f32[9,8,128]{2,1,0:T(8,128)S(1)} custom-call(f32[9,8,128]{2,1,0:T(8,128)S(1)} %get-tuple-element.63.middle_ref, f32[9,8,128]{2,1,0:T(8,128)S(1)} %get-tuple-element.64.late_ref, f32[243,8,128]{2,1,0:T(8,128)S(1)} %get-tuple-element.42.star_ref, f32[81,2,8,128]{3,2,1,0:T(8,128)S(1)} %get-tuple-element.65.flux_ref, ...), custom_call_target="tpu_custom_call" | custom-call | flops 200000000 | bytes 4000000 | tf_op jit(solution)/shard_map/local_late/pallas_call | solution.py:473
  21.0 0.0 collective-permute-done.4.second_near_dom
  21.0 0.0 collective-permute-done.5.second_near_sub
  21.0 0.0 collective-permute-done.6.second_far_sub
  21.0 2.3 %collective-permute-done.7.second_far_dom = f32[16,128]{1,0:T(8,128)S(1)} collective-permute-done((f32[16,128]{1,0:T(8,128)S(1)}, f32[16,128]{1,0:T(8,128)S(1)}, u32[]{:S(2)}, u32[]{:S(2)}) %collective-permute-start.7) | collective-permute-done | bytes 8224 | tf_op jit(solution)/shard_map/ppermute | solution.py:494
  23.3 1.5 %final.1 = f32[9,16,56]{2,1,0:T(8,128)} custom-call(f32[9,8,128]{2,1,0:T(8,128)S(1)} %local_late.1.base_ref, f32[9,8,128]{2,1,0:T(8,128)S(1)} %get-tuple-element.64.late_ref, f32[180,16,128]{2,1,0:T(8,128)S(1)} %get-tuple-element.53.remote_ref, bf16[256,256]{1,0:T(8,128)(2,1)S(1)} %get-tuple-element.55.compose_ref, ...), custom_call_target="tpu_custom_call" | custom-call | flops 200000000 | bytes 4000000 | tf_op jit(solution)/shard_map/final/pallas_call | solution.py:473
Async XLA Ops:
  2.9 10.4 %collective-permute-start = (f32[32,128]{1,0:T(8,128)S(1)}, f32[32,128]{1,0:T(8,128)S(1)}, u32[]{:S(2)}, u32[]{:S(2)}) collective-permute-start(f32[32,128]{1,0:T(8,128)S(1)} %get-tuple-element.59), channel_id=1, source_target_pairs={{0,4},{4,0},{8,12},{12,8},{16,20},{20,16},{24,28},{28,24},{1,5},{5... | collective-permute-start | bytes 49160 | tf_op jit(solution)/shard_map/ppermute | solution.py:494
  5.9 7.4 %collective-permute-start.1 = (f32[32,128]{1,0:T(8,128)S(1)}, f32[32,128]{1,0:T(8,128)S(1)}, u32[]{:S(2)}, u32[]{:S(2)}) collective-permute-start(f32[32,128]{1,0:T(8,128)S(1)} %get-tuple-element.60), channel_id=1, source_target_pairs={{0,1},{1,0},{2,3},{3,2},{4,5},{5,4},{6,7},{7,6},{8,9},{9,8},{10,11... | collective-permute-start | bytes 49160 | tf_op jit(solution)/shard_map/ppermute | solution.py:494
  5.9 7.4 %collective-permute-start.2 = (f32[32,128]{1,0:T(8,128)S(1)}, f32[32,128]{1,0:T(8,128)S(1)}, u32[]{:S(2)}, u32[]{:S(2)}) collective-permute-start(f32[32,128]{1,0:T(8,128)S(1)} %get-tuple-element.61), channel_id=1, source_target_pairs={{1,2},{2,1},{3,0},{0,3},{5,6},{6,5},{7,4},{4,7},{9,10},{10,9},{11,... | collective-permute-start | bytes 49160 | tf_op jit(solution)/shard_map/ppermute | solution.py:494
  7.6 6.4 %collective-permute-start.3 = (f32[32,128]{1,0:T(8,128)S(1)}, f32[32,128]{1,0:T(8,128)S(1)}, u32[]{:S(2)}, u32[]{:S(2)}) collective-permute-start(f32[32,128]{1,0:T(8,128)S(1)} %get-tuple-element.62), channel_id=1, source_target_pairs={{4,8},{8,4},{12,16},{16,12},{20,24},{24,20},{28,0},{0,28},{5,9},{9... | collective-permute-start | bytes 49160 | tf_op jit(solution)/shard_map/ppermute | solution.py:494
  16.2 4.8 %collective-permute-start.4 = (f32[16,128]{1,0:T(8,128)S(1)}, f32[16,128]{1,0:T(8,128)S(1)}, u32[]{:S(2)}, u32[]{:S(2)}) collective-permute-start(f32[16,128]{1,0:T(8,128)S(1)} %get-tuple-element.69), channel_id=1, source_target_pairs={{0,4},{4,0},{8,12},{12,8},{16,20},{20,16},{24,28},{28,24},{1,5},{5... | collective-permute-start | bytes 24584 | tf_op jit(solution)/shard_map/ppermute | solution.py:494
  16.2 4.7 %collective-permute-start.5 = (f32[16,128]{1,0:T(8,128)S(1)}, f32[16,128]{1,0:T(8,128)S(1)}, u32[]{:S(2)}, u32[]{:S(2)}) collective-permute-start(f32[16,128]{1,0:T(8,128)S(1)} %get-tuple-element.70), channel_id=1, source_target_pairs={{0,1},{1,0},{2,3},{3,2},{4,5},{5,4},{6,7},{7,6},{8,9},{9,8},{10,11... | collective-permute-start | bytes 24584 | tf_op jit(solution)/shard_map/ppermute | solution.py:494
  16.3 4.7 %collective-permute-start.6 = (f32[16,128]{1,0:T(8,128)S(1)}, f32[16,128]{1,0:T(8,128)S(1)}, u32[]{:S(2)}, u32[]{:S(2)}) collective-permute-start(f32[16,128]{1,0:T(8,128)S(1)} %get-tuple-element.71), channel_id=1, source_target_pairs={{1,2},{2,1},{3,0},{0,3},{5,6},{6,5},{7,4},{4,7},{9,10},{10,9},{11,... | collective-permute-start | bytes 24584 | tf_op jit(solution)/shard_map/ppermute | solution.py:494
  16.9 6.3 %collective-permute-start.7 = (f32[16,128]{1,0:T(8,128)S(1)}, f32[16,128]{1,0:T(8,128)S(1)}, u32[]{:S(2)}, u32[]{:S(2)}) collective-permute-start(f32[16,128]{1,0:T(8,128)S(1)} %get-tuple-element.72), channel_id=1, source_target_pairs={{4,8},{8,4},{12,16},{16,12},{20,24},{24,20},{28,0},{0,28},{5,9},{9... | collective-permute-start | bytes 24584 | tf_op jit(solution)/shard_map/ppermute | solution.py:494

commit v6 on v5

--- a/solution.py
+++ b/solution.py
@@ -15,7 +15,7 @@
 BF16 = jnp.bfloat16
 LATER = ("flux_local", "flux_remote", "face_restrict", "face_lift", "orient_maps", "slot", "face", "turn")
 AXES = ("dom", "sub")
-SWAPS = (("dom", False), ("sub", False), ("sub", True), ("dom", True))
+SWAPS = (("dom", True), ("sub", True), ("sub", False), ("dom", False))
 
 
 def taylor_weight(lower, upper, degree):
@@ -84,38 +84,32 @@
     packed_ref[:, :, HALF : HALF + modes] = values_ref[:, ROWS : 2 * ROWS, :]
 
 
-def turn_matrices(source_ref, work_ref):
-    fields, kinds, elements = source_ref.shape[0], source_ref.shape[2], source_ref.shape[3]
-    tiles = []
-    for pair in range((fields + 1) // 2):
-        for row in range(2 * pair, min(2 * pair + 2, fields)):
-            for col in range(fields):
-                at = (row % 2) * HALF + col * 4
-                work_ref[pair, at : at + kinds, 0:elements] = source_ref[row, col]
-        tiles.append(work_ref[pair].T[0:elements, :])
-    return tiles
-
-
-def spread(tile, index):
-    return jnp.take_along_axis(tile, index, axis=1, mode="promise_in_bounds")
+def high_and_low(values, shift):
+    high = values.astype(BF16).astype(F32)
+    return high + pltpu.roll(values - high, shift, 1)
+
+
+def row_index(shape):
+    return lax.broadcasted_iota(jnp.int32, shape, len(shape) - 2)
+
+
+def one_where(condition):
+    return jnp.where(condition, 1.0, 0.0)
 
 
 def star_coefficients(star_ref, stage_ref, star_out):
     fields, kinds, elements = star_ref.shape[0], star_ref.shape[2], star_ref.shape[3]
     lanes = lane_index((ROWS, LANES))
-    sublanes = lax.broadcasted_iota(jnp.int32, (ROWS, LANES), 0)
-    pick = jnp.where((lanes % ROWS == sublanes) & (lanes < 2 * elements), 1.0, 0.0)
-    to_lane = lane_index((LANES, LANES))
-    from_lane = lax.broadcasted_iota(jnp.int32, (LANES, LANES), 0)
-    same_half = (from_lane % elements) // ROWS == to_lane // HALF
-    right = jnp.where(same_half & (from_lane < 2 * elements), 1.0, 0.0).astype(BF16)
+    pick = one_where((lanes % ROWS == row_index((ROWS, LANES))) & (lanes < 2 * elements))
+    from_lane = row_index((LANES, LANES))
+    same_half = (from_lane % elements) // ROWS == lane_index((LANES, LANES)) // HALF
+    right = one_where(same_half & (from_lane < 2 * elements)).astype(BF16)
     filled = lane_index(stage_ref.shape[1:]) < elements
     for row in range(fields):
         for col in range(fields):
             stage_ref[row, col * 4 : col * 4 + kinds, 0:elements] = star_ref[row, col]
         values = jnp.where(filled, stage_ref[row], 0.0)
-        high = values.astype(BF16).astype(F32)
-        stage_ref[row] = high + pltpu.roll(values - high, elements, 1)
+        stage_ref[row] = high_and_low(values, elements)
         spreads = []
         for kind in range(kinds):
             for col in range(fields):
@@ -151,7 +145,7 @@
     later = len(LATER)
     solution_hbm, stiffness_hbm, star_hbm, send_hbm = refs[0:4]
     later_hbm, refs = refs[4 : 4 + later], refs[4 + later :]
-    early_out, late_out, near_dom_out, near_sub_out, far_sub_out, far_dom_out = refs[0:6]
+    early_out, late_out, send_0, send_1, send_2, send_3 = refs[0:6]
     packed_ref, coef_ref, derive_ref, stiffness_ref = refs[6:10]
     later_out, refs = refs[10 : 10 + later], refs[10 + later :]
     work_ref, early_rows, late_rows, solution_ref, block_ref, star_ref, send_ref, sems = refs
@@ -190,7 +184,7 @@
     copies[3].wait()
     sends = send_ref.shape[2]
     fast = sends // 2
-    for side, out in enumerate((near_dom_out, near_sub_out, far_sub_out, far_dom_out)):
+    for side, out in enumerate((send_0, send_1, send_2, send_3)):
         out[...] = jnp.zeros(out.shape, F32)
         for place in range(sends):
             element = send_ref[0, message_side(side), place]
@@ -216,31 +210,55 @@
         out_ref[pair, ROWS : 2 * ROWS, :] = jnp.where(lower, swap_halves(even), odd)
 
 
-def flux_local_coefficients(flux_ref, work_ref, out_ref):
-    fields = flux_ref.shape[0]
-    tiles = turn_matrices(flux_ref, work_ref)
-    lanes = lane_index((ROWS, LANES))
+def flux_local_coefficients(flux_ref, stage_ref, out_ref):
+    fields, faces, elements = flux_ref.shape[0], flux_ref.shape[2], flux_ref.shape[3]
+    rows = 2 * ROWS
+    filled = lane_index((rows, LANES)) < elements
+    lanes, sublanes = lane_index((ROWS, LANES)), row_index((ROWS, LANES))
+    picks = [one_where(lanes % elements == half * ROWS + sublanes) for half in range(2)]
+    square = (LANES, LANES)
+    right = one_where(row_index(square) // (2 * elements) == lane_index(square) % faces).astype(BF16)
     for row in range(fields):
-        for col in range(fields):
-            index = (row % 2) * HALF + col * 4 + lanes % 4
-            for half in range(2):
-                tile = tiles[row // 2][half * ROWS : (half + 1) * ROWS]
-                out_ref[row * fields + col, half] = spread(tile, index)
-
-
-def flux_remote_coefficients(flux_ref, work_ref, out_ref):
-    fields, faces = flux_ref.shape[0], flux_ref.shape[2]
+        values = None
+        for face in range(faces):
+            stage_ref[row, face * rows : face * rows + fields, 0:elements] = flux_ref[row, :, face, :]
+            part = jnp.where(filled, stage_ref[row, face * rows : (face + 1) * rows, :], 0.0)
+            values = part if values is None else values + pltpu.roll(part, face * 2 * elements, 1)
+        stage_ref[row, 0:rows, :] = high_and_low(values, elements)
+        left = [stage_ref[row, col : col + 1, :] * pick for col in range(fields) for pick in picks]
+        spread = product(jnp.concatenate(left, axis=0).astype(BF16), right)
+        out_ref[row * fields : (row + 1) * fields] = spread.reshape(fields, 2, ROWS, LANES)
+
+
+def flux_remote_coefficients(flux_ref, stage_ref, out_ref):
+    fields, faces, elements = flux_ref.shape[0], flux_ref.shape[2], flux_ref.shape[3]
     pairs = (fields + 1) // 2
-    tiles = turn_matrices(flux_ref, work_ref)
-    lanes = lane_index((ROWS, LANES))
-    base = (lanes // HALF) * HALF
+    rows = stage_ref.shape[1] // 2
+    filled = lane_index((rows, LANES)) < elements
+    lanes, sublanes = lane_index((elements, LANES)), row_index((elements, LANES))
+    pick = one_where((lanes % elements == sublanes) & (lanes < 4 * elements))
+    square = (LANES, LANES)
+    from_lane = row_index(square)
+    same_parity = (from_lane // elements) % 2 == lane_index(square) // HALF
+    right = one_where(same_parity & (from_lane < 4 * elements)).astype(BF16)
     for pair in range(pairs):
+        values = None
+        for row in range(2 * pair, min(2 * pair + 2, fields)):
+            start = (row % 2) * rows
+            for col in range(fields):
+                at = start + col * faces
+                stage_ref[pair, at : at + faces, 0:elements] = flux_ref[row, col]
+            part = jnp.where(filled, stage_ref[pair, start : start + rows, :], 0.0)
+            values = part if values is None else values + pltpu.roll(part, elements, 1)
+        stage_ref[pair, 0:rows, :] = high_and_low(values, 2 * elements)
         for face in range(faces):
+            left = []
             for col in range(fields):
-                at = (face * pairs + pair) * fields + col
-                for half in range(2):
-                    tile = tiles[pair][half * ROWS : (half + 1) * ROWS]
-                    out_ref[at, half * ROWS : (half + 1) * ROWS, :] = spread(tile, base + (col * 4 + face))
+                at = col * faces + face
+                left.append(stage_ref[pair, at : at + 1, :] * pick)
+            spread = product(jnp.concatenate(left, axis=0).astype(BF16), right)
+            at = (face * pairs + pair) * fields
+            out_ref[at : at + fields] = spread.reshape(fields, elements, LANES)
 
 
 def local_terms(packed, star_ref, flux_ref, volume_ref, trace_ref, lift_ref, fields, kinds):
@@ -266,14 +284,13 @@
     slot_ref, face_ref, turn_ref,
     base_out, local_out, remote_out, volume_out, trace_out, local_lift_out, compose_out,
     remote_lift_out, choose_out, mask_out,
-    work_ref, block_ref, wide_ref, face_work_ref, orient_work_ref, code_ref,
+    local_work_ref, remote_work_ref, block_ref, wide_ref, face_work_ref, orient_work_ref, code_ref,
 ):
     fields, kinds = packed_ref.shape[0], stiffness_ref.shape[0]
     face_modes, faces, modes = restrict_ref.shape
     turns = orient_ref.shape[0]
-    work_ref[...] = jnp.zeros(work_ref.shape, F32)
-    flux_local_coefficients(flux_local_ref, work_ref, local_out)
-    flux_remote_coefficients(flux_remote_ref, work_ref, remote_out)
+    flux_local_coefficients(flux_local_ref, local_work_ref, local_out)
+    flux_remote_coefficients(flux_remote_ref, remote_work_ref, remote_out)
 
     volume_out[...] = stack_right(stiffness_blocks(stiffness_ref, block_ref, False))
 
@@ -372,8 +389,8 @@
 
 def middle_kernel(
     base_ref, early_ref, late_ref, star_ref, remote_ref, derive_ref, compose_ref, lift_ref, choose_ref, mask_ref,
-    rate_hbm, send_hbm, near_dom, near_sub, far_sub, far_dom,
-    middle_out, late_out, near_dom_out, near_sub_out, far_sub_out, far_dom_out,
+    rate_hbm, send_hbm, from_0, from_1, from_2, from_3,
+    middle_out, late_out, send_0, send_1, send_2, send_3,
     rows_ref, late_rows, rate_ref, send_ref, sems,
 ):
     copies = [
@@ -389,7 +406,7 @@
     fast = sends // 2
     elements = 2 * ROWS
     rows_by_pair(early_ref[...].reshape(fields * ROWS, LANES), rows_ref, fields)
-    for side, arrived in enumerate((near_dom, near_sub, far_sub, far_dom)):
+    for side, arrived in enumerate((from_0, from_1, from_2, from_3)):
         at = elements + side * sends
         for pair in range(pairs):
             rows_ref[pair, at : at + sends, :] = arrived[pair * sends : (pair + 1) * sends, :]
@@ -416,7 +433,7 @@
     late = jnp.where((is_fast == 2)[None], restart.reshape(fields, ROWS, LANES), late_ref[...])
     late_out[...] = late
     rows_by_pair(late.reshape(fields * ROWS, LANES), late_rows, fields)
-    for side, out in enumerate((near_dom_out, near_sub_out, far_sub_out, far_dom_out)):
+    for side, out in enumerate((send_0, send_1, send_2, send_3)):
         out[...] = jnp.zeros(out.shape, F32)
         for place in range(fast):
             element = send_ref[0, message_side(side), place]
@@ -435,8 +452,8 @@
 
 def final_kernel(
     base_ref, late_ref, remote_ref, compose_ref, lift_ref, choose_ref, mask_ref,
-    first_near_dom, first_near_sub, first_far_sub, first_far_dom,
-    second_near_dom, second_near_sub, second_far_sub, second_far_dom,
+    first_0, first_1, first_2, first_3,
+    second_0, second_1, second_2, second_3,
     result_out, rows_ref,
 ):
     fields = base_ref.shape[0]
@@ -446,8 +463,8 @@
     sends = (rows_ref.shape[1] - elements) // 4
     fast = sends // 2
     rows_by_pair(late_ref[...].reshape(fields * ROWS, LANES), rows_ref, fields)
-    firsts = (first_near_dom, first_near_sub, first_far_sub, first_far_dom)
-    seconds = (second_near_dom, second_near_sub, second_far_sub, second_far_dom)
+    firsts = (first_0, first_1, first_2, first_3)
+    seconds = (second_0, second_1, second_2, second_3)
     for side, (first, second) in enumerate(zip(firsts, seconds)):
         at = elements + side * sends
         for pair in range(pairs):
@@ -520,7 +537,6 @@
     packed = (fields, ROWS, LANES)
     first_shape = (up_to(pairs * (sends + fast), ROWS), LANES)
     second_shape = (up_to(pairs * fast, ROWS), LANES)
-    work = (pairs, LANES, LANES)
     star_shape = (fields * fields * kinds, ROWS, LANES)
     combos = faces * HALF
     sources = elements + sides * sends
@@ -558,7 +574,8 @@
             ((faces * elements, 2 * sources), BF16), ((faces * elements, combos), F32),
         ],
         [
-            (work, F32), ((kinds, LANES, LANES), F32), ((2 * LANES, LANES), F32),
+            ((fields, 2 * ROWS * faces, LANES), F32), ((pairs, 2 * up_to(4 * fields, ROWS), LANES), F32),
+            ((kinds, LANES, LANES), F32), ((2 * LANES, LANES), F32),
             ((LANES, faces * LANES), F32), ((HALF, LANES), F32), ((LANES, LANES), F32),
         ],
         (start, early, stiffness_kept, star_coef, *waiting),

time: 24.9 us -> 24.6 us (0.988)
  waiting for transfers between devices: 2.94 us -> 5.54 us
  starting transfers between devices: 12.6 us -> 10.5 us
  Pallas kernels: 9.16 us -> 8.42 us
    ppermute x8, waiting for transfers between devices: 2.94 us -> 5.54 us  [exchange(): arrived.append(lax.ppermute(message, axis, pairs))]
    ppermute x8, starting transfers between devices: 12.6 us -> 10.5 us  [exchange(): arrived.append(lax.ppermute(message, axis, pairs))]
    pallas_call x5, Pallas kernels: 9.16 us -> 8.42 us  [call(): pl.pallas_call(kernel, out_shape=shapes, in_specs=ins, out_specs=[VMEM] *...]
  transfers between devices with their start and end apart: 8 -> 8, of which waited for: 2 -> 4; matrix products, arithmetic and copies ran while one was open for 0% -> 0% of each run, Pallas kernels for 11% -> 8%
where the time goes in v6:
time: 24.6 us; the launch traced here: 24.5 us
  starting transfers between devices  10.5 us (43%)
  Pallas kernels  8.42 us (34%)
  waiting for transfers between devices  5.54 us (23%)
    ppermute x8, starting transfers between devices, exchange(): arrived.append(lax.ppermute(message, axis, pairs))  10.5 us
    pallas_call x5, Pallas kernels, call(): pl.pallas_call(kernel, out_shape=shapes, in_specs=ins, out_specs=[VMEM] *...  8.42 us
    ppermute x8, waiting for transfers between devices, exchange(): arrived.append(lax.ppermute(message, axis, pairs))  5.54 us
  transfers between devices with their start and end apart: 8, of which 4 were waited for; matrix products, arithmetic and copies ran while one was open for 0% of the time, Pallas kernels for 8%

profile of v6, /device:TPU:0, one launch (start us, length us, event | category | flops | bytes accessed | tf_op | source)
XLA Modules:
  0.0 24.5 jit_solution(6787717770602332470)
XLA Ops:
  0.0 2.9 %predict.1 = (f32[9,8,128]{2,1,0:T(8,128)S(1)}, f32[9,8,128]{2,1,0:T(8,128)S(1)}, f32[32,128]{1,0:T(8,128)S(1)}, f32[32,128]{1,0:T(8,128)S(1)}, f32[32,128]{1,0:...) custom-call(f32[9,16,56]{2,1,0:T(8,128)} %bitcast.10, ...), custom_call_target="tpu_custom_call" | custom-call | flops 100000000 | bytes 4000000 | tf_op jit(solution)/shard_map/predict/pallas_call | solution.py:490
  2.9 6.0 %collective-permute-start = (f32[32,128]{1,0:T(8,128)S(1)}, f32[32,128]{1,0:T(8,128)S(1)}, u32[]{:S(2)}, u32[]{:S(2)}) collective-permute-start(f32[32,128]{1,0:T(8,128)S(1)} %get-tuple-element.59), channel_id=1, source_target_pairs={{4,8},{8,4},{12,16},{16,12},{20,24},{24,20},{28,0},{0,28},{5,9},{9... | collective-permute-start | bytes 49160 | tf_op jit(solution)/shard_map/ppermute | solution.py:511
  9.0 0.7 %collective-permute-start.1 = (f32[32,128]{1,0:T(8,128)S(1)}, f32[32,128]{1,0:T(8,128)S(1)}, u32[]{:S(2)}, u32[]{:S(2)}) collective-permute-start(f32[32,128]{1,0:T(8,128)S(1)} %get-tuple-element.60), channel_id=1, source_target_pairs={{1,2},{2,1},{3,0},{0,3},{5,6},{6,5},{7,4},{4,7},{9,10},{10,9},{11,... | collective-permute-start | bytes 49160 | tf_op jit(solution)/shard_map/ppermute | solution.py:511
  9.7 1.0 %collective-permute-start.2 = (f32[32,128]{1,0:T(8,128)S(1)}, f32[32,128]{1,0:T(8,128)S(1)}, u32[]{:S(2)}, u32[]{:S(2)}) collective-permute-start(f32[32,128]{1,0:T(8,128)S(1)} %get-tuple-element.61), channel_id=1, source_target_pairs={{0,1},{1,0},{2,3},{3,2},{4,5},{5,4},{6,7},{7,6},{8,9},{9,8},{10,11... | collective-permute-start | bytes 49160 | tf_op jit(solution)/shard_map/ppermute | solution.py:511
  10.6 0.0 collective-permute-start.3
  10.6 1.4 %prepare.1 = (f32[9,8,128]{2,1,0:T(8,128)S(1)}, f32[81,2,8,128]{3,2,1,0:T(8,128)S(1)}, f32[180,16,128]{2,1,0:T(8,128)S(1)}, bf16[384,384]{1,0:T(8,128)(2,1)S(1)}...) custom-call(f32[9,8,128]{2,1,0:T(8,128)S(1)} %get-tuple-element.39.p, ...), custom_call_target="tpu_custom_call" | custom-call | flops 200000000 | bytes 4000000 | tf_op jit(solution)/shard_map/prepare/pallas_call | solution.py:490
  12.1 0.0 collective-permute-done.from_0.first_0
  12.1 0.2 collective-permute-done.1.from_1.first_1
  12.3 0.0 collective-permute-done.2.from_2.first_2
  12.3 2.1 %collective-permute-done.3.from_3.first_3 = f32[32,128]{1,0:T(8,128)S(1)} collective-permute-done((f32[32,128]{1,0:T(8,128)S(1)}, f32[32,128]{1,0:T(8,128)S(1)}, u32[]{:S(2)}, u32[]{:S(2)}) %collective-permute-start.3) | collective-permute-done | bytes 16416 | tf_op jit(solution)/shard_map/ppermute | solution.py:511
  14.4 2.1 %middle.1 = (f32[9,8,128]{2,1,0:T(8,128)S(1)}, f32[9,8,128]{2,1,0:T(8,128)S(1)}, f32[16,128]{1,0:T(8,128)S(1)}, f32[16,128]{1,0:T(8,128)S(1)}, f32[16,128]{1,0:T(8,128)S(1)}, /*index=5*/f32[16,128]{1,0:T(8,128)S(1)}) custom-call(f32[9,8,128]{2,1,0:T(8,128)S(1)} %get-tuple-element.51.base_ref, f32[9,8,128]{2,1,0:T(8,128)S(1)} %get-tuple-element.40.early_ref, ...), custom_call_target="tpu_custom_call" | custom-call | flops 200000000 | bytes 4000000 | tf_op jit(solution)/shard_map/middle/pallas_call | solution.py:490
  16.5 1.1 %collective-permute-start.4 = (f32[16,128]{1,0:T(8,128)S(1)}, f32[16,128]{1,0:T(8,128)S(1)}, u32[]{:S(2)}, u32[]{:S(2)}) collective-permute-start(f32[16,128]{1,0:T(8,128)S(1)} %get-tuple-element.69), channel_id=1, source_target_pairs={{4,8},{8,4},{12,16},{16,12},{20,24},{24,20},{28,0},{0,28},{5,9},{9... | collective-permute-start | bytes 24584 | tf_op jit(solution)/shard_map/ppermute | solution.py:511
  17.7 0.0 collective-permute-start.5
  17.7 1.6 %collective-permute-start.6 = (f32[16,128]{1,0:T(8,128)S(1)}, f32[16,128]{1,0:T(8,128)S(1)}, u32[]{:S(2)}, u32[]{:S(2)}) collective-permute-start(f32[16,128]{1,0:T(8,128)S(1)} %get-tuple-element.71), channel_id=1, source_target_pairs={{0,1},{1,0},{2,3},{3,2},{4,5},{5,4},{6,7},{7,6},{8,9},{9,8},{10,11... | collective-permute-start | bytes 24584 | tf_op jit(solution)/shard_map/ppermute | solution.py:511
  19.3 0.0 collective-permute-start.7
  19.3 0.4 %local_late.1.base_ref = f32[9,8,128]{2,1,0:T(8,128)S(1)} custom-call(f32[9,8,128]{2,1,0:T(8,128)S(1)} %get-tuple-element.63.middle_ref, f32[9,8,128]{2,1,0:T(8,128)S(1)} %get-tuple-element.64.late_ref, f32[243,8,128]{2,1,0:T(8,128)S(1)} %get-tuple-element.42.star_ref, f32[81,2,8,128]{3,2,1,0:T(8,128)S(1)} %get-tuple-element.65.flux_ref, ...), custom_call_target="tpu_custom_call" | custom-call | flops 200000000 | bytes 4000000 | tf_op jit(solution)/shard_map/local_late/pallas_call | solution.py:490
  19.7 3.2 %collective-permute-done.4.second_0 = f32[16,128]{1,0:T(8,128)S(1)} collective-permute-done((f32[16,128]{1,0:T(8,128)S(1)}, f32[16,128]{1,0:T(8,128)S(1)}, u32[]{:S(2)}, u32[]{:S(2)}) %collective-permute-start.4) | collective-permute-done | bytes 8224 | tf_op jit(solution)/shard_map/ppermute | solution.py:511
  22.9 0.0 collective-permute-done.5.second_1
  22.9 0.0 collective-permute-done.6.second_2
  22.9 0.1 collective-permute-done.7.second_3
  23.0 1.5 %final.1 = f32[9,16,56]{2,1,0:T(8,128)} custom-call(f32[9,8,128]{2,1,0:T(8,128)S(1)} %local_late.1.base_ref, f32[9,8,128]{2,1,0:T(8,128)S(1)} %get-tuple-element.64.late_ref, f32[180,16,128]{2,1,0:T(8,128)S(1)} %get-tuple-element.53.remote_ref, bf16[256,256]{1,0:T(8,128)(2,1)S(1)} %get-tuple-element.55.compose_ref, ...), custom_call_target="tpu_custom_call" | custom-call | flops 200000000 | bytes 4000000 | tf_op jit(solution)/shard_map/final/pallas_call | solution.py:490
Async XLA Ops:
  2.9 9.1 %collective-permute-start = (f32[32,128]{1,0:T(8,128)S(1)}, f32[32,128]{1,0:T(8,128)S(1)}, u32[]{:S(2)}, u32[]{:S(2)}) collective-permute-start(f32[32,128]{1,0:T(8,128)S(1)} %get-tuple-element.59), channel_id=1, source_target_pairs={{4,8},{8,4},{12,16},{16,12},{20,24},{24,20},{28,0},{0,28},{5,9},{9... | collective-permute-start | bytes 49160 | tf_op jit(solution)/shard_map/ppermute | solution.py:511
  9.0 3.3 %collective-permute-start.1 = (f32[32,128]{1,0:T(8,128)S(1)}, f32[32,128]{1,0:T(8,128)S(1)}, u32[]{:S(2)}, u32[]{:S(2)}) collective-permute-start(f32[32,128]{1,0:T(8,128)S(1)} %get-tuple-element.60), channel_id=1, source_target_pairs={{1,2},{2,1},{3,0},{0,3},{5,6},{6,5},{7,4},{4,7},{9,10},{10,9},{11,... | collective-permute-start | bytes 49160 | tf_op jit(solution)/shard_map/ppermute | solution.py:511
  9.7 2.6 %collective-permute-start.2 = (f32[32,128]{1,0:T(8,128)S(1)}, f32[32,128]{1,0:T(8,128)S(1)}, u32[]{:S(2)}, u32[]{:S(2)}) collective-permute-start(f32[32,128]{1,0:T(8,128)S(1)} %get-tuple-element.61), channel_id=1, source_target_pairs={{0,1},{1,0},{2,3},{3,2},{4,5},{5,4},{6,7},{7,6},{8,9},{9,8},{10,11... | collective-permute-start | bytes 49160 | tf_op jit(solution)/shard_map/ppermute | solution.py:511
  10.6 3.7 %collective-permute-start.3 = (f32[32,128]{1,0:T(8,128)S(1)}, f32[32,128]{1,0:T(8,128)S(1)}, u32[]{:S(2)}, u32[]{:S(2)}) collective-permute-start(f32[32,128]{1,0:T(8,128)S(1)} %get-tuple-element.62), channel_id=1, source_target_pairs={{0,4},{4,0},{8,12},{12,8},{16,20},{20,16},{24,28},{28,24},{1,5},{5... | collective-permute-start | bytes 49160 | tf_op jit(solution)/shard_map/ppermute | solution.py:511
  16.5 6.4 %collective-permute-start.4 = (f32[16,128]{1,0:T(8,128)S(1)}, f32[16,128]{1,0:T(8,128)S(1)}, u32[]{:S(2)}, u32[]{:S(2)}) collective-permute-start(f32[16,128]{1,0:T(8,128)S(1)} %get-tuple-element.69), channel_id=1, source_target_pairs={{4,8},{8,4},{12,16},{16,12},{20,24},{24,20},{28,0},{0,28},{5,9},{9... | collective-permute-start | bytes 24584 | tf_op jit(solution)/shard_map/ppermute | solution.py:511
  17.7 5.3 %collective-permute-start.5 = (f32[16,128]{1,0:T(8,128)S(1)}, f32[16,128]{1,0:T(8,128)S(1)}, u32[]{:S(2)}, u32[]{:S(2)}) collective-permute-start(f32[16,128]{1,0:T(8,128)S(1)} %get-tuple-element.70), channel_id=1, source_target_pairs={{1,2},{2,1},{3,0},{0,3},{5,6},{6,5},{7,4},{4,7},{9,10},{10,9},{11,... | collective-permute-start | bytes 24584 | tf_op jit(solution)/shard_map/ppermute | solution.py:511
  17.7 5.3 %collective-permute-start.6 = (f32[16,128]{1,0:T(8,128)S(1)}, f32[16,128]{1,0:T(8,128)S(1)}, u32[]{:S(2)}, u32[]{:S(2)}) collective-permute-start(f32[16,128]{1,0:T(8,128)S(1)} %get-tuple-element.71), channel_id=1, source_target_pairs={{0,1},{1,0},{2,3},{3,2},{4,5},{5,4},{6,7},{7,6},{8,9},{9,8},{10,11... | collective-permute-start | bytes 24584 | tf_op jit(solution)/shard_map/ppermute | solution.py:511
  19.3 3.7 %collective-permute-start.7 = (f32[16,128]{1,0:T(8,128)S(1)}, f32[16,128]{1,0:T(8,128)S(1)}, u32[]{:S(2)}, u32[]{:S(2)}) collective-permute-start(f32[16,128]{1,0:T(8,128)S(1)} %get-tuple-element.72), channel_id=1, source_target_pairs={{0,4},{4,0},{8,12},{12,8},{16,20},{20,16},{24,28},{28,24},{1,5},{5... | collective-permute-start | bytes 24584 | tf_op jit(solution)/shard_map/ppermute | solution.py:511

commit v7 on v6

--- a/solution.py
+++ b/solution.py
@@ -15,7 +15,7 @@
 BF16 = jnp.bfloat16
 LATER = ("flux_local", "flux_remote", "face_restrict", "face_lift", "orient_maps", "slot", "face", "turn")
 AXES = ("dom", "sub")
-SWAPS = (("dom", True), ("sub", True), ("sub", False), ("dom", False))
+SWAPS = (("dom", True), ("dom", False), ("sub", True), ("sub", False))
 
 
 def taylor_weight(lower, upper, degree):

time: 24.6 us -> 23 us (0.935)
  waiting for transfers between devices: 5.54 us -> 2.31 us
  starting transfers between devices: 10.5 us -> 12.1 us
    ppermute x8, waiting for transfers between devices: 5.54 us -> 2.31 us  [exchange(): arrived.append(lax.ppermute(message, axis, pairs))]
    ppermute x8, starting transfers between devices: 10.5 us -> 12.1 us  [exchange(): arrived.append(lax.ppermute(message, axis, pairs))]
  transfers between devices with their start and end apart: 8 -> 8, of which waited for: 4 -> 3; matrix products, arithmetic and copies ran while one was open for 0% -> 0% of each run, Pallas kernels for 8% -> 8%
where the time goes in v7:
time: 23 us; the launch traced here: 22.9 us
  starting transfers between devices  12.1 us (53%)
  Pallas kernels  8.42 us (37%)
  waiting for transfers between devices  2.31 us (10%)
    ppermute x8, starting transfers between devices, exchange(): arrived.append(lax.ppermute(message, axis, pairs))  12.1 us
    pallas_call x5, Pallas kernels, call(): pl.pallas_call(kernel, out_shape=shapes, in_specs=ins, out_specs=[VMEM] *...  8.42 us
    ppermute x8, waiting for transfers between devices, exchange(): arrived.append(lax.ppermute(message, axis, pairs))  2.31 us
  transfers between devices with their start and end apart: 8, of which 3 were waited for; matrix products, arithmetic and copies ran while one was open for 0% of the time, Pallas kernels for 8%

profile of v7, /device:TPU:0, one launch (start us, length us, event | category | flops | bytes accessed | tf_op | source)
XLA Modules:
  0.0 22.9 jit_solution(4235774542811166459)
XLA Ops:
  0.0 2.9 %predict.1 = (f32[9,8,128]{2,1,0:T(8,128)S(1)}, f32[9,8,128]{2,1,0:T(8,128)S(1)}, f32[32,128]{1,0:T(8,128)S(1)}, f32[32,128]{1,0:T(8,128)S(1)}, f32[32,128]{1,0:...) custom-call(f32[9,16,56]{2,1,0:T(8,128)} %bitcast.10, ...), custom_call_target="tpu_custom_call" | custom-call | flops 100000000 | bytes 4000000 | tf_op jit(solution)/shard_map/predict/pallas_call | solution.py:490
  2.9 6.0 %collective-permute-start = (f32[32,128]{1,0:T(8,128)S(1)}, f32[32,128]{1,0:T(8,128)S(1)}, u32[]{:S(2)}, u32[]{:S(2)}) collective-permute-start(f32[32,128]{1,0:T(8,128)S(1)} %get-tuple-element.59), channel_id=1, source_target_pairs={{4,8},{8,4},{12,16},{16,12},{20,24},{24,20},{28,0},{0,28},{5,9},{9... | collective-permute-start | bytes 49160 | tf_op jit(solution)/shard_map/ppermute | solution.py:511
  9.0 0.0 collective-permute-start.1
  9.0 0.7 %collective-permute-start.2 = (f32[32,128]{1,0:T(8,128)S(1)}, f32[32,128]{1,0:T(8,128)S(1)}, u32[]{:S(2)}, u32[]{:S(2)}) collective-permute-start(f32[32,128]{1,0:T(8,128)S(1)} %get-tuple-element.61), channel_id=1, source_target_pairs={{1,2},{2,1},{3,0},{0,3},{5,6},{6,5},{7,4},{4,7},{9,10},{10,9},{11,... | collective-permute-start | bytes 49160 | tf_op jit(solution)/shard_map/ppermute | solution.py:511
  9.7 1.0 %collective-permute-start.3 = (f32[32,128]{1,0:T(8,128)S(1)}, f32[32,128]{1,0:T(8,128)S(1)}, u32[]{:S(2)}, u32[]{:S(2)}) collective-permute-start(f32[32,128]{1,0:T(8,128)S(1)} %get-tuple-element.62), channel_id=1, source_target_pairs={{0,1},{1,0},{2,3},{3,2},{4,5},{5,4},{6,7},{7,6},{8,9},{9,8},{10,11... | collective-permute-start | bytes 49160 | tf_op jit(solution)/shard_map/ppermute | solution.py:511
  10.6 1.4 %prepare.1 = (f32[9,8,128]{2,1,0:T(8,128)S(1)}, f32[81,2,8,128]{3,2,1,0:T(8,128)S(1)}, f32[180,16,128]{2,1,0:T(8,128)S(1)}, bf16[384,384]{1,0:T(8,128)(2,1)S(1)}...) custom-call(f32[9,8,128]{2,1,0:T(8,128)S(1)} %get-tuple-element.39.p, ...), custom_call_target="tpu_custom_call" | custom-call | flops 200000000 | bytes 4000000 | tf_op jit(solution)/shard_map/prepare/pallas_call | solution.py:490
  12.1 0.0 collective-permute-done.from_0.first_0
  12.1 0.7 %collective-permute-done.1.from_1.first_1 = f32[32,128]{1,0:T(8,128)S(1)} collective-permute-done((f32[32,128]{1,0:T(8,128)S(1)}, f32[32,128]{1,0:T(8,128)S(1)}, u32[]{:S(2)}, u32[]{:S(2)}) %collective-permute-start.1) | collective-permute-done | bytes 16416 | tf_op jit(solution)/shard_map/ppermute | solution.py:511
  12.7 0.0 collective-permute-done.2.from_2.first_2
  12.7 0.0 collective-permute-done.3.from_3.first_3
  12.7 2.1 %middle.1 = (f32[9,8,128]{2,1,0:T(8,128)S(1)}, f32[9,8,128]{2,1,0:T(8,128)S(1)}, f32[16,128]{1,0:T(8,128)S(1)}, f32[16,128]{1,0:T(8,128)S(1)}, f32[16,128]{1,0:T(8,128)S(1)}, /*index=5*/f32[16,128]{1,0:T(8,128)S(1)}) custom-call(f32[9,8,128]{2,1,0:T(8,128)S(1)} %get-tuple-element.51.base_ref, f32[9,8,128]{2,1,0:T(8,128)S(1)} %get-tuple-element.40.early_ref, ...), custom_call_target="tpu_custom_call" | custom-call | flops 200000000 | bytes 4000000 | tf_op jit(solution)/shard_map/middle/pallas_call | solution.py:490
  14.9 2.8 %collective-permute-start.4 = (f32[16,128]{1,0:T(8,128)S(1)}, f32[16,128]{1,0:T(8,128)S(1)}, u32[]{:S(2)}, u32[]{:S(2)}) collective-permute-start(f32[16,128]{1,0:T(8,128)S(1)} %get-tuple-element.69), channel_id=1, source_target_pairs={{4,8},{8,4},{12,16},{16,12},{20,24},{24,20},{28,0},{0,28},{5,9},{9... | collective-permute-start | bytes 24584 | tf_op jit(solution)/shard_map/ppermute | solution.py:511
  17.7 0.0 collective-permute-start.5
  17.7 0.0 collective-permute-start.6
  17.7 1.6 %collective-permute-start.7 = (f32[16,128]{1,0:T(8,128)S(1)}, f32[16,128]{1,0:T(8,128)S(1)}, u32[]{:S(2)}, u32[]{:S(2)}) collective-permute-start(f32[16,128]{1,0:T(8,128)S(1)} %get-tuple-element.72), channel_id=1, source_target_pairs={{0,1},{1,0},{2,3},{3,2},{4,5},{5,4},{6,7},{7,6},{8,9},{9,8},{10,11... | collective-permute-start | bytes 24584 | tf_op jit(solution)/shard_map/ppermute | solution.py:511
  19.3 0.4 %local_late.1.base_ref = f32[9,8,128]{2,1,0:T(8,128)S(1)} custom-call(f32[9,8,128]{2,1,0:T(8,128)S(1)} %get-tuple-element.63.middle_ref, f32[9,8,128]{2,1,0:T(8,128)S(1)} %get-tuple-element.64.late_ref, f32[243,8,128]{2,1,0:T(8,128)S(1)} %get-tuple-element.42.star_ref, f32[81,2,8,128]{3,2,1,0:T(8,128)S(1)} %get-tuple-element.65.flux_ref, ...), custom_call_target="tpu_custom_call" | custom-call | flops 200000000 | bytes 4000000 | tf_op jit(solution)/shard_map/local_late/pallas_call | solution.py:490
  19.7 1.6 %collective-permute-done.4.second_0 = f32[16,128]{1,0:T(8,128)S(1)} collective-permute-done((f32[16,128]{1,0:T(8,128)S(1)}, f32[16,128]{1,0:T(8,128)S(1)}, u32[]{:S(2)}, u32[]{:S(2)}) %collective-permute-start.4) | collective-permute-done | bytes 8224 | tf_op jit(solution)/shard_map/ppermute | solution.py:511
  21.3 0.1 collective-permute-done.5.second_1
  21.4 0.0 collective-permute-done.6.second_2
  21.4 0.0 collective-permute-done.7.second_3
  21.4 1.5 %final.1 = f32[9,16,56]{2,1,0:T(8,128)} custom-call(f32[9,8,128]{2,1,0:T(8,128)S(1)} %local_late.1.base_ref, f32[9,8,128]{2,1,0:T(8,128)S(1)} %get-tuple-element.64.late_ref, f32[180,16,128]{2,1,0:T(8,128)S(1)} %get-tuple-element.53.remote_ref, bf16[256,256]{1,0:T(8,128)(2,1)S(1)} %get-tuple-element.55.compose_ref, ...), custom_call_target="tpu_custom_call" | custom-call | flops 200000000 | bytes 4000000 | tf_op jit(solution)/shard_map/final/pallas_call | solution.py:490
Async XLA Ops:
  2.9 9.1 %collective-permute-start = (f32[32,128]{1,0:T(8,128)S(1)}, f32[32,128]{1,0:T(8,128)S(1)}, u32[]{:S(2)}, u32[]{:S(2)}) collective-permute-start(f32[32,128]{1,0:T(8,128)S(1)} %get-tuple-element.59), channel_id=1, source_target_pairs={{4,8},{8,4},{12,16},{16,12},{20,24},{24,20},{28,0},{0,28},{5,9},{9... | collective-permute-start | bytes 49160 | tf_op jit(solution)/shard_map/ppermute | solution.py:511
  9.0 3.7 %collective-permute-start.1 = (f32[32,128]{1,0:T(8,128)S(1)}, f32[32,128]{1,0:T(8,128)S(1)}, u32[]{:S(2)}, u32[]{:S(2)}) collective-permute-start(f32[32,128]{1,0:T(8,128)S(1)} %get-tuple-element.60), channel_id=1, source_target_pairs={{0,4},{4,0},{8,12},{12,8},{16,20},{20,16},{24,28},{28,24},{1,5},{5... | collective-permute-start | bytes 49160 | tf_op jit(solution)/shard_map/ppermute | solution.py:511
  9.0 3.7 %collective-permute-start.2 = (f32[32,128]{1,0:T(8,128)S(1)}, f32[32,128]{1,0:T(8,128)S(1)}, u32[]{:S(2)}, u32[]{:S(2)}) collective-permute-start(f32[32,128]{1,0:T(8,128)S(1)} %get-tuple-element.61), channel_id=1, source_target_pairs={{1,2},{2,1},{3,0},{0,3},{5,6},{6,5},{7,4},{4,7},{9,10},{10,9},{11,... | collective-permute-start | bytes 49160 | tf_op jit(solution)/shard_map/ppermute | solution.py:511
  9.7 3.1 %collective-permute-start.3 = (f32[32,128]{1,0:T(8,128)S(1)}, f32[32,128]{1,0:T(8,128)S(1)}, u32[]{:S(2)}, u32[]{:S(2)}) collective-permute-start(f32[32,128]{1,0:T(8,128)S(1)} %get-tuple-element.62), channel_id=1, source_target_pairs={{0,1},{1,0},{2,3},{3,2},{4,5},{5,4},{6,7},{7,6},{8,9},{9,8},{10,11... | collective-permute-start | bytes 49160 | tf_op jit(solution)/shard_map/ppermute | solution.py:511
  14.9 6.4 %collective-permute-start.4 = (f32[16,128]{1,0:T(8,128)S(1)}, f32[16,128]{1,0:T(8,128)S(1)}, u32[]{:S(2)}, u32[]{:S(2)}) collective-permute-start(f32[16,128]{1,0:T(8,128)S(1)} %get-tuple-element.69), channel_id=1, source_target_pairs={{4,8},{8,4},{12,16},{16,12},{20,24},{24,20},{28,0},{0,28},{5,9},{9... | collective-permute-start | bytes 24584 | tf_op jit(solution)/shard_map/ppermute | solution.py:511
  17.7 3.7 %collective-permute-start.5 = (f32[16,128]{1,0:T(8,128)S(1)}, f32[16,128]{1,0:T(8,128)S(1)}, u32[]{:S(2)}, u32[]{:S(2)}) collective-permute-start(f32[16,128]{1,0:T(8,128)S(1)} %get-tuple-element.70), channel_id=1, source_target_pairs={{0,4},{4,0},{8,12},{12,8},{16,20},{20,16},{24,28},{28,24},{1,5},{5... | collective-permute-start | bytes 24584 | tf_op jit(solution)/shard_map/ppermute | solution.py:511
  17.7 3.7 %collective-permute-start.6 = (f32[16,128]{1,0:T(8,128)S(1)}, f32[16,128]{1,0:T(8,128)S(1)}, u32[]{:S(2)}, u32[]{:S(2)}) collective-permute-start(f32[16,128]{1,0:T(8,128)S(1)} %get-tuple-element.71), channel_id=1, source_target_pairs={{1,2},{2,1},{3,0},{0,3},{5,6},{6,5},{7,4},{4,7},{9,10},{10,9},{11,... | collective-permute-start | bytes 24584 | tf_op jit(solution)/shard_map/ppermute | solution.py:511
  17.7 3.7 %collective-permute-start.7 = (f32[16,128]{1,0:T(8,128)S(1)}, f32[16,128]{1,0:T(8,128)S(1)}, u32[]{:S(2)}, u32[]{:S(2)}) collective-permute-start(f32[16,128]{1,0:T(8,128)S(1)} %get-tuple-element.72), channel_id=1, source_target_pairs={{0,1},{1,0},{2,3},{3,2},{4,5},{5,4},{6,7},{7,6},{8,9},{9,8},{10,11... | collective-permute-start | bytes 24584 | tf_op jit(solution)/shard_map/ppermute | solution.py:511

commit v8 on v7

--- a/solution.py
+++ b/solution.py
@@ -279,12 +279,75 @@
     return volume + product(stack_left(jnp.concatenate(sums, axis=0)), lift_ref[...])
 
 
+def ghost_terms(
+    flux_ref, stage_ref, code_ref, composed, lift_sides, lane_code, flux_out, operator_out, scatter_out, sends, fields
+):
+    faces, elements = flux_ref.shape[2], flux_ref.shape[3]
+    rows = 2 * ROWS
+    shape = (rows, LANES)
+    lanes = lane_index(shape)
+
+    def along_lanes(start):
+        row = code_ref[start : start + 1, :]
+        for face in range(1, faces):
+            row = row + pltpu.roll(code_ref[start + face : start + face + 1, :], face * elements, 1)
+        return row + swap_halves(row)
+
+    slots, codes = along_lanes(0), along_lanes(faces)
+    ghosts = elements + row_index(shape)
+    found = one_where(jnp.broadcast_to(slots, shape) == ghosts.astype(F32))
+    first = jnp.where(lanes < HALF, found, 0.0)
+    code = jnp.sum(first * codes, axis=1, keepdims=True)
+    face_of = jnp.sum(first * (lanes // elements).astype(F32), axis=1, keepdims=True)
+    element_of = jnp.sum(first * (lanes % elements).astype(F32), axis=1, keepdims=True)
+    numbers = [slot * sends + place for slot in range(4) for place in range(sends // 2)]
+
+    filled = lanes < elements
+    values = []
+    for field in range(fields):
+        total = None
+        for face in range(faces):
+            stage_ref[field, face * rows : face * rows + fields, 0:elements] = flux_ref[field, :, face, :]
+            part = jnp.where(filled, stage_ref[field, face * rows : (face + 1) * rows, :], 0.0)
+            total = part if total is None else total + pltpu.roll(part, face * elements, 1)
+        total = jnp.where(row_index(shape) < fields, total, 0.0)
+        values.append(high_and_low(total, HALF))
+    picked = jnp.concatenate([jnp.broadcast_to(found[number : number + 1], (HALF, LANES)) for number in numbers], axis=0)
+    flux_out[...] = lax.dot_general(
+        jnp.concatenate(values, axis=0).astype(BF16), picked.astype(BF16), (((1,), (1,)), ((), ())),
+        preferred_element_type=F32,
+    )
+
+    left = []
+    for number in numbers:
+        chosen = composed * one_where(lane_code == code[number : number + 1])
+        both = chosen[:, 0:LANES] + chosen[:, LANES : 2 * LANES]
+        high, low = split(both + swap_halves(both))
+        left.append(jnp.concatenate([jnp.where(lower_half(high.shape), high, low), high], axis=1))
+    high, low = split(lift_sides)
+    lifts = product(jnp.concatenate(left, axis=0), jnp.concatenate([high, high, low, jnp.zeros_like(low)], axis=0))
+    side_lane = (lane_index((1, faces * HALF)) // HALF).astype(F32)
+    place_of = jnp.zeros((1, LANES), F32)
+    for at, number in enumerate(numbers):
+        chosen = lifts[at * HALF : (at + 1) * HALF] * one_where(side_lane == face_of[number : number + 1])
+        both = chosen[:, 0:LANES] + chosen[:, LANES : 2 * LANES]
+        high, low = split(both + swap_halves(both))
+        operator_out[at] = jnp.concatenate([high, high, low, jnp.zeros_like(low)], axis=0)
+        place_of = jnp.where(lane_index((1, LANES)) // rows == at, element_of[number : number + 1], place_of)
+    square = (fields * elements, LANES)
+    here = (row_index(square) // elements == lane_index(square) % rows) & (
+        (row_index(square) % elements).astype(F32) == place_of
+    )
+    one = one_where(here).astype(BF16)
+    scatter_out[...] = jnp.concatenate([one, one], axis=1)
+
+
 def prepare_kernel(
     packed_ref, early_ref, stiffness_ref, star_ref, flux_local_ref, flux_remote_ref, restrict_ref, lift_ref, orient_ref,
     slot_ref, face_ref, turn_ref,
     base_out, local_out, remote_out, volume_out, trace_out, local_lift_out, compose_out,
-    remote_lift_out, choose_out, mask_out,
-    local_work_ref, remote_work_ref, block_ref, wide_ref, face_work_ref, orient_work_ref, code_ref,
+    remote_lift_out, choose_out, mask_out, ghost_flux_out, ghost_operator_out, scatter_out,
+    sides_ref, local_work_ref, remote_work_ref, block_ref, wide_ref, face_work_ref, orient_work_ref, code_ref,
 ):
     fields, kinds = packed_ref.shape[0], stiffness_ref.shape[0]
     face_modes, faces, modes = restrict_ref.shape
@@ -350,6 +413,16 @@
         masks.append(jnp.where(codes[:, faces + face : faces + face + 1] == lane_code, 1.0, 0.0))
     choose_out[...] = jnp.concatenate(picks, axis=0).astype(BF16)
     mask_out[...] = jnp.concatenate(masks, axis=0)
+
+    sides_ref[...] = jnp.zeros(sides_ref.shape, F32)
+    for face in range(faces):
+        for turn in range(turns):
+            rows = slice(turn * face_modes, (turn + 1) * face_modes)
+            sides_ref[rows, face * HALF : face * HALF + modes] = -lift_ref[:, face, :]
+    ghost_terms(
+        flux_remote_ref, local_work_ref, code_ref, stacked.T[0:HALF], sides_ref[...], lane_code[0:1],
+        ghost_flux_out, ghost_operator_out, scatter_out, sends, fields,
+    )
 
     early = early_ref[...].reshape(fields * ROWS, LANES)
     terms = local_terms(early, star_ref, local_out, volume_out, trace_out, local_lift_out, fields, kinds)
@@ -432,48 +505,67 @@
         is_fast = jnp.where(here, rate_ref[element], is_fast)
     late = jnp.where((is_fast == 2)[None], restart.reshape(fields, ROWS, LANES), late_ref[...])
     late_out[...] = late
-    rows_by_pair(late.reshape(fields * ROWS, LANES), late_rows, fields)
-    for side, out in enumerate((send_0, send_1, send_2, send_3)):
+    both = late.reshape(fields * ROWS, LANES)
+    swapped = swap_halves(both)
+    wide = lower_half(both.shape)
+    late_rows[:, 0:ROWS, :] = jnp.where(wide, both, swapped).reshape(late.shape)
+    late_rows[:, ROWS : 2 * ROWS, :] = jnp.where(wide, swapped, both).reshape(late.shape)
+    first_half = lower_half((1, LANES))
+    for slot, out in enumerate((send_0, send_1, send_2, send_3)):
         out[...] = jnp.zeros(out.shape, F32)
-        for place in range(fast):
-            element = send_ref[0, message_side(side), place]
-            for pair in range(pairs):
-                row = pair * fast + place
-                out[row : row + 1, :] = late_rows[pair, pl.ds(element, 1), :]
-
-
-def local_kernel(middle_ref, late_ref, star_ref, flux_ref, volume_ref, trace_ref, lift_ref, base_out):
+        side = message_side(slot)
+        places = [send_ref[0, side, place] for place in range(fast)]
+        for field in range(fields):
+            halves = [late_rows[field, pl.ds(element, 1), :] for element in places]
+            out[field : field + 1, :] = jnp.where(first_half, *halves)
+
+
+def local_kernel(
+    middle_ref, late_ref, star_ref, flux_ref, volume_ref, trace_ref, lift_ref,
+    remote_ref, compose_ref, remote_lift_ref, choose_ref, mask_ref, first_0, first_1, first_2, first_3,
+    base_out, rows_ref,
+):
     fields = middle_ref.shape[0]
     kinds = star_ref.shape[0] // (fields * fields)
-    late = late_ref[...].reshape(fields * ROWS, LANES)
-    terms = local_terms(late, star_ref, flux_ref, volume_ref, trace_ref, lift_ref, fields, kinds)
-    base_out[...] = middle_ref[...] + terms.reshape(fields, ROWS, LANES)
-
-
-def final_kernel(
-    base_ref, late_ref, remote_ref, compose_ref, lift_ref, choose_ref, mask_ref,
-    first_0, first_1, first_2, first_3,
-    second_0, second_1, second_2, second_3,
-    result_out, rows_ref,
-):
-    fields = base_ref.shape[0]
-    modes = result_out.shape[2]
     pairs = rows_ref.shape[0]
     elements = 2 * ROWS
     sends = (rows_ref.shape[1] - elements) // 4
     fast = sends // 2
-    rows_by_pair(late_ref[...].reshape(fields * ROWS, LANES), rows_ref, fields)
-    firsts = (first_0, first_1, first_2, first_3)
-    seconds = (second_0, second_1, second_2, second_3)
-    for side, (first, second) in enumerate(zip(firsts, seconds)):
-        at = elements + side * sends
+    late = late_ref[...].reshape(fields * ROWS, LANES)
+    rows_by_pair(late, rows_ref, fields)
+    for slot, first in enumerate((first_0, first_1, first_2, first_3)):
+        at = elements + slot * sends
         for pair in range(pairs):
-            rows_ref[pair, at : at + fast, :] = second[pair * fast : (pair + 1) * fast, :]
+            rows_ref[pair, at : at + fast, :] = jnp.zeros((fast, LANES), F32)
             row = pairs * sends + pair * fast
             rows_ref[pair, at + fast : at + sends, :] = first[row : row + fast, :]
-    result = base_ref[...] + remote_terms(
-        rows_ref, remote_ref, compose_ref, lift_ref, choose_ref, mask_ref, fields
-    )
+    terms = local_terms(late, star_ref, flux_ref, volume_ref, trace_ref, lift_ref, fields, kinds)
+    remote = remote_terms(rows_ref, remote_ref, compose_ref, remote_lift_ref, choose_ref, mask_ref, fields)
+    base_out[...] = middle_ref[...] + terms.reshape(fields, ROWS, LANES) + remote
+
+
+def final_kernel(
+    base_ref, ghost_flux_ref, ghost_operator_ref, scatter_ref, second_0, second_1, second_2, second_3, result_out,
+):
+    fields = base_ref.shape[0]
+    modes = result_out.shape[2]
+    rows = second_0.shape[0]
+    lower = lower_half((rows, LANES))
+    added = []
+    for slot, second in enumerate((second_0, second_1, second_2, second_3)):
+        mixed = None
+        for field in range(fields):
+            coefficient = ghost_flux_ref[field * rows : (field + 1) * rows, slot * LANES : (slot + 1) * LANES]
+            term = coefficient * second[field : field + 1, :]
+            mixed = term if mixed is None else mixed + term
+        high, low = split(mixed)
+        high_swapped, low_swapped = split(swap_halves(mixed))
+        for place, parts in enumerate(((high, low_swapped, high), (high_swapped, low, high_swapped))):
+            left = jnp.concatenate([jnp.where(lower, parts[0], parts[1]), parts[2]], axis=1)
+            added.append(product(left, ghost_operator_ref[2 * slot + place]))
+    right = jnp.concatenate(split(jnp.concatenate(added, axis=0)), axis=0)
+    scattered = product(scatter_ref[...], right).reshape(fields, 2, ROWS, LANES)
+    result = base_ref[...] + jnp.where(lower_half((ROWS, LANES))[None], scattered[:, 0], scattered[:, 1])
     result_out[:, 0:ROWS, :] = result[:, :, 0:modes]
     result_out[:, ROWS : 2 * ROWS, :] = result[:, :, HALF : HALF + modes]
 
@@ -526,7 +618,7 @@
     sides, sends = send_list.shape[1], send_list.shape[2]
     fast = sends // 2
     pairs = (fields + 1) // 2
-    assert elements == 2 * ROWS and solution.shape[0] <= HALF
+    assert elements == 2 * ROWS and solution.shape[0] <= HALF and fast == 2
     values = jnp.transpose(solution, (1, 2, 0))
     star = jnp.transpose(star_matrices, (1, 2, 0, 3))
     local_part = jnp.transpose(flux_local, (1, 2, 0, 3))
@@ -536,7 +628,7 @@
 
     packed = (fields, ROWS, LANES)
     first_shape = (up_to(pairs * (sends + fast), ROWS), LANES)
-    second_shape = (up_to(pairs * fast, ROWS), LANES)
+    second_shape = (up_to(fields, 2 * ROWS), LANES)
     star_shape = (fields * fields * kinds, ROWS, LANES)
     combos = faces * HALF
     sources = elements + sides * sends
@@ -563,6 +655,7 @@
     first = exchange(outgoing)
     (
         base, local_coef, remote_coef, volume_op, trace_op, local_lift, compose_op, remote_lift, choose, mask,
+        ghost_flux, ghost_op, scatter,
     ) = call(
         prepare_kernel,
         [VMEM] * 12,
@@ -572,9 +665,11 @@
             ((3 * LANES, kinds * LANES), BF16), ((3 * LANES, 2 * LANES), BF16),
             ((6 * LANES, LANES), BF16), ((2 * LANES, combos), BF16), ((3 * faces * HALF, LANES), BF16),
             ((faces * elements, 2 * sources), BF16), ((faces * elements, combos), F32),
+            ((fields * second_shape[0], sides * LANES), F32), ((sides * fast, 2 * LANES, LANES), BF16),
+            ((fields * elements, 2 * LANES), BF16),
         ],
         [
-            ((fields, 2 * ROWS * faces, LANES), F32), ((pairs, 2 * up_to(4 * fields, ROWS), LANES), F32),
+            ((HALF, faces * HALF), F32), ((fields, 2 * ROWS * faces, LANES), F32), ((pairs, 2 * up_to(4 * fields, ROWS), LANES), F32),
             ((kinds, LANES, LANES), F32), ((2 * LANES, LANES), F32),
             ((LANES, faces * LANES), F32), ((HALF, LANES), F32), ((LANES, LANES), F32),
         ],
@@ -586,7 +681,7 @@
         [VMEM] * 10 + [HBM] * 2 + [VMEM] * 4,
         [(packed, F32)] * 2 + [(second_shape, F32)] * sides,
         [
-            ((pairs, sources, LANES), F32), ((pairs, elements, LANES), F32),
+            ((pairs, sources, LANES), F32), ((fields, elements, LANES), F32),
             pltpu.SMEM(cluster_rate.shape, jnp.int32), pltpu.SMEM(send_list.shape, jnp.int32),
             pltpu.SemaphoreType.DMA((2,)),
         ],
@@ -599,18 +694,21 @@
     second = exchange(outgoing)
     (base,) = call(
         local_kernel,
-        [VMEM] * 7,
+        [VMEM] * 16,
         [(packed, F32)],
-        [],
-        (middle, late_value, star_coef, local_coef, volume_op, trace_op, local_lift),
+        [((pairs, sources, LANES), F32)],
+        (
+            middle, late_value, star_coef, local_coef, volume_op, trace_op, local_lift,
+            remote_coef, compose_op, remote_lift, choose, mask, *first,
+        ),
         "local_late", 200_000_000,
     )
     (result,) = call(
         final_kernel,
-        [VMEM] * 15,
+        [VMEM] * 8,
         [(values.shape, F32)],
-        [((pairs, sources, LANES), F32)],
-        (base, late_value, remote_coef, compose_op, remote_lift, choose, mask, *first, *second),
+        [],
+        (base, ghost_flux, ghost_op, scatter, *second),
         "final", 200_000_000,
     )
     return jnp.transpose(result, (2, 0, 1))

time: 23 us -> 22.7 us (0.987)
  waiting for transfers between devices: 2.31 us -> 1.11 us
  Pallas kernels: 8.42 us -> 9.32 us
    ppermute x8, waiting for transfers between devices: 2.31 us -> 1.11 us  [exchange(): arrived.append(lax.ppermute(message, axis, pairs))]
    pallas_call x5, Pallas kernels: 8.42 us -> 9.32 us  [call(): pl.pallas_call(kernel, out_shape=shapes, in_specs=ins, out_specs=[VMEM] *...]
  transfers between devices with their start and end apart: 8 -> 8, of which waited for: 3 -> 3; matrix products, arithmetic and copies ran while one was open for 0% -> 0% of each run, Pallas kernels for 8% -> 14%
where the time goes in v8:
time: 22.7 us; the launch traced here: 22.6 us
  starting transfers between devices  12.1 us (53%)
  Pallas kernels  9.32 us (41%)
  waiting for transfers between devices  1.11 us (5%)
    ppermute x8, starting transfers between devices, exchange(): arrived.append(lax.ppermute(message, axis, pairs))  12.1 us
    pallas_call x5, Pallas kernels, call(): pl.pallas_call(kernel, out_shape=shapes, in_specs=ins, out_specs=[VMEM] *...  9.32 us
    ppermute x8, waiting for transfers between devices, exchange(): arrived.append(lax.ppermute(message, axis, pairs))  1.11 us
  transfers between devices with their start and end apart: 8, of which 3 were waited for; matrix products, arithmetic and copies ran while one was open for 0% of the time, Pallas kernels for 14%

profile of v8, /device:TPU:0, one launch (start us, length us, event | category | flops | bytes accessed | tf_op | source)
XLA Modules:
  0.0 22.6 jit_solution(8581133036117393373)
XLA Ops:
  0.0 2.9 %predict.1 = (f32[9,8,128]{2,1,0:T(8,128)S(1)}, f32[9,8,128]{2,1,0:T(8,128)S(1)}, f32[32,128]{1,0:T(8,128)S(1)}, f32[32,128]{1,0:T(8,128)S(1)}, f32[32,128]{1,0:...) custom-call(f32[9,16,56]{2,1,0:T(8,128)} %bitcast.10, ...), custom_call_target="tpu_custom_call" | custom-call | flops 100000000 | bytes 4000000 | tf_op jit(solution)/shard_map/predict/pallas_call | solution.py:582
  2.9 6.0 %collective-permute-start = (f32[32,128]{1,0:T(8,128)S(1)}, f32[32,128]{1,0:T(8,128)S(1)}, u32[]{:S(2)}, u32[]{:S(2)}) collective-permute-start(f32[32,128]{1,0:T(8,128)S(1)} %get-tuple-element.62), channel_id=1, source_target_pairs={{4,8},{8,4},{12,16},{16,12},{20,24},{24,20},{28,0},{0,28},{5,9},{9... | collective-permute-start | bytes 49160 | tf_op jit(solution)/shard_map/ppermute | solution.py:603
  9.0 0.0 collective-permute-start.1
  9.0 0.7 %collective-permute-start.2 = (f32[32,128]{1,0:T(8,128)S(1)}, f32[32,128]{1,0:T(8,128)S(1)}, u32[]{:S(2)}, u32[]{:S(2)}) collective-permute-start(f32[32,128]{1,0:T(8,128)S(1)} %get-tuple-element.64), channel_id=1, source_target_pairs={{1,2},{2,1},{3,0},{0,3},{5,6},{6,5},{7,4},{4,7},{9,10},{10,9},{11,... | collective-permute-start | bytes 49160 | tf_op jit(solution)/shard_map/ppermute | solution.py:603
  9.7 1.0 %collective-permute-start.3 = (f32[32,128]{1,0:T(8,128)S(1)}, f32[32,128]{1,0:T(8,128)S(1)}, u32[]{:S(2)}, u32[]{:S(2)}) collective-permute-start(f32[32,128]{1,0:T(8,128)S(1)} %get-tuple-element.65), channel_id=1, source_target_pairs={{0,1},{1,0},{2,3},{3,2},{4,5},{5,4},{6,7},{7,6},{8,9},{9,8},{10,11... | collective-permute-start | bytes 49160 | tf_op jit(solution)/shard_map/ppermute | solution.py:603
  10.6 2.0 %prepare.1 = (f32[9,8,128]{2,1,0:T(8,128)S(1)}, f32[81,2,8,128]{3,2,1,0:T(8,128)S(1)}, f32[180,16,128]{2,1,0:T(8,128)S(1)}, bf16[384,384]{1,0:T(8,128)(2,1)S(1)}...) custom-call(f32[9,8,128]{2,1,0:T(8,128)S(1)} %get-tuple-element.42.p, ...), custom_call_target="tpu_custom_call" | custom-call | flops 200000000 | bytes 4000000 | tf_op jit(solution)/shard_map/prepare/pallas_call | solution.py:582
  12.6 0.0 collective-permute-done.from_0.first_0
  12.6 0.1 collective-permute-done.1.from_1.first_1
  12.7 0.0 collective-permute-done.2.from_2.first_2
  12.7 0.0 collective-permute-done.3.from_3.first_3
  12.7 2.2 %middle.1 = (f32[9,8,128]{2,1,0:T(8,128)S(1)}, f32[9,8,128]{2,1,0:T(8,128)S(1)}, f32[16,128]{1,0:T(8,128)S(1)}, f32[16,128]{1,0:T(8,128)S(1)}, f32[16,128]{1,0:T(8,128)S(1)}, /*index=5*/f32[16,128]{1,0:T(8,128)S(1)}) custom-call(f32[9,8,128]{2,1,0:T(8,128)S(1)} %get-tuple-element.54.base_ref, f32[9,8,128]{2,1,0:T(8,128)S(1)} %get-tuple-element.43.early_ref, ...), custom_call_target="tpu_custom_call" | custom-call | flops 200000000 | bytes 4000000 | tf_op jit(solution)/shard_map/middle/pallas_call | solution.py:582
  14.9 2.8 %collective-permute-start.4 = (f32[16,128]{1,0:T(8,128)S(1)}, f32[16,128]{1,0:T(8,128)S(1)}, u32[]{:S(2)}, u32[]{:S(2)}) collective-permute-start(f32[16,128]{1,0:T(8,128)S(1)} %get-tuple-element.75), channel_id=1, source_target_pairs={{4,8},{8,4},{12,16},{16,12},{20,24},{24,20},{28,0},{0,28},{5,9},{9... | collective-permute-start | bytes 24584 | tf_op jit(solution)/shard_map/ppermute | solution.py:603
  17.7 0.0 collective-permute-start.5
  17.7 0.0 collective-permute-start.6
  17.7 1.6 %collective-permute-start.7 = (f32[16,128]{1,0:T(8,128)S(1)}, f32[16,128]{1,0:T(8,128)S(1)}, u32[]{:S(2)}, u32[]{:S(2)}) collective-permute-start(f32[16,128]{1,0:T(8,128)S(1)} %get-tuple-element.78), channel_id=1, source_target_pairs={{0,1},{1,0},{2,3},{3,2},{4,5},{5,4},{6,7},{7,6},{8,9},{9,8},{10,11... | collective-permute-start | bytes 24584 | tf_op jit(solution)/shard_map/ppermute | solution.py:603
  19.3 1.1 %local_late.1.base_ref = f32[9,8,128]{2,1,0:T(8,128)S(1)} custom-call(f32[9,8,128]{2,1,0:T(8,128)S(1)} %get-tuple-element.66.middle_ref, f32[9,8,128]{2,1,0:T(8,128)S(1)} %get-tuple-element.67.late_ref, f32[243,8,128]{2,1,0:T(8,128)S(1)} %get-tuple-element.45.star_ref, f32[81,2,8,128]{3,2,1,0:T(8,128)S(1)} %get-tuple-element.68.flux_ref, ...), custom_call_target="tpu_custom_call" | custom-call | flops 200000000 | bytes 4000000 | tf_op jit(solution)/shard_map/local_late/pallas_call | solution.py:582
  20.4 0.9 %collective-permute-done.4.second_0 = f32[16,128]{1,0:T(8,128)S(1)} collective-permute-done((f32[16,128]{1,0:T(8,128)S(1)}, f32[16,128]{1,0:T(8,128)S(1)}, u32[]{:S(2)}, u32[]{:S(2)}) %collective-permute-start.4) | collective-permute-done | bytes 8224 | tf_op jit(solution)/shard_map/ppermute | solution.py:603
  21.3 0.1 collective-permute-done.5.second_1
  21.4 0.0 collective-permute-done.6.second_2
  21.4 0.0 collective-permute-done.7.second_3
  21.4 1.1 %final.1 = f32[9,16,56]{2,1,0:T(8,128)} custom-call(f32[9,8,128]{2,1,0:T(8,128)S(1)} %local_late.1.base_ref, f32[144,512]{1,0:T(8,128)S(1)} %get-tuple-element.72.ghost_flux_ref, bf16[8,256,128]{2,1,0:T(8,128)(2,1)S(1)} %get-tuple-element.73.ghost_operator_ref, bf16[144,256]{1,0:T(8,128)(2,1)S(1)} %get-tuple-element.74.scatter_ref, ...), custom_call_target="tpu_custom_call" | custom-call | flops 200000000 | bytes 4000000 | tf_op jit(solution)/shard_map/final/pallas_call | solution.py:582
Async XLA Ops:
  2.9 9.7 %collective-permute-start = (f32[32,128]{1,0:T(8,128)S(1)}, f32[32,128]{1,0:T(8,128)S(1)}, u32[]{:S(2)}, u32[]{:S(2)}) collective-permute-start(f32[32,128]{1,0:T(8,128)S(1)} %get-tuple-element.62), channel_id=1, source_target_pairs={{4,8},{8,4},{12,16},{16,12},{20,24},{24,20},{28,0},{0,28},{5,9},{9... | collective-permute-start | bytes 49160 | tf_op jit(solution)/shard_map/ppermute | solution.py:603
  9.0 3.7 %collective-permute-start.1 = (f32[32,128]{1,0:T(8,128)S(1)}, f32[32,128]{1,0:T(8,128)S(1)}, u32[]{:S(2)}, u32[]{:S(2)}) collective-permute-start(f32[32,128]{1,0:T(8,128)S(1)} %get-tuple-element.63), channel_id=1, source_target_pairs={{0,4},{4,0},{8,12},{12,8},{16,20},{20,16},{24,28},{28,24},{1,5},{5... | collective-permute-start | bytes 49160 | tf_op jit(solution)/shard_map/ppermute | solution.py:603
  9.0 3.7 %collective-permute-start.2 = (f32[32,128]{1,0:T(8,128)S(1)}, f32[32,128]{1,0:T(8,128)S(1)}, u32[]{:S(2)}, u32[]{:S(2)}) collective-permute-start(f32[32,128]{1,0:T(8,128)S(1)} %get-tuple-element.64), channel_id=1, source_target_pairs={{1,2},{2,1},{3,0},{0,3},{5,6},{6,5},{7,4},{4,7},{9,10},{10,9},{11,... | collective-permute-start | bytes 49160 | tf_op jit(solution)/shard_map/ppermute | solution.py:603
  9.7 3.1 %collective-permute-start.3 = (f32[32,128]{1,0:T(8,128)S(1)}, f32[32,128]{1,0:T(8,128)S(1)}, u32[]{:S(2)}, u32[]{:S(2)}) collective-permute-start(f32[32,128]{1,0:T(8,128)S(1)} %get-tuple-element.65), channel_id=1, source_target_pairs={{0,1},{1,0},{2,3},{3,2},{4,5},{5,4},{6,7},{7,6},{8,9},{9,8},{10,11... | collective-permute-start | bytes 49160 | tf_op jit(solution)/shard_map/ppermute | solution.py:603
  14.9 6.4 %collective-permute-start.4 = (f32[16,128]{1,0:T(8,128)S(1)}, f32[16,128]{1,0:T(8,128)S(1)}, u32[]{:S(2)}, u32[]{:S(2)}) collective-permute-start(f32[16,128]{1,0:T(8,128)S(1)} %get-tuple-element.75), channel_id=1, source_target_pairs={{4,8},{8,4},{12,16},{16,12},{20,24},{24,20},{28,0},{0,28},{5,9},{9... | collective-permute-start | bytes 24584 | tf_op jit(solution)/shard_map/ppermute | solution.py:603
  17.7 3.7 %collective-permute-start.5 = (f32[16,128]{1,0:T(8,128)S(1)}, f32[16,128]{1,0:T(8,128)S(1)}, u32[]{:S(2)}, u32[]{:S(2)}) collective-permute-start(f32[16,128]{1,0:T(8,128)S(1)} %get-tuple-element.76), channel_id=1, source_target_pairs={{0,4},{4,0},{8,12},{12,8},{16,20},{20,16},{24,28},{28,24},{1,5},{5... | collective-permute-start | bytes 24584 | tf_op jit(solution)/shard_map/ppermute | solution.py:603
  17.7 3.7 %collective-permute-start.6 = (f32[16,128]{1,0:T(8,128)S(1)}, f32[16,128]{1,0:T(8,128)S(1)}, u32[]{:S(2)}, u32[]{:S(2)}) collective-permute-start(f32[16,128]{1,0:T(8,128)S(1)} %get-tuple-element.77), channel_id=1, source_target_pairs={{1,2},{2,1},{3,0},{0,3},{5,6},{6,5},{7,4},{4,7},{9,10},{10,9},{11,... | collective-permute-start | bytes 24584 | tf_op jit(solution)/shard_map/ppermute | solution.py:603
  17.7 3.7 %collective-permute-start.7 = (f32[16,128]{1,0:T(8,128)S(1)}, f32[16,128]{1,0:T(8,128)S(1)}, u32[]{:S(2)}, u32[]{:S(2)}) collective-permute-start(f32[16,128]{1,0:T(8,128)S(1)} %get-tuple-element.78), channel_id=1, source_target_pairs={{0,1},{1,0},{2,3},{3,2},{4,5},{5,4},{6,7},{7,6},{8,9},{9,8},{10,11... | collective-permute-start | bytes 24584 | tf_op jit(solution)/shard_map/ppermute | solution.py:603

commit v9 on v8

--- a/solution.py
+++ b/solution.py
@@ -15,6 +15,7 @@
 BF16 = jnp.bfloat16
 LATER = ("flux_local", "flux_remote", "face_restrict", "face_lift", "orient_maps", "slot", "face", "turn")
 AXES = ("dom", "sub")
+AHEAD = 1
 SWAPS = (("dom", True), ("dom", False), ("sub", True), ("sub", False))
 
 
@@ -79,7 +80,6 @@
 
 def pack(values_ref, packed_ref):
     modes = values_ref.shape[2]
-    packed_ref[...] = jnp.zeros(packed_ref.shape, F32)
     packed_ref[:, :, 0:modes] = values_ref[:, 0:ROWS, :]
     packed_ref[:, :, HALF : HALF + modes] = values_ref[:, ROWS : 2 * ROWS, :]
 
@@ -99,25 +99,28 @@
 
 def star_coefficients(star_ref, stage_ref, star_out):
     fields, kinds, elements = star_ref.shape[0], star_ref.shape[2], star_ref.shape[3]
+    rows = 2 * ROWS
     lanes = lane_index((ROWS, LANES))
-    pick = one_where((lanes % ROWS == row_index((ROWS, LANES))) & (lanes < 2 * elements))
-    from_lane = row_index((LANES, LANES))
-    same_half = (from_lane % elements) // ROWS == lane_index((LANES, LANES)) // HALF
-    right = one_where(same_half & (from_lane < 2 * elements)).astype(BF16)
-    filled = lane_index(stage_ref.shape[1:]) < elements
+    pick = one_where((lanes % ROWS == row_index((ROWS, LANES))) & (lanes < 2 * kinds * elements))
+    shape = (LANES, kinds * LANES)
+    from_lane, to_lane = row_index(shape), lane_index(shape)
+    same_kind = from_lane // (2 * elements) == to_lane // LANES
+    same_half = (from_lane % elements) // ROWS == (to_lane % LANES) // HALF
+    right = one_where(same_kind & same_half).astype(BF16)
+    filled = lane_index((rows, LANES)) < elements
     for row in range(fields):
-        for col in range(fields):
-            stage_ref[row, col * 4 : col * 4 + kinds, 0:elements] = star_ref[row, col]
-        values = jnp.where(filled, stage_ref[row], 0.0)
-        stage_ref[row] = high_and_low(values, elements)
-        spreads = []
+        values = None
         for kind in range(kinds):
-            for col in range(fields):
-                at = col * 4 + kind
-                spreads.append(stage_ref[row, at : at + 1, :] * pick)
-        spread_out = product(jnp.concatenate(spreads, axis=0).astype(BF16), right)
-        count = kinds * fields
-        star_out[row * count : (row + 1) * count] = spread_out.reshape(count, ROWS, LANES)
+            stage_ref[row, kind * rows : kind * rows + fields, 0:elements] = star_ref[row, :, kind, :]
+            part = jnp.where(filled, stage_ref[row, kind * rows : (kind + 1) * rows, :], 0.0)
+            values = part if values is None else values + pltpu.roll(part, kind * 2 * elements, 1)
+        stage_ref[row, 0:rows, :] = high_and_low(values, elements)
+        left = [stage_ref[row, col : col + 1, :] * pick for col in range(fields)]
+        spread = product(jnp.concatenate(left, axis=0).astype(BF16), right)
+        for kind in range(kinds):
+            at = (row * kinds + kind) * fields
+            part = spread[:, kind * LANES : (kind + 1) * LANES]
+            star_out[at : at + fields] = part.reshape(fields, ROWS, LANES)
 
 
 def star_mix(columns, star_ref, fields, kinds):
@@ -133,7 +136,6 @@
 
 def stiffness_blocks(stiffness_ref, block_ref, turned):
     kinds, modes = stiffness_ref.shape[0], stiffness_ref.shape[1]
-    block_ref[...] = jnp.zeros(block_ref.shape, F32)
     for kind in range(kinds):
         matrix = -stiffness_ref[kind].T if turned else stiffness_ref[kind]
         block_ref[kind, 0:modes, 0:modes] = matrix
@@ -145,9 +147,9 @@
     later = len(LATER)
     solution_hbm, stiffness_hbm, star_hbm, send_hbm = refs[0:4]
     later_hbm, refs = refs[4 : 4 + later], refs[4 + later :]
-    early_out, late_out, send_0, send_1, send_2, send_3 = refs[0:6]
-    packed_ref, coef_ref, derive_ref, stiffness_ref = refs[6:10]
-    later_out, refs = refs[10 : 10 + later], refs[10 + later :]
+    early_out, late_out, ahead_out, send_0, send_1, send_2, send_3 = refs[0:7]
+    packed_ref, coef_ref, derive_ref, stiffness_ref = refs[7:11]
+    later_out, refs = refs[11 : 11 + later], refs[11 + later :]
     work_ref, early_rows, late_rows, solution_ref, block_ref, star_ref, send_ref, sems = refs
 
     sources = (star_hbm, stiffness_hbm, solution_hbm, send_hbm, *later_hbm)
@@ -156,10 +158,14 @@
         pltpu.make_async_copy(source, target, sems.at[number])
         for number, (source, target) in enumerate(zip(sources, targets))
     ]
-    for copy in copies:
+    for copy in copies[0:4]:
         copy.start()
     fields, kinds = star_ref.shape[0], star_ref.shape[2]
     pairs = (fields + 1) // 2
+    for cleared in (packed_ref, block_ref, send_0, send_1, send_2, send_3):
+        cleared[...] = jnp.zeros(cleared.shape, F32)
+    for copy in copies[4:]:
+        copy.start()
     for copy in copies[0:3]:
         copy.wait()
     derive_ref[...] = stack_right(stiffness_blocks(stiffness_ref, block_ref, True))
@@ -185,7 +191,6 @@
     sends = send_ref.shape[2]
     fast = sends // 2
     for side, out in enumerate((send_0, send_1, send_2, send_3)):
-        out[...] = jnp.zeros(out.shape, F32)
         for place in range(sends):
             element = send_ref[0, message_side(side), place]
             for pair in range(pairs):
@@ -195,6 +200,7 @@
                 for pair in range(pairs):
                     row = pairs * sends + pair * fast + place - fast
                     out[row : row + 1, :] = late_rows[pair, pl.ds(element, 1), :]
+    ahead_out[...] = (send_0, send_1, send_2, send_3)[AHEAD][...]
     for copy in copies[4:]:
         copy.wait()
 
@@ -279,6 +285,12 @@
     return volume + product(stack_left(jnp.concatenate(sums, axis=0)), lift_ref[...])
 
 
+def combo_code(lanes, turns, face_modes):
+    in_face = lanes % HALF
+    code = jnp.where(in_face < turns * face_modes, (lanes // HALF) * turns + in_face // face_modes, -1)
+    return code.astype(F32)
+
+
 def ghost_terms(
     flux_ref, stage_ref, code_ref, composed, lift_sides, lane_code, flux_out, operator_out, scatter_out, sends, fields
 ):
@@ -346,8 +358,8 @@
     packed_ref, early_ref, stiffness_ref, star_ref, flux_local_ref, flux_remote_ref, restrict_ref, lift_ref, orient_ref,
     slot_ref, face_ref, turn_ref,
     base_out, local_out, remote_out, volume_out, trace_out, local_lift_out, compose_out,
-    remote_lift_out, choose_out, mask_out, ghost_flux_out, ghost_operator_out, scatter_out,
-    sides_ref, local_work_ref, remote_work_ref, block_ref, wide_ref, face_work_ref, orient_work_ref, code_ref,
+    remote_lift_out, choose_out, mask_out, code_ref, composed_out, sides_ref,
+    local_work_ref, remote_work_ref, block_ref, wide_ref, face_work_ref, orient_work_ref, code_work_ref,
 ):
     fields, kinds = packed_ref.shape[0], stiffness_ref.shape[0]
     face_modes, faces, modes = restrict_ref.shape
@@ -355,6 +367,7 @@
     flux_local_coefficients(flux_local_ref, local_work_ref, local_out)
     flux_remote_coefficients(flux_remote_ref, remote_work_ref, remote_out)
 
+    block_ref[...] = jnp.zeros(block_ref.shape, F32)
     volume_out[...] = stack_right(stiffness_blocks(stiffness_ref, block_ref, False))
 
     wide_ref[...] = jnp.zeros(wide_ref.shape, F32)
@@ -391,22 +404,21 @@
     remote_lift_out[...] = stack_right(wide_ref[...])
 
     elements = slot_ref.shape[1]
-    code_ref[...] = jnp.zeros(code_ref.shape, F32)
+    code_work_ref[...] = jnp.zeros(code_work_ref.shape, F32)
     slots = slot_ref[...]
     sends = (choose_out.shape[1] // 2 - elements) // 4
     group = (slots - elements) // sends
     moved = slots
     for side in range(4):
         moved = jnp.where(group == side, slots + (ghost_slot(side) - side) * sends, moved)
-    code_ref[0:faces, 0:elements] = jnp.where(slots < elements, slots, moved).astype(F32)
-    code_ref[faces : 2 * faces, 0:elements] = (face_ref[...] * turns + turn_ref[...]).astype(F32)
-    codes = code_ref[...].T[0:elements, :]
+    code_work_ref[0:faces, 0:elements] = jnp.where(slots < elements, slots, moved).astype(F32)
+    code_work_ref[faces : 2 * faces, 0:elements] = (face_ref[...] * turns + turn_ref[...]).astype(F32)
+    code_ref[...] = code_work_ref[0 : 2 * faces, :]
+    codes = code_work_ref[...].T[0:elements, :]
     sources = choose_out.shape[1] // 2
     source_lane = (lane_index((elements, 2 * sources)) % sources).astype(F32)
     lanes = lane_index((elements, mask_out.shape[1]))
-    in_face = lanes % HALF
-    lane_code = jnp.where(in_face < turns * face_modes, (lanes // HALF) * turns + in_face // face_modes, -1)
-    lane_code = lane_code.astype(F32)
+    lane_code = combo_code(lanes, turns, face_modes)
     picks, masks = [], []
     for face in range(faces):
         picks.append(jnp.where(codes[:, face : face + 1] == source_lane, 1.0, 0.0))
@@ -419,10 +431,7 @@
         for turn in range(turns):
             rows = slice(turn * face_modes, (turn + 1) * face_modes)
             sides_ref[rows, face * HALF : face * HALF + modes] = -lift_ref[:, face, :]
-    ghost_terms(
-        flux_remote_ref, local_work_ref, code_ref, stacked.T[0:HALF], sides_ref[...], lane_code[0:1],
-        ghost_flux_out, ghost_operator_out, scatter_out, sends, fields,
-    )
+    composed_out[...] = stacked.T[0:HALF]
 
     early = early_ref[...].reshape(fields * ROWS, LANES)
     terms = local_terms(early, star_ref, local_out, volume_out, trace_out, local_lift_out, fields, kinds)
@@ -462,7 +471,7 @@
 
 def middle_kernel(
     base_ref, early_ref, late_ref, star_ref, remote_ref, derive_ref, compose_ref, lift_ref, choose_ref, mask_ref,
-    rate_hbm, send_hbm, from_0, from_1, from_2, from_3,
+    rate_hbm, send_hbm, ahead_1, from_0, from_1, from_2, from_3,
     middle_out, late_out, send_0, send_1, send_2, send_3,
     rows_ref, late_rows, rate_ref, send_ref, sems,
 ):
@@ -482,7 +491,9 @@
     for side, arrived in enumerate((from_0, from_1, from_2, from_3)):
         at = elements + side * sends
         for pair in range(pairs):
-            rows_ref[pair, at : at + sends, :] = arrived[pair * sends : (pair + 1) * sends, :]
+            rows = slice(pair * sends, (pair + 1) * sends)
+            got = arrived[rows, :]
+            rows_ref[pair, at : at + sends, :] = got + ahead_1[rows, :] if side == AHEAD else got
     middle = base_ref[...] + remote_terms(
         rows_ref, remote_ref, compose_ref, lift_ref, choose_ref, mask_ref, fields
     )
@@ -522,8 +533,9 @@
 
 def local_kernel(
     middle_ref, late_ref, star_ref, flux_ref, volume_ref, trace_ref, lift_ref,
-    remote_ref, compose_ref, remote_lift_ref, choose_ref, mask_ref, first_0, first_1, first_2, first_3,
-    base_out, rows_ref,
+    remote_ref, compose_ref, remote_lift_ref, choose_ref, mask_ref, flux_remote_ref, code_ref, composed_ref, sides_ref,
+    orient_ref, ahead_1, first_0, first_1, first_2, first_3,
+    base_out, ghost_flux_out, ghost_operator_out, scatter_out, rows_ref, stage_ref,
 ):
     fields = middle_ref.shape[0]
     kinds = star_ref.shape[0] // (fields * fields)
@@ -538,10 +550,16 @@
         for pair in range(pairs):
             rows_ref[pair, at : at + fast, :] = jnp.zeros((fast, LANES), F32)
             row = pairs * sends + pair * fast
-            rows_ref[pair, at + fast : at + sends, :] = first[row : row + fast, :]
+            got = first[row : row + fast, :]
+            rows_ref[pair, at + fast : at + sends, :] = got + ahead_1[row : row + fast, :] if slot == AHEAD else got
     terms = local_terms(late, star_ref, flux_ref, volume_ref, trace_ref, lift_ref, fields, kinds)
     remote = remote_terms(rows_ref, remote_ref, compose_ref, remote_lift_ref, choose_ref, mask_ref, fields)
     base_out[...] = middle_ref[...] + terms.reshape(fields, ROWS, LANES) + remote
+    lane_code = combo_code(lane_index((1, composed_ref.shape[1])), orient_ref.shape[0], orient_ref.shape[1])
+    ghost_terms(
+        flux_remote_ref, stage_ref, code_ref, composed_ref[...], sides_ref[...], lane_code,
+        ghost_flux_out, ghost_operator_out, scatter_out, sends, fields,
+    )
 
 
 def final_kernel(
@@ -591,17 +609,20 @@
     )(*args)
 
 
-def exchange(outgoing):
-    arrived = []
-    for (axis, far), message in zip(SWAPS, outgoing):
+def exchange(outgoing, ahead=None):
+    arrived, early = [], []
+    for slot, ((axis, far), message) in enumerate(zip(SWAPS, outgoing)):
         size = lax.axis_size(axis)
         assert size % 2 == 0
         pairs = []
         for first in range(1 if far else 0, size, 2):
             second = (first + 1) % size
             pairs += [(first, second), (second, first)]
+        if ahead is not None and slot == AHEAD:
+            early.append(lax.ppermute(ahead, axis, pairs[0:2]))
+            pairs = pairs[2:]
         arrived.append(lax.ppermute(message, axis, pairs))
-    return arrived
+    return early + arrived
 
 
 def up_to(count, multiple):
@@ -637,11 +658,11 @@
     made = call(
         predict_kernel,
         [HBM] * (4 + len(LATER)),
-        [(packed, F32)] * 2 + [(first_shape, F32)] * sides + [
+        [(packed, F32)] * 2 + [(first_shape, F32)] * (1 + sides) + [
             (packed, F32), (star_shape, F32), ((3 * LANES, kinds * LANES), BF16), (stiffness.shape, F32),
         ] + [(array.shape, array.dtype) for array in waiting],
         [
-            ((fields, up_to(4 * fields, ROWS), LANES), F32),
+            ((fields, kinds * up_to(fields, 2 * ROWS), LANES), F32),
             ((pairs, elements, LANES), F32), ((pairs, elements, LANES), F32),
             (values.shape, F32), ((kinds, LANES, LANES), F32), (star.shape, F32),
             pltpu.SMEM(send_list.shape, jnp.int32), pltpu.SemaphoreType.DMA((4 + len(LATER),)),
@@ -649,13 +670,13 @@
         (values, stiffness, star, send_list, *waiting),
         "predict", 100_000_000,
     )
-    early, late, outgoing = made[0], made[1], made[2 : 2 + sides]
-    start, star_coef, derive_op, stiffness_kept = made[2 + sides : 6 + sides]
-    waiting = made[6 + sides :]
-    first = exchange(outgoing)
+    early, late, ahead, outgoing = made[0], made[1], made[2], made[3 : 3 + sides]
+    start, star_coef, derive_op, stiffness_kept = made[3 + sides : 7 + sides]
+    waiting = made[7 + sides :]
+    first = exchange(outgoing, ahead)
     (
         base, local_coef, remote_coef, volume_op, trace_op, local_lift, compose_op, remote_lift, choose, mask,
-        ghost_flux, ghost_op, scatter,
+        codes, composed, lift_sides,
     ) = call(
         prepare_kernel,
         [VMEM] * 12,
@@ -665,11 +686,10 @@
             ((3 * LANES, kinds * LANES), BF16), ((3 * LANES, 2 * LANES), BF16),
             ((6 * LANES, LANES), BF16), ((2 * LANES, combos), BF16), ((3 * faces * HALF, LANES), BF16),
             ((faces * elements, 2 * sources), BF16), ((faces * elements, combos), F32),
-            ((fields * second_shape[0], sides * LANES), F32), ((sides * fast, 2 * LANES, LANES), BF16),
-            ((fields * elements, 2 * LANES), BF16),
+            ((2 * faces, LANES), F32), ((HALF, combos), F32), ((HALF, faces * HALF), F32),
         ],
         [
-            ((HALF, faces * HALF), F32), ((fields, 2 * ROWS * faces, LANES), F32), ((pairs, 2 * up_to(4 * fields, ROWS), LANES), F32),
+            ((fields, 2 * ROWS * faces, LANES), F32), ((pairs, 2 * up_to(4 * fields, ROWS), LANES), F32),
             ((kinds, LANES, LANES), F32), ((2 * LANES, LANES), F32),
             ((LANES, faces * LANES), F32), ((HALF, LANES), F32), ((LANES, LANES), F32),
         ],
@@ -678,7 +698,7 @@
     )
     middle, late_value, *outgoing = call(
         middle_kernel,
-        [VMEM] * 10 + [HBM] * 2 + [VMEM] * 4,
+        [VMEM] * 10 + [HBM] * 2 + [VMEM] * len(first),
         [(packed, F32)] * 2 + [(second_shape, F32)] * sides,
         [
             ((pairs, sources, LANES), F32), ((fields, elements, LANES), F32),
@@ -692,14 +712,18 @@
         "middle", 200_000_000,
     )
     second = exchange(outgoing)
-    (base,) = call(
+    base, ghost_flux, ghost_op, scatter = call(
         local_kernel,
-        [VMEM] * 16,
-        [(packed, F32)],
-        [((pairs, sources, LANES), F32)],
+        [VMEM] * (17 + len(first)),
+        [
+            (packed, F32), ((fields * second_shape[0], sides * LANES), F32),
+            ((sides * fast, 2 * LANES, LANES), BF16), ((fields * elements, 2 * LANES), BF16),
+        ],
+        [((pairs, sources, LANES), F32), ((fields, 2 * ROWS * faces, LANES), F32)],
         (
             middle, late_value, star_coef, local_coef, volume_op, trace_op, local_lift,
-            remote_coef, compose_op, remote_lift, choose, mask, *first,
+            remote_coef, compose_op, remote_lift, choose, mask, waiting[1], codes, composed, lift_sides, waiting[4],
+            *first,
         ),
         "local_late", 200_000_000,
     )

time: 22.7 us -> 25.7 us (1.13)
  starting transfers between devices: 12.1 us -> 14.7 us
  waiting for transfers between devices: 1.11 us -> 1.48 us
    ppermute x0 -> x1, starting transfers between devices: none -> 4.85 us  [exchange(): early.append(lax.ppermute(ahead, axis, pairs[0:2]))]
    ppermute x8, starting transfers between devices: 12.1 us -> 9.81 us  [exchange(): arrived.append(lax.ppermute(message, axis, pairs))]
    ppermute x8, waiting for transfers between devices: 1.11 us -> 1.48 us  [exchange(): arrived.append(lax.ppermute(message, axis, pairs))]
  transfers between devices with their start and end apart: 8 -> 9, of which waited for: 3 -> 2; matrix products, arithmetic and copies ran while one was open for 0% -> 0% of each run, Pallas kernels for 14% -> 11%
where the time goes in v9:
time: 25.7 us; the launch traced here: 25.5 us
  starting transfers between devices  14.7 us (57%)
  Pallas kernels  9.32 us (36%)
  waiting for transfers between devices  1.48 us (6%)
    ppermute x8, starting transfers between devices, exchange(): arrived.append(lax.ppermute(message, axis, pairs))  9.81 us
    pallas_call x5, Pallas kernels, call(): pl.pallas_call(kernel, out_shape=shapes, in_specs=ins, out_specs=[VMEM] *...  9.32 us
    ppermute x1, starting transfers between devices, exchange(): early.append(lax.ppermute(ahead, axis, pairs[0:2]))  4.85 us
    ppermute x8, waiting for transfers between devices, exchange(): arrived.append(lax.ppermute(message, axis, pairs))  1.48 us
  transfers between devices with their start and end apart: 9, of which 2 were waited for; matrix products, arithmetic and copies ran while one was open for 0% of the time, Pallas kernels for 11%

profile of v9, /device:TPU:0, one launch (start us, length us, event | category | flops | bytes accessed | tf_op | source)
XLA Modules:
  0.0 25.5 jit_solution(8790944948165150683)
XLA Ops:
  0.0 3.2 %predict.1 = (f32[9,8,128]{2,1,0:T(8,128)S(1)}, f32[9,8,128]{2,1,0:T(8,128)S(1)}, f32[32,128]{1,0:T(8,128)S(1)}, f32[32,128]{1,0:T(8,128)S(1)}, f32[32,128]{1,0:...) custom-call(f32[9,16,56]{2,1,0:T(8,128)} %bitcast.10, ...), custom_call_target="tpu_custom_call" | custom-call | flops 100000000 | bytes 4000000 | tf_op jit(solution)/shard_map/predict/pallas_call | solution.py:600
  3.2 4.8 %collective-permute-start = (f32[32,128]{1,0:T(8,128)S(1)}, f32[32,128]{1,0:T(8,128)S(1)}, u32[]{:S(2)}, u32[]{:S(2)}) collective-permute-start(f32[32,128]{1,0:T(8,128)S(1)} %get-tuple-element.67), channel_id=1, source_target_pairs={{0,4},{4,0},{1,5},{5,1},{2,6},{6,2},{3,7},{7,3}} | collective-permute-start | bytes 49160 | tf_op jit(solution)/shard_map/ppermute | solution.py:622
  8.1 1.9 %collective-permute-start.1 = (f32[32,128]{1,0:T(8,128)S(1)}, f32[32,128]{1,0:T(8,128)S(1)}, u32[]{:S(2)}, u32[]{:S(2)}) collective-permute-start(f32[32,128]{1,0:T(8,128)S(1)} %get-tuple-element.68), channel_id=1, source_target_pairs={{4,8},{8,4},{12,16},{16,12},{20,24},{24,20},{28,0},{0,28},{5,9},{9... | collective-permute-start | bytes 49160 | tf_op jit(solution)/shard_map/ppermute | solution.py:624
  9.9 0.7 %collective-permute-start.2 = (f32[32,128]{1,0:T(8,128)S(1)}, f32[32,128]{1,0:T(8,128)S(1)}, u32[]{:S(2)}, u32[]{:S(2)}) collective-permute-start(f32[32,128]{1,0:T(8,128)S(1)} %get-tuple-element.69), channel_id=1, source_target_pairs={{8,12},{12,8},{16,20},{20,16},{24,28},{28,24},{9,13},{13,9},{17,21... | collective-permute-start | bytes 49160 | tf_op jit(solution)/shard_map/ppermute | solution.py:624
  10.6 0.7 %collective-permute-start.3 = (f32[32,128]{1,0:T(8,128)S(1)}, f32[32,128]{1,0:T(8,128)S(1)}, u32[]{:S(2)}, u32[]{:S(2)}) collective-permute-start(f32[32,128]{1,0:T(8,128)S(1)} %get-tuple-element.70), channel_id=1, source_target_pairs={{1,2},{2,1},{3,0},{0,3},{5,6},{6,5},{7,4},{4,7},{9,10},{10,9},{11,... | collective-permute-start | bytes 49160 | tf_op jit(solution)/shard_map/ppermute | solution.py:624
  11.3 1.0 %collective-permute-start.4 = (f32[32,128]{1,0:T(8,128)S(1)}, f32[32,128]{1,0:T(8,128)S(1)}, u32[]{:S(2)}, u32[]{:S(2)}) collective-permute-start(f32[32,128]{1,0:T(8,128)S(1)} %get-tuple-element.71), channel_id=1, source_target_pairs={{0,1},{1,0},{2,3},{3,2},{4,5},{5,4},{6,7},{7,6},{8,9},{9,8},{10,11... | collective-permute-start | bytes 49160 | tf_op jit(solution)/shard_map/ppermute | solution.py:624
  12.3 1.5 %prepare.1 = (f32[9,8,128]{2,1,0:T(8,128)S(1)}, f32[81,2,8,128]{3,2,1,0:T(8,128)S(1)}, f32[180,16,128]{2,1,0:T(8,128)S(1)}, bf16[384,384]{1,0:T(8,128)(2,1)S(1)}...) custom-call(f32[9,8,128]{2,1,0:T(8,128)S(1)} %get-tuple-element.47.p, ...), custom_call_target="tpu_custom_call" | custom-call | flops 200000000 | bytes 4000000 | tf_op jit(solution)/shard_map/prepare/pallas_call | solution.py:600
  13.8 0.0 collective-permute-done.ahead_1
  13.8 0.8 %collective-permute-done.1.from_0.first_0 = f32[32,128]{1,0:T(8,128)S(1)} collective-permute-done((f32[32,128]{1,0:T(8,128)S(1)}, f32[32,128]{1,0:T(8,128)S(1)}, u32[]{:S(2)}, u32[]{:S(2)}) %collective-permute-start.1) | collective-permute-done | bytes 16416 | tf_op jit(solution)/shard_map/ppermute | solution.py:624
  14.6 0.0 collective-permute-done.2.from_1.first_1
  14.6 0.0 collective-permute-done.3.from_2.first_2
  14.6 0.0 collective-permute-done.4.from_3.first_3
  14.6 2.2 %middle.1 = (f32[9,8,128]{2,1,0:T(8,128)S(1)}, f32[9,8,128]{2,1,0:T(8,128)S(1)}, f32[16,128]{1,0:T(8,128)S(1)}, f32[16,128]{1,0:T(8,128)S(1)}, f32[16,128]{1,0:T(8,128)S(1)}, /*index=5*/f32[16,128]{1,0:T(8,128)S(1)}) custom-call(f32[9,8,128]{2,1,0:T(8,128)S(1)} %get-tuple-element.59.base_ref, f32[9,8,128]{2,1,0:T(8,128)S(1)} %get-tuple-element.48.early_ref, ...), custom_call_target="tpu_custom_call" | custom-call | flops 200000000 | bytes 4000000 | tf_op jit(solution)/shard_map/middle/pallas_call | solution.py:600
  16.8 4.0 %collective-permute-start.5 = (f32[16,128]{1,0:T(8,128)S(1)}, f32[16,128]{1,0:T(8,128)S(1)}, u32[]{:S(2)}, u32[]{:S(2)}) collective-permute-start(f32[16,128]{1,0:T(8,128)S(1)} %get-tuple-element.85), channel_id=1, source_target_pairs={{4,8},{8,4},{12,16},{16,12},{20,24},{24,20},{28,0},{0,28},{5,9},{9... | collective-permute-start | bytes 24584 | tf_op jit(solution)/shard_map/ppermute | solution.py:624
  20.7 0.0 collective-permute-start.6
  20.7 0.0 collective-permute-start.7
  20.7 1.6 %collective-permute-start.8 = (f32[16,128]{1,0:T(8,128)S(1)}, f32[16,128]{1,0:T(8,128)S(1)}, u32[]{:S(2)}, u32[]{:S(2)}) collective-permute-start(f32[16,128]{1,0:T(8,128)S(1)} %get-tuple-element.88), channel_id=1, source_target_pairs={{0,1},{1,0},{2,3},{3,2},{4,5},{5,4},{6,7},{7,6},{8,9},{9,8},{10,11... | collective-permute-start | bytes 24584 | tf_op jit(solution)/shard_map/ppermute | solution.py:624
  22.4 1.3 %local_late.1 = (f32[9,8,128]{2,1,0:T(8,128)S(1)}, f32[144,512]{1,0:T(8,128)S(1)}, bf16[8,256,128]{2,1,0:T(8,128)(2,1)S(1)}, bf16[144,256]{1,0:T(8,128)(2,1)S(1)}) custom-call(f32[9,8,128]{2,1,0:T(8,128)S(1)} %get-tuple-element.72.middle_ref, f32[9,8,128]{2,1,0:T(8,128)S(1)} %get-tuple-element.73.late_ref, f32[243,8,128]{2,1,0:T(8,128)S(1)} %get-tuple-element.50.star_ref, ...), custom_call_target="tpu_custom_call" | custom-call | flops 200000000 | bytes 4000000 | tf_op jit(solution)/shard_map/local_late/pallas_call | solution.py:600
  23.7 0.0 collective-permute-done.5.second_0
  23.7 0.7 %collective-permute-done.6.second_1 = f32[16,128]{1,0:T(8,128)S(1)} collective-permute-done((f32[16,128]{1,0:T(8,128)S(1)}, f32[16,128]{1,0:T(8,128)S(1)}, u32[]{:S(2)}, u32[]{:S(2)}) %collective-permute-start.6) | collective-permute-done | bytes 8224 | tf_op jit(solution)/shard_map/ppermute | solution.py:624
  24.4 0.0 collective-permute-done.7.second_2
  24.4 0.0 collective-permute-done.8.second_3
  24.4 1.1 %final.1 = f32[9,16,56]{2,1,0:T(8,128)} custom-call(f32[9,8,128]{2,1,0:T(8,128)S(1)} %get-tuple-element.81.base_ref, f32[144,512]{1,0:T(8,128)S(1)} %get-tuple-element.82.ghost_flux_ref, bf16[8,256,128]{2,1,0:T(8,128)(2,1)S(1)} %get-tuple-element.83.ghost_operator_ref, bf16[144,256]{1,0:T(8,128)(2,1)S(1)} %get-tuple-element.84.scatter_ref, ...), custom_call_target="tpu_custom_call" | custom-call | flops 200000000 | bytes 4000000 | tf_op jit(solution)/shard_map/final/pallas_call | solution.py:600
Async XLA Ops:
  3.2 10.6 %collective-permute-start = (f32[32,128]{1,0:T(8,128)S(1)}, f32[32,128]{1,0:T(8,128)S(1)}, u32[]{:S(2)}, u32[]{:S(2)}) collective-permute-start(f32[32,128]{1,0:T(8,128)S(1)} %get-tuple-element.67), channel_id=1, source_target_pairs={{0,4},{4,0},{1,5},{5,1},{2,6},{6,2},{3,7},{7,3}} | collective-permute-start | bytes 49160 | tf_op jit(solution)/shard_map/ppermute | solution.py:622
  8.1 6.5 %collective-permute-start.1 = (f32[32,128]{1,0:T(8,128)S(1)}, f32[32,128]{1,0:T(8,128)S(1)}, u32[]{:S(2)}, u32[]{:S(2)}) collective-permute-start(f32[32,128]{1,0:T(8,128)S(1)} %get-tuple-element.68), channel_id=1, source_target_pairs={{4,8},{8,4},{12,16},{16,12},{20,24},{24,20},{28,0},{0,28},{5,9},{9... | collective-permute-start | bytes 49160 | tf_op jit(solution)/shard_map/ppermute | solution.py:624
  9.9 4.6 %collective-permute-start.2 = (f32[32,128]{1,0:T(8,128)S(1)}, f32[32,128]{1,0:T(8,128)S(1)}, u32[]{:S(2)}, u32[]{:S(2)}) collective-permute-start(f32[32,128]{1,0:T(8,128)S(1)} %get-tuple-element.69), channel_id=1, source_target_pairs={{8,12},{12,8},{16,20},{20,16},{24,28},{28,24},{9,13},{13,9},{17,21... | collective-permute-start | bytes 49160 | tf_op jit(solution)/shard_map/ppermute | solution.py:624
  10.6 4.0 %collective-permute-start.3 = (f32[32,128]{1,0:T(8,128)S(1)}, f32[32,128]{1,0:T(8,128)S(1)}, u32[]{:S(2)}, u32[]{:S(2)}) collective-permute-start(f32[32,128]{1,0:T(8,128)S(1)} %get-tuple-element.70), channel_id=1, source_target_pairs={{1,2},{2,1},{3,0},{0,3},{5,6},{6,5},{7,4},{4,7},{9,10},{10,9},{11,... | collective-permute-start | bytes 49160 | tf_op jit(solution)/shard_map/ppermute | solution.py:624
  11.3 3.2 %collective-permute-start.4 = (f32[32,128]{1,0:T(8,128)S(1)}, f32[32,128]{1,0:T(8,128)S(1)}, u32[]{:S(2)}, u32[]{:S(2)}) collective-permute-start(f32[32,128]{1,0:T(8,128)S(1)} %get-tuple-element.71), channel_id=1, source_target_pairs={{0,1},{1,0},{2,3},{3,2},{4,5},{5,4},{6,7},{7,6},{8,9},{9,8},{10,11... | collective-permute-start | bytes 49160 | tf_op jit(solution)/shard_map/ppermute | solution.py:624
  16.8 6.9 %collective-permute-start.5 = (f32[16,128]{1,0:T(8,128)S(1)}, f32[16,128]{1,0:T(8,128)S(1)}, u32[]{:S(2)}, u32[]{:S(2)}) collective-permute-start(f32[16,128]{1,0:T(8,128)S(1)} %get-tuple-element.85), channel_id=1, source_target_pairs={{4,8},{8,4},{12,16},{16,12},{20,24},{24,20},{28,0},{0,28},{5,9},{9... | collective-permute-start | bytes 24584 | tf_op jit(solution)/shard_map/ppermute | solution.py:624
  20.7 3.7 %collective-permute-start.6 = (f32[16,128]{1,0:T(8,128)S(1)}, f32[16,128]{1,0:T(8,128)S(1)}, u32[]{:S(2)}, u32[]{:S(2)}) collective-permute-start(f32[16,128]{1,0:T(8,128)S(1)} %get-tuple-element.86), channel_id=1, source_target_pairs={{0,4},{4,0},{8,12},{12,8},{16,20},{20,16},{24,28},{28,24},{1,5},{5... | collective-permute-start | bytes 24584 | tf_op jit(solution)/shard_map/ppermute | solution.py:624
  20.7 3.7 %collective-permute-start.7 = (f32[16,128]{1,0:T(8,128)S(1)}, f32[16,128]{1,0:T(8,128)S(1)}, u32[]{:S(2)}, u32[]{:S(2)}) collective-permute-start(f32[16,128]{1,0:T(8,128)S(1)} %get-tuple-element.87), channel_id=1, source_target_pairs={{1,2},{2,1},{3,0},{0,3},{5,6},{6,5},{7,4},{4,7},{9,10},{10,9},{11,... | collective-permute-start | bytes 24584 | tf_op jit(solution)/shard_map/ppermute | solution.py:624
  20.7 3.7 %collective-permute-start.8 = (f32[16,128]{1,0:T(8,128)S(1)}, f32[16,128]{1,0:T(8,128)S(1)}, u32[]{:S(2)}, u32[]{:S(2)}) collective-permute-start(f32[16,128]{1,0:T(8,128)S(1)} %get-tuple-element.88), channel_id=1, source_target_pairs={{0,1},{1,0},{2,3},{3,2},{4,5},{5,4},{6,7},{7,6},{8,9},{9,8},{10,11... | collective-permute-start | bytes 24584 | tf_op jit(solution)/shard_map/ppermute | solution.py:624

commit v10 on v8

--- a/solution.py
+++ b/solution.py
@@ -121,13 +121,17 @@
 
 
 def star_mix(columns, star_ref, fields, kinds):
-    sums = [None] * fields
-    for row in range(fields):
+    sums = []
+    for col in range(fields):
+        parts = []
         for kind in range(kinds):
-            part = columns[row * ROWS : (row + 1) * ROWS, kind * LANES : (kind + 1) * LANES]
-            for col in range(fields):
+            total = None
+            for row in range(fields):
+                part = columns[row * ROWS : (row + 1) * ROWS, kind * LANES : (kind + 1) * LANES]
                 term = star_ref[(row * kinds + kind) * fields + col] * part
-                sums[col] = term if sums[col] is None else sums[col] + term
+                total = term if total is None else total + term
+            parts.append(total)
+        sums.append(sum(parts[1:], parts[0]))
     return jnp.concatenate(sums, axis=0)
 
 
@@ -279,6 +283,12 @@
     return volume + product(stack_left(jnp.concatenate(sums, axis=0)), lift_ref[...])
 
 
+def combo_code(lanes, turns, face_modes):
+    in_face = lanes % HALF
+    code = jnp.where(in_face < turns * face_modes, (lanes // HALF) * turns + in_face // face_modes, -1)
+    return code.astype(F32)
+
+
 def ghost_terms(
     flux_ref, stage_ref, code_ref, composed, lift_sides, lane_code, flux_out, operator_out, scatter_out, sends, fields
 ):
@@ -346,8 +356,8 @@
     packed_ref, early_ref, stiffness_ref, star_ref, flux_local_ref, flux_remote_ref, restrict_ref, lift_ref, orient_ref,
     slot_ref, face_ref, turn_ref,
     base_out, local_out, remote_out, volume_out, trace_out, local_lift_out, compose_out,
-    remote_lift_out, choose_out, mask_out, ghost_flux_out, ghost_operator_out, scatter_out,
-    sides_ref, local_work_ref, remote_work_ref, block_ref, wide_ref, face_work_ref, orient_work_ref, code_ref,
+    remote_lift_out, choose_out, mask_out, code_ref, composed_out, sides_ref,
+    local_work_ref, remote_work_ref, block_ref, wide_ref, face_work_ref, orient_work_ref, code_work_ref,
 ):
     fields, kinds = packed_ref.shape[0], stiffness_ref.shape[0]
     face_modes, faces, modes = restrict_ref.shape
@@ -391,22 +401,21 @@
     remote_lift_out[...] = stack_right(wide_ref[...])
 
     elements = slot_ref.shape[1]
-    code_ref[...] = jnp.zeros(code_ref.shape, F32)
+    code_work_ref[...] = jnp.zeros(code_work_ref.shape, F32)
     slots = slot_ref[...]
     sends = (choose_out.shape[1] // 2 - elements) // 4
     group = (slots - elements) // sends
     moved = slots
     for side in range(4):
         moved = jnp.where(group == side, slots + (ghost_slot(side) - side) * sends, moved)
-    code_ref[0:faces, 0:elements] = jnp.where(slots < elements, slots, moved).astype(F32)
-    code_ref[faces : 2 * faces, 0:elements] = (face_ref[...] * turns + turn_ref[...]).astype(F32)
-    codes = code_ref[...].T[0:elements, :]
+    code_work_ref[0:faces, 0:elements] = jnp.where(slots < elements, slots, moved).astype(F32)
+    code_work_ref[faces : 2 * faces, 0:elements] = (face_ref[...] * turns + turn_ref[...]).astype(F32)
+    code_ref[...] = code_work_ref[0 : 2 * faces, :]
+    codes = code_work_ref[...].T[0:elements, :]
     sources = choose_out.shape[1] // 2
     source_lane = (lane_index((elements, 2 * sources)) % sources).astype(F32)
     lanes = lane_index((elements, mask_out.shape[1]))
-    in_face = lanes % HALF
-    lane_code = jnp.where(in_face < turns * face_modes, (lanes // HALF) * turns + in_face // face_modes, -1)
-    lane_code = lane_code.astype(F32)
+    lane_code = combo_code(lanes, turns, face_modes)
     picks, masks = [], []
     for face in range(faces):
         picks.append(jnp.where(codes[:, face : face + 1] == source_lane, 1.0, 0.0))
@@ -419,10 +428,7 @@
         for turn in range(turns):
             rows = slice(turn * face_modes, (turn + 1) * face_modes)
             sides_ref[rows, face * HALF : face * HALF + modes] = -lift_ref[:, face, :]
-    ghost_terms(
-        flux_remote_ref, local_work_ref, code_ref, stacked.T[0:HALF], sides_ref[...], lane_code[0:1],
-        ghost_flux_out, ghost_operator_out, scatter_out, sends, fields,
-    )
+    composed_out[...] = stacked.T[0:HALF]
 
     early = early_ref[...].reshape(fields * ROWS, LANES)
     terms = local_terms(early, star_ref, local_out, volume_out, trace_out, local_lift_out, fields, kinds)
@@ -522,8 +528,9 @@
 
 def local_kernel(
     middle_ref, late_ref, star_ref, flux_ref, volume_ref, trace_ref, lift_ref,
-    remote_ref, compose_ref, remote_lift_ref, choose_ref, mask_ref, first_0, first_1, first_2, first_3,
-    base_out, rows_ref,
+    remote_ref, compose_ref, remote_lift_ref, choose_ref, mask_ref, flux_remote_ref, code_ref, composed_ref, sides_ref,
+    orient_ref, first_0, first_1, first_2, first_3,
+    base_out, ghost_flux_out, ghost_operator_out, scatter_out, rows_ref, stage_ref,
 ):
     fields = middle_ref.shape[0]
     kinds = star_ref.shape[0] // (fields * fields)
@@ -542,6 +549,11 @@
     terms = local_terms(late, star_ref, flux_ref, volume_ref, trace_ref, lift_ref, fields, kinds)
     remote = remote_terms(rows_ref, remote_ref, compose_ref, remote_lift_ref, choose_ref, mask_ref, fields)
     base_out[...] = middle_ref[...] + terms.reshape(fields, ROWS, LANES) + remote
+    lane_code = combo_code(lane_index((1, composed_ref.shape[1])), orient_ref.shape[0], orient_ref.shape[1])
+    ghost_terms(
+        flux_remote_ref, stage_ref, code_ref, composed_ref[...], sides_ref[...], lane_code,
+        ghost_flux_out, ghost_operator_out, scatter_out, sends, fields,
+    )
 
 
 def final_kernel(
@@ -655,7 +667,7 @@
     first = exchange(outgoing)
     (
         base, local_coef, remote_coef, volume_op, trace_op, local_lift, compose_op, remote_lift, choose, mask,
-        ghost_flux, ghost_op, scatter,
+        codes, composed, lift_sides,
     ) = call(
         prepare_kernel,
         [VMEM] * 12,
@@ -665,11 +677,10 @@
             ((3 * LANES, kinds * LANES), BF16), ((3 * LANES, 2 * LANES), BF16),
             ((6 * LANES, LANES), BF16), ((2 * LANES, combos), BF16), ((3 * faces * HALF, LANES), BF16),
             ((faces * elements, 2 * sources), BF16), ((faces * elements, combos), F32),
-            ((fields * second_shape[0], sides * LANES), F32), ((sides * fast, 2 * LANES, LANES), BF16),
-            ((fields * elements, 2 * LANES), BF16),
+            ((2 * faces, LANES), F32), ((HALF, combos), F32), ((HALF, faces * HALF), F32),
         ],
         [
-            ((HALF, faces * HALF), F32), ((fields, 2 * ROWS * faces, LANES), F32), ((pairs, 2 * up_to(4 * fields, ROWS), LANES), F32),
+            ((fields, 2 * ROWS * faces, LANES), F32), ((pairs, 2 * up_to(4 * fields, ROWS), LANES), F32),
             ((kinds, LANES, LANES), F32), ((2 * LANES, LANES), F32),
             ((LANES, faces * LANES), F32), ((HALF, LANES), F32), ((LANES, LANES), F32),
         ],
@@ -692,14 +703,18 @@
         "middle", 200_000_000,
     )
     second = exchange(outgoing)
-    (base,) = call(
+    base, ghost_flux, ghost_op, scatter = call(
         local_kernel,
-        [VMEM] * 16,
-        [(packed, F32)],
-        [((pairs, sources, LANES), F32)],
+        [VMEM] * (17 + len(first)),
+        [
+            (packed, F32), ((fields * second_shape[0], sides * LANES), F32),
+            ((sides * fast, 2 * LANES, LANES), BF16), ((fields * elements, 2 * LANES), BF16),
+        ],
+        [((pairs, sources, LANES), F32), ((fields, 2 * ROWS * faces, LANES), F32)],
         (
             middle, late_value, star_coef, local_coef, volume_op, trace_op, local_lift,
-            remote_coef, compose_op, remote_lift, choose, mask, *first,
+            remote_coef, compose_op, remote_lift, choose, mask, waiting[1], codes, composed, lift_sides, waiting[4],
+            *first,
         ),
         "local_late", 200_000_000,
     )

time: 22.7 us -> 22.6 us (level)
  Pallas kernels: 9.32 us -> 8.93 us
  waiting for transfers between devices: 1.11 us -> 1.4 us
    pallas_call x5, Pallas kernels: 9.32 us -> 8.93 us  [call(): pl.pallas_call(kernel, out_shape=shapes, in_specs=ins, out_specs=[VMEM] *...]
    ppermute x8, waiting for transfers between devices: 1.11 us -> 1.4 us  [exchange(): arrived.append(lax.ppermute(message, axis, pairs))]
  transfers between devices with their start and end apart: 8 -> 8, of which waited for: 3 -> 3; matrix products, arithmetic and copies ran while one was open for 0% -> 0% of each run, Pallas kernels for 14% -> 12%
where the time goes in v10:
time: 22.6 us; the launch traced here: 22.5 us
  starting transfers between devices  12.1 us (54%)
  Pallas kernels  8.93 us (40%)
  waiting for transfers between devices  1.4 us (6%)
    ppermute x8, starting transfers between devices, exchange(): arrived.append(lax.ppermute(message, axis, pairs))  12.1 us
    pallas_call x5, Pallas kernels, call(): pl.pallas_call(kernel, out_shape=shapes, in_specs=ins, out_specs=[VMEM] *...  8.93 us
    ppermute x8, waiting for transfers between devices, exchange(): arrived.append(lax.ppermute(message, axis, pairs))  1.4 us
  transfers between devices with their start and end apart: 8, of which 3 were waited for; matrix products, arithmetic and copies ran while one was open for 0% of the time, Pallas kernels for 12%

profile of v10, /device:TPU:0, one launch (start us, length us, event | category | flops | bytes accessed | tf_op | source)
XLA Modules:
  0.0 22.5 jit_solution(57990743882486794)
XLA Ops:
  0.0 2.9 %predict.1 = (f32[9,8,128]{2,1,0:T(8,128)S(1)}, f32[9,8,128]{2,1,0:T(8,128)S(1)}, f32[32,128]{1,0:T(8,128)S(1)}, f32[32,128]{1,0:T(8,128)S(1)}, f32[32,128]{1,0:...) custom-call(f32[9,16,56]{2,1,0:T(8,128)} %bitcast.10, ...), custom_call_target="tpu_custom_call" | custom-call | flops 100000000 | bytes 4000000 | tf_op jit(solution)/shard_map/predict/pallas_call | solution.py:594
  2.9 6.0 %collective-permute-start = (f32[32,128]{1,0:T(8,128)S(1)}, f32[32,128]{1,0:T(8,128)S(1)}, u32[]{:S(2)}, u32[]{:S(2)}) collective-permute-start(f32[32,128]{1,0:T(8,128)S(1)} %get-tuple-element.66), channel_id=1, source_target_pairs={{4,8},{8,4},{12,16},{16,12},{20,24},{24,20},{28,0},{0,28},{5,9},{9... | collective-permute-start | bytes 49160 | tf_op jit(solution)/shard_map/ppermute | solution.py:615
  8.9 0.0 collective-permute-start.1
  8.9 0.7 %collective-permute-start.2 = (f32[32,128]{1,0:T(8,128)S(1)}, f32[32,128]{1,0:T(8,128)S(1)}, u32[]{:S(2)}, u32[]{:S(2)}) collective-permute-start(f32[32,128]{1,0:T(8,128)S(1)} %get-tuple-element.68), channel_id=1, source_target_pairs={{1,2},{2,1},{3,0},{0,3},{5,6},{6,5},{7,4},{4,7},{9,10},{10,9},{11,... | collective-permute-start | bytes 49160 | tf_op jit(solution)/shard_map/ppermute | solution.py:615
  9.6 1.0 %collective-permute-start.3 = (f32[32,128]{1,0:T(8,128)S(1)}, f32[32,128]{1,0:T(8,128)S(1)}, u32[]{:S(2)}, u32[]{:S(2)}) collective-permute-start(f32[32,128]{1,0:T(8,128)S(1)} %get-tuple-element.69), channel_id=1, source_target_pairs={{0,1},{1,0},{2,3},{3,2},{4,5},{5,4},{6,7},{7,6},{8,9},{9,8},{10,11... | collective-permute-start | bytes 49160 | tf_op jit(solution)/shard_map/ppermute | solution.py:615
  10.6 1.5 %prepare.1 = (f32[9,8,128]{2,1,0:T(8,128)S(1)}, f32[81,2,8,128]{3,2,1,0:T(8,128)S(1)}, f32[180,16,128]{2,1,0:T(8,128)S(1)}, bf16[384,384]{1,0:T(8,128)(2,1)S(1)}...) custom-call(f32[9,8,128]{2,1,0:T(8,128)S(1)} %get-tuple-element.46.p, ...), custom_call_target="tpu_custom_call" | custom-call | flops 200000000 | bytes 4000000 | tf_op jit(solution)/shard_map/prepare/pallas_call | solution.py:594
  12.0 0.0 collective-permute-done.from_0.first_0
  12.1 0.6 %collective-permute-done.1.from_1.first_1 = f32[32,128]{1,0:T(8,128)S(1)} collective-permute-done((f32[32,128]{1,0:T(8,128)S(1)}, f32[32,128]{1,0:T(8,128)S(1)}, u32[]{:S(2)}, u32[]{:S(2)}) %collective-permute-start.1) | collective-permute-done | bytes 16416 | tf_op jit(solution)/shard_map/ppermute | solution.py:615
  12.7 0.0 collective-permute-done.2.from_2.first_2
  12.7 0.0 collective-permute-done.3.from_3.first_3
  12.7 2.1 %middle.1 = (f32[9,8,128]{2,1,0:T(8,128)S(1)}, f32[9,8,128]{2,1,0:T(8,128)S(1)}, f32[16,128]{1,0:T(8,128)S(1)}, f32[16,128]{1,0:T(8,128)S(1)}, f32[16,128]{1,0:T(8,128)S(1)}, /*index=5*/f32[16,128]{1,0:T(8,128)S(1)}) custom-call(f32[9,8,128]{2,1,0:T(8,128)S(1)} %get-tuple-element.58.base_ref, f32[9,8,128]{2,1,0:T(8,128)S(1)} %get-tuple-element.47.early_ref, ...), custom_call_target="tpu_custom_call" | custom-call | flops 200000000 | bytes 4000000 | tf_op jit(solution)/shard_map/middle/pallas_call | solution.py:594
  14.8 2.8 %collective-permute-start.4 = (f32[16,128]{1,0:T(8,128)S(1)}, f32[16,128]{1,0:T(8,128)S(1)}, u32[]{:S(2)}, u32[]{:S(2)}) collective-permute-start(f32[16,128]{1,0:T(8,128)S(1)} %get-tuple-element.83), channel_id=1, source_target_pairs={{4,8},{8,4},{12,16},{16,12},{20,24},{24,20},{28,0},{0,28},{5,9},{9... | collective-permute-start | bytes 24584 | tf_op jit(solution)/shard_map/ppermute | solution.py:615
  17.6 0.0 collective-permute-start.5
  17.6 0.0 collective-permute-start.6
  17.6 1.6 %collective-permute-start.7 = (f32[16,128]{1,0:T(8,128)S(1)}, f32[16,128]{1,0:T(8,128)S(1)}, u32[]{:S(2)}, u32[]{:S(2)}) collective-permute-start(f32[16,128]{1,0:T(8,128)S(1)} %get-tuple-element.86), channel_id=1, source_target_pairs={{0,1},{1,0},{2,3},{3,2},{4,5},{5,4},{6,7},{7,6},{8,9},{9,8},{10,11... | collective-permute-start | bytes 24584 | tf_op jit(solution)/shard_map/ppermute | solution.py:615
  19.2 1.3 %local_late.1 = (f32[9,8,128]{2,1,0:T(8,128)S(1)}, f32[144,512]{1,0:T(8,128)S(1)}, bf16[8,256,128]{2,1,0:T(8,128)(2,1)S(1)}, bf16[144,256]{1,0:T(8,128)(2,1)S(1)}) custom-call(f32[9,8,128]{2,1,0:T(8,128)S(1)} %get-tuple-element.70.middle_ref, f32[9,8,128]{2,1,0:T(8,128)S(1)} %get-tuple-element.71.late_ref, f32[243,8,128]{2,1,0:T(8,128)S(1)} %get-tuple-element.49.star_ref, ...), custom_call_target="tpu_custom_call" | custom-call | flops 200000000 | bytes 4000000 | tf_op jit(solution)/shard_map/local_late/pallas_call | solution.py:594
  20.5 0.7 %collective-permute-done.4.second_0 = f32[16,128]{1,0:T(8,128)S(1)} collective-permute-done((f32[16,128]{1,0:T(8,128)S(1)}, f32[16,128]{1,0:T(8,128)S(1)}, u32[]{:S(2)}, u32[]{:S(2)}) %collective-permute-start.4) | collective-permute-done | bytes 8224 | tf_op jit(solution)/shard_map/ppermute | solution.py:615
  21.2 0.1 collective-permute-done.5.second_1
  21.3 0.0 collective-permute-done.6.second_2
  21.3 0.0 collective-permute-done.7.second_3
  21.3 1.1 %final.1 = f32[9,16,56]{2,1,0:T(8,128)} custom-call(f32[9,8,128]{2,1,0:T(8,128)S(1)} %get-tuple-element.79.base_ref, f32[144,512]{1,0:T(8,128)S(1)} %get-tuple-element.80.ghost_flux_ref, bf16[8,256,128]{2,1,0:T(8,128)(2,1)S(1)} %get-tuple-element.81.ghost_operator_ref, bf16[144,256]{1,0:T(8,128)(2,1)S(1)} %get-tuple-element.82.scatter_ref, ...), custom_call_target="tpu_custom_call" | custom-call | flops 200000000 | bytes 4000000 | tf_op jit(solution)/shard_map/final/pallas_call | solution.py:594
Async XLA Ops:
  2.9 9.2 %collective-permute-start = (f32[32,128]{1,0:T(8,128)S(1)}, f32[32,128]{1,0:T(8,128)S(1)}, u32[]{:S(2)}, u32[]{:S(2)}) collective-permute-start(f32[32,128]{1,0:T(8,128)S(1)} %get-tuple-element.66), channel_id=1, source_target_pairs={{4,8},{8,4},{12,16},{16,12},{20,24},{24,20},{28,0},{0,28},{5,9},{9... | collective-permute-start | bytes 49160 | tf_op jit(solution)/shard_map/ppermute | solution.py:615
  8.9 3.7 %collective-permute-start.1 = (f32[32,128]{1,0:T(8,128)S(1)}, f32[32,128]{1,0:T(8,128)S(1)}, u32[]{:S(2)}, u32[]{:S(2)}) collective-permute-start(f32[32,128]{1,0:T(8,128)S(1)} %get-tuple-element.67), channel_id=1, source_target_pairs={{0,4},{4,0},{8,12},{12,8},{16,20},{20,16},{24,28},{28,24},{1,5},{5... | collective-permute-start | bytes 49160 | tf_op jit(solution)/shard_map/ppermute | solution.py:615
  8.9 3.7 %collective-permute-start.2 = (f32[32,128]{1,0:T(8,128)S(1)}, f32[32,128]{1,0:T(8,128)S(1)}, u32[]{:S(2)}, u32[]{:S(2)}) collective-permute-start(f32[32,128]{1,0:T(8,128)S(1)} %get-tuple-element.68), channel_id=1, source_target_pairs={{1,2},{2,1},{3,0},{0,3},{5,6},{6,5},{7,4},{4,7},{9,10},{10,9},{11,... | collective-permute-start | bytes 49160 | tf_op jit(solution)/shard_map/ppermute | solution.py:615
  9.6 3.1 %collective-permute-start.3 = (f32[32,128]{1,0:T(8,128)S(1)}, f32[32,128]{1,0:T(8,128)S(1)}, u32[]{:S(2)}, u32[]{:S(2)}) collective-permute-start(f32[32,128]{1,0:T(8,128)S(1)} %get-tuple-element.69), channel_id=1, source_target_pairs={{0,1},{1,0},{2,3},{3,2},{4,5},{5,4},{6,7},{7,6},{8,9},{9,8},{10,11... | collective-permute-start | bytes 49160 | tf_op jit(solution)/shard_map/ppermute | solution.py:615
  14.8 6.4 %collective-permute-start.4 = (f32[16,128]{1,0:T(8,128)S(1)}, f32[16,128]{1,0:T(8,128)S(1)}, u32[]{:S(2)}, u32[]{:S(2)}) collective-permute-start(f32[16,128]{1,0:T(8,128)S(1)} %get-tuple-element.83), channel_id=1, source_target_pairs={{4,8},{8,4},{12,16},{16,12},{20,24},{24,20},{28,0},{0,28},{5,9},{9... | collective-permute-start | bytes 24584 | tf_op jit(solution)/shard_map/ppermute | solution.py:615
  17.6 3.7 %collective-permute-start.5 = (f32[16,128]{1,0:T(8,128)S(1)}, f32[16,128]{1,0:T(8,128)S(1)}, u32[]{:S(2)}, u32[]{:S(2)}) collective-permute-start(f32[16,128]{1,0:T(8,128)S(1)} %get-tuple-element.84), channel_id=1, source_target_pairs={{0,4},{4,0},{8,12},{12,8},{16,20},{20,16},{24,28},{28,24},{1,5},{5... | collective-permute-start | bytes 24584 | tf_op jit(solution)/shard_map/ppermute | solution.py:615
  17.6 3.7 %collective-permute-start.6 = (f32[16,128]{1,0:T(8,128)S(1)}, f32[16,128]{1,0:T(8,128)S(1)}, u32[]{:S(2)}, u32[]{:S(2)}) collective-permute-start(f32[16,128]{1,0:T(8,128)S(1)} %get-tuple-element.85), channel_id=1, source_target_pairs={{1,2},{2,1},{3,0},{0,3},{5,6},{6,5},{7,4},{4,7},{9,10},{10,9},{11,... | collective-permute-start | bytes 24584 | tf_op jit(solution)/shard_map/ppermute | solution.py:615
  17.6 3.7 %collective-permute-start.7 = (f32[16,128]{1,0:T(8,128)S(1)}, f32[16,128]{1,0:T(8,128)S(1)}, u32[]{:S(2)}, u32[]{:S(2)}) collective-permute-start(f32[16,128]{1,0:T(8,128)S(1)} %get-tuple-element.86), channel_id=1, source_target_pairs={{0,1},{1,0},{2,3},{3,2},{4,5},{5,4},{6,7},{7,6},{8,9},{9,8},{10,11... | collective-permute-start | bytes 24584 | tf_op jit(solution)/shard_map/ppermute | solution.py:615

commit v11 on v10

--- a/solution.py
+++ b/solution.py
@@ -13,9 +13,9 @@
 ROWS = 8
 F32 = jnp.float32
 BF16 = jnp.bfloat16
-LATER = ("flux_local", "flux_remote", "face_restrict", "face_lift", "orient_maps", "slot", "face", "turn")
+LATER = ("flux_local", "flux_remote", "face_restrict", "face_lift", "orient_maps", "slot", "face", "turn", "rate")
 AXES = ("dom", "sub")
-SWAPS = (("dom", True), ("dom", False), ("sub", True), ("sub", False))
+SWAPS = (("dom", True), ("dom", False), ("sub", False), ("sub", True))
 
 
 def taylor_weight(lower, upper, degree):
@@ -150,9 +150,9 @@
     solution_hbm, stiffness_hbm, star_hbm, send_hbm = refs[0:4]
     later_hbm, refs = refs[4 : 4 + later], refs[4 + later :]
     early_out, late_out, send_0, send_1, send_2, send_3 = refs[0:6]
-    packed_ref, coef_ref, derive_ref, stiffness_ref = refs[6:10]
-    later_out, refs = refs[10 : 10 + later], refs[10 + later :]
-    work_ref, early_rows, late_rows, solution_ref, block_ref, star_ref, send_ref, sems = refs
+    packed_ref, coef_ref, derive_ref, stiffness_ref, early_rows = refs[6:11]
+    later_out, refs = refs[11 : 11 + later], refs[11 + later :]
+    work_ref, late_rows, solution_ref, block_ref, star_ref, send_ref, sems = refs
 
     sources = (star_hbm, stiffness_hbm, solution_hbm, send_hbm, *later_hbm)
     targets = (star_ref, stiffness_ref, solution_ref, send_ref, *later_out)
@@ -179,7 +179,8 @@
         return current, early, late
 
     _, early, late = lax.fori_loop(
-        1, DERIVS, step, (start, taylor_weight(0.0, 0.5, 0) * start, taylor_weight(0.5, 1.0, 0) * start)
+        1, DERIVS, step, (start, taylor_weight(0.0, 0.5, 0) * start, taylor_weight(0.5, 1.0, 0) * start),
+        unroll=True,
     )
     early_out[...] = early.reshape(fields, ROWS, LANES)
     late_out[...] = late.reshape(fields, ROWS, LANES)
@@ -354,9 +355,9 @@
 
 def prepare_kernel(
     packed_ref, early_ref, stiffness_ref, star_ref, flux_local_ref, flux_remote_ref, restrict_ref, lift_ref, orient_ref,
-    slot_ref, face_ref, turn_ref,
+    slot_ref, face_ref, turn_ref, rate_ref,
     base_out, local_out, remote_out, volume_out, trace_out, local_lift_out, compose_out,
-    remote_lift_out, choose_out, mask_out, code_ref, composed_out, sides_ref,
+    remote_lift_out, choose_out, mask_out, code_ref, composed_out, sides_ref, fast_out,
     local_work_ref, remote_work_ref, block_ref, wide_ref, face_work_ref, orient_work_ref, code_work_ref,
 ):
     fields, kinds = packed_ref.shape[0], stiffness_ref.shape[0]
@@ -410,8 +411,11 @@
         moved = jnp.where(group == side, slots + (ghost_slot(side) - side) * sends, moved)
     code_work_ref[0:faces, 0:elements] = jnp.where(slots < elements, slots, moved).astype(F32)
     code_work_ref[faces : 2 * faces, 0:elements] = (face_ref[...] * turns + turn_ref[...]).astype(F32)
+    code_work_ref[2 * faces : 2 * faces + 1, 0:elements] = rate_ref[...].astype(F32)
     code_ref[...] = code_work_ref[0 : 2 * faces, :]
     codes = code_work_ref[...].T[0:elements, :]
+    rates = codes[:, 2 * faces : 2 * faces + 1]
+    fast_out[...] = jnp.where(lower_half((ROWS, LANES)), rates[0:ROWS], rates[ROWS : 2 * ROWS])
     sources = choose_out.shape[1] // 2
     source_lane = (lane_index((elements, 2 * sources)) % sources).astype(F32)
     lanes = lane_index((elements, mask_out.shape[1]))
@@ -435,11 +439,11 @@
     base_out[...] = packed_ref[...] + terms.reshape(fields, ROWS, LANES)
 
 
-def remote_terms(rows_ref, remote_ref, compose_ref, lift_ref, choose_ref, mask_ref, fields):
-    pairs = rows_ref.shape[0]
+def remote_terms(rows, remote_ref, compose_ref, lift_ref, choose_ref, mask_ref, fields):
+    pairs = len(rows)
     faces = lift_ref.shape[0] // (3 * HALF)
     elements = choose_ref.shape[0] // faces
-    sources = jnp.concatenate([rows_ref[pair] for pair in range(pairs)], axis=1)
+    sources = jnp.concatenate(rows, axis=1)
     gathered = product(choose_ref[...], jnp.concatenate(split(sources), axis=0))
     folded = []
     for face in range(faces):
@@ -467,31 +471,23 @@
 
 
 def middle_kernel(
-    base_ref, early_ref, late_ref, star_ref, remote_ref, derive_ref, compose_ref, lift_ref, choose_ref, mask_ref,
-    rate_hbm, send_hbm, from_0, from_1, from_2, from_3,
+    base_ref, early_rows, late_ref, star_ref, remote_ref, derive_ref, compose_ref, lift_ref, choose_ref, mask_ref,
+    fast_ref, send_hbm, from_0, from_1, from_2, from_3,
     middle_out, late_out, send_0, send_1, send_2, send_3,
-    rows_ref, late_rows, rate_ref, send_ref, sems,
+    rows_ref, late_rows, send_ref, sem,
 ):
-    copies = [
-        pltpu.make_async_copy(rate_hbm, rate_ref, sems.at[0]),
-        pltpu.make_async_copy(send_hbm, send_ref, sems.at[1]),
-    ]
-    for copy in copies:
-        copy.start()
+    copy = pltpu.make_async_copy(send_hbm, send_ref, sem)
+    copy.start()
     fields = base_ref.shape[0]
     kinds = star_ref.shape[0] // (fields * fields)
     pairs = rows_ref.shape[0]
     sends = send_ref.shape[2]
     fast = sends // 2
-    elements = 2 * ROWS
-    rows_by_pair(early_ref[...].reshape(fields * ROWS, LANES), rows_ref, fields)
     for side, arrived in enumerate((from_0, from_1, from_2, from_3)):
-        at = elements + side * sends
         for pair in range(pairs):
-            rows_ref[pair, at : at + sends, :] = arrived[pair * sends : (pair + 1) * sends, :]
-    middle = base_ref[...] + remote_terms(
-        rows_ref, remote_ref, compose_ref, lift_ref, choose_ref, mask_ref, fields
-    )
+            rows_ref[pair, side * sends : (side + 1) * sends, :] = arrived[pair * sends : (pair + 1) * sends, :]
+    rows = [jnp.concatenate([early_rows[pair], rows_ref[pair]], axis=0) for pair in range(pairs)]
+    middle = base_ref[...] + remote_terms(rows, remote_ref, compose_ref, lift_ref, choose_ref, mask_ref, fields)
     middle_out[...] = middle
     start = middle.reshape(fields * ROWS, LANES)
 
@@ -500,15 +496,9 @@
         current = star_mix(product(stack_left(current), derive_ref[...]), star_ref, fields, kinds)
         return current, early + weight_at(0.0, 0.5, degree) * current
 
-    _, restart = lax.fori_loop(1, DERIVS, step, (start, taylor_weight(0.0, 0.5, 0) * start))
-    for copy in copies:
-        copy.wait()
-    sublane = lax.broadcasted_iota(jnp.int32, (ROWS, LANES), 0)
-    lower = lower_half((ROWS, LANES))
-    is_fast = jnp.zeros((ROWS, LANES), jnp.int32)
-    for element in range(elements):
-        here = (sublane == element % ROWS) & (lower if element < ROWS else jnp.logical_not(lower))
-        is_fast = jnp.where(here, rate_ref[element], is_fast)
+    _, restart = lax.fori_loop(1, DERIVS, step, (start, taylor_weight(0.0, 0.5, 0) * start), unroll=True)
+    copy.wait()
+    is_fast = fast_ref[...]
     late = jnp.where((is_fast == 2)[None], restart.reshape(fields, ROWS, LANES), late_ref[...])
     late_out[...] = late
     both = late.reshape(fields * ROWS, LANES)
@@ -547,7 +537,8 @@
             row = pairs * sends + pair * fast
             rows_ref[pair, at + fast : at + sends, :] = first[row : row + fast, :]
     terms = local_terms(late, star_ref, flux_ref, volume_ref, trace_ref, lift_ref, fields, kinds)
-    remote = remote_terms(rows_ref, remote_ref, compose_ref, remote_lift_ref, choose_ref, mask_ref, fields)
+    rows = [rows_ref[pair] for pair in range(pairs)]
+    remote = remote_terms(rows, remote_ref, compose_ref, remote_lift_ref, choose_ref, mask_ref, fields)
     base_out[...] = middle_ref[...] + terms.reshape(fields, ROWS, LANES) + remote
     lane_code = combo_code(lane_index((1, composed_ref.shape[1])), orient_ref.shape[0], orient_ref.shape[1])
     ghost_terms(
@@ -645,16 +636,20 @@
     combos = faces * HALF
     sources = elements + sides * sends
 
-    waiting = (local_part, remote_part, restrict, lift, orient_maps, neighbour_slot, neighbour_face, neighbour_turn)
+    waiting = (
+        local_part, remote_part, restrict, lift, orient_maps, neighbour_slot, neighbour_face, neighbour_turn,
+        cluster_rate.reshape(1, elements),
+    )
     made = call(
         predict_kernel,
         [HBM] * (4 + len(LATER)),
         [(packed, F32)] * 2 + [(first_shape, F32)] * sides + [
             (packed, F32), (star_shape, F32), ((3 * LANES, kinds * LANES), BF16), (stiffness.shape, F32),
+            ((pairs, elements, LANES), F32),
         ] + [(array.shape, array.dtype) for array in waiting],
         [
             ((fields, up_to(4 * fields, ROWS), LANES), F32),
-            ((pairs, elements, LANES), F32), ((pairs, elements, LANES), F32),
+            ((pairs, elements, LANES), F32),
             (values.shape, F32), ((kinds, LANES, LANES), F32), (star.shape, F32),
             pltpu.SMEM(send_list.shape, jnp.int32), pltpu.SemaphoreType.DMA((4 + len(LATER),)),
         ],
@@ -662,15 +657,15 @@
         "predict", 100_000_000,
     )
     early, late, outgoing = made[0], made[1], made[2 : 2 + sides]
-    start, star_coef, derive_op, stiffness_kept = made[2 + sides : 6 + sides]
-    waiting = made[6 + sides :]
+    start, star_coef, derive_op, stiffness_kept, early_rows = made[2 + sides : 7 + sides]
+    waiting = made[7 + sides :]
     first = exchange(outgoing)
     (
         base, local_coef, remote_coef, volume_op, trace_op, local_lift, compose_op, remote_lift, choose, mask,
-        codes, composed, lift_sides,
+        codes, composed, lift_sides, fast_mask,
     ) = call(
         prepare_kernel,
-        [VMEM] * 12,
+        [VMEM] * 13,
         [
             (packed, F32), ((fields * fields, 2, ROWS, LANES), F32),
             ((faces * pairs * fields, elements, LANES), F32),
@@ -678,6 +673,7 @@
             ((6 * LANES, LANES), BF16), ((2 * LANES, combos), BF16), ((3 * faces * HALF, LANES), BF16),
             ((faces * elements, 2 * sources), BF16), ((faces * elements, combos), F32),
             ((2 * faces, LANES), F32), ((HALF, combos), F32), ((HALF, faces * HALF), F32),
+            ((ROWS, LANES), F32),
         ],
         [
             ((fields, 2 * ROWS * faces, LANES), F32), ((pairs, 2 * up_to(4 * fields, ROWS), LANES), F32),
@@ -689,16 +685,15 @@
     )
     middle, late_value, *outgoing = call(
         middle_kernel,
-        [VMEM] * 10 + [HBM] * 2 + [VMEM] * 4,
+        [VMEM] * 11 + [HBM] + [VMEM] * 4,
         [(packed, F32)] * 2 + [(second_shape, F32)] * sides,
         [
-            ((pairs, sources, LANES), F32), ((fields, elements, LANES), F32),
-            pltpu.SMEM(cluster_rate.shape, jnp.int32), pltpu.SMEM(send_list.shape, jnp.int32),
-            pltpu.SemaphoreType.DMA((2,)),
+            ((pairs, sides * sends, LANES), F32), ((fields, elements, LANES), F32),
+            pltpu.SMEM(send_list.shape, jnp.int32), pltpu.SemaphoreType.DMA,
         ],
         (
-            base, early, late, star_coef, remote_coef, derive_op, compose_op, remote_lift, choose, mask,
-            cluster_rate, send_list, *first,
+            base, early_rows, late, star_coef, remote_coef, derive_op, compose_op, remote_lift, choose, mask,
+            fast_mask, send_list, *first,
         ),
         "middle", 200_000_000,
     )

time: 22.6 us -> 22.7 us (level)
  no operation moved by 1% of the time
where the time goes in v11:
time: 22.7 us; the launch traced here: 22.6 us
  starting transfers between devices  12.1 us (53%)
  Pallas kernels  9.06 us (40%)
  waiting for transfers between devices  1.4 us (6%)
    ppermute x8, starting transfers between devices, exchange(): arrived.append(lax.ppermute(message, axis, pairs))  12.1 us
    pallas_call x5, Pallas kernels, call(): pl.pallas_call(kernel, out_shape=shapes, in_specs=ins, out_specs=[VMEM] *...  9.06 us
    ppermute x8, waiting for transfers between devices, exchange(): arrived.append(lax.ppermute(message, axis, pairs))  1.4 us
  transfers between devices with their start and end apart: 8, of which 3 were waited for; matrix products, arithmetic and copies ran while one was open for 0% of the time, Pallas kernels for 12%

profile of v11, /device:TPU:0, one launch (start us, length us, event | category | flops | bytes accessed | tf_op | source)
XLA Modules:
  0.0 22.6 jit_solution(15688009992601130093)
XLA Ops:
  0.0 2.7 %predict.1 = (f32[9,8,128]{2,1,0:T(8,128)S(1)}, f32[9,8,128]{2,1,0:T(8,128)S(1)}, f32[32,128]{1,0:T(8,128)S(1)}, f32[32,128]{1,0:T(8,128)S(1)}, f32[32,128]{1,0:...) custom-call(f32[9,16,56]{2,1,0:T(8,128)} %bitcast.11, ...), custom_call_target="tpu_custom_call" | custom-call | flops 100000000 | bytes 4000000 | tf_op jit(solution)/shard_map/predict/pallas_call | solution.py:585
  2.8 6.0 %collective-permute-start = (f32[32,128]{1,0:T(8,128)S(1)}, f32[32,128]{1,0:T(8,128)S(1)}, u32[]{:S(2)}, u32[]{:S(2)}) collective-permute-start(f32[32,128]{1,0:T(8,128)S(1)} %get-tuple-element.72), channel_id=1, source_target_pairs={{4,8},{8,4},{12,16},{16,12},{20,24},{24,20},{28,0},{0,28},{5,9},{9... | collective-permute-start | bytes 49160 | tf_op jit(solution)/shard_map/ppermute | solution.py:606
  8.8 0.0 collective-permute-start.1
  8.8 0.0 collective-permute-start.2
  8.8 1.6 %collective-permute-start.3 = (f32[32,128]{1,0:T(8,128)S(1)}, f32[32,128]{1,0:T(8,128)S(1)}, u32[]{:S(2)}, u32[]{:S(2)}) collective-permute-start(f32[32,128]{1,0:T(8,128)S(1)} %get-tuple-element.75), channel_id=1, source_target_pairs={{1,2},{2,1},{3,0},{0,3},{5,6},{6,5},{7,4},{4,7},{9,10},{10,9},{11,... | collective-permute-start | bytes 49160 | tf_op jit(solution)/shard_map/ppermute | solution.py:606
  10.4 1.5 %prepare.1 = (f32[9,8,128]{2,1,0:T(8,128)S(1)}, f32[81,2,8,128]{3,2,1,0:T(8,128)S(1)}, f32[180,16,128]{2,1,0:T(8,128)S(1)}, bf16[384,384]{1,0:T(8,128)(2,1)S(1)}...) custom-call(f32[9,8,128]{2,1,0:T(8,128)S(1)} %get-tuple-element.49.p, ...), custom_call_target="tpu_custom_call" | custom-call | flops 200000000 | bytes 4000000 | tf_op jit(solution)/shard_map/prepare/pallas_call | solution.py:585
  11.9 0.0 collective-permute-done.from_0.first_0
  11.9 0.6 %collective-permute-done.1.from_1.first_1 = f32[32,128]{1,0:T(8,128)S(1)} collective-permute-done((f32[32,128]{1,0:T(8,128)S(1)}, f32[32,128]{1,0:T(8,128)S(1)}, u32[]{:S(2)}, u32[]{:S(2)}) %collective-permute-start.1) | collective-permute-done | bytes 16416 | tf_op jit(solution)/shard_map/ppermute | solution.py:606
  12.5 0.0 collective-permute-done.2.from_2.first_2
  12.5 0.0 collective-permute-done.3.from_3.first_3
  12.5 2.4 %middle.1 = (f32[9,8,128]{2,1,0:T(8,128)S(1)}, f32[9,8,128]{2,1,0:T(8,128)S(1)}, f32[16,128]{1,0:T(8,128)S(1)}, f32[16,128]{1,0:T(8,128)S(1)}, f32[16,128]{1,0:T(8,128)S(1)}, /*index=5*/f32[16,128]{1,0:T(8,128)S(1)}) custom-call(f32[9,8,128]{2,1,0:T(8,128)S(1)} %get-tuple-element.62.base_ref, f32[5,16,128]{2,1,0:T(8,128)S(1)} %get-tuple-element.63.early_rows, ...), custom_call_target="tpu_custom_call" | custom-call | flops 200000000 | bytes 4000000 | tf_op jit(solution)/shard_map/middle/pallas_call | solution.py:585
  14.9 2.8 %collective-permute-start.4 = (f32[16,128]{1,0:T(8,128)S(1)}, f32[16,128]{1,0:T(8,128)S(1)}, u32[]{:S(2)}, u32[]{:S(2)}) collective-permute-start(f32[16,128]{1,0:T(8,128)S(1)} %get-tuple-element.89), channel_id=1, source_target_pairs={{4,8},{8,4},{12,16},{16,12},{20,24},{24,20},{28,0},{0,28},{5,9},{9... | collective-permute-start | bytes 24584 | tf_op jit(solution)/shard_map/ppermute | solution.py:606
  17.7 0.0 collective-permute-start.5
  17.7 0.0 collective-permute-start.6
  17.7 1.6 %collective-permute-start.7 = (f32[16,128]{1,0:T(8,128)S(1)}, f32[16,128]{1,0:T(8,128)S(1)}, u32[]{:S(2)}, u32[]{:S(2)}) collective-permute-start(f32[16,128]{1,0:T(8,128)S(1)} %get-tuple-element.92), channel_id=1, source_target_pairs={{1,2},{2,1},{3,0},{0,3},{5,6},{6,5},{7,4},{4,7},{9,10},{10,9},{11,... | collective-permute-start | bytes 24584 | tf_op jit(solution)/shard_map/ppermute | solution.py:606
  19.4 1.3 %local_late.1 = (f32[9,8,128]{2,1,0:T(8,128)S(1)}, f32[144,512]{1,0:T(8,128)S(1)}, bf16[8,256,128]{2,1,0:T(8,128)(2,1)S(1)}, bf16[144,256]{1,0:T(8,128)(2,1)S(1)}) custom-call(f32[9,8,128]{2,1,0:T(8,128)S(1)} %get-tuple-element.76.middle_ref, f32[9,8,128]{2,1,0:T(8,128)S(1)} %get-tuple-element.77.late_ref, f32[243,8,128]{2,1,0:T(8,128)S(1)} %get-tuple-element.52.star_ref, ...), custom_call_target="tpu_custom_call" | custom-call | flops 200000000 | bytes 4000000 | tf_op jit(solution)/shard_map/local_late/pallas_call | solution.py:585
  20.7 0.7 %collective-permute-done.4.second_0 = f32[16,128]{1,0:T(8,128)S(1)} collective-permute-done((f32[16,128]{1,0:T(8,128)S(1)}, f32[16,128]{1,0:T(8,128)S(1)}, u32[]{:S(2)}, u32[]{:S(2)}) %collective-permute-start.4) | collective-permute-done | bytes 8224 | tf_op jit(solution)/shard_map/ppermute | solution.py:606
  21.4 0.1 collective-permute-done.5.second_1
  21.4 0.0 collective-permute-done.6.second_2
  21.4 0.0 collective-permute-done.7.second_3
  21.4 1.1 %final.1 = f32[9,16,56]{2,1,0:T(8,128)} custom-call(f32[9,8,128]{2,1,0:T(8,128)S(1)} %get-tuple-element.85.base_ref, f32[144,512]{1,0:T(8,128)S(1)} %get-tuple-element.86.ghost_flux_ref, bf16[8,256,128]{2,1,0:T(8,128)(2,1)S(1)} %get-tuple-element.87.ghost_operator_ref, bf16[144,256]{1,0:T(8,128)(2,1)S(1)} %get-tuple-element.88.scatter_ref, ...), custom_call_target="tpu_custom_call" | custom-call | flops 200000000 | bytes 4000000 | tf_op jit(solution)/shard_map/final/pallas_call | solution.py:585
Async XLA Ops:
  2.8 9.2 %collective-permute-start = (f32[32,128]{1,0:T(8,128)S(1)}, f32[32,128]{1,0:T(8,128)S(1)}, u32[]{:S(2)}, u32[]{:S(2)}) collective-permute-start(f32[32,128]{1,0:T(8,128)S(1)} %get-tuple-element.72), channel_id=1, source_target_pairs={{4,8},{8,4},{12,16},{16,12},{20,24},{24,20},{28,0},{0,28},{5,9},{9... | collective-permute-start | bytes 49160 | tf_op jit(solution)/shard_map/ppermute | solution.py:606
  8.8 3.7 %collective-permute-start.1 = (f32[32,128]{1,0:T(8,128)S(1)}, f32[32,128]{1,0:T(8,128)S(1)}, u32[]{:S(2)}, u32[]{:S(2)}) collective-permute-start(f32[32,128]{1,0:T(8,128)S(1)} %get-tuple-element.73), channel_id=1, source_target_pairs={{0,4},{4,0},{8,12},{12,8},{16,20},{20,16},{24,28},{28,24},{1,5},{5... | collective-permute-start | bytes 49160 | tf_op jit(solution)/shard_map/ppermute | solution.py:606
  8.8 3.7 %collective-permute-start.2 = (f32[32,128]{1,0:T(8,128)S(1)}, f32[32,128]{1,0:T(8,128)S(1)}, u32[]{:S(2)}, u32[]{:S(2)}) collective-permute-start(f32[32,128]{1,0:T(8,128)S(1)} %get-tuple-element.74), channel_id=1, source_target_pairs={{0,1},{1,0},{2,3},{3,2},{4,5},{5,4},{6,7},{7,6},{8,9},{9,8},{10,11... | collective-permute-start | bytes 49160 | tf_op jit(solution)/shard_map/ppermute | solution.py:606
  8.8 3.7 %collective-permute-start.3 = (f32[32,128]{1,0:T(8,128)S(1)}, f32[32,128]{1,0:T(8,128)S(1)}, u32[]{:S(2)}, u32[]{:S(2)}) collective-permute-start(f32[32,128]{1,0:T(8,128)S(1)} %get-tuple-element.75), channel_id=1, source_target_pairs={{1,2},{2,1},{3,0},{0,3},{5,6},{6,5},{7,4},{4,7},{9,10},{10,9},{11,... | collective-permute-start | bytes 49160 | tf_op jit(solution)/shard_map/ppermute | solution.py:606
  14.9 6.4 %collective-permute-start.4 = (f32[16,128]{1,0:T(8,128)S(1)}, f32[16,128]{1,0:T(8,128)S(1)}, u32[]{:S(2)}, u32[]{:S(2)}) collective-permute-start(f32[16,128]{1,0:T(8,128)S(1)} %get-tuple-element.89), channel_id=1, source_target_pairs={{4,8},{8,4},{12,16},{16,12},{20,24},{24,20},{28,0},{0,28},{5,9},{9... | collective-permute-start | bytes 24584 | tf_op jit(solution)/shard_map/ppermute | solution.py:606
  17.7 3.7 %collective-permute-start.5 = (f32[16,128]{1,0:T(8,128)S(1)}, f32[16,128]{1,0:T(8,128)S(1)}, u32[]{:S(2)}, u32[]{:S(2)}) collective-permute-start(f32[16,128]{1,0:T(8,128)S(1)} %get-tuple-element.90), channel_id=1, source_target_pairs={{0,4},{4,0},{8,12},{12,8},{16,20},{20,16},{24,28},{28,24},{1,5},{5... | collective-permute-start | bytes 24584 | tf_op jit(solution)/shard_map/ppermute | solution.py:606
  17.7 3.7 %collective-permute-start.6 = (f32[16,128]{1,0:T(8,128)S(1)}, f32[16,128]{1,0:T(8,128)S(1)}, u32[]{:S(2)}, u32[]{:S(2)}) collective-permute-start(f32[16,128]{1,0:T(8,128)S(1)} %get-tuple-element.91), channel_id=1, source_target_pairs={{0,1},{1,0},{2,3},{3,2},{4,5},{5,4},{6,7},{7,6},{8,9},{9,8},{10,11... | collective-permute-start | bytes 24584 | tf_op jit(solution)/shard_map/ppermute | solution.py:606
  17.7 3.7 %collective-permute-start.7 = (f32[16,128]{1,0:T(8,128)S(1)}, f32[16,128]{1,0:T(8,128)S(1)}, u32[]{:S(2)}, u32[]{:S(2)}) collective-permute-start(f32[16,128]{1,0:T(8,128)S(1)} %get-tuple-element.92), channel_id=1, source_target_pairs={{1,2},{2,1},{3,0},{0,3},{5,6},{6,5},{7,4},{4,7},{9,10},{10,9},{11,... | collective-permute-start | bytes 24584 | tf_op jit(solution)/shard_map/ppermute | solution.py:606

commit v12 on v11

--- a/solution.py
+++ b/solution.py
@@ -15,7 +15,7 @@
 BF16 = jnp.bfloat16
 LATER = ("flux_local", "flux_remote", "face_restrict", "face_lift", "orient_maps", "slot", "face", "turn", "rate")
 AXES = ("dom", "sub")
-SWAPS = (("dom", True), ("dom", False), ("sub", False), ("sub", True))
+SWAPS = (("dom", True), ("dom", False), ("sub", True), ("sub", False))
 
 
 def taylor_weight(lower, upper, degree):
@@ -496,7 +496,7 @@
         current = star_mix(product(stack_left(current), derive_ref[...]), star_ref, fields, kinds)
         return current, early + weight_at(0.0, 0.5, degree) * current
 
-    _, restart = lax.fori_loop(1, DERIVS, step, (start, taylor_weight(0.0, 0.5, 0) * start), unroll=True)
+    _, restart = lax.fori_loop(1, DERIVS, step, (start, taylor_weight(0.0, 0.5, 0) * start))
     copy.wait()
     is_fast = fast_ref[...]
     late = jnp.where((is_fast == 2)[None], restart.reshape(fields, ROWS, LANES), late_ref[...])

time: 22.7 us -> 22.4 us (0.987)
  Pallas kernels: 9.06 us -> 8.7 us
    pallas_call x5, Pallas kernels: 9.06 us -> 8.7 us  [call(): pl.pallas_call(kernel, out_shape=shapes, in_specs=ins, out_specs=[VMEM] *...]
  transfers between devices with their start and end apart: 8 -> 8, of which waited for: 3 -> 3; matrix products, arithmetic and copies ran while one was open for 0% -> 0% of each run, Pallas kernels for 12% -> 13%
where the time goes in v12:
time: 22.4 us; the launch traced here: 22.2 us
  starting transfers between devices  12.1 us (54%)
  Pallas kernels  8.7 us (39%)
  waiting for transfers between devices  1.4 us (6%)
    ppermute x8, starting transfers between devices, exchange(): arrived.append(lax.ppermute(message, axis, pairs))  12.1 us
    pallas_call x5, Pallas kernels, call(): pl.pallas_call(kernel, out_shape=shapes, in_specs=ins, out_specs=[VMEM] *...  8.7 us
    ppermute x8, waiting for transfers between devices, exchange(): arrived.append(lax.ppermute(message, axis, pairs))  1.4 us
  transfers between devices with their start and end apart: 8, of which 3 were waited for; matrix products, arithmetic and copies ran while one was open for 0% of the time, Pallas kernels for 13%

profile of v12, /device:TPU:0, one launch (start us, length us, event | category | flops | bytes accessed | tf_op | source)
XLA Modules:
  0.0 22.2 jit_solution(9330230372795936348)
XLA Ops:
  0.0 2.7 %predict.1 = (f32[9,8,128]{2,1,0:T(8,128)S(1)}, f32[9,8,128]{2,1,0:T(8,128)S(1)}, f32[32,128]{1,0:T(8,128)S(1)}, f32[32,128]{1,0:T(8,128)S(1)}, f32[32,128]{1,0:...) custom-call(f32[9,16,56]{2,1,0:T(8,128)} %bitcast.11, ...), custom_call_target="tpu_custom_call" | custom-call | flops 100000000 | bytes 4000000 | tf_op jit(solution)/shard_map/predict/pallas_call | solution.py:585
  2.8 6.0 %collective-permute-start = (f32[32,128]{1,0:T(8,128)S(1)}, f32[32,128]{1,0:T(8,128)S(1)}, u32[]{:S(2)}, u32[]{:S(2)}) collective-permute-start(f32[32,128]{1,0:T(8,128)S(1)} %get-tuple-element.72), channel_id=1, source_target_pairs={{4,8},{8,4},{12,16},{16,12},{20,24},{24,20},{28,0},{0,28},{5,9},{9... | collective-permute-start | bytes 49160 | tf_op jit(solution)/shard_map/ppermute | solution.py:606
  8.8 0.0 collective-permute-start.1
  8.8 0.7 %collective-permute-start.2 = (f32[32,128]{1,0:T(8,128)S(1)}, f32[32,128]{1,0:T(8,128)S(1)}, u32[]{:S(2)}, u32[]{:S(2)}) collective-permute-start(f32[32,128]{1,0:T(8,128)S(1)} %get-tuple-element.74), channel_id=1, source_target_pairs={{1,2},{2,1},{3,0},{0,3},{5,6},{6,5},{7,4},{4,7},{9,10},{10,9},{11,... | collective-permute-start | bytes 49160 | tf_op jit(solution)/shard_map/ppermute | solution.py:606
  9.5 1.0 %collective-permute-start.3 = (f32[32,128]{1,0:T(8,128)S(1)}, f32[32,128]{1,0:T(8,128)S(1)}, u32[]{:S(2)}, u32[]{:S(2)}) collective-permute-start(f32[32,128]{1,0:T(8,128)S(1)} %get-tuple-element.75), channel_id=1, source_target_pairs={{0,1},{1,0},{2,3},{3,2},{4,5},{5,4},{6,7},{7,6},{8,9},{9,8},{10,11... | collective-permute-start | bytes 49160 | tf_op jit(solution)/shard_map/ppermute | solution.py:606
  10.4 1.5 %prepare.1 = (f32[9,8,128]{2,1,0:T(8,128)S(1)}, f32[81,2,8,128]{3,2,1,0:T(8,128)S(1)}, f32[180,16,128]{2,1,0:T(8,128)S(1)}, bf16[384,384]{1,0:T(8,128)(2,1)S(1)}...) custom-call(f32[9,8,128]{2,1,0:T(8,128)S(1)} %get-tuple-element.49.p, ...), custom_call_target="tpu_custom_call" | custom-call | flops 200000000 | bytes 4000000 | tf_op jit(solution)/shard_map/prepare/pallas_call | solution.py:585
  11.9 0.0 collective-permute-done.from_0.first_0
  11.9 0.6 %collective-permute-done.1.from_1.first_1 = f32[32,128]{1,0:T(8,128)S(1)} collective-permute-done((f32[32,128]{1,0:T(8,128)S(1)}, f32[32,128]{1,0:T(8,128)S(1)}, u32[]{:S(2)}, u32[]{:S(2)}) %collective-permute-start.1) | collective-permute-done | bytes 16416 | tf_op jit(solution)/shard_map/ppermute | solution.py:606
  12.5 0.0 collective-permute-done.2.from_2.first_2
  12.5 0.0 collective-permute-done.3.from_3.first_3
  12.5 2.0 %middle.1 = (f32[9,8,128]{2,1,0:T(8,128)S(1)}, f32[9,8,128]{2,1,0:T(8,128)S(1)}, f32[16,128]{1,0:T(8,128)S(1)}, f32[16,128]{1,0:T(8,128)S(1)}, f32[16,128]{1,0:T(8,128)S(1)}, /*index=5*/f32[16,128]{1,0:T(8,128)S(1)}) custom-call(f32[9,8,128]{2,1,0:T(8,128)S(1)} %get-tuple-element.62.base_ref, f32[5,16,128]{2,1,0:T(8,128)S(1)} %get-tuple-element.63.early_rows, ...), custom_call_target="tpu_custom_call" | custom-call | flops 200000000 | bytes 4000000 | tf_op jit(solution)/shard_map/middle/pallas_call | solution.py:585
  14.6 2.8 %collective-permute-start.4 = (f32[16,128]{1,0:T(8,128)S(1)}, f32[16,128]{1,0:T(8,128)S(1)}, u32[]{:S(2)}, u32[]{:S(2)}) collective-permute-start(f32[16,128]{1,0:T(8,128)S(1)} %get-tuple-element.89), channel_id=1, source_target_pairs={{4,8},{8,4},{12,16},{16,12},{20,24},{24,20},{28,0},{0,28},{5,9},{9... | collective-permute-start | bytes 24584 | tf_op jit(solution)/shard_map/ppermute | solution.py:606
  17.4 0.0 collective-permute-start.5
  17.4 0.0 collective-permute-start.6
  17.4 1.6 %collective-permute-start.7 = (f32[16,128]{1,0:T(8,128)S(1)}, f32[16,128]{1,0:T(8,128)S(1)}, u32[]{:S(2)}, u32[]{:S(2)}) collective-permute-start(f32[16,128]{1,0:T(8,128)S(1)} %get-tuple-element.92), channel_id=1, source_target_pairs={{0,1},{1,0},{2,3},{3,2},{4,5},{5,4},{6,7},{7,6},{8,9},{9,8},{10,11... | collective-permute-start | bytes 24584 | tf_op jit(solution)/shard_map/ppermute | solution.py:606
  19.0 1.3 %local_late.1 = (f32[9,8,128]{2,1,0:T(8,128)S(1)}, f32[144,512]{1,0:T(8,128)S(1)}, bf16[8,256,128]{2,1,0:T(8,128)(2,1)S(1)}, bf16[144,256]{1,0:T(8,128)(2,1)S(1)}) custom-call(f32[9,8,128]{2,1,0:T(8,128)S(1)} %get-tuple-element.76.middle_ref, f32[9,8,128]{2,1,0:T(8,128)S(1)} %get-tuple-element.77.late_ref, f32[243,8,128]{2,1,0:T(8,128)S(1)} %get-tuple-element.52.star_ref, ...), custom_call_target="tpu_custom_call" | custom-call | flops 200000000 | bytes 4000000 | tf_op jit(solution)/shard_map/local_late/pallas_call | solution.py:585
  20.3 0.7 %collective-permute-done.4.second_0 = f32[16,128]{1,0:T(8,128)S(1)} collective-permute-done((f32[16,128]{1,0:T(8,128)S(1)}, f32[16,128]{1,0:T(8,128)S(1)}, u32[]{:S(2)}, u32[]{:S(2)}) %collective-permute-start.4) | collective-permute-done | bytes 8224 | tf_op jit(solution)/shard_map/ppermute | solution.py:606
  21.0 0.1 collective-permute-done.5.second_1
  21.1 0.0 collective-permute-done.6.second_2
  21.1 0.0 collective-permute-done.7.second_3
  21.1 1.1 %final.1 = f32[9,16,56]{2,1,0:T(8,128)} custom-call(f32[9,8,128]{2,1,0:T(8,128)S(1)} %get-tuple-element.85.base_ref, f32[144,512]{1,0:T(8,128)S(1)} %get-tuple-element.86.ghost_flux_ref, bf16[8,256,128]{2,1,0:T(8,128)(2,1)S(1)} %get-tuple-element.87.ghost_operator_ref, bf16[144,256]{1,0:T(8,128)(2,1)S(1)} %get-tuple-element.88.scatter_ref, ...), custom_call_target="tpu_custom_call" | custom-call | flops 200000000 | bytes 4000000 | tf_op jit(solution)/shard_map/final/pallas_call | solution.py:585
Async XLA Ops:
  2.8 9.2 %collective-permute-start = (f32[32,128]{1,0:T(8,128)S(1)}, f32[32,128]{1,0:T(8,128)S(1)}, u32[]{:S(2)}, u32[]{:S(2)}) collective-permute-start(f32[32,128]{1,0:T(8,128)S(1)} %get-tuple-element.72), channel_id=1, source_target_pairs={{4,8},{8,4},{12,16},{16,12},{20,24},{24,20},{28,0},{0,28},{5,9},{9... | collective-permute-start | bytes 49160 | tf_op jit(solution)/shard_map/ppermute | solution.py:606
  8.8 3.7 %collective-permute-start.1 = (f32[32,128]{1,0:T(8,128)S(1)}, f32[32,128]{1,0:T(8,128)S(1)}, u32[]{:S(2)}, u32[]{:S(2)}) collective-permute-start(f32[32,128]{1,0:T(8,128)S(1)} %get-tuple-element.73), channel_id=1, source_target_pairs={{0,4},{4,0},{8,12},{12,8},{16,20},{20,16},{24,28},{28,24},{1,5},{5... | collective-permute-start | bytes 49160 | tf_op jit(solution)/shard_map/ppermute | solution.py:606
  8.8 3.7 %collective-permute-start.2 = (f32[32,128]{1,0:T(8,128)S(1)}, f32[32,128]{1,0:T(8,128)S(1)}, u32[]{:S(2)}, u32[]{:S(2)}) collective-permute-start(f32[32,128]{1,0:T(8,128)S(1)} %get-tuple-element.74), channel_id=1, source_target_pairs={{1,2},{2,1},{3,0},{0,3},{5,6},{6,5},{7,4},{4,7},{9,10},{10,9},{11,... | collective-permute-start | bytes 49160 | tf_op jit(solution)/shard_map/ppermute | solution.py:606
  9.5 3.1 %collective-permute-start.3 = (f32[32,128]{1,0:T(8,128)S(1)}, f32[32,128]{1,0:T(8,128)S(1)}, u32[]{:S(2)}, u32[]{:S(2)}) collective-permute-start(f32[32,128]{1,0:T(8,128)S(1)} %get-tuple-element.75), channel_id=1, source_target_pairs={{0,1},{1,0},{2,3},{3,2},{4,5},{5,4},{6,7},{7,6},{8,9},{9,8},{10,11... | collective-permute-start | bytes 49160 | tf_op jit(solution)/shard_map/ppermute | solution.py:606
  14.6 6.4 %collective-permute-start.4 = (f32[16,128]{1,0:T(8,128)S(1)}, f32[16,128]{1,0:T(8,128)S(1)}, u32[]{:S(2)}, u32[]{:S(2)}) collective-permute-start(f32[16,128]{1,0:T(8,128)S(1)} %get-tuple-element.89), channel_id=1, source_target_pairs={{4,8},{8,4},{12,16},{16,12},{20,24},{24,20},{28,0},{0,28},{5,9},{9... | collective-permute-start | bytes 24584 | tf_op jit(solution)/shard_map/ppermute | solution.py:606
  17.4 3.7 %collective-permute-start.5 = (f32[16,128]{1,0:T(8,128)S(1)}, f32[16,128]{1,0:T(8,128)S(1)}, u32[]{:S(2)}, u32[]{:S(2)}) collective-permute-start(f32[16,128]{1,0:T(8,128)S(1)} %get-tuple-element.90), channel_id=1, source_target_pairs={{0,4},{4,0},{8,12},{12,8},{16,20},{20,16},{24,28},{28,24},{1,5},{5... | collective-permute-start | bytes 24584 | tf_op jit(solution)/shard_map/ppermute | solution.py:606
  17.4 3.7 %collective-permute-start.6 = (f32[16,128]{1,0:T(8,128)S(1)}, f32[16,128]{1,0:T(8,128)S(1)}, u32[]{:S(2)}, u32[]{:S(2)}) collective-permute-start(f32[16,128]{1,0:T(8,128)S(1)} %get-tuple-element.91), channel_id=1, source_target_pairs={{1,2},{2,1},{3,0},{0,3},{5,6},{6,5},{7,4},{4,7},{9,10},{10,9},{11,... | collective-permute-start | bytes 24584 | tf_op jit(solution)/shard_map/ppermute | solution.py:606
  17.4 3.7 %collective-permute-start.7 = (f32[16,128]{1,0:T(8,128)S(1)}, f32[16,128]{1,0:T(8,128)S(1)}, u32[]{:S(2)}, u32[]{:S(2)}) collective-permute-start(f32[16,128]{1,0:T(8,128)S(1)} %get-tuple-element.92), channel_id=1, source_target_pairs={{0,1},{1,0},{2,3},{3,2},{4,5},{5,4},{6,7},{7,6},{8,9},{9,8},{10,11... | collective-permute-start | bytes 24584 | tf_op jit(solution)/shard_map/ppermute | solution.py:606

commit v13 on v12

--- a/solution.py
+++ b/solution.py
@@ -79,7 +79,6 @@
 
 def pack(values_ref, packed_ref):
     modes = values_ref.shape[2]
-    packed_ref[...] = jnp.zeros(packed_ref.shape, F32)
     packed_ref[:, :, 0:modes] = values_ref[:, 0:ROWS, :]
     packed_ref[:, :, HALF : HALF + modes] = values_ref[:, ROWS : 2 * ROWS, :]
 
@@ -137,7 +136,6 @@
 
 def stiffness_blocks(stiffness_ref, block_ref, turned):
     kinds, modes = stiffness_ref.shape[0], stiffness_ref.shape[1]
-    block_ref[...] = jnp.zeros(block_ref.shape, F32)
     for kind in range(kinds):
         matrix = -stiffness_ref[kind].T if turned else stiffness_ref[kind]
         block_ref[kind, 0:modes, 0:modes] = matrix
@@ -164,6 +162,8 @@
         copy.start()
     fields, kinds = star_ref.shape[0], star_ref.shape[2]
     pairs = (fields + 1) // 2
+    for cleared in (packed_ref, block_ref, send_0, send_1, send_2, send_3):
+        cleared[...] = jnp.zeros(cleared.shape, F32)
     for copy in copies[0:3]:
         copy.wait()
     derive_ref[...] = stack_right(stiffness_blocks(stiffness_ref, block_ref, True))
@@ -190,7 +190,6 @@
     sends = send_ref.shape[2]
     fast = sends // 2
     for side, out in enumerate((send_0, send_1, send_2, send_3)):
-        out[...] = jnp.zeros(out.shape, F32)
         for place in range(sends):
             element = send_ref[0, message_side(side), place]
             for pair in range(pairs):
@@ -339,11 +338,16 @@
     lifts = product(jnp.concatenate(left, axis=0), jnp.concatenate([high, high, low, jnp.zeros_like(low)], axis=0))
     side_lane = (lane_index((1, faces * HALF)) // HALF).astype(F32)
     place_of = jnp.zeros((1, LANES), F32)
+    columns = []
     for at, number in enumerate(numbers):
         chosen = lifts[at * HALF : (at + 1) * HALF] * one_where(side_lane == face_of[number : number + 1])
         both = chosen[:, 0:LANES] + chosen[:, LANES : 2 * LANES]
         high, low = split(both + swap_halves(both))
-        operator_out[at] = jnp.concatenate([high, high, low, jnp.zeros_like(low)], axis=0)
+        none = jnp.zeros_like(low)
+        order = [high, none, high, none, low, none] if at % 2 == 0 else [none, high, none, high, none, low]
+        columns.append(jnp.concatenate(order, axis=0))
+        if at % 2 == 1:
+            operator_out[at // 2] = jnp.concatenate(columns[-2:], axis=1)
         place_of = jnp.where(lane_index((1, LANES)) // rows == at, element_of[number : number + 1], place_of)
     square = (fields * elements, LANES)
     here = (row_index(square) // elements == lane_index(square) % rows) & (
@@ -366,6 +370,7 @@
     flux_local_coefficients(flux_local_ref, local_work_ref, local_out)
     flux_remote_coefficients(flux_remote_ref, remote_work_ref, remote_out)
 
+    block_ref[...] = jnp.zeros(block_ref.shape, F32)
     volume_out[...] = stack_right(stiffness_blocks(stiffness_ref, block_ref, False))
 
     wide_ref[...] = jnp.zeros(wide_ref.shape, F32)
@@ -539,7 +544,9 @@
     terms = local_terms(late, star_ref, flux_ref, volume_ref, trace_ref, lift_ref, fields, kinds)
     rows = [rows_ref[pair] for pair in range(pairs)]
     remote = remote_terms(rows, remote_ref, compose_ref, remote_lift_ref, choose_ref, mask_ref, fields)
-    base_out[...] = middle_ref[...] + terms.reshape(fields, ROWS, LANES) + remote
+    base = middle_ref[...] + terms.reshape(fields, ROWS, LANES) + remote
+    base_out[:, 0:ROWS, :] = base
+    base_out[:, ROWS : 2 * ROWS, :] = swap_halves(base.reshape(fields * ROWS, LANES)).reshape(base.shape)
     lane_code = combo_code(lane_index((1, composed_ref.shape[1])), orient_ref.shape[0], orient_ref.shape[1])
     ghost_terms(
         flux_remote_ref, stage_ref, code_ref, composed_ref[...], sides_ref[...], lane_code,
@@ -553,24 +560,18 @@
     fields = base_ref.shape[0]
     modes = result_out.shape[2]
     rows = second_0.shape[0]
-    lower = lower_half((rows, LANES))
     added = []
     for slot, second in enumerate((second_0, second_1, second_2, second_3)):
-        mixed = None
+        sums = [None] * 3
         for field in range(fields):
             coefficient = ghost_flux_ref[field * rows : (field + 1) * rows, slot * LANES : (slot + 1) * LANES]
             term = coefficient * second[field : field + 1, :]
-            mixed = term if mixed is None else mixed + term
-        high, low = split(mixed)
-        high_swapped, low_swapped = split(swap_halves(mixed))
-        for place, parts in enumerate(((high, low_swapped, high), (high_swapped, low, high_swapped))):
-            left = jnp.concatenate([jnp.where(lower, parts[0], parts[1]), parts[2]], axis=1)
-            added.append(product(left, ghost_operator_ref[2 * slot + place]))
+            sums[field % 3] = term if sums[field % 3] is None else sums[field % 3] + term
+        both = product(stack_left(sums[0] + sums[1] + sums[2]), ghost_operator_ref[slot])
+        added += [both[:, 0:LANES], both[:, LANES : 2 * LANES]]
     right = jnp.concatenate(split(jnp.concatenate(added, axis=0)), axis=0)
-    scattered = product(scatter_ref[...], right).reshape(fields, 2, ROWS, LANES)
-    result = base_ref[...] + jnp.where(lower_half((ROWS, LANES))[None], scattered[:, 0], scattered[:, 1])
-    result_out[:, 0:ROWS, :] = result[:, :, 0:modes]
-    result_out[:, ROWS : 2 * ROWS, :] = result[:, :, HALF : HALF + modes]
+    result = base_ref[...] + product(scatter_ref[...], right).reshape(base_ref.shape)
+    result_out[...] = result[:, :, 0:modes]
 
 
 VMEM = pl.BlockSpec(memory_space=pltpu.VMEM)
@@ -702,8 +703,8 @@
         local_kernel,
         [VMEM] * (17 + len(first)),
         [
-            (packed, F32), ((fields * second_shape[0], sides * LANES), F32),
-            ((sides * fast, 2 * LANES, LANES), BF16), ((fields * elements, 2 * LANES), BF16),
+            ((fields, elements, LANES), F32), ((fields * second_shape[0], sides * LANES), F32),
+            ((sides, 3 * LANES, 2 * LANES), BF16), ((fields * elements, 2 * LANES), BF16),
         ],
         [((pairs, sources, LANES), F32), ((fields, 2 * ROWS * faces, LANES), F32)],
         (

time: 22.4 us -> 22.3 us (level)
  no operation moved by 1% of the time
where the time goes in v13:
time: 22.3 us; the launch traced here: 22.1 us
  starting transfers between devices  12.1 us (54%)
  Pallas kernels  8.61 us (39%)
  waiting for transfers between devices  1.38 us (6%)
    ppermute x8, starting transfers between devices, exchange(): arrived.append(lax.ppermute(message, axis, pairs))  12.1 us
    pallas_call x5, Pallas kernels, call(): pl.pallas_call(kernel, out_shape=shapes, in_specs=ins, out_specs=[VMEM] *...  8.61 us
    ppermute x8, waiting for transfers between devices, exchange(): arrived.append(lax.ppermute(message, axis, pairs))  1.38 us
  transfers between devices with their start and end apart: 8, of which 3 were waited for; matrix products, arithmetic and copies ran while one was open for 0% of the time, Pallas kernels for 13%

profile of v13, /device:TPU:0, one launch (start us, length us, event | category | flops | bytes accessed | tf_op | source)
XLA Modules:
  0.0 22.1 jit_solution(17666724304963023288)
XLA Ops:
  0.0 2.7 %predict.1 = (f32[9,8,128]{2,1,0:T(8,128)S(1)}, f32[9,8,128]{2,1,0:T(8,128)S(1)}, f32[32,128]{1,0:T(8,128)S(1)}, f32[32,128]{1,0:T(8,128)S(1)}, f32[32,128]{1,0:...) custom-call(f32[9,16,56]{2,1,0:T(8,128)} %bitcast.11, ...), custom_call_target="tpu_custom_call" | custom-call | flops 100000000 | bytes 4000000 | tf_op jit(solution)/shard_map/predict/pallas_call | solution.py:586
  2.8 6.0 %collective-permute-start = (f32[32,128]{1,0:T(8,128)S(1)}, f32[32,128]{1,0:T(8,128)S(1)}, u32[]{:S(2)}, u32[]{:S(2)}) collective-permute-start(f32[32,128]{1,0:T(8,128)S(1)} %get-tuple-element.72), channel_id=1, source_target_pairs={{4,8},{8,4},{12,16},{16,12},{20,24},{24,20},{28,0},{0,28},{5,9},{9... | collective-permute-start | bytes 49160 | tf_op jit(solution)/shard_map/ppermute | solution.py:607
  8.8 0.0 collective-permute-start.1
  8.8 0.7 %collective-permute-start.2 = (f32[32,128]{1,0:T(8,128)S(1)}, f32[32,128]{1,0:T(8,128)S(1)}, u32[]{:S(2)}, u32[]{:S(2)}) collective-permute-start(f32[32,128]{1,0:T(8,128)S(1)} %get-tuple-element.74), channel_id=1, source_target_pairs={{1,2},{2,1},{3,0},{0,3},{5,6},{6,5},{7,4},{4,7},{9,10},{10,9},{11,... | collective-permute-start | bytes 49160 | tf_op jit(solution)/shard_map/ppermute | solution.py:607
  9.5 1.0 %collective-permute-start.3 = (f32[32,128]{1,0:T(8,128)S(1)}, f32[32,128]{1,0:T(8,128)S(1)}, u32[]{:S(2)}, u32[]{:S(2)}) collective-permute-start(f32[32,128]{1,0:T(8,128)S(1)} %get-tuple-element.75), channel_id=1, source_target_pairs={{0,1},{1,0},{2,3},{3,2},{4,5},{5,4},{6,7},{7,6},{8,9},{9,8},{10,11... | collective-permute-start | bytes 49160 | tf_op jit(solution)/shard_map/ppermute | solution.py:607
  10.4 1.5 %prepare.1 = (f32[9,8,128]{2,1,0:T(8,128)S(1)}, f32[81,2,8,128]{3,2,1,0:T(8,128)S(1)}, f32[180,16,128]{2,1,0:T(8,128)S(1)}, bf16[384,384]{1,0:T(8,128)(2,1)S(1)}...) custom-call(f32[9,8,128]{2,1,0:T(8,128)S(1)} %get-tuple-element.49.p, ...), custom_call_target="tpu_custom_call" | custom-call | flops 200000000 | bytes 4000000 | tf_op jit(solution)/shard_map/prepare/pallas_call | solution.py:586
  11.9 0.0 collective-permute-done.from_0.first_0
  11.9 0.6 %collective-permute-done.1.from_1.first_1 = f32[32,128]{1,0:T(8,128)S(1)} collective-permute-done((f32[32,128]{1,0:T(8,128)S(1)}, f32[32,128]{1,0:T(8,128)S(1)}, u32[]{:S(2)}, u32[]{:S(2)}) %collective-permute-start.1) | collective-permute-done | bytes 16416 | tf_op jit(solution)/shard_map/ppermute | solution.py:607
  12.5 0.0 collective-permute-done.2.from_2.first_2
  12.5 0.0 collective-permute-done.3.from_3.first_3
  12.5 2.0 %middle.1 = (f32[9,8,128]{2,1,0:T(8,128)S(1)}, f32[9,8,128]{2,1,0:T(8,128)S(1)}, f32[16,128]{1,0:T(8,128)S(1)}, f32[16,128]{1,0:T(8,128)S(1)}, f32[16,128]{1,0:T(8,128)S(1)}, /*index=5*/f32[16,128]{1,0:T(8,128)S(1)}) custom-call(f32[9,8,128]{2,1,0:T(8,128)S(1)} %get-tuple-element.62.base_ref, f32[5,16,128]{2,1,0:T(8,128)S(1)} %get-tuple-element.63.early_rows, ...), custom_call_target="tpu_custom_call" | custom-call | flops 200000000 | bytes 4000000 | tf_op jit(solution)/shard_map/middle/pallas_call | solution.py:586
  14.6 2.8 %collective-permute-start.4 = (f32[16,128]{1,0:T(8,128)S(1)}, f32[16,128]{1,0:T(8,128)S(1)}, u32[]{:S(2)}, u32[]{:S(2)}) collective-permute-start(f32[16,128]{1,0:T(8,128)S(1)} %get-tuple-element.89), channel_id=1, source_target_pairs={{4,8},{8,4},{12,16},{16,12},{20,24},{24,20},{28,0},{0,28},{5,9},{9... | collective-permute-start | bytes 24584 | tf_op jit(solution)/shard_map/ppermute | solution.py:607
  17.3 0.0 collective-permute-start.5
  17.3 0.0 collective-permute-start.6
  17.3 1.6 %collective-permute-start.7 = (f32[16,128]{1,0:T(8,128)S(1)}, f32[16,128]{1,0:T(8,128)S(1)}, u32[]{:S(2)}, u32[]{:S(2)}) collective-permute-start(f32[16,128]{1,0:T(8,128)S(1)} %get-tuple-element.92), channel_id=1, source_target_pairs={{0,1},{1,0},{2,3},{3,2},{4,5},{5,4},{6,7},{7,6},{8,9},{9,8},{10,11... | collective-permute-start | bytes 24584 | tf_op jit(solution)/shard_map/ppermute | solution.py:607
  19.0 1.3 %local_late.1 = (f32[9,16,128]{2,1,0:T(8,128)S(1)}, f32[144,512]{1,0:T(8,128)S(1)}, bf16[4,384,256]{2,1,0:T(8,128)(2,1)S(1)}, bf16[144,256]{1,0:T(8,128)(2,1)S(1)}) custom-call(f32[9,8,128]{2,1,0:T(8,128)S(1)} %get-tuple-element.76.middle_ref, f32[9,8,128]{2,1,0:T(8,128)S(1)} %get-tuple-element.77.late_ref, f32[243,8,128]{2,1,0:T(8,128)S(1)} %get-tuple-element.52.star_ref, ...), custom_call_target="tpu_custom_call" | custom-call | flops 200000000 | bytes 4000000 | tf_op jit(solution)/shard_map/local_late/pallas_call | solution.py:586
  20.3 0.7 %collective-permute-done.4.second_0 = f32[16,128]{1,0:T(8,128)S(1)} collective-permute-done((f32[16,128]{1,0:T(8,128)S(1)}, f32[16,128]{1,0:T(8,128)S(1)}, u32[]{:S(2)}, u32[]{:S(2)}) %collective-permute-start.4) | collective-permute-done | bytes 8224 | tf_op jit(solution)/shard_map/ppermute | solution.py:607
  21.0 0.1 collective-permute-done.5.second_1
  21.1 0.0 collective-permute-done.6.second_2
  21.1 0.0 collective-permute-done.7.second_3
  21.1 1.0 %final.1 = f32[9,16,56]{2,1,0:T(8,128)} custom-call(f32[9,16,128]{2,1,0:T(8,128)S(1)} %get-tuple-element.85.base_ref, f32[144,512]{1,0:T(8,128)S(1)} %get-tuple-element.86.ghost_flux_ref, bf16[4,384,256]{2,1,0:T(8,128)(2,1)S(1)} %get-tuple-element.87.ghost_operator_ref, bf16[144,256]{1,0:T(8,128)(2,1)S(1)} %get-tuple-element.88.scatter_ref, ...), custom_call_target="tpu_custom_call" | custom-call | flops 200000000 | bytes 4000000 | tf_op jit(solution)/shard_map/final/pallas_call | solution.py:586
Async XLA Ops:
  2.8 9.2 %collective-permute-start = (f32[32,128]{1,0:T(8,128)S(1)}, f32[32,128]{1,0:T(8,128)S(1)}, u32[]{:S(2)}, u32[]{:S(2)}) collective-permute-start(f32[32,128]{1,0:T(8,128)S(1)} %get-tuple-element.72), channel_id=1, source_target_pairs={{4,8},{8,4},{12,16},{16,12},{20,24},{24,20},{28,0},{0,28},{5,9},{9... | collective-permute-start | bytes 49160 | tf_op jit(solution)/shard_map/ppermute | solution.py:607
  8.8 3.7 %collective-permute-start.1 = (f32[32,128]{1,0:T(8,128)S(1)}, f32[32,128]{1,0:T(8,128)S(1)}, u32[]{:S(2)}, u32[]{:S(2)}) collective-permute-start(f32[32,128]{1,0:T(8,128)S(1)} %get-tuple-element.73), channel_id=1, source_target_pairs={{0,4},{4,0},{8,12},{12,8},{16,20},{20,16},{24,28},{28,24},{1,5},{5... | collective-permute-start | bytes 49160 | tf_op jit(solution)/shard_map/ppermute | solution.py:607
  8.8 3.7 %collective-permute-start.2 = (f32[32,128]{1,0:T(8,128)S(1)}, f32[32,128]{1,0:T(8,128)S(1)}, u32[]{:S(2)}, u32[]{:S(2)}) collective-permute-start(f32[32,128]{1,0:T(8,128)S(1)} %get-tuple-element.74), channel_id=1, source_target_pairs={{1,2},{2,1},{3,0},{0,3},{5,6},{6,5},{7,4},{4,7},{9,10},{10,9},{11,... | collective-permute-start | bytes 49160 | tf_op jit(solution)/shard_map/ppermute | solution.py:607
  9.5 3.1 %collective-permute-start.3 = (f32[32,128]{1,0:T(8,128)S(1)}, f32[32,128]{1,0:T(8,128)S(1)}, u32[]{:S(2)}, u32[]{:S(2)}) collective-permute-start(f32[32,128]{1,0:T(8,128)S(1)} %get-tuple-element.75), channel_id=1, source_target_pairs={{0,1},{1,0},{2,3},{3,2},{4,5},{5,4},{6,7},{7,6},{8,9},{9,8},{10,11... | collective-permute-start | bytes 49160 | tf_op jit(solution)/shard_map/ppermute | solution.py:607
  14.6 6.4 %collective-permute-start.4 = (f32[16,128]{1,0:T(8,128)S(1)}, f32[16,128]{1,0:T(8,128)S(1)}, u32[]{:S(2)}, u32[]{:S(2)}) collective-permute-start(f32[16,128]{1,0:T(8,128)S(1)} %get-tuple-element.89), channel_id=1, source_target_pairs={{4,8},{8,4},{12,16},{16,12},{20,24},{24,20},{28,0},{0,28},{5,9},{9... | collective-permute-start | bytes 24584 | tf_op jit(solution)/shard_map/ppermute | solution.py:607
  17.3 3.7 %collective-permute-start.5 = (f32[16,128]{1,0:T(8,128)S(1)}, f32[16,128]{1,0:T(8,128)S(1)}, u32[]{:S(2)}, u32[]{:S(2)}) collective-permute-start(f32[16,128]{1,0:T(8,128)S(1)} %get-tuple-element.90), channel_id=1, source_target_pairs={{0,4},{4,0},{8,12},{12,8},{16,20},{20,16},{24,28},{28,24},{1,5},{5... | collective-permute-start | bytes 24584 | tf_op jit(solution)/shard_map/ppermute | solution.py:607
  17.3 3.7 %collective-permute-start.6 = (f32[16,128]{1,0:T(8,128)S(1)}, f32[16,128]{1,0:T(8,128)S(1)}, u32[]{:S(2)}, u32[]{:S(2)}) collective-permute-start(f32[16,128]{1,0:T(8,128)S(1)} %get-tuple-element.91), channel_id=1, source_target_pairs={{1,2},{2,1},{3,0},{0,3},{5,6},{6,5},{7,4},{4,7},{9,10},{10,9},{11,... | collective-permute-start | bytes 24584 | tf_op jit(solution)/shard_map/ppermute | solution.py:607
  17.3 3.7 %collective-permute-start.7 = (f32[16,128]{1,0:T(8,128)S(1)}, f32[16,128]{1,0:T(8,128)S(1)}, u32[]{:S(2)}, u32[]{:S(2)}) collective-permute-start(f32[16,128]{1,0:T(8,128)S(1)} %get-tuple-element.92), channel_id=1, source_target_pairs={{0,1},{1,0},{2,3},{3,2},{4,5},{5,4},{6,7},{7,6},{8,9},{9,8},{10,11... | collective-permute-start | bytes 24584 | tf_op jit(solution)/shard_map/ppermute | solution.py:607

commit v14 on v13

--- a/solution.py
+++ b/solution.py
@@ -1,3 +1,4 @@
+import functools
 import math
 
 import jax
@@ -150,7 +151,7 @@
     early_out, late_out, send_0, send_1, send_2, send_3 = refs[0:6]
     packed_ref, coef_ref, derive_ref, stiffness_ref, early_rows = refs[6:11]
     later_out, refs = refs[11 : 11 + later], refs[11 + later :]
-    work_ref, late_rows, solution_ref, block_ref, star_ref, send_ref, sems = refs
+    work_ref, late_rows, early_squeezed, late_squeezed, solution_ref, block_ref, star_ref, send_ref, sems = refs
 
     sources = (star_hbm, stiffness_hbm, solution_hbm, send_hbm, *later_hbm)
     targets = (star_ref, stiffness_ref, solution_ref, send_ref, *later_out)
@@ -162,7 +163,7 @@
         copy.start()
     fields, kinds = star_ref.shape[0], star_ref.shape[2]
     pairs = (fields + 1) // 2
-    for cleared in (packed_ref, block_ref, send_0, send_1, send_2, send_3):
+    for cleared in (packed_ref, block_ref):
         cleared[...] = jnp.zeros(cleared.shape, F32)
     for copy in copies[0:3]:
         copy.wait()
@@ -186,19 +187,22 @@
     late_out[...] = late.reshape(fields, ROWS, LANES)
     rows_by_pair(early, early_rows, fields)
     rows_by_pair(late, late_rows, fields)
+    modes = solution_ref.shape[2]
+    squeeze(early_rows, early_squeezed, modes)
+    squeeze(late_rows, late_squeezed, modes)
     copies[3].wait()
     sends = send_ref.shape[2]
     fast = sends // 2
     for side, out in enumerate((send_0, send_1, send_2, send_3)):
         for place in range(sends):
             element = send_ref[0, message_side(side), place]
-            for pair in range(pairs):
+            for pair in range(pairs - 1):
                 row = pair * sends + place
-                out[row : row + 1, :] = early_rows[pair, pl.ds(element, 1), :]
+                out[row : row + 1, :] = early_squeezed[pair, pl.ds(element, 1), :]
             if place >= fast:
-                for pair in range(pairs):
-                    row = pairs * sends + pair * fast + place - fast
-                    out[row : row + 1, :] = late_rows[pair, pl.ds(element, 1), :]
+                for pair in range(pairs - 1):
+                    row = (pairs - 1) * sends + pair * fast + place - fast
+                    out[row : row + 1, :] = late_squeezed[pair, pl.ds(element, 1), :]
     for copy in copies[4:]:
         copy.wait()
 
@@ -212,6 +216,37 @@
             odd = packed[(2 * pair + 1) * ROWS : (2 * pair + 2) * ROWS]
         out_ref[pair, 0:ROWS, :] = jnp.where(lower, even, swap_halves(odd))
         out_ref[pair, ROWS : 2 * ROWS, :] = jnp.where(lower, swap_halves(even), odd)
+
+
+def last_pieces(pairs, modes):
+    gap = HALF - modes
+    pieces = []
+    for pair in range(pairs - 1):
+        for half in range(2):
+            first = half * HALF + modes
+            pieces.append((pair, first, first - (2 * pair + half) * gap))
+    assert len(pieces) * gap >= modes
+    return pieces
+
+
+def squeeze(rows_ref, out_ref, modes):
+    pairs = rows_ref.shape[0]
+    lanes = lane_index(rows_ref.shape[1:])
+    for pair in range(pairs - 1):
+        out_ref[pair] = rows_ref[pair]
+    for pair, first, shift in last_pieces(pairs, modes):
+        here = (lanes >= first) & (lanes < first + HALF - modes)
+        out_ref[pair] = jnp.where(here, pltpu.roll(rows_ref[pairs - 1], shift, 1), out_ref[pair])
+
+
+def unsqueeze(rows, modes):
+    lanes = lane_index(rows[0].shape)
+    last = None
+    for pair, first, shift in last_pieces(len(rows) + 1, modes):
+        here = (lanes >= first) & (lanes < first + HALF - modes)
+        piece = pltpu.roll(jnp.where(here, rows[pair], 0.0), LANES - shift, 1)
+        last = piece if last is None else last + piece
+    return last
 
 
 def flux_local_coefficients(flux_ref, stage_ref, out_ref):
@@ -476,7 +511,7 @@
 
 
 def middle_kernel(
-    base_ref, early_rows, late_ref, star_ref, remote_ref, derive_ref, compose_ref, lift_ref, choose_ref, mask_ref,
+    modes, base_ref, early_rows, late_ref, star_ref, remote_ref, derive_ref, compose_ref, lift_ref, choose_ref, mask_ref,
     fast_ref, send_hbm, from_0, from_1, from_2, from_3,
     middle_out, late_out, send_0, send_1, send_2, send_3,
     rows_ref, late_rows, send_ref, sem,
@@ -485,13 +520,15 @@
     copy.start()
     fields = base_ref.shape[0]
     kinds = star_ref.shape[0] // (fields * fields)
-    pairs = rows_ref.shape[0]
+    pairs = early_rows.shape[0]
     sends = send_ref.shape[2]
     fast = sends // 2
     for side, arrived in enumerate((from_0, from_1, from_2, from_3)):
-        for pair in range(pairs):
+        for pair in range(pairs - 1):
             rows_ref[pair, side * sends : (side + 1) * sends, :] = arrived[pair * sends : (pair + 1) * sends, :]
-    rows = [jnp.concatenate([early_rows[pair], rows_ref[pair]], axis=0) for pair in range(pairs)]
+    ghosts = [rows_ref[pair] for pair in range(pairs - 1)]
+    ghosts.append(unsqueeze(ghosts, modes))
+    rows = [jnp.concatenate([early_rows[pair], ghosts[pair]], axis=0) for pair in range(pairs)]
     middle = base_ref[...] + remote_terms(rows, remote_ref, compose_ref, lift_ref, choose_ref, mask_ref, fields)
     middle_out[...] = middle
     start = middle.reshape(fields * ROWS, LANES)
@@ -522,7 +559,7 @@
 
 
 def local_kernel(
-    middle_ref, late_ref, star_ref, flux_ref, volume_ref, trace_ref, lift_ref,
+    modes, middle_ref, late_ref, star_ref, flux_ref, volume_ref, trace_ref, lift_ref,
     remote_ref, compose_ref, remote_lift_ref, choose_ref, mask_ref, flux_remote_ref, code_ref, composed_ref, sides_ref,
     orient_ref, first_0, first_1, first_2, first_3,
     base_out, ghost_flux_out, ghost_operator_out, scatter_out, rows_ref, stage_ref,
@@ -537,10 +574,12 @@
     rows_by_pair(late, rows_ref, fields)
     for slot, first in enumerate((first_0, first_1, first_2, first_3)):
         at = elements + slot * sends
-        for pair in range(pairs):
+        for pair in range(pairs - 1):
             rows_ref[pair, at : at + fast, :] = jnp.zeros((fast, LANES), F32)
-            row = pairs * sends + pair * fast
+            row = (pairs - 1) * sends + pair * fast
             rows_ref[pair, at + fast : at + sends, :] = first[row : row + fast, :]
+    ghosts = [rows_ref[pair, elements:, :] for pair in range(pairs - 1)]
+    rows_ref[pairs - 1, elements:, :] = unsqueeze(ghosts, modes)
     terms = local_terms(late, star_ref, flux_ref, volume_ref, trace_ref, lift_ref, fields, kinds)
     rows = [rows_ref[pair] for pair in range(pairs)]
     remote = remote_terms(rows, remote_ref, compose_ref, remote_lift_ref, choose_ref, mask_ref, fields)
@@ -616,13 +655,13 @@
     solution, stiffness, star_matrices, face_restrict, face_lift, orient_maps, flux_local, flux_remote,
     cluster_rate, send_list, neighbour_slot, neighbour_face, neighbour_turn,
 ):
-    fields, elements = solution.shape[1], solution.shape[2]
+    modes, fields, elements = solution.shape
     kinds = stiffness.shape[0]
     faces = face_restrict.shape[0]
     sides, sends = send_list.shape[1], send_list.shape[2]
     fast = sends // 2
     pairs = (fields + 1) // 2
-    assert elements == 2 * ROWS and solution.shape[0] <= HALF and fast == 2
+    assert elements == 2 * ROWS and modes <= HALF and fast == 2 and fields % 2 == 1
     values = jnp.transpose(solution, (1, 2, 0))
     star = jnp.transpose(star_matrices, (1, 2, 0, 3))
     local_part = jnp.transpose(flux_local, (1, 2, 0, 3))
@@ -631,7 +670,7 @@
     lift = jnp.transpose(face_lift, (2, 0, 1))
 
     packed = (fields, ROWS, LANES)
-    first_shape = (up_to(pairs * (sends + fast), ROWS), LANES)
+    first_shape = (up_to((pairs - 1) * (sends + fast), ROWS), LANES)
     second_shape = (up_to(fields, 2 * ROWS), LANES)
     star_shape = (fields * fields * kinds, ROWS, LANES)
     combos = faces * HALF
@@ -651,6 +690,7 @@
         [
             ((fields, up_to(4 * fields, ROWS), LANES), F32),
             ((pairs, elements, LANES), F32),
+            ((pairs - 1, elements, LANES), F32), ((pairs - 1, elements, LANES), F32),
             (values.shape, F32), ((kinds, LANES, LANES), F32), (star.shape, F32),
             pltpu.SMEM(send_list.shape, jnp.int32), pltpu.SemaphoreType.DMA((4 + len(LATER),)),
         ],
@@ -685,7 +725,7 @@
         "prepare", 200_000_000,
     )
     middle, late_value, *outgoing = call(
-        middle_kernel,
+        functools.partial(middle_kernel, modes),
         [VMEM] * 11 + [HBM] + [VMEM] * 4,
         [(packed, F32)] * 2 + [(second_shape, F32)] * sides,
         [
@@ -700,7 +740,7 @@
     )
     second = exchange(outgoing)
     base, ghost_flux, ghost_op, scatter = call(
-        local_kernel,
+        functools.partial(local_kernel, modes),
         [VMEM] * (17 + len(first)),
         [
             ((fields, elements, LANES), F32), ((fields * second_shape[0], sides * LANES), F32),

time: 22.3 us -> 22.3 us (level)
  no operation moved by 1% of the time
where the time goes in v14:
time: 22.3 us; the launch traced here: 22.2 us
  starting transfers between devices  12.1 us (54%)
  Pallas kernels  8.73 us (39%)
  waiting for transfers between devices  1.33 us (6%)
    ppermute x8, starting transfers between devices, exchange(): arrived.append(lax.ppermute(message, axis, pairs))  12.1 us
    pallas_call x5, Pallas kernels, call(): pl.pallas_call(kernel, out_shape=shapes, in_specs=ins, out_specs=[VMEM] *...  8.73 us
    ppermute x8, waiting for transfers between devices, exchange(): arrived.append(lax.ppermute(message, axis, pairs))  1.33 us
  transfers between devices with their start and end apart: 8, of which 3 were waited for; matrix products, arithmetic and copies ran while one was open for 0% of the time, Pallas kernels for 13%

profile of v14, /device:TPU:0, one launch (start us, length us, event | category | flops | bytes accessed | tf_op | source)
XLA Modules:
  0.0 22.2 jit_solution(12902391946447542208)
XLA Ops:
  0.0 2.8 %predict.1 = (f32[9,8,128]{2,1,0:T(8,128)S(1)}, f32[9,8,128]{2,1,0:T(8,128)S(1)}, f32[24,128]{1,0:T(8,128)S(1)}, f32[24,128]{1,0:T(8,128)S(1)}, f32[24,128]{1,0:...) custom-call(f32[9,16,56]{2,1,0:T(8,128)} %bitcast.11, ...), custom_call_target="tpu_custom_call" | custom-call | flops 100000000 | bytes 4000000 | tf_op jit(solution)/shard_map/predict/pallas_call | solution.py:625
  2.8 6.0 %collective-permute-start = (f32[24,128]{1,0:T(8,128)S(1)}, f32[24,128]{1,0:T(8,128)S(1)}, u32[]{:S(2)}, u32[]{:S(2)}) collective-permute-start(f32[24,128]{1,0:T(8,128)S(1)} %get-tuple-element.72), channel_id=1, source_target_pairs={{4,8},{8,4},{12,16},{16,12},{20,24},{24,20},{28,0},{0,28},{5,9},{9... | collective-permute-start | bytes 36872 | tf_op jit(solution)/shard_map/ppermute | solution.py:646
  8.8 0.0 collective-permute-start.1
  8.8 0.7 %collective-permute-start.2 = (f32[24,128]{1,0:T(8,128)S(1)}, f32[24,128]{1,0:T(8,128)S(1)}, u32[]{:S(2)}, u32[]{:S(2)}) collective-permute-start(f32[24,128]{1,0:T(8,128)S(1)} %get-tuple-element.74), channel_id=1, source_target_pairs={{1,2},{2,1},{3,0},{0,3},{5,6},{6,5},{7,4},{4,7},{9,10},{10,9},{11,... | collective-permute-start | bytes 36872 | tf_op jit(solution)/shard_map/ppermute | solution.py:646
  9.5 1.0 %collective-permute-start.3 = (f32[24,128]{1,0:T(8,128)S(1)}, f32[24,128]{1,0:T(8,128)S(1)}, u32[]{:S(2)}, u32[]{:S(2)}) collective-permute-start(f32[24,128]{1,0:T(8,128)S(1)} %get-tuple-element.75), channel_id=1, source_target_pairs={{0,1},{1,0},{2,3},{3,2},{4,5},{5,4},{6,7},{7,6},{8,9},{9,8},{10,11... | collective-permute-start | bytes 36872 | tf_op jit(solution)/shard_map/ppermute | solution.py:646
  10.5 1.5 %prepare.1 = (f32[9,8,128]{2,1,0:T(8,128)S(1)}, f32[81,2,8,128]{3,2,1,0:T(8,128)S(1)}, f32[180,16,128]{2,1,0:T(8,128)S(1)}, bf16[384,384]{1,0:T(8,128)(2,1)S(1)}...) custom-call(f32[9,8,128]{2,1,0:T(8,128)S(1)} %get-tuple-element.49.p, ...), custom_call_target="tpu_custom_call" | custom-call | flops 200000000 | bytes 4000000 | tf_op jit(solution)/shard_map/prepare/pallas_call | solution.py:625
  12.0 0.0 collective-permute-done.from_0.first_0
  12.0 0.6 %collective-permute-done.1.from_1.first_1 = f32[24,128]{1,0:T(8,128)S(1)} collective-permute-done((f32[24,128]{1,0:T(8,128)S(1)}, f32[24,128]{1,0:T(8,128)S(1)}, u32[]{:S(2)}, u32[]{:S(2)}) %collective-permute-start.1) | collective-permute-done | bytes 12320 | tf_op jit(solution)/shard_map/ppermute | solution.py:646
  12.5 0.0 collective-permute-done.2.from_2.first_2
  12.5 0.0 collective-permute-done.3.from_3.first_3
  12.5 2.1 %middle.1 = (f32[9,8,128]{2,1,0:T(8,128)S(1)}, f32[9,8,128]{2,1,0:T(8,128)S(1)}, f32[16,128]{1,0:T(8,128)S(1)}, f32[16,128]{1,0:T(8,128)S(1)}, f32[16,128]{1,0:T(8,128)S(1)}, /*index=5*/f32[16,128]{1,0:T(8,128)S(1)}) custom-call(f32[9,8,128]{2,1,0:T(8,128)S(1)} %get-tuple-element.62.base_ref, f32[5,16,128]{2,1,0:T(8,128)S(1)} %get-tuple-element.63.early_rows, ...), custom_call_target="tpu_custom_call" | custom-call | flops 200000000 | bytes 4000000 | tf_op jit(solution)/shard_map/middle/pallas_call | solution.py:625
  14.6 2.8 %collective-permute-start.4 = (f32[16,128]{1,0:T(8,128)S(1)}, f32[16,128]{1,0:T(8,128)S(1)}, u32[]{:S(2)}, u32[]{:S(2)}) collective-permute-start(f32[16,128]{1,0:T(8,128)S(1)} %get-tuple-element.89), channel_id=1, source_target_pairs={{4,8},{8,4},{12,16},{16,12},{20,24},{24,20},{28,0},{0,28},{5,9},{9... | collective-permute-start | bytes 24584 | tf_op jit(solution)/shard_map/ppermute | solution.py:646
  17.4 0.0 collective-permute-start.5
  17.4 0.0 collective-permute-start.6
  17.4 1.6 %collective-permute-start.7 = (f32[16,128]{1,0:T(8,128)S(1)}, f32[16,128]{1,0:T(8,128)S(1)}, u32[]{:S(2)}, u32[]{:S(2)}) collective-permute-start(f32[16,128]{1,0:T(8,128)S(1)} %get-tuple-element.92), channel_id=1, source_target_pairs={{0,1},{1,0},{2,3},{3,2},{4,5},{5,4},{6,7},{7,6},{8,9},{9,8},{10,11... | collective-permute-start | bytes 24584 | tf_op jit(solution)/shard_map/ppermute | solution.py:646
  19.0 1.3 %local_late.1 = (f32[9,16,128]{2,1,0:T(8,128)S(1)}, f32[144,512]{1,0:T(8,128)S(1)}, bf16[4,384,256]{2,1,0:T(8,128)(2,1)S(1)}, bf16[144,256]{1,0:T(8,128)(2,1)S(1)}) custom-call(f32[9,8,128]{2,1,0:T(8,128)S(1)} %get-tuple-element.76.middle_ref, f32[9,8,128]{2,1,0:T(8,128)S(1)} %get-tuple-element.77.late_ref, f32[243,8,128]{2,1,0:T(8,128)S(1)} %get-tuple-element.52.star_ref, ...), custom_call_target="tpu_custom_call" | custom-call | flops 200000000 | bytes 4000000 | tf_op jit(solution)/shard_map/local_late/pallas_call | solution.py:625
  20.4 0.7 %collective-permute-done.4.second_0 = f32[16,128]{1,0:T(8,128)S(1)} collective-permute-done((f32[16,128]{1,0:T(8,128)S(1)}, f32[16,128]{1,0:T(8,128)S(1)}, u32[]{:S(2)}, u32[]{:S(2)}) %collective-permute-start.4) | collective-permute-done | bytes 8224 | tf_op jit(solution)/shard_map/ppermute | solution.py:646
  21.1 0.1 collective-permute-done.5.second_1
  21.1 0.0 collective-permute-done.6.second_2
  21.1 0.0 collective-permute-done.7.second_3
  21.1 1.0 %final.1 = f32[9,16,56]{2,1,0:T(8,128)} custom-call(f32[9,16,128]{2,1,0:T(8,128)S(1)} %get-tuple-element.85.base_ref, f32[144,512]{1,0:T(8,128)S(1)} %get-tuple-element.86.ghost_flux_ref, bf16[4,384,256]{2,1,0:T(8,128)(2,1)S(1)} %get-tuple-element.87.ghost_operator_ref, bf16[144,256]{1,0:T(8,128)(2,1)S(1)} %get-tuple-element.88.scatter_ref, ...), custom_call_target="tpu_custom_call" | custom-call | flops 200000000 | bytes 4000000 | tf_op jit(solution)/shard_map/final/pallas_call | solution.py:625
Async XLA Ops:
  2.8 9.2 %collective-permute-start = (f32[24,128]{1,0:T(8,128)S(1)}, f32[24,128]{1,0:T(8,128)S(1)}, u32[]{:S(2)}, u32[]{:S(2)}) collective-permute-start(f32[24,128]{1,0:T(8,128)S(1)} %get-tuple-element.72), channel_id=1, source_target_pairs={{4,8},{8,4},{12,16},{16,12},{20,24},{24,20},{28,0},{0,28},{5,9},{9... | collective-permute-start | bytes 36872 | tf_op jit(solution)/shard_map/ppermute | solution.py:646
  8.8 3.7 %collective-permute-start.1 = (f32[24,128]{1,0:T(8,128)S(1)}, f32[24,128]{1,0:T(8,128)S(1)}, u32[]{:S(2)}, u32[]{:S(2)}) collective-permute-start(f32[24,128]{1,0:T(8,128)S(1)} %get-tuple-element.73), channel_id=1, source_target_pairs={{0,4},{4,0},{8,12},{12,8},{16,20},{20,16},{24,28},{28,24},{1,5},{5... | collective-permute-start | bytes 36872 | tf_op jit(solution)/shard_map/ppermute | solution.py:646
  8.8 3.7 %collective-permute-start.2 = (f32[24,128]{1,0:T(8,128)S(1)}, f32[24,128]{1,0:T(8,128)S(1)}, u32[]{:S(2)}, u32[]{:S(2)}) collective-permute-start(f32[24,128]{1,0:T(8,128)S(1)} %get-tuple-element.74), channel_id=1, source_target_pairs={{1,2},{2,1},{3,0},{0,3},{5,6},{6,5},{7,4},{4,7},{9,10},{10,9},{11,... | collective-permute-start | bytes 36872 | tf_op jit(solution)/shard_map/ppermute | solution.py:646
  9.5 3.0 %collective-permute-start.3 = (f32[24,128]{1,0:T(8,128)S(1)}, f32[24,128]{1,0:T(8,128)S(1)}, u32[]{:S(2)}, u32[]{:S(2)}) collective-permute-start(f32[24,128]{1,0:T(8,128)S(1)} %get-tuple-element.75), channel_id=1, source_target_pairs={{0,1},{1,0},{2,3},{3,2},{4,5},{5,4},{6,7},{7,6},{8,9},{9,8},{10,11... | collective-permute-start | bytes 36872 | tf_op jit(solution)/shard_map/ppermute | solution.py:646
  14.6 6.4 %collective-permute-start.4 = (f32[16,128]{1,0:T(8,128)S(1)}, f32[16,128]{1,0:T(8,128)S(1)}, u32[]{:S(2)}, u32[]{:S(2)}) collective-permute-start(f32[16,128]{1,0:T(8,128)S(1)} %get-tuple-element.89), channel_id=1, source_target_pairs={{4,8},{8,4},{12,16},{16,12},{20,24},{24,20},{28,0},{0,28},{5,9},{9... | collective-permute-start | bytes 24584 | tf_op jit(solution)/shard_map/ppermute | solution.py:646
  17.4 3.7 %collective-permute-start.5 = (f32[16,128]{1,0:T(8,128)S(1)}, f32[16,128]{1,0:T(8,128)S(1)}, u32[]{:S(2)}, u32[]{:S(2)}) collective-permute-start(f32[16,128]{1,0:T(8,128)S(1)} %get-tuple-element.90), channel_id=1, source_target_pairs={{0,4},{4,0},{8,12},{12,8},{16,20},{20,16},{24,28},{28,24},{1,5},{5... | collective-permute-start | bytes 24584 | tf_op jit(solution)/shard_map/ppermute | solution.py:646
  17.4 3.7 %collective-permute-start.6 = (f32[16,128]{1,0:T(8,128)S(1)}, f32[16,128]{1,0:T(8,128)S(1)}, u32[]{:S(2)}, u32[]{:S(2)}) collective-permute-start(f32[16,128]{1,0:T(8,128)S(1)} %get-tuple-element.91), channel_id=1, source_target_pairs={{1,2},{2,1},{3,0},{0,3},{5,6},{6,5},{7,4},{4,7},{9,10},{10,9},{11,... | collective-permute-start | bytes 24584 | tf_op jit(solution)/shard_map/ppermute | solution.py:646
  17.4 3.7 %collective-permute-start.7 = (f32[16,128]{1,0:T(8,128)S(1)}, f32[16,128]{1,0:T(8,128)S(1)}, u32[]{:S(2)}, u32[]{:S(2)}) collective-permute-start(f32[16,128]{1,0:T(8,128)S(1)} %get-tuple-element.92), channel_id=1, source_target_pairs={{0,1},{1,0},{2,3},{3,2},{4,5},{5,4},{6,7},{7,6},{8,9},{9,8},{10,11... | collective-permute-start | bytes 24584 | tf_op jit(solution)/shard_map/ppermute | solution.py:646

commit v15 on v13

--- a/solution.py
+++ b/solution.py
@@ -152,11 +152,14 @@
     later_out, refs = refs[11 : 11 + later], refs[11 + later :]
     work_ref, late_rows, solution_ref, block_ref, star_ref, send_ref, sems = refs
 
-    sources = (star_hbm, stiffness_hbm, solution_hbm, send_hbm, *later_hbm)
-    targets = (star_ref, stiffness_ref, solution_ref, send_ref, *later_out)
+    pieces = []
+    for source, target in ((star_hbm, star_ref), (stiffness_hbm, stiffness_ref), (solution_hbm, solution_ref)):
+        step = source.shape[0] // 3
+        pieces += [(source.at[pl.ds(at, step)], target.at[pl.ds(at, step)]) for at in range(0, source.shape[0], step)]
+    first = len(pieces)
+    pieces += zip((send_hbm, *later_hbm), (send_ref, *later_out))
     copies = [
-        pltpu.make_async_copy(source, target, sems.at[number])
-        for number, (source, target) in enumerate(zip(sources, targets))
+        pltpu.make_async_copy(source, target, sems.at[number]) for number, (source, target) in enumerate(pieces)
     ]
     for copy in copies:
         copy.start()
@@ -164,7 +167,7 @@
     pairs = (fields + 1) // 2
     for cleared in (packed_ref, block_ref, send_0, send_1, send_2, send_3):
         cleared[...] = jnp.zeros(cleared.shape, F32)
-    for copy in copies[0:3]:
+    for copy in copies[0:first]:
         copy.wait()
     derive_ref[...] = stack_right(stiffness_blocks(stiffness_ref, block_ref, True))
     star_coefficients(star_ref, work_ref, coef_ref)
@@ -186,7 +189,7 @@
     late_out[...] = late.reshape(fields, ROWS, LANES)
     rows_by_pair(early, early_rows, fields)
     rows_by_pair(late, late_rows, fields)
-    copies[3].wait()
+    copies[first].wait()
     sends = send_ref.shape[2]
     fast = sends // 2
     for side, out in enumerate((send_0, send_1, send_2, send_3)):
@@ -199,7 +202,7 @@
                 for pair in range(pairs):
                     row = pairs * sends + pair * fast + place - fast
                     out[row : row + 1, :] = late_rows[pair, pl.ds(element, 1), :]
-    for copy in copies[4:]:
+    for copy in copies[first + 1 :]:
         copy.wait()
 
 
@@ -555,10 +558,11 @@
 
 
 def final_kernel(
-    base_ref, ghost_flux_ref, ghost_operator_ref, scatter_ref, second_0, second_1, second_2, second_3, result_out,
+    base_ref, ghost_flux_ref, ghost_operator_ref, scatter_ref, second_0, second_1, second_2, second_3, result_hbm,
+    result_ref, sems,
 ):
     fields = base_ref.shape[0]
-    modes = result_out.shape[2]
+    modes = result_ref.shape[2]
     rows = second_0.shape[0]
     added = []
     for slot, second in enumerate((second_0, second_1, second_2, second_3)):
@@ -571,14 +575,20 @@
         added += [both[:, 0:LANES], both[:, LANES : 2 * LANES]]
     right = jnp.concatenate(split(jnp.concatenate(added, axis=0)), axis=0)
     result = base_ref[...] + product(scatter_ref[...], right).reshape(base_ref.shape)
-    result_out[...] = result[:, :, 0:modes]
+    copies = []
+    for field in range(fields):
+        result_ref[field] = result[field, :, 0:modes]
+        copies.append(pltpu.make_async_copy(result_ref.at[field], result_hbm.at[field], sems.at[field]))
+        copies[-1].start()
+    for copy in copies:
+        copy.wait()
 
 
 VMEM = pl.BlockSpec(memory_space=pltpu.VMEM)
 HBM = pl.BlockSpec(memory_space=pltpu.HBM)
 
 
-def call(kernel, ins, outs, scratch, args, name, flops):
+def call(kernel, ins, outs, scratch, args, name, flops, out_spec=VMEM):
     shapes = [jax.ShapeDtypeStruct(shape, dtype) for shape, dtype in outs]
     args = [
         pltpu.with_memory_space_constraint(arg, pltpu.HBM) if spec is HBM else arg for spec, arg in zip(ins, args)
@@ -587,7 +597,7 @@
         kernel,
         out_shape=shapes,
         in_specs=ins,
-        out_specs=[VMEM] * len(outs),
+        out_specs=[out_spec] * len(outs),
         scratch_shapes=[pltpu.VMEM(*one) if isinstance(one, tuple) else one for one in scratch],
         compiler_params=pltpu.CompilerParams(vmem_limit_bytes=16 * 1024 * 1024),
         cost_estimate=pl.CostEstimate(flops=flops, bytes_accessed=4_000_000, transcendentals=0),
@@ -652,7 +662,7 @@
             ((fields, up_to(4 * fields, ROWS), LANES), F32),
             ((pairs, elements, LANES), F32),
             (values.shape, F32), ((kinds, LANES, LANES), F32), (star.shape, F32),
-            pltpu.SMEM(send_list.shape, jnp.int32), pltpu.SemaphoreType.DMA((4 + len(LATER),)),
+            pltpu.SMEM(send_list.shape, jnp.int32), pltpu.SemaphoreType.DMA((10 + len(LATER),)),
         ],
         (values, stiffness, star, send_list, *waiting),
         "predict", 100_000_000,
@@ -718,9 +728,9 @@
         final_kernel,
         [VMEM] * 8,
         [(values.shape, F32)],
-        [],
+        [(values.shape, F32), pltpu.SemaphoreType.DMA((fields,))],
         (base, ghost_flux, ghost_op, scatter, *second),
-        "final", 200_000_000,
+        "final", 200_000_000, HBM,
     )
     return jnp.transpose(result, (2, 0, 1))
 

time: 22.3 us -> 22.3 us (level)
  no operation moved by 1% of the time
where the time goes in v15:
time: 22.3 us; the launch traced here: 22.1 us
  starting transfers between devices  12.1 us (54%)
  Pallas kernels  8.6 us (39%)
  waiting for transfers between devices  1.39 us (6%)
    ppermute x8, starting transfers between devices, exchange(): arrived.append(lax.ppermute(message, axis, pairs))  12.1 us
    pallas_call x5, Pallas kernels, call(): pl.pallas_call(kernel, out_shape=shapes, in_specs=ins, out_specs=[out_spe...  8.6 us
    ppermute x8, waiting for transfers between devices, exchange(): arrived.append(lax.ppermute(message, axis, pairs))  1.39 us
  transfers between devices with their start and end apart: 8, of which 3 were waited for; matrix products, arithmetic and copies ran while one was open for 0% of the time, Pallas kernels for 13%

profile of v15, /device:TPU:0, one launch (start us, length us, event | category | flops | bytes accessed | tf_op | source)
XLA Modules:
  0.0 22.1 jit_solution(16889369916077298534)
XLA Ops:
  0.0 2.7 %predict.1 = (f32[9,8,128]{2,1,0:T(8,128)S(1)}, f32[9,8,128]{2,1,0:T(8,128)S(1)}, f32[32,128]{1,0:T(8,128)S(1)}, f32[32,128]{1,0:T(8,128)S(1)}, f32[32,128]{1,0:...) custom-call(f32[9,16,56]{2,1,0:T(8,128)} %bitcast.11, ...), custom_call_target="tpu_custom_call" | custom-call | flops 100000000 | bytes 4000000 | tf_op jit(solution)/shard_map/predict/pallas_call | solution.py:596
  2.7 6.0 %collective-permute-start = (f32[32,128]{1,0:T(8,128)S(1)}, f32[32,128]{1,0:T(8,128)S(1)}, u32[]{:S(2)}, u32[]{:S(2)}) collective-permute-start(f32[32,128]{1,0:T(8,128)S(1)} %get-tuple-element.72), channel_id=1, source_target_pairs={{4,8},{8,4},{12,16},{16,12},{20,24},{24,20},{28,0},{0,28},{5,9},{9... | collective-permute-start | bytes 49160 | tf_op jit(solution)/shard_map/ppermute | solution.py:617
  8.7 0.0 collective-permute-start.1
  8.7 0.7 %collective-permute-start.2 = (f32[32,128]{1,0:T(8,128)S(1)}, f32[32,128]{1,0:T(8,128)S(1)}, u32[]{:S(2)}, u32[]{:S(2)}) collective-permute-start(f32[32,128]{1,0:T(8,128)S(1)} %get-tuple-element.74), channel_id=1, source_target_pairs={{1,2},{2,1},{3,0},{0,3},{5,6},{6,5},{7,4},{4,7},{9,10},{10,9},{11,... | collective-permute-start | bytes 49160 | tf_op jit(solution)/shard_map/ppermute | solution.py:617
  9.4 1.0 %collective-permute-start.3 = (f32[32,128]{1,0:T(8,128)S(1)}, f32[32,128]{1,0:T(8,128)S(1)}, u32[]{:S(2)}, u32[]{:S(2)}) collective-permute-start(f32[32,128]{1,0:T(8,128)S(1)} %get-tuple-element.75), channel_id=1, source_target_pairs={{0,1},{1,0},{2,3},{3,2},{4,5},{5,4},{6,7},{7,6},{8,9},{9,8},{10,11... | collective-permute-start | bytes 49160 | tf_op jit(solution)/shard_map/ppermute | solution.py:617
  10.4 1.5 %prepare.1 = (f32[9,8,128]{2,1,0:T(8,128)S(1)}, f32[81,2,8,128]{3,2,1,0:T(8,128)S(1)}, f32[180,16,128]{2,1,0:T(8,128)S(1)}, bf16[384,384]{1,0:T(8,128)(2,1)S(1)}...) custom-call(f32[9,8,128]{2,1,0:T(8,128)S(1)} %get-tuple-element.49.p, ...), custom_call_target="tpu_custom_call" | custom-call | flops 200000000 | bytes 4000000 | tf_op jit(solution)/shard_map/prepare/pallas_call | solution.py:596
  11.9 0.0 collective-permute-done.from_0.first_0
  11.9 0.6 %collective-permute-done.1.from_1.first_1 = f32[32,128]{1,0:T(8,128)S(1)} collective-permute-done((f32[32,128]{1,0:T(8,128)S(1)}, f32[32,128]{1,0:T(8,128)S(1)}, u32[]{:S(2)}, u32[]{:S(2)}) %collective-permute-start.1) | collective-permute-done | bytes 16416 | tf_op jit(solution)/shard_map/ppermute | solution.py:617
  12.5 0.0 collective-permute-done.2.from_2.first_2
  12.5 0.0 collective-permute-done.3.from_3.first_3
  12.5 2.0 %middle.1 = (f32[9,8,128]{2,1,0:T(8,128)S(1)}, f32[9,8,128]{2,1,0:T(8,128)S(1)}, f32[16,128]{1,0:T(8,128)S(1)}, f32[16,128]{1,0:T(8,128)S(1)}, f32[16,128]{1,0:T(8,128)S(1)}, /*index=5*/f32[16,128]{1,0:T(8,128)S(1)}) custom-call(f32[9,8,128]{2,1,0:T(8,128)S(1)} %get-tuple-element.62.base_ref, f32[5,16,128]{2,1,0:T(8,128)S(1)} %get-tuple-element.63.early_rows, ...), custom_call_target="tpu_custom_call" | custom-call | flops 200000000 | bytes 4000000 | tf_op jit(solution)/shard_map/middle/pallas_call | solution.py:596
  14.5 2.8 %collective-permute-start.4 = (f32[16,128]{1,0:T(8,128)S(1)}, f32[16,128]{1,0:T(8,128)S(1)}, u32[]{:S(2)}, u32[]{:S(2)}) collective-permute-start(f32[16,128]{1,0:T(8,128)S(1)} %get-tuple-element.89), channel_id=1, source_target_pairs={{4,8},{8,4},{12,16},{16,12},{20,24},{24,20},{28,0},{0,28},{5,9},{9... | collective-permute-start | bytes 24584 | tf_op jit(solution)/shard_map/ppermute | solution.py:617
  17.3 0.0 collective-permute-start.5
  17.3 0.0 collective-permute-start.6
  17.3 1.6 %collective-permute-start.7 = (f32[16,128]{1,0:T(8,128)S(1)}, f32[16,128]{1,0:T(8,128)S(1)}, u32[]{:S(2)}, u32[]{:S(2)}) collective-permute-start(f32[16,128]{1,0:T(8,128)S(1)} %get-tuple-element.92), channel_id=1, source_target_pairs={{0,1},{1,0},{2,3},{3,2},{4,5},{5,4},{6,7},{7,6},{8,9},{9,8},{10,11... | collective-permute-start | bytes 24584 | tf_op jit(solution)/shard_map/ppermute | solution.py:617
  18.9 1.3 %local_late.1 = (f32[9,16,128]{2,1,0:T(8,128)S(1)}, f32[144,512]{1,0:T(8,128)S(1)}, bf16[4,384,256]{2,1,0:T(8,128)(2,1)S(1)}, bf16[144,256]{1,0:T(8,128)(2,1)S(1)}) custom-call(f32[9,8,128]{2,1,0:T(8,128)S(1)} %get-tuple-element.76.middle_ref, f32[9,8,128]{2,1,0:T(8,128)S(1)} %get-tuple-element.77.late_ref, f32[243,8,128]{2,1,0:T(8,128)S(1)} %get-tuple-element.52.star_ref, ...), custom_call_target="tpu_custom_call" | custom-call | flops 200000000 | bytes 4000000 | tf_op jit(solution)/shard_map/local_late/pallas_call | solution.py:596
  20.2 0.7 %collective-permute-done.4.second_0 = f32[16,128]{1,0:T(8,128)S(1)} collective-permute-done((f32[16,128]{1,0:T(8,128)S(1)}, f32[16,128]{1,0:T(8,128)S(1)}, u32[]{:S(2)}, u32[]{:S(2)}) %collective-permute-start.4) | collective-permute-done | bytes 8224 | tf_op jit(solution)/shard_map/ppermute | solution.py:617
  20.9 0.1 collective-permute-done.5.second_1
  21.0 0.0 collective-permute-done.6.second_2
  21.0 0.0 collective-permute-done.7.second_3
  21.0 1.1 %final.1 = f32[9,16,56]{2,1,0:T(8,128)} custom-call(f32[9,16,128]{2,1,0:T(8,128)S(1)} %get-tuple-element.85.base_ref, f32[144,512]{1,0:T(8,128)S(1)} %get-tuple-element.86.ghost_flux_ref, bf16[4,384,256]{2,1,0:T(8,128)(2,1)S(1)} %get-tuple-element.87.ghost_operator_ref, bf16[144,256]{1,0:T(8,128)(2,1)S(1)} %get-tuple-element.88.scatter_ref, ...), custom_call_target="tpu_custom_call" | custom-call | flops 200000000 | bytes 4000000 | tf_op jit(solution)/shard_map/final/pallas_call | solution.py:596
Async XLA Ops:
  2.7 9.2 %collective-permute-start = (f32[32,128]{1,0:T(8,128)S(1)}, f32[32,128]{1,0:T(8,128)S(1)}, u32[]{:S(2)}, u32[]{:S(2)}) collective-permute-start(f32[32,128]{1,0:T(8,128)S(1)} %get-tuple-element.72), channel_id=1, source_target_pairs={{4,8},{8,4},{12,16},{16,12},{20,24},{24,20},{28,0},{0,28},{5,9},{9... | collective-permute-start | bytes 49160 | tf_op jit(solution)/shard_map/ppermute | solution.py:617
  8.7 3.7 %collective-permute-start.1 = (f32[32,128]{1,0:T(8,128)S(1)}, f32[32,128]{1,0:T(8,128)S(1)}, u32[]{:S(2)}, u32[]{:S(2)}) collective-permute-start(f32[32,128]{1,0:T(8,128)S(1)} %get-tuple-element.73), channel_id=1, source_target_pairs={{0,4},{4,0},{8,12},{12,8},{16,20},{20,16},{24,28},{28,24},{1,5},{5... | collective-permute-start | bytes 49160 | tf_op jit(solution)/shard_map/ppermute | solution.py:617
  8.7 3.7 %collective-permute-start.2 = (f32[32,128]{1,0:T(8,128)S(1)}, f32[32,128]{1,0:T(8,128)S(1)}, u32[]{:S(2)}, u32[]{:S(2)}) collective-permute-start(f32[32,128]{1,0:T(8,128)S(1)} %get-tuple-element.74), channel_id=1, source_target_pairs={{1,2},{2,1},{3,0},{0,3},{5,6},{6,5},{7,4},{4,7},{9,10},{10,9},{11,... | collective-permute-start | bytes 49160 | tf_op jit(solution)/shard_map/ppermute | solution.py:617
  9.4 3.1 %collective-permute-start.3 = (f32[32,128]{1,0:T(8,128)S(1)}, f32[32,128]{1,0:T(8,128)S(1)}, u32[]{:S(2)}, u32[]{:S(2)}) collective-permute-start(f32[32,128]{1,0:T(8,128)S(1)} %get-tuple-element.75), channel_id=1, source_target_pairs={{0,1},{1,0},{2,3},{3,2},{4,5},{5,4},{6,7},{7,6},{8,9},{9,8},{10,11... | collective-permute-start | bytes 49160 | tf_op jit(solution)/shard_map/ppermute | solution.py:617
  14.5 6.4 %collective-permute-start.4 = (f32[16,128]{1,0:T(8,128)S(1)}, f32[16,128]{1,0:T(8,128)S(1)}, u32[]{:S(2)}, u32[]{:S(2)}) collective-permute-start(f32[16,128]{1,0:T(8,128)S(1)} %get-tuple-element.89), channel_id=1, source_target_pairs={{4,8},{8,4},{12,16},{16,12},{20,24},{24,20},{28,0},{0,28},{5,9},{9... | collective-permute-start | bytes 24584 | tf_op jit(solution)/shard_map/ppermute | solution.py:617
  17.3 3.7 %collective-permute-start.5 = (f32[16,128]{1,0:T(8,128)S(1)}, f32[16,128]{1,0:T(8,128)S(1)}, u32[]{:S(2)}, u32[]{:S(2)}) collective-permute-start(f32[16,128]{1,0:T(8,128)S(1)} %get-tuple-element.90), channel_id=1, source_target_pairs={{0,4},{4,0},{8,12},{12,8},{16,20},{20,16},{24,28},{28,24},{1,5},{5... | collective-permute-start | bytes 24584 | tf_op jit(solution)/shard_map/ppermute | solution.py:617
  17.3 3.7 %collective-permute-start.6 = (f32[16,128]{1,0:T(8,128)S(1)}, f32[16,128]{1,0:T(8,128)S(1)}, u32[]{:S(2)}, u32[]{:S(2)}) collective-permute-start(f32[16,128]{1,0:T(8,128)S(1)} %get-tuple-element.91), channel_id=1, source_target_pairs={{1,2},{2,1},{3,0},{0,3},{5,6},{6,5},{7,4},{4,7},{9,10},{10,9},{11,... | collective-permute-start | bytes 24584 | tf_op jit(solution)/shard_map/ppermute | solution.py:617
  17.3 3.7 %collective-permute-start.7 = (f32[16,128]{1,0:T(8,128)S(1)}, f32[16,128]{1,0:T(8,128)S(1)}, u32[]{:S(2)}, u32[]{:S(2)}) collective-permute-start(f32[16,128]{1,0:T(8,128)S(1)} %get-tuple-element.92), channel_id=1, source_target_pairs={{0,1},{1,0},{2,3},{3,2},{4,5},{5,4},{6,7},{7,6},{8,9},{9,8},{10,11... | collective-permute-start | bytes 24584 | tf_op jit(solution)/shard_map/ppermute | solution.py:617

commit v16 on v13

--- a/solution.py
+++ b/solution.py
@@ -104,19 +104,17 @@
     same_half = (from_lane % elements) // ROWS == lane_index((LANES, LANES)) // HALF
     right = one_where(same_half & (from_lane < 2 * elements)).astype(BF16)
     filled = lane_index(stage_ref.shape[1:]) < elements
+    spreads = []
     for row in range(fields):
         for col in range(fields):
             stage_ref[row, col * 4 : col * 4 + kinds, 0:elements] = star_ref[row, col]
         values = jnp.where(filled, stage_ref[row], 0.0)
         stage_ref[row] = high_and_low(values, elements)
-        spreads = []
         for kind in range(kinds):
             for col in range(fields):
                 at = col * 4 + kind
                 spreads.append(stage_ref[row, at : at + 1, :] * pick)
-        spread_out = product(jnp.concatenate(spreads, axis=0).astype(BF16), right)
-        count = kinds * fields
-        star_out[row * count : (row + 1) * count] = spread_out.reshape(count, ROWS, LANES)
+    star_out[...] = product(jnp.concatenate(spreads, axis=0).astype(BF16), right).reshape(star_out.shape)
 
 
 def star_mix(columns, star_ref, fields, kinds):
@@ -152,11 +150,14 @@
     later_out, refs = refs[11 : 11 + later], refs[11 + later :]
     work_ref, late_rows, solution_ref, block_ref, star_ref, send_ref, sems = refs
 
-    sources = (star_hbm, stiffness_hbm, solution_hbm, send_hbm, *later_hbm)
-    targets = (star_ref, stiffness_ref, solution_ref, send_ref, *later_out)
+    pieces = []
+    for source, target in ((star_hbm, star_ref), (stiffness_hbm, stiffness_ref), (solution_hbm, solution_ref)):
+        step = source.shape[0] // 3
+        pieces += [(source.at[pl.ds(at, step)], target.at[pl.ds(at, step)]) for at in range(0, source.shape[0], step)]
+    first = len(pieces)
+    pieces += zip((send_hbm, *later_hbm), (send_ref, *later_out))
     copies = [
-        pltpu.make_async_copy(source, target, sems.at[number])
-        for number, (source, target) in enumerate(zip(sources, targets))
+        pltpu.make_async_copy(source, target, sems.at[number]) for number, (source, target) in enumerate(pieces)
     ]
     for copy in copies:
         copy.start()
@@ -164,7 +165,7 @@
     pairs = (fields + 1) // 2
     for cleared in (packed_ref, block_ref, send_0, send_1, send_2, send_3):
         cleared[...] = jnp.zeros(cleared.shape, F32)
-    for copy in copies[0:3]:
+    for copy in copies[0:first]:
         copy.wait()
     derive_ref[...] = stack_right(stiffness_blocks(stiffness_ref, block_ref, True))
     star_coefficients(star_ref, work_ref, coef_ref)
@@ -186,7 +187,7 @@
     late_out[...] = late.reshape(fields, ROWS, LANES)
     rows_by_pair(early, early_rows, fields)
     rows_by_pair(late, late_rows, fields)
-    copies[3].wait()
+    copies[first].wait()
     sends = send_ref.shape[2]
     fast = sends // 2
     for side, out in enumerate((send_0, send_1, send_2, send_3)):
@@ -199,7 +200,7 @@
                 for pair in range(pairs):
                     row = pairs * sends + pair * fast + place - fast
                     out[row : row + 1, :] = late_rows[pair, pl.ds(element, 1), :]
-    for copy in copies[4:]:
+    for copy in copies[first + 1 :]:
         copy.wait()
 
 
@@ -652,7 +653,7 @@
             ((fields, up_to(4 * fields, ROWS), LANES), F32),
             ((pairs, elements, LANES), F32),
             (values.shape, F32), ((kinds, LANES, LANES), F32), (star.shape, F32),
-            pltpu.SMEM(send_list.shape, jnp.int32), pltpu.SemaphoreType.DMA((4 + len(LATER),)),
+            pltpu.SMEM(send_list.shape, jnp.int32), pltpu.SemaphoreType.DMA((10 + len(LATER),)),
         ],
         (values, stiffness, star, send_list, *waiting),
         "predict", 100_000_000,

time: 22.3 us -> 22.2 us (level)
  no operation moved by 1% of the time
where the time goes in v16:
time: 22.2 us; the launch traced here: 22.1 us
  starting transfers between devices  12.1 us (55%)
  Pallas kernels  8.56 us (39%)
  waiting for transfers between devices  1.38 us (6%)
    ppermute x8, starting transfers between devices, exchange(): arrived.append(lax.ppermute(message, axis, pairs))  12.1 us
    pallas_call x5, Pallas kernels, call(): pl.pallas_call(kernel, out_shape=shapes, in_specs=ins, out_specs=[VMEM] *...  8.56 us
    ppermute x8, waiting for transfers between devices, exchange(): arrived.append(lax.ppermute(message, axis, pairs))  1.38 us
  transfers between devices with their start and end apart: 8, of which 3 were waited for; matrix products, arithmetic and copies ran while one was open for 0% of the time, Pallas kernels for 13%

profile of v16, /device:TPU:0, one launch (start us, length us, event | category | flops | bytes accessed | tf_op | source)
XLA Modules:
  0.0 22.1 jit_solution(7851557594267451479)
XLA Ops:
  0.0 2.7 %predict.1 = (f32[9,8,128]{2,1,0:T(8,128)S(1)}, f32[9,8,128]{2,1,0:T(8,128)S(1)}, f32[32,128]{1,0:T(8,128)S(1)}, f32[32,128]{1,0:T(8,128)S(1)}, f32[32,128]{1,0:...) custom-call(f32[9,16,56]{2,1,0:T(8,128)} %bitcast.11, ...), custom_call_target="tpu_custom_call" | custom-call | flops 100000000 | bytes 4000000 | tf_op jit(solution)/shard_map/predict/pallas_call | solution.py:587
  2.7 6.0 %collective-permute-start = (f32[32,128]{1,0:T(8,128)S(1)}, f32[32,128]{1,0:T(8,128)S(1)}, u32[]{:S(2)}, u32[]{:S(2)}) collective-permute-start(f32[32,128]{1,0:T(8,128)S(1)} %get-tuple-element.72), channel_id=1, source_target_pairs={{4,8},{8,4},{12,16},{16,12},{20,24},{24,20},{28,0},{0,28},{5,9},{9... | collective-permute-start | bytes 49160 | tf_op jit(solution)/shard_map/ppermute | solution.py:608
  8.7 0.0 collective-permute-start.1
  8.7 0.7 %collective-permute-start.2 = (f32[32,128]{1,0:T(8,128)S(1)}, f32[32,128]{1,0:T(8,128)S(1)}, u32[]{:S(2)}, u32[]{:S(2)}) collective-permute-start(f32[32,128]{1,0:T(8,128)S(1)} %get-tuple-element.74), channel_id=1, source_target_pairs={{1,2},{2,1},{3,0},{0,3},{5,6},{6,5},{7,4},{4,7},{9,10},{10,9},{11,... | collective-permute-start | bytes 49160 | tf_op jit(solution)/shard_map/ppermute | solution.py:608
  9.4 1.0 %collective-permute-start.3 = (f32[32,128]{1,0:T(8,128)S(1)}, f32[32,128]{1,0:T(8,128)S(1)}, u32[]{:S(2)}, u32[]{:S(2)}) collective-permute-start(f32[32,128]{1,0:T(8,128)S(1)} %get-tuple-element.75), channel_id=1, source_target_pairs={{0,1},{1,0},{2,3},{3,2},{4,5},{5,4},{6,7},{7,6},{8,9},{9,8},{10,11... | collective-permute-start | bytes 49160 | tf_op jit(solution)/shard_map/ppermute | solution.py:608
  10.4 1.5 %prepare.1 = (f32[9,8,128]{2,1,0:T(8,128)S(1)}, f32[81,2,8,128]{3,2,1,0:T(8,128)S(1)}, f32[180,16,128]{2,1,0:T(8,128)S(1)}, bf16[384,384]{1,0:T(8,128)(2,1)S(1)}...) custom-call(f32[9,8,128]{2,1,0:T(8,128)S(1)} %get-tuple-element.49.p, ...), custom_call_target="tpu_custom_call" | custom-call | flops 200000000 | bytes 4000000 | tf_op jit(solution)/shard_map/prepare/pallas_call | solution.py:587
  11.9 0.0 collective-permute-done.from_0.first_0
  11.9 0.6 %collective-permute-done.1.from_1.first_1 = f32[32,128]{1,0:T(8,128)S(1)} collective-permute-done((f32[32,128]{1,0:T(8,128)S(1)}, f32[32,128]{1,0:T(8,128)S(1)}, u32[]{:S(2)}, u32[]{:S(2)}) %collective-permute-start.1) | collective-permute-done | bytes 16416 | tf_op jit(solution)/shard_map/ppermute | solution.py:608
  12.5 0.0 collective-permute-done.2.from_2.first_2
  12.5 0.0 collective-permute-done.3.from_3.first_3
  12.5 2.0 %middle.1 = (f32[9,8,128]{2,1,0:T(8,128)S(1)}, f32[9,8,128]{2,1,0:T(8,128)S(1)}, f32[16,128]{1,0:T(8,128)S(1)}, f32[16,128]{1,0:T(8,128)S(1)}, f32[16,128]{1,0:T(8,128)S(1)}, /*index=5*/f32[16,128]{1,0:T(8,128)S(1)}) custom-call(f32[9,8,128]{2,1,0:T(8,128)S(1)} %get-tuple-element.62.base_ref, f32[5,16,128]{2,1,0:T(8,128)S(1)} %get-tuple-element.63.early_rows, ...), custom_call_target="tpu_custom_call" | custom-call | flops 200000000 | bytes 4000000 | tf_op jit(solution)/shard_map/middle/pallas_call | solution.py:587
  14.5 2.8 %collective-permute-start.4 = (f32[16,128]{1,0:T(8,128)S(1)}, f32[16,128]{1,0:T(8,128)S(1)}, u32[]{:S(2)}, u32[]{:S(2)}) collective-permute-start(f32[16,128]{1,0:T(8,128)S(1)} %get-tuple-element.89), channel_id=1, source_target_pairs={{4,8},{8,4},{12,16},{16,12},{20,24},{24,20},{28,0},{0,28},{5,9},{9... | collective-permute-start | bytes 24584 | tf_op jit(solution)/shard_map/ppermute | solution.py:608
  17.3 0.0 collective-permute-start.5
  17.3 0.0 collective-permute-start.6
  17.3 1.6 %collective-permute-start.7 = (f32[16,128]{1,0:T(8,128)S(1)}, f32[16,128]{1,0:T(8,128)S(1)}, u32[]{:S(2)}, u32[]{:S(2)}) collective-permute-start(f32[16,128]{1,0:T(8,128)S(1)} %get-tuple-element.92), channel_id=1, source_target_pairs={{0,1},{1,0},{2,3},{3,2},{4,5},{5,4},{6,7},{7,6},{8,9},{9,8},{10,11... | collective-permute-start | bytes 24584 | tf_op jit(solution)/shard_map/ppermute | solution.py:608
  18.9 1.3 %local_late.1 = (f32[9,16,128]{2,1,0:T(8,128)S(1)}, f32[144,512]{1,0:T(8,128)S(1)}, bf16[4,384,256]{2,1,0:T(8,128)(2,1)S(1)}, bf16[144,256]{1,0:T(8,128)(2,1)S(1)}) custom-call(f32[9,8,128]{2,1,0:T(8,128)S(1)} %get-tuple-element.76.middle_ref, f32[9,8,128]{2,1,0:T(8,128)S(1)} %get-tuple-element.77.late_ref, f32[243,8,128]{2,1,0:T(8,128)S(1)} %get-tuple-element.52.star_ref, ...), custom_call_target="tpu_custom_call" | custom-call | flops 200000000 | bytes 4000000 | tf_op jit(solution)/shard_map/local_late/pallas_call | solution.py:587
  20.2 0.7 %collective-permute-done.4.second_0 = f32[16,128]{1,0:T(8,128)S(1)} collective-permute-done((f32[16,128]{1,0:T(8,128)S(1)}, f32[16,128]{1,0:T(8,128)S(1)}, u32[]{:S(2)}, u32[]{:S(2)}) %collective-permute-start.4) | collective-permute-done | bytes 8224 | tf_op jit(solution)/shard_map/ppermute | solution.py:608
  20.9 0.1 collective-permute-done.5.second_1
  21.0 0.0 collective-permute-done.6.second_2
  21.0 0.0 collective-permute-done.7.second_3
  21.0 1.0 %final.1 = f32[9,16,56]{2,1,0:T(8,128)} custom-call(f32[9,16,128]{2,1,0:T(8,128)S(1)} %get-tuple-element.85.base_ref, f32[144,512]{1,0:T(8,128)S(1)} %get-tuple-element.86.ghost_flux_ref, bf16[4,384,256]{2,1,0:T(8,128)(2,1)S(1)} %get-tuple-element.87.ghost_operator_ref, bf16[144,256]{1,0:T(8,128)(2,1)S(1)} %get-tuple-element.88.scatter_ref, ...), custom_call_target="tpu_custom_call" | custom-call | flops 200000000 | bytes 4000000 | tf_op jit(solution)/shard_map/final/pallas_call | solution.py:587
Async XLA Ops:
  2.7 9.2 %collective-permute-start = (f32[32,128]{1,0:T(8,128)S(1)}, f32[32,128]{1,0:T(8,128)S(1)}, u32[]{:S(2)}, u32[]{:S(2)}) collective-permute-start(f32[32,128]{1,0:T(8,128)S(1)} %get-tuple-element.72), channel_id=1, source_target_pairs={{4,8},{8,4},{12,16},{16,12},{20,24},{24,20},{28,0},{0,28},{5,9},{9... | collective-permute-start | bytes 49160 | tf_op jit(solution)/shard_map/ppermute | solution.py:608
  8.7 3.7 %collective-permute-start.1 = (f32[32,128]{1,0:T(8,128)S(1)}, f32[32,128]{1,0:T(8,128)S(1)}, u32[]{:S(2)}, u32[]{:S(2)}) collective-permute-start(f32[32,128]{1,0:T(8,128)S(1)} %get-tuple-element.73), channel_id=1, source_target_pairs={{0,4},{4,0},{8,12},{12,8},{16,20},{20,16},{24,28},{28,24},{1,5},{5... | collective-permute-start | bytes 49160 | tf_op jit(solution)/shard_map/ppermute | solution.py:608
  8.7 3.7 %collective-permute-start.2 = (f32[32,128]{1,0:T(8,128)S(1)}, f32[32,128]{1,0:T(8,128)S(1)}, u32[]{:S(2)}, u32[]{:S(2)}) collective-permute-start(f32[32,128]{1,0:T(8,128)S(1)} %get-tuple-element.74), channel_id=1, source_target_pairs={{1,2},{2,1},{3,0},{0,3},{5,6},{6,5},{7,4},{4,7},{9,10},{10,9},{11,... | collective-permute-start | bytes 49160 | tf_op jit(solution)/shard_map/ppermute | solution.py:608
  9.4 3.1 %collective-permute-start.3 = (f32[32,128]{1,0:T(8,128)S(1)}, f32[32,128]{1,0:T(8,128)S(1)}, u32[]{:S(2)}, u32[]{:S(2)}) collective-permute-start(f32[32,128]{1,0:T(8,128)S(1)} %get-tuple-element.75), channel_id=1, source_target_pairs={{0,1},{1,0},{2,3},{3,2},{4,5},{5,4},{6,7},{7,6},{8,9},{9,8},{10,11... | collective-permute-start | bytes 49160 | tf_op jit(solution)/shard_map/ppermute | solution.py:608
  14.5 6.4 %collective-permute-start.4 = (f32[16,128]{1,0:T(8,128)S(1)}, f32[16,128]{1,0:T(8,128)S(1)}, u32[]{:S(2)}, u32[]{:S(2)}) collective-permute-start(f32[16,128]{1,0:T(8,128)S(1)} %get-tuple-element.89), channel_id=1, source_target_pairs={{4,8},{8,4},{12,16},{16,12},{20,24},{24,20},{28,0},{0,28},{5,9},{9... | collective-permute-start | bytes 24584 | tf_op jit(solution)/shard_map/ppermute | solution.py:608
  17.3 3.7 %collective-permute-start.5 = (f32[16,128]{1,0:T(8,128)S(1)}, f32[16,128]{1,0:T(8,128)S(1)}, u32[]{:S(2)}, u32[]{:S(2)}) collective-permute-start(f32[16,128]{1,0:T(8,128)S(1)} %get-tuple-element.90), channel_id=1, source_target_pairs={{0,4},{4,0},{8,12},{12,8},{16,20},{20,16},{24,28},{28,24},{1,5},{5... | collective-permute-start | bytes 24584 | tf_op jit(solution)/shard_map/ppermute | solution.py:608
  17.3 3.7 %collective-permute-start.6 = (f32[16,128]{1,0:T(8,128)S(1)}, f32[16,128]{1,0:T(8,128)S(1)}, u32[]{:S(2)}, u32[]{:S(2)}) collective-permute-start(f32[16,128]{1,0:T(8,128)S(1)} %get-tuple-element.91), channel_id=1, source_target_pairs={{1,2},{2,1},{3,0},{0,3},{5,6},{6,5},{7,4},{4,7},{9,10},{10,9},{11,... | collective-permute-start | bytes 24584 | tf_op jit(solution)/shard_map/ppermute | solution.py:608
  17.3 3.7 %collective-permute-start.7 = (f32[16,128]{1,0:T(8,128)S(1)}, f32[16,128]{1,0:T(8,128)S(1)}, u32[]{:S(2)}, u32[]{:S(2)}) collective-permute-start(f32[16,128]{1,0:T(8,128)S(1)} %get-tuple-element.92), channel_id=1, source_target_pairs={{0,1},{1,0},{2,3},{3,2},{4,5},{5,4},{6,7},{7,6},{8,9},{9,8},{10,11... | collective-permute-start | bytes 24584 | tf_op jit(solution)/shard_map/ppermute | solution.py:608

commit v17 on v16

--- a/solution.py
+++ b/solution.py
@@ -104,17 +104,19 @@
     same_half = (from_lane % elements) // ROWS == lane_index((LANES, LANES)) // HALF
     right = one_where(same_half & (from_lane < 2 * elements)).astype(BF16)
     filled = lane_index(stage_ref.shape[1:]) < elements
-    spreads = []
     for row in range(fields):
         for col in range(fields):
             stage_ref[row, col * 4 : col * 4 + kinds, 0:elements] = star_ref[row, col]
         values = jnp.where(filled, stage_ref[row], 0.0)
         stage_ref[row] = high_and_low(values, elements)
+        spreads = []
         for kind in range(kinds):
             for col in range(fields):
                 at = col * 4 + kind
                 spreads.append(stage_ref[row, at : at + 1, :] * pick)
-    star_out[...] = product(jnp.concatenate(spreads, axis=0).astype(BF16), right).reshape(star_out.shape)
+        spread_out = product(jnp.concatenate(spreads, axis=0).astype(BF16), right)
+        count = kinds * fields
+        star_out[row * count : (row + 1) * count] = spread_out.reshape(count, ROWS, LANES)
 
 
 def star_mix(columns, star_ref, fields, kinds):
@@ -484,6 +486,8 @@
 ):
     copy = pltpu.make_async_copy(send_hbm, send_ref, sem)
     copy.start()
+    for cleared in (send_0, send_1, send_2, send_3):
+        cleared[...] = jnp.zeros(cleared.shape, F32)
     fields = base_ref.shape[0]
     kinds = star_ref.shape[0] // (fields * fields)
     pairs = rows_ref.shape[0]
@@ -514,7 +518,6 @@
     late_rows[:, ROWS : 2 * ROWS, :] = jnp.where(wide, swapped, both).reshape(late.shape)
     first_half = lower_half((1, LANES))
     for slot, out in enumerate((send_0, send_1, send_2, send_3)):
-        out[...] = jnp.zeros(out.shape, F32)
         side = message_side(slot)
         places = [send_ref[0, side, place] for place in range(fast)]
         for field in range(fields):

time: 22.2 us -> 22.2 us (level)
  no operation moved by 1% of the time
where the time goes in v17:
time: 22.2 us; the launch traced here: 22.1 us
  starting transfers between devices  12.1 us (55%)
  Pallas kernels  8.56 us (39%)
  waiting for transfers between devices  1.39 us (6%)
    ppermute x8, starting transfers between devices, exchange(): arrived.append(lax.ppermute(message, axis, pairs))  12.1 us
    pallas_call x5, Pallas kernels, call(): pl.pallas_call(kernel, out_shape=shapes, in_specs=ins, out_specs=[VMEM] *...  8.56 us
    ppermute x8, waiting for transfers between devices, exchange(): arrived.append(lax.ppermute(message, axis, pairs))  1.39 us
  transfers between devices with their start and end apart: 8, of which 3 were waited for; matrix products, arithmetic and copies ran while one was open for 0% of the time, Pallas kernels for 13%

profile of v17, /device:TPU:0, one launch (start us, length us, event | category | flops | bytes accessed | tf_op | source)
XLA Modules:
  0.0 22.1 jit_solution(4396957496586622626)
XLA Ops:
  0.0 2.7 %predict.1 = (f32[9,8,128]{2,1,0:T(8,128)S(1)}, f32[9,8,128]{2,1,0:T(8,128)S(1)}, f32[32,128]{1,0:T(8,128)S(1)}, f32[32,128]{1,0:T(8,128)S(1)}, f32[32,128]{1,0:...) custom-call(f32[9,16,56]{2,1,0:T(8,128)} %bitcast.11, ...), custom_call_target="tpu_custom_call" | custom-call | flops 100000000 | bytes 4000000 | tf_op jit(solution)/shard_map/predict/pallas_call | solution.py:590
  2.7 6.0 %collective-permute-start = (f32[32,128]{1,0:T(8,128)S(1)}, f32[32,128]{1,0:T(8,128)S(1)}, u32[]{:S(2)}, u32[]{:S(2)}) collective-permute-start(f32[32,128]{1,0:T(8,128)S(1)} %get-tuple-element.72), channel_id=1, source_target_pairs={{4,8},{8,4},{12,16},{16,12},{20,24},{24,20},{28,0},{0,28},{5,9},{9... | collective-permute-start | bytes 49160 | tf_op jit(solution)/shard_map/ppermute | solution.py:611
  8.7 0.0 collective-permute-start.1
  8.7 0.7 %collective-permute-start.2 = (f32[32,128]{1,0:T(8,128)S(1)}, f32[32,128]{1,0:T(8,128)S(1)}, u32[]{:S(2)}, u32[]{:S(2)}) collective-permute-start(f32[32,128]{1,0:T(8,128)S(1)} %get-tuple-element.74), channel_id=1, source_target_pairs={{1,2},{2,1},{3,0},{0,3},{5,6},{6,5},{7,4},{4,7},{9,10},{10,9},{11,... | collective-permute-start | bytes 49160 | tf_op jit(solution)/shard_map/ppermute | solution.py:611
  9.4 1.0 %collective-permute-start.3 = (f32[32,128]{1,0:T(8,128)S(1)}, f32[32,128]{1,0:T(8,128)S(1)}, u32[]{:S(2)}, u32[]{:S(2)}) collective-permute-start(f32[32,128]{1,0:T(8,128)S(1)} %get-tuple-element.75), channel_id=1, source_target_pairs={{0,1},{1,0},{2,3},{3,2},{4,5},{5,4},{6,7},{7,6},{8,9},{9,8},{10,11... | collective-permute-start | bytes 49160 | tf_op jit(solution)/shard_map/ppermute | solution.py:611
  10.4 1.5 %prepare.1 = (f32[9,8,128]{2,1,0:T(8,128)S(1)}, f32[81,2,8,128]{3,2,1,0:T(8,128)S(1)}, f32[180,16,128]{2,1,0:T(8,128)S(1)}, bf16[384,384]{1,0:T(8,128)(2,1)S(1)}...) custom-call(f32[9,8,128]{2,1,0:T(8,128)S(1)} %get-tuple-element.49.p, ...), custom_call_target="tpu_custom_call" | custom-call | flops 200000000 | bytes 4000000 | tf_op jit(solution)/shard_map/prepare/pallas_call | solution.py:590
  11.9 0.0 collective-permute-done.from_0.first_0
  11.9 0.6 %collective-permute-done.1.from_1.first_1 = f32[32,128]{1,0:T(8,128)S(1)} collective-permute-done((f32[32,128]{1,0:T(8,128)S(1)}, f32[32,128]{1,0:T(8,128)S(1)}, u32[]{:S(2)}, u32[]{:S(2)}) %collective-permute-start.1) | collective-permute-done | bytes 16416 | tf_op jit(solution)/shard_map/ppermute | solution.py:611
  12.5 0.0 collective-permute-done.2.from_2.first_2
  12.5 0.0 collective-permute-done.3.from_3.first_3
  12.5 2.0 %middle.1 = (f32[9,8,128]{2,1,0:T(8,128)S(1)}, f32[9,8,128]{2,1,0:T(8,128)S(1)}, f32[16,128]{1,0:T(8,128)S(1)}, f32[16,128]{1,0:T(8,128)S(1)}, f32[16,128]{1,0:T(8,128)S(1)}, /*index=5*/f32[16,128]{1,0:T(8,128)S(1)}) custom-call(f32[9,8,128]{2,1,0:T(8,128)S(1)} %get-tuple-element.62.base_ref, f32[5,16,128]{2,1,0:T(8,128)S(1)} %get-tuple-element.63.early_rows, ...), custom_call_target="tpu_custom_call" | custom-call | flops 200000000 | bytes 4000000 | tf_op jit(solution)/shard_map/middle/pallas_call | solution.py:590
  14.5 2.8 %collective-permute-start.4 = (f32[16,128]{1,0:T(8,128)S(1)}, f32[16,128]{1,0:T(8,128)S(1)}, u32[]{:S(2)}, u32[]{:S(2)}) collective-permute-start(f32[16,128]{1,0:T(8,128)S(1)} %get-tuple-element.89), channel_id=1, source_target_pairs={{4,8},{8,4},{12,16},{16,12},{20,24},{24,20},{28,0},{0,28},{5,9},{9... | collective-permute-start | bytes 24584 | tf_op jit(solution)/shard_map/ppermute | solution.py:611
  17.3 0.0 collective-permute-start.5
  17.3 0.0 collective-permute-start.6
  17.3 1.6 %collective-permute-start.7 = (f32[16,128]{1,0:T(8,128)S(1)}, f32[16,128]{1,0:T(8,128)S(1)}, u32[]{:S(2)}, u32[]{:S(2)}) collective-permute-start(f32[16,128]{1,0:T(8,128)S(1)} %get-tuple-element.92), channel_id=1, source_target_pairs={{0,1},{1,0},{2,3},{3,2},{4,5},{5,4},{6,7},{7,6},{8,9},{9,8},{10,11... | collective-permute-start | bytes 24584 | tf_op jit(solution)/shard_map/ppermute | solution.py:611
  18.9 1.3 %local_late.1 = (f32[9,16,128]{2,1,0:T(8,128)S(1)}, f32[144,512]{1,0:T(8,128)S(1)}, bf16[4,384,256]{2,1,0:T(8,128)(2,1)S(1)}, bf16[144,256]{1,0:T(8,128)(2,1)S(1)}) custom-call(f32[9,8,128]{2,1,0:T(8,128)S(1)} %get-tuple-element.76.middle_ref, f32[9,8,128]{2,1,0:T(8,128)S(1)} %get-tuple-element.77.late_ref, f32[243,8,128]{2,1,0:T(8,128)S(1)} %get-tuple-element.52.star_ref, ...), custom_call_target="tpu_custom_call" | custom-call | flops 200000000 | bytes 4000000 | tf_op jit(solution)/shard_map/local_late/pallas_call | solution.py:590
  20.2 0.7 %collective-permute-done.4.second_0 = f32[16,128]{1,0:T(8,128)S(1)} collective-permute-done((f32[16,128]{1,0:T(8,128)S(1)}, f32[16,128]{1,0:T(8,128)S(1)}, u32[]{:S(2)}, u32[]{:S(2)}) %collective-permute-start.4) | collective-permute-done | bytes 8224 | tf_op jit(solution)/shard_map/ppermute | solution.py:611
  20.9 0.1 collective-permute-done.5.second_1
  21.0 0.0 collective-permute-done.6.second_2
  21.0 0.0 collective-permute-done.7.second_3
  21.0 1.0 %final.1 = f32[9,16,56]{2,1,0:T(8,128)} custom-call(f32[9,16,128]{2,1,0:T(8,128)S(1)} %get-tuple-element.85.base_ref, f32[144,512]{1,0:T(8,128)S(1)} %get-tuple-element.86.ghost_flux_ref, bf16[4,384,256]{2,1,0:T(8,128)(2,1)S(1)} %get-tuple-element.87.ghost_operator_ref, bf16[144,256]{1,0:T(8,128)(2,1)S(1)} %get-tuple-element.88.scatter_ref, ...), custom_call_target="tpu_custom_call" | custom-call | flops 200000000 | bytes 4000000 | tf_op jit(solution)/shard_map/final/pallas_call | solution.py:590
Async XLA Ops:
  2.7 9.2 %collective-permute-start = (f32[32,128]{1,0:T(8,128)S(1)}, f32[32,128]{1,0:T(8,128)S(1)}, u32[]{:S(2)}, u32[]{:S(2)}) collective-permute-start(f32[32,128]{1,0:T(8,128)S(1)} %get-tuple-element.72), channel_id=1, source_target_pairs={{4,8},{8,4},{12,16},{16,12},{20,24},{24,20},{28,0},{0,28},{5,9},{9... | collective-permute-start | bytes 49160 | tf_op jit(solution)/shard_map/ppermute | solution.py:611
  8.7 3.7 %collective-permute-start.1 = (f32[32,128]{1,0:T(8,128)S(1)}, f32[32,128]{1,0:T(8,128)S(1)}, u32[]{:S(2)}, u32[]{:S(2)}) collective-permute-start(f32[32,128]{1,0:T(8,128)S(1)} %get-tuple-element.73), channel_id=1, source_target_pairs={{0,4},{4,0},{8,12},{12,8},{16,20},{20,16},{24,28},{28,24},{1,5},{5... | collective-permute-start | bytes 49160 | tf_op jit(solution)/shard_map/ppermute | solution.py:611
  8.7 3.7 %collective-permute-start.2 = (f32[32,128]{1,0:T(8,128)S(1)}, f32[32,128]{1,0:T(8,128)S(1)}, u32[]{:S(2)}, u32[]{:S(2)}) collective-permute-start(f32[32,128]{1,0:T(8,128)S(1)} %get-tuple-element.74), channel_id=1, source_target_pairs={{1,2},{2,1},{3,0},{0,3},{5,6},{6,5},{7,4},{4,7},{9,10},{10,9},{11,... | collective-permute-start | bytes 49160 | tf_op jit(solution)/shard_map/ppermute | solution.py:611
  9.4 3.1 %collective-permute-start.3 = (f32[32,128]{1,0:T(8,128)S(1)}, f32[32,128]{1,0:T(8,128)S(1)}, u32[]{:S(2)}, u32[]{:S(2)}) collective-permute-start(f32[32,128]{1,0:T(8,128)S(1)} %get-tuple-element.75), channel_id=1, source_target_pairs={{0,1},{1,0},{2,3},{3,2},{4,5},{5,4},{6,7},{7,6},{8,9},{9,8},{10,11... | collective-permute-start | bytes 49160 | tf_op jit(solution)/shard_map/ppermute | solution.py:611
  14.5 6.4 %collective-permute-start.4 = (f32[16,128]{1,0:T(8,128)S(1)}, f32[16,128]{1,0:T(8,128)S(1)}, u32[]{:S(2)}, u32[]{:S(2)}) collective-permute-start(f32[16,128]{1,0:T(8,128)S(1)} %get-tuple-element.89), channel_id=1, source_target_pairs={{4,8},{8,4},{12,16},{16,12},{20,24},{24,20},{28,0},{0,28},{5,9},{9... | collective-permute-start | bytes 24584 | tf_op jit(solution)/shard_map/ppermute | solution.py:611
  17.3 3.7 %collective-permute-start.5 = (f32[16,128]{1,0:T(8,128)S(1)}, f32[16,128]{1,0:T(8,128)S(1)}, u32[]{:S(2)}, u32[]{:S(2)}) collective-permute-start(f32[16,128]{1,0:T(8,128)S(1)} %get-tuple-element.90), channel_id=1, source_target_pairs={{0,4},{4,0},{8,12},{12,8},{16,20},{20,16},{24,28},{28,24},{1,5},{5... | collective-permute-start | bytes 24584 | tf_op jit(solution)/shard_map/ppermute | solution.py:611
  17.3 3.7 %collective-permute-start.6 = (f32[16,128]{1,0:T(8,128)S(1)}, f32[16,128]{1,0:T(8,128)S(1)}, u32[]{:S(2)}, u32[]{:S(2)}) collective-permute-start(f32[16,128]{1,0:T(8,128)S(1)} %get-tuple-element.91), channel_id=1, source_target_pairs={{1,2},{2,1},{3,0},{0,3},{5,6},{6,5},{7,4},{4,7},{9,10},{10,9},{11,... | collective-permute-start | bytes 24584 | tf_op jit(solution)/shard_map/ppermute | solution.py:611
  17.3 3.7 %collective-permute-start.7 = (f32[16,128]{1,0:T(8,128)S(1)}, f32[16,128]{1,0:T(8,128)S(1)}, u32[]{:S(2)}, u32[]{:S(2)}) collective-permute-start(f32[16,128]{1,0:T(8,128)S(1)} %get-tuple-element.92), channel_id=1, source_target_pairs={{0,1},{1,0},{2,3},{3,2},{4,5},{5,4},{6,7},{7,6},{8,9},{9,8},{10,11... | collective-permute-start | bytes 24584 | tf_op jit(solution)/shard_map/ppermute | solution.py:611
